TPU v7x, 32 devices: a whole 2x2x4 slice. The times are simulated.
32 devices in a mesh: section: 4 (over x, core), mp: 8 (over z, y).
Axes of the slice: x: 2, y: 2, z: 4, core: 2. Of those that a mesh axis runs over, the one named last changes fastest.
Arguments:
- text_state: bfloat16 [4, 512, 8192], P('section', 'mp'), may hold values from -1.5 to 1.5
- tile_feats: bfloat16 [1280, 7680], P('section', 'mp'), may hold values from -6 to 6
- w_proj: bfloat16 [7680, 8192], P('mp'), may hold values from -0.0625 to 0.0625
- w_query: bfloat16 [4, 8192, 4096], P('section', None, 'mp'), may hold values from -0.0625 to 0.0625
- w_kv: bfloat16 [4, 8192, 1024], P('section', 'mp'), may hold values from -0.0625 to 0.0625
- w_out: bfloat16 [4, 4096, 8192], P('section', 'mp'), may hold values from -0.09375 to 0.09375
- attn_gate: float32 [4], P('section'), may hold values from 0.3 to 1.5
- tile_counts: int32 [16], replicated, may hold values from 1 to 4, 40 in all
- section_table: int32 [16], replicated, may hold values from 0 to 3, as said below
Outputs:
- advanced: bfloat16 [4, 512, 8192], P('section', 'mp')
Inputs may be any that keep to these rules, and one draw needn't show every extreme that they name: `section_table`: each section is named by exactly 4 samples. `tile_counts`: the counts add up to 40, and some sample has exactly 4 tiles.
All inputs are finite; a program needn't handle non-finite values.
Results may differ from a plain program's by a relative error of at most 0.02.
Values may be sent and summed in bfloat16 or wider, within the bound.
No kernel may reach another device: no remote copies, remote signals or barrier semaphores. Data moves between devices by JAX's collectives and lax.ppermute only.
A program may use at most 128 MiB of HBM per device.

v0:
```python
import math

import jax
import jax.numpy as jnp
from jax import lax
from jax.sharding import PartitionSpec as P

HD = 128
HEADS = 32
KVH = 4
SAMP_SECTION = 4
TXT = 128
TT = 32
MAXT = 4


def shifted(value, axis, by):
    length = lax.axis_size(axis)
    return lax.ppermute(value, axis, [(i, (i + by) % length) for i in range(length)])


def root_scale(values, epsilon):
    return values * lax.rsqrt(jnp.mean(values * values, axis=-1, keepdims=True) + epsilon)


def slot_index(tile_counts, section_table, section_id):
    samples_all = tile_counts.shape[0]
    sample_ids = jnp.arange(samples_all, dtype=jnp.int32)
    same_section = section_table[None, :] == section_table[:, None]
    before = sample_ids[None, :] < sample_ids[:, None]
    ranking = jnp.sum((same_section & before).astype(jnp.int32), axis=1)
    picked = (section_table[None, :] == section_id) & (
        ranking[None, :] == jnp.arange(SAMP_SECTION, dtype=jnp.int32)[:, None]
    )
    first_row = TT * (jnp.cumsum(tile_counts) - tile_counts)
    counts_own = jnp.sum(jnp.where(picked, tile_counts[None, :], 0), axis=1)
    starts_own = jnp.sum(jnp.where(picked, first_row[None, :], 0), axis=1)
    offsets = jnp.arange(MAXT * TT, dtype=jnp.int32)
    live_slot = offsets[None, :] < (TT * counts_own)[:, None]
    row_index = jnp.where(live_slot, starts_own[:, None] + offsets[None, :], 0)
    return (row_index.reshape(-1), live_slot)


def local(
    text_state, tile_feats, w_proj, w_query, w_kv, w_out, attn_gate, tile_counts, section_table
):
    mp_count = lax.axis_size("mp")
    section_id = lax.axis_index("section")
    mp_place = lax.axis_index("mp")
    row_index, live_slot = slot_index(tile_counts, section_table, section_id)
    live_flat = live_slot.reshape(-1)
    every_feat = lax.all_gather(tile_feats, "section", axis=0, tiled=True)
    slot_feats = jnp.where(live_flat[:, None], jnp.take(every_feat, row_index, axis=0), 0)
    image_cols = lax.psum_scatter(
        lax.dot_general(
            w_proj, slot_feats, (((0,), (1,)), ((), ())), preferred_element_type=jnp.float32
        ).astype(jnp.bfloat16),
        "mp",
        scatter_dimension=0,
        tiled=True,
    )
    weight_kv = w_kv[0]
    half_width = weight_kv.shape[1] // 2
    chosen = image_cols
    kv_whole = lax.psum(
        lax.dot_general(
            chosen, weight_kv, (((0,), (0,)), ((), ())), preferred_element_type=jnp.float32
        ).astype(jnp.bfloat16),
        "mp",
    ).astype(jnp.float32)
    row_count = kv_whole.shape[0]
    keys_part = root_scale(kv_whole[:, :half_width].reshape(row_count, KVH, HD), 1e-06)
    keys_part = keys_part.reshape(row_count, half_width).astype(jnp.bfloat16)
    values_all = kv_whole[:, half_width:].astype(jnp.bfloat16)
    head_dev = HEADS // mp_count
    group_size = HEADS // KVH
    kv_head = mp_place * head_dev // group_size
    own_keys = lax.dynamic_slice_in_dim(keys_part, kv_head * HD, HD, 1)
    own_values = lax.dynamic_slice_in_dim(values_all, kv_head * HD, HD, 1)
    weight_query = w_query[0]
    normed = root_scale(
        lax.all_gather(text_state[0], "mp", axis=0, tiled=True).astype(jnp.float32), 1e-05
    ).astype(jnp.bfloat16)
    projected = jnp.dot(normed, weight_query, preferred_element_type=jnp.float32)
    row_count = projected.shape[0]
    projected = root_scale(projected.reshape(row_count, head_dev, HD), 1e-06)
    queries = projected.reshape(row_count, head_dev * HD).astype(jnp.bfloat16)
    query_grid = queries.reshape(SAMP_SECTION, TXT, head_dev, HD)
    key_grid = own_keys.reshape(SAMP_SECTION, MAXT * TT, HD)
    value_grid = own_values.reshape(SAMP_SECTION, MAXT * TT, HD)
    scores = jnp.einsum(
        "sthd,skd->shtk", query_grid, key_grid, preferred_element_type=jnp.float32
    ) / math.sqrt(HD)
    raised = jnp.where(live_slot[:, None, None, :], jnp.exp(scores), 0.0)
    weights = (raised / jnp.sum(raised, axis=-1, keepdims=True)).astype(jnp.bfloat16)
    attended = jnp.einsum("shtk,skd->sthd", weights, value_grid, preferred_element_type=jnp.float32)
    attended = attended.astype(jnp.bfloat16).reshape(SAMP_SECTION * TXT, head_dev * HD)
    weight_out = w_out[0]
    chosen = attended
    branch = lax.psum_scatter(
        jnp.dot(chosen, weight_out, preferred_element_type=jnp.float32).astype(jnp.bfloat16),
        "mp",
        scatter_dimension=0,
        tiled=True,
    ).astype(jnp.float32)
    result = (text_state[0].astype(jnp.float32) + jnp.tanh(attn_gate[0]) * branch).astype(
        jnp.bfloat16
    )
    moved = shifted(result, "section", 1)
    return moved[None]


def solution(mesh):
    return jax.shard_map(
        local,
        mesh=mesh,
        in_specs=(
            P("section", "mp", None),
            P("section", "mp"),
            P("mp", None),
            P("section", None, "mp"),
            P("section", "mp", None),
            P("section", "mp", None),
            P("section"),
            P(),
            P(),
        ),
        out_specs=P("section", "mp", None),
        check_vma=False,
    )
```

profile of v0, /device:TPU:0, one launch (start us, length us, event | category | flops | bytes accessed | tf_op | source)
XLA Modules:
  0.0 583.1 jit_solution(4649220842544456504)
XLA Ops:
  6.5 0.7 all-gather.4.cloned.1.call-update
  7.3 0.7 all-gather.6.cloned.1.call-update
  8.1 0.7 copy.45
  9.0 0.9 convert_reduce_fusion
  9.9 0.7 broadcast_compare_fusion
  10.5 0.7 subtract_multiply_fusion
  11.2 0.8 select_reduce_fusion.1
  12.2 25.0 %all-gather.4.cloned.1.call-done = bf16[1280,960]{1,0:T(8,128)(2,1)} async-done(((bf16[320,960]{1,0:T(8,128)(2,1)}), bf16[1280,960]{1,0:T(8,128)(2,1)}) %all-gather.4.cloned.1.call-update) | async-done | bytes 2457616 | tf_op jit(solution)/shard_map/all_gather | solution.py:52
  37.2 4.8 gather_fusion
  42.0 17.2 %fusion.2 = bf16[8192,512]{0,1:T(8,128)(2,1)} fusion(bf16[960,8192]{1,0:T(8,128)(2,1)} %param.11, bf16[512,960]{1,0:T(8,128)(2,1)S(1)} %gather_fusion, pred[512]{0:T(512)(128)(4,1)S(1)} %compare_and_fusion, pred[512]{0:T(512)(128)(4,1)S(1)} %get-tuple-element.10), kind=kOutput, calls=%fused_computation.7 | convolution fusion | flops 8058241024 | bytes 25101312 | tf_op jit(solution)/shard_map/dot_general | solution.py:55
  59.3 11.4 %copy.58 = bf16[512,8192]{1,0:T(8,128)(2,1)} copy(bf16[512,8192]{0,1:T(8,128)(2,1)} %bitcast.75) | data formatting | bytes 16777216 | tf_op jit(solution)/shard_map/dot_general | solution.py:84
  70.7 93.6 %all-gather.6.cloned.1.call-done = bf16[1,512,8192]{2,1,0:T(8,128)(2,1)} async-done(((bf16[1,64,8192]{2,1,0:T(8,128)(2,1)}), bf16[1,512,8192]{2,1,0:T(8,128)(2,1)}) %all-gather.6.cloned.1.call-update) | async-done | bytes 8388624 | tf_op jit(solution)/shard_map/all_gather | solution.py:82
  164.3 5.1 fusion
  169.4 146.2 %reduce-scatter.3.cloned.1.call-done = bf16[1024,512]{0,1:T(8,128)(2,1)} async-done(((bf16[8192,512]{0,1:T(8,128)(2,1)}), bf16[1024,512]{0,1:T(8,128)(2,1)}) %reduce-scatter.3.cloned.1.call-update) | async-done | bytes 1048592 | tf_op jit(solution)/shard_map/reduce_scatter | solution.py:54
  315.6 3.4 fusion.12
  319.3 8.8 %multiply_reduce_fusion = (f32[512,4]{0,1:T(4,128)S(1)}, f32[512,4,128]{2,0,1:T(8,128)S(1)}) fusion(bf16[4,128,8192]{2,1,0:T(8,128)(2,1)} %bitcast.76, bf16[1,512,8192]{2,1,0:T(8,128)(2,1)} %all-gather.6.cloned.1.call-done, f32[512]{0:T(512)S(1)} %add_rsqrt_fusion.2), kind=kOutput, calls=%fused_computation.27 | convolution fusion | flops 4308072448 | bytes 17836032 | tf_op jit(solution)/shard_map/dot_general | solution.py:84
  328.2 1.1 multiply_convert_fusion
  329.3 67.1 %all-reduce.2.cloned.1.call-done = bf16[512,1024]{1,0:T(8,128)(2,1)} async-done(((bf16[512,1024]{1,0:T(8,128)(2,1)}), bf16[512,1024]{1,0:T(8,128)(2,1)}) %all-reduce.2.cloned.1.call-update) | async-done | bytes 1048592 | tf_op jit(solution)/shard_map/psum | solution.py:65
  396.4 1.3 fusion.30
  400.7 10.2 %convolution_convert_fusion = bf16[512,8192]{1,0:T(8,128)(2,1)} fusion(bf16[1,512,8192]{2,1,0:T(8,128)(2,1)} %param.14, bf16[64,8,4,128]{3,2,1,0:T(4,128)(2,1)S(1)} %bitcast.81), kind=kOutput, calls=%fused_computation.5 | convolution fusion | flops 4299161600 | bytes 17301504 | tf_op jit(solution)/shard_map/dot_general | solution.py:101
  411.8 148.0 %reduce-scatter.5.cloned.1.call-done = bf16[64,8192]{1,0:T(8,128)(2,1)} async-done(((bf16[512,8192]{1,0:T(8,128)(2,1)}), bf16[64,8192]{1,0:T(8,128)(2,1)}) %reduce-scatter.5.cloned.1.call-update) | async-done | bytes 1048592 | tf_op jit(solution)/shard_map/reduce_scatter | solution.py:100
  559.7 1.5 fusion.9
  561.3 14.2 %collective-permute-done = bf16[64,8192]{1,0:T(8,128)(2,1)S(1)} collective-permute-done((bf16[64,8192]{1,0:T(8,128)(2,1)S(1)}, bf16[64,8192]{1,0:T(8,128)(2,1)S(1)}, u32[]{:S(2)}, u32[]{:S(2)}) %collective-permute-start) | collective-permute-done | bytes 1048608 | tf_op jit(solution)/shard_map/ppermute | solution.py:19
  575.6 1.0 copy.73
  (40 shorter events, 3.8 us)
Async XLA Ops:
  6.5 309.0 %copy-start = (bf16[1,1024,1024]{2,1,0:T(8,128)(2,1)S(1)}, bf16[1,1024,1024]{2,1,0:T(8,128)(2,1)}, u32[]{:S(2)}) copy-start(bf16[1,1024,1024]{2,1,0:T(8,128)(2,1)} %param.13) | copy-start | bytes 6291460
  6.5 30.7 %all-gather.4.cloned.1.call-start = ((), (), s32[]{:S(2)}) async-start(), calls=%async_computation.2 | async-start | bytes 3276800 | tf_op jit(solution)/shard_map/all_gather | solution.py:52
  7.3 157.1 %all-gather.6.cloned.1.call-start = ((), (), s32[]{:S(2)}) async-start(), calls=%async_computation.6 | async-start | bytes 9437184 | tf_op jit(solution)/shard_map/all_gather | solution.py:82
  8.0 307.6 %reduce-scatter.3.cloned.1.call-start = ((), (), s32[]{:S(2)}) async-start(), calls=%async_computation.3 | async-start | bytes 9437184 | tf_op jit(solution)/shard_map/reduce_scatter | solution.py:54
  59.3 337.1 %all-reduce.2.cloned.1.call-start = ((), (), s32[]{:S(2)}) async-start(), calls=%async_computation.4 | async-start | bytes 2097152 | tf_op jit(solution)/shard_map/psum | solution.py:65
  319.0 240.7 %reduce-scatter.5.cloned.1.call-start = ((), (), s32[]{:S(2)}) async-start(), calls=%async_computation.5 | async-start | bytes 9437184 | tf_op jit(solution)/shard_map/reduce_scatter | solution.py:100
  396.4 3.0 copy-start.3
  398.0 1.6 copy-start.4
  400.7 175.8 %copy-start.1 = (bf16[1,1024,1024]{2,1,0:T(8,128)(2,1)S(1)}, bf16[1,1024,1024]{2,1,0:T(8,128)(2,1)}, u32[]{:S(2)}) copy-start(bf16[1,1024,1024]{2,1,0:T(8,128)(2,1)} %param.13) | copy-start | bytes 6291460
  411.0 148.8 %copy-start.2 = (bf16[1,64,8192]{2,1,0:T(8,128)(2,1)S(1)}, bf16[1,64,8192]{2,1,0:T(8,128)(2,1)}, u32[]{:S(2)}) copy-start(bf16[1,64,8192]{2,1,0:T(8,128)(2,1)} %param.9) | copy-start | bytes 3145732
  561.3 14.3 %collective-permute-start = (bf16[64,8192]{1,0:T(8,128)(2,1)S(1)}, bf16[64,8192]{1,0:T(8,128)(2,1)S(1)}, u32[]{:S(2)}, u32[]{:S(2)}) collective-permute-start(bf16[64,8192]{1,0:T(8,128)(2,1)S(1)} %fusion.9), channel_id=1, source_target_pairs={{0,8},{8,16},{16,24},{24,0},{1,9},{9,17},{17,25},{25,1},{2,10},{10... | collective-permute-start | bytes 3145736 | tf_op jit(solution)/shard_map/ppermute | solution.py:19
Sparse Core Ops, SparseCore 0:
  8.9 28.2 all-gather.3
  39.3 124.9 all-gather.5
  167.9 147.5 reduce-scatter.2
  319.3 77.0 all-reduce.1
  411.1 148.5 reduce-scatter.4
where the time goes:
time: 584 us; the launch traced here: 583 us
  waiting for transfers between devices  496 us (85%)
  matrix products  40.4 us (7%)
  local copies, waits for them, and re-layouts  19.2 us (3%)
  between operations  14.1 us (2%)
  other arithmetic  13.3 us (2%)
    reduce_scatter x1, waiting for transfers between devices, local(): lax.psum_scatter(jnp.dot(chosen, weight_out, preferred_element_type=jnp.f...  148 us
    reduce_scatter x1, waiting for transfers between devices, local(): lax.psum_scatter(lax.dot_general(w_proj, slot_feats, (((0,), (1,)), ((),...  146 us
    all_gather x1, waiting for transfers between devices, local(): lax.all_gather(text_state[0], 'mp', axis=0, tiled=True).astype(jnp.float32)  93.6 us
    psum x1, waiting for transfers between devices, local(): lax.psum(lax.dot_general(chosen, weight_kv, (((0,), (0,)), ((), ())), pre...  67.1 us
    all_gather x1, waiting for transfers between devices, local(): every_feat = lax.all_gather(tile_feats, 'section', axis=0, tiled=True)  25 us
    dot_general x1, matrix products, local(): lax.dot_general(w_proj, slot_feats, (((0,), (1,)), ((), ())), preferred_e...  17.2 us
    ppermute x1, waiting for transfers between devices, shifted(): lax.ppermute(value, axis, [(i, (i + by) % length) for i in range(length)])  14.2 us
  transfers between devices with their start and end apart: 6, of which 6 were waited for; matrix products, arithmetic and copies ran while one was open for 9% of the time, Pallas kernels for 0%

commit v1 on v0

v1 whole, which is shorter than its diff:
```python
import math

import jax
import jax.numpy as jnp
from jax import lax
from jax.sharding import PartitionSpec as P

HD = 128
HEADS = 32
KVH = 4
SAMP_SECTION = 4
TXT = 128
TT = 32
MAXT = 4
F32 = jnp.float32
BF16 = jnp.bfloat16


def ring_order(count):
    wide = 2 if count <= 8 else 4
    tall = count // wide
    if count < 4 or count % wide or tall % 2:
        return list(range(count))
    order = [row * wide for row in range(tall)]
    for turn, row in enumerate(reversed(range(tall))):
        columns = range(1, wide) if turn % 2 == 0 else range(wide - 1, 0, -1)
        order += [row * wide + column for column in columns]
    return order


def slot_index(tile_counts, section_table, section_id):
    samples_all = tile_counts.shape[0]
    sample_ids = jnp.arange(samples_all, dtype=jnp.int32)
    same_section = section_table[None, :] == section_table[:, None]
    before = sample_ids[None, :] < sample_ids[:, None]
    ranking = jnp.sum((same_section & before).astype(jnp.int32), axis=1)
    picked = (section_table[None, :] == section_id) & (
        ranking[None, :] == jnp.arange(SAMP_SECTION, dtype=jnp.int32)[:, None]
    )
    first_row = TT * jnp.sum(jnp.where(before, tile_counts[None, :], 0), axis=1)
    counts_own = jnp.sum(jnp.where(picked, tile_counts[None, :], 0), axis=1)
    starts_own = jnp.sum(jnp.where(picked, first_row[None, :], 0), axis=1)
    offsets = jnp.arange(MAXT * TT, dtype=jnp.int32)
    live_slot = offsets[None, :] < (TT * counts_own)[:, None]
    row_index = jnp.where(live_slot, starts_own[:, None] + offsets[None, :], -1)
    return (row_index.reshape(-1), live_slot)


def add(one, other):
    return (one.astype(F32) + other.astype(F32)).astype(BF16)


def local(
    mesh_shape,
    text_state,
    tile_feats,
    w_proj,
    w_query,
    w_kv,
    w_out,
    attn_gate,
    tile_counts,
    section_table,
):
    mp_count, section_count = mesh_shape["mp"], mesh_shape["section"]
    section_id = lax.axis_index("section")
    mp_place = lax.axis_index("mp")
    ring = ring_order(mp_count)
    far = mp_count // 2
    place = jnp.asarray([ring.index(i) for i in range(mp_count)], jnp.int32)[mp_place]
    ring_ids = jnp.asarray(ring, jnp.int32)

    def member(offset):
        return ring_ids[(place + offset) % mp_count]

    up_pairs = [(ring[i], ring[(i + 1) % mp_count]) for i in range(mp_count)]
    down_pairs = [(target, source) for source, target in up_pairs]

    def up(value):
        return lax.ppermute(value, "mp", up_pairs)

    def down(value):
        return lax.ppermute(value, "mp", down_pairs)

    def across(pairs):
        return [
            (s * mp_count + a, ((s + 1) % section_count) * mp_count + b)
            for s in range(section_count)
            for a, b in pairs
        ]

    def up_across(value):
        return lax.ppermute(value, ("section", "mp"), across(up_pairs))

    def down_across(value):
        return lax.ppermute(value, ("section", "mp"), across(down_pairs))

    def to_next(value):
        return lax.ppermute(
            value, "section", [(s, (s + 1) % section_count) for s in range(section_count)]
        )

    def ring_sum(part, start_up, start_down, last_up=up, last_down=down):
        arrived = []
        for start, sign, move, last in (
            (start_up, 1, up, last_up),
            (start_down, -1, down, last_down),
        ):
            running = part(sign * start)
            for distance in range(start, 1, -1):
                running = add(move(running), part(sign * (distance - 1)))
            arrived.append(last(running))
        return arrived

    text_own = text_state[0]
    text_rows = text_own.shape[0]
    cut = text_rows // 2
    halves = (text_own[:cut], text_own[cut:])
    from_below = [halves]
    from_above = [halves]
    for distance in range(1, far + 1):
        top_up = up(from_below[-1][0])
        low_down = down(from_above[-1][1])
        if distance < far:
            low_up = up(from_below[-1][1])
            top_down = down(from_above[-1][0])
        else:
            low_up = top_down = None
        from_below.append((top_up, low_up))
        from_above.append((top_down, low_down))
    text_next = to_next(text_own)
    gate_next = to_next(attn_gate)

    image_part = lax.optimization_barrier(
        jnp.dot(tile_feats, w_proj, preferred_element_type=F32).astype(BF16)
    )
    feat_rows = tile_feats.shape[0]
    wide = w_proj.shape[1] // mp_count
    image_halves = []
    for half, (start_up, start_down) in enumerate(((far, far - 1), (far - 1, far))):
        rows = feat_rows // 2

        def image_block(offset, half=half, rows=rows):
            return lax.dynamic_slice(
                image_part, (half * rows, member(offset) * wide), (rows, wide)
            )

        arrived = ring_sum(image_block, start_up, start_down)
        total = image_block(0).astype(F32) + arrived[0].astype(F32) + arrived[1].astype(F32)
        image_halves.append(total.astype(BF16))
    image_cols = jnp.concatenate(image_halves, axis=0)

    def pair_swap(value):
        return lax.ppermute(value, "section", [(s, s ^ 1) for s in range(section_count)])

    own_ids = jnp.arange(feat_rows, dtype=jnp.int32)
    pieces, piece_ids = [], []
    moving, moving_from = image_cols, section_id
    for step in range(section_count // 2):
        pieces += [moving, pair_swap(moving)]
        piece_ids += [
            moving_from * feat_rows + own_ids,
            (moving_from ^ 1) * feat_rows + own_ids,
        ]
        if step + 1 < section_count // 2:
            moving = lax.ppermute(
                moving,
                "section",
                [(s, (s + 2) % section_count) for s in range(section_count)],
            )
            moving_from = (moving_from + section_count - 2) % section_count
    row_index, live_slot = slot_index(tile_counts, section_table, section_id)
    choose = (row_index[:, None] == jnp.concatenate(piece_ids)[None, :]).astype(BF16)
    slot_image = jnp.dot(
        choose, jnp.concatenate(pieces, axis=0), preferred_element_type=F32
    ).astype(BF16)

    weight_kv = w_kv[0]
    kv_part = lax.optimization_barrier(
        jnp.dot(slot_image, weight_kv, preferred_element_type=F32).astype(BF16)
    )
    slots = kv_part.shape[0]
    half_width = weight_kv.shape[1] // 2
    sharing = mp_count // KVH
    kv_rows = slots // sharing

    def kv_block(offset):
        target = member(offset)
        row = (target % sharing) * kv_rows
        column = (target // sharing) * HD
        return jnp.concatenate(
            [
                lax.dynamic_slice(kv_part, (row, column), (kv_rows, HD)),
                lax.dynamic_slice(kv_part, (row, half_width + column), (kv_rows, HD)),
            ],
            axis=1,
        )

    arrived = ring_sum(kv_block, far, far - 1)
    kv_own = (
        kv_block(0).astype(F32) + arrived[0].astype(F32) + arrived[1].astype(F32)
    ).astype(BF16)
    kv_pieces = [kv_own]
    for step in range(1, sharing):
        pairs = [
            (m, m // sharing * sharing + (m % sharing + step) % sharing) for m in range(mp_count)
        ]
        kv_pieces.insert(0, lax.ppermute(kv_own, "mp", pairs))
    mine = mp_place % sharing
    kv_twice = jnp.concatenate(kv_pieces + kv_pieces, axis=0)
    kv_all = lax.dynamic_slice(
        kv_twice, ((sharing - 1 - mine) % sharing * kv_rows, 0), (slots, 2 * HD)
    ).astype(F32)
    keys = kv_all[:, :HD]
    keys = keys * lax.rsqrt(jnp.mean(keys * keys, axis=-1, keepdims=True) + 1e-06)
    keys = keys.astype(BF16).reshape(SAMP_SECTION, MAXT * TT, HD)
    values = kv_all[:, HD:].astype(BF16).reshape(SAMP_SECTION, MAXT * TT, HD)

    head_dev = HEADS // mp_count
    weight_query, weight_out = w_query[0], w_out[0]

    def query_of(rows):
        wide_rows = rows.astype(F32)
        scale = lax.rsqrt(jnp.mean(wide_rows * wide_rows, axis=-1, keepdims=True) + 1e-05)
        projected = jnp.dot(rows, weight_query, preferred_element_type=F32) * scale
        projected = projected.reshape(rows.shape[0], head_dev, HD)
        projected = projected * lax.rsqrt(
            jnp.mean(projected * projected, axis=-1, keepdims=True) + 1e-06
        )
        return projected.astype(BF16).reshape(rows.shape[0], head_dev * HD)

    def attend(queries, offsets):
        samples = jnp.stack([member(o) * text_rows // TXT for o in offsets])
        grid = queries.reshape(len(offsets), text_rows, head_dev, HD)
        scores = jnp.einsum(
            "sthd,skd->shtk", grid, keys[samples], preferred_element_type=F32
        ) / math.sqrt(HD)
        raised = jnp.where(live_slot[samples][:, None, None, :], jnp.exp(scores), 0.0)
        weights = (raised / jnp.sum(raised, axis=-1, keepdims=True)).astype(BF16)
        attended = jnp.einsum(
            "shtk,skd->sthd", weights, values[samples], preferred_element_type=F32
        )
        return attended.astype(BF16).reshape(len(offsets) * text_rows, head_dev * HD)

    near = [0]
    near_queries = [None]
    for distance in range(1, far):
        near += [-distance, distance]
        rows = from_below[distance] + from_above[distance]
        if distance == 1:
            rows = halves + rows
        near_queries.append(query_of(jnp.concatenate(rows, axis=0)))
    near_queries = jnp.concatenate(near_queries[1:], axis=0)
    far_rows = jnp.concatenate([from_below[far][0], from_above[far][1]], axis=0)
    far_attended = attend(query_of(far_rows), [far])
    far_part = lax.optimization_barrier(
        jnp.dot(far_attended, weight_out, preferred_element_type=F32).astype(BF16)
    )
    near_attended = attend(near_queries, near)
    near_part = lax.optimization_barrier(
        jnp.dot(near_attended, weight_out, preferred_element_type=F32).astype(BF16)
    )

    own_next = to_next(near_part[:text_rows])
    results = []
    for half, (start_up, start_down) in enumerate(((far, far - 1), (far - 1, far))):

        def out_block(offset, half=half):
            if abs(offset) == far:
                return far_part[half * cut : (half + 1) * cut]
            first = near.index(offset) * text_rows + half * cut
            return near_part[first : first + cut]

        arrived = ring_sum(out_block, start_up, start_down, up_across, down_across)
        rows = slice(half * cut, (half + 1) * cut)
        branch = own_next[rows].astype(F32) + arrived[0].astype(F32) + arrived[1].astype(F32)
        results.append(
            (text_next[rows].astype(F32) + jnp.tanh(gate_next[0]) * branch).astype(BF16)
        )
    return jnp.concatenate(results, axis=0)[None]


def solution(mesh):
    mesh_shape = dict(mesh.shape)

    def body(*arrays):
        return local(mesh_shape, *arrays)

    return jax.shard_map(
        body,
        mesh=mesh,
        in_specs=(
            P("section", "mp", None),
            P("section", "mp"),
            P("mp", None),
            P("section", None, "mp"),
            P("section", "mp", None),
            P("section", "mp", None),
            P("section"),
            P(),
            P(),
        ),
        out_specs=P("section", "mp", None),
        check_vma=False,
    )
```

time: 584 us -> 335 us (0.57)
  waiting for transfers between devices: 496 us -> 139 us
  starting transfers between devices: 0.4 us -> 55.1 us
  between operations: 14.1 us -> 38.3 us
  local copies, waits for them, and re-layouts: 19.2 us -> 30.6 us
  other arithmetic: 13.3 us -> 22.8 us
  matrix products: 40.4 us -> 47.9 us
    reduce_scatter x2 -> x0, waiting for transfers between devices: 294 us -> none  [the longest x1 148 us: local(): lax.psum_scatter(jnp.dot(chosen, weight_out, preferred_element_type=jnp.f...]
    ppermute x1 -> x56, waiting for transfers between devices: 14.2 us -> 139 us  [the longest x22 54 us: down(): return lax.ppermute(value, 'mp', down_pairs)]
    all_gather x2 -> x0, waiting for transfers between devices: 119 us -> none  [the longest x1 93.6 us: local(): lax.all_gather(text_state[0], 'mp', axis=0, tiled=True).astype(jnp.float32)]
    psum x1 -> x0, waiting for transfers between devices: 67.1 us -> none  [local(): lax.psum(lax.dot_general(chosen, weight_kv, (((0,), (0,)), ((), ())), pre...]
    ppermute x1 -> x56, starting transfers between devices: 0.06 us -> 55.1 us  [the longest x23 31.6 us: up(): return lax.ppermute(value, 'mp', up_pairs)]
    unnamed x12 -> x48, local copies, waits for them, and re-layouts: 1.06 us -> 13 us
    dot_general x1 -> x0, local copies, waits for them, and re-layouts: 11.4 us -> none  [local(): jnp.dot(normed, weight_query, preferred_element_type=jnp.float32)]
    dynamic_slice x1 -> x5, local copies, waits for them, and re-layouts: 0.03 us -> 7.63 us  [the longest x1 2.4 us: image_block(): lax.dynamic_slice(image_part, (half * rows, member(offset) * wide), (rows...]
  transfers between devices with their start and end apart: 6 -> 56, of which waited for: 6 -> 31; matrix products, arithmetic and copies ran while one was open for 9% -> 23% of each run, Pallas kernels for 0% -> 0%
where the time goes in v1:
time: 335 us; the launch traced here: 333 us
  waiting for transfers between devices  139 us (41%)
  starting transfers between devices  55.1 us (16%)
  matrix products  47.9 us (14%)
  between operations  38.3 us (11%)
  local copies, waits for them, and re-layouts  30.6 us (9%)
  other arithmetic  22.8 us (7%)
    ppermute x22, waiting for transfers between devices, down(): return lax.ppermute(value, 'mp', down_pairs)  54 us
    ppermute x23, waiting for transfers between devices, up(): return lax.ppermute(value, 'mp', up_pairs)  51 us
    ppermute x23, starting transfers between devices, up(): return lax.ppermute(value, 'mp', up_pairs)  31.6 us
    ppermute x22, starting transfers between devices, down(): return lax.ppermute(value, 'mp', down_pairs)  17 us
    dot_general x4, matrix products, query_of(): projected = jnp.dot(rows, weight_query, preferred_element_type=F32) * scale  15.5 us
    ppermute x3, waiting for transfers between devices, to_next(): lax.ppermute(value, 'section', [(s, (s + 1) % section_count) for s in ran...  15.4 us
    ppermute x2, waiting for transfers between devices, up_across(): return lax.ppermute(value, ('section', 'mp'), across(up_pairs))  13.6 us
    unnamed x48, local copies, waits for them, and re-layouts  13 us
  transfers between devices with their start and end apart: 56, of which 31 were waited for; matrix products, arithmetic and copies ran while one was open for 23% of the time, Pallas kernels for 0%

profile of v1, /device:TPU:0, one launch (start us, length us, event | category | flops | bytes accessed | tf_op | source)
XLA Modules:
  0.0 333.2 jit_solution(13991725881199953619)
XLA Ops:
  2.4 3.0 collective-permute-start.30
  17.7 10.7 %convolution_convert_fusion.1 = bf16[320,8192]{1,0:T(8,128)(2,1)} fusion(bf16[320,960]{1,0:T(8,128)(2,1)} %param.12, bf16[960,8192]{1,0:T(8,128)(2,1)} %param.13), kind=kOutput, calls=%fused_computation.4 | convolution fusion | flops 5035786240 | bytes 21585920 | tf_op jit(solution)/shard_map/dot_general | solution.py:135
  75.9 4.9 %collective-permute-done.29 = bf16[32,8192]{1,0:T(8,128)(2,1)S(1)} collective-permute-done((bf16[32,8192]{1,0:T(8,128)(2,1)}, bf16[32,8192]{1,0:T(8,128)(2,1)S(1)}, u32[]{:S(2)}, u32[]{:S(2)}) %collective-permute-start.29) | collective-permute-done | bytes 524320 | tf_op jit(solution)/shard_map/ppermute | solution.py:83
  87.8 4.5 %fusion.92 = (f32[192,512]{1,0:T(8,128)S(1)}, f32[192,512]{1,0:T(8,128)}) fusion(f32[192]{0:T(256)S(1)} %add_rsqrt_fusion.5, bf16[192,8192]{1,0:T(8,128)(2,1)} %constant_dynamic-update-slice_fusion.5, bf16[1,8192,512]{2,1,0:T(8,128)(2,1)S(1)} %copy-done.2), kind=kOutput, calls=%fused_computation.188 | convolution fusion | flops 1610809344 | bytes 12321536 | tf_op jit(solution)/shard_map/dot_general | solution.py:225
  101.3 4.6 %collective-permute-done.10 = bf16[160,1024]{1,0:T(8,128)(2,1)S(1)} collective-permute-done((bf16[160,1024]{1,0:T(8,128)(2,1)S(1)}, bf16[160,1024]{1,0:T(8,128)(2,1)S(1)}, u32[]{:S(2)}, u32[]{:S(2)}) %collective-permute-start.10) | collective-permute-done | bytes 327712 | tf_op jit(solution)/shard_map/ppermute | solution.py:80
  109.0 5.5 %collective-permute-done.7 = bf16[160,1024]{1,0:T(8,128)(2,1)S(1)} collective-permute-done((bf16[160,1024]{1,0:T(8,128)(2,1)S(1)}, bf16[160,1024]{1,0:T(8,128)(2,1)S(1)}, u32[]{:S(2)}, u32[]{:S(2)}) %collective-permute-start.7) | collective-permute-done | bytes 327712 | tf_op jit(solution)/shard_map/ppermute | solution.py:83
  118.1 6.1 %collective-permute-done.31 = bf16[32,8192]{1,0:T(8,128)(2,1)S(1)} collective-permute-done((bf16[32,8192]{1,0:T(8,128)(2,1)}, bf16[32,8192]{1,0:T(8,128)(2,1)S(1)}, u32[]{:S(2)}, u32[]{:S(2)}) %collective-permute-start.31) | collective-permute-done | bytes 524320 | tf_op jit(solution)/shard_map/ppermute | solution.py:80
  125.8 9.6 %collective-permute-done.32 = bf16[32,8192]{1,0:T(8,128)(2,1)S(1)} collective-permute-done((bf16[32,8192]{1,0:T(8,128)(2,1)}, bf16[32,8192]{1,0:T(8,128)(2,1)S(1)}, u32[]{:S(2)}, u32[]{:S(2)}) %collective-permute-start.32) | collective-permute-done | bytes 524320 | tf_op jit(solution)/shard_map/ppermute | solution.py:80
  154.5 6.1 %collective-permute-done.35 = bf16[32,8192]{1,0:T(8,128)(2,1)S(1)} collective-permute-done((bf16[32,8192]{1,0:T(8,128)(2,1)}, bf16[32,8192]{1,0:T(8,128)(2,1)S(1)}, u32[]{:S(2)}, u32[]{:S(2)}) %collective-permute-start.35) | collective-permute-done | bytes 524320 | tf_op jit(solution)/shard_map/ppermute | solution.py:80
  162.2 5.7 %collective-permute-done.36 = bf16[32,8192]{1,0:T(8,128)(2,1)S(1)} collective-permute-done((bf16[32,8192]{1,0:T(8,128)(2,1)}, bf16[32,8192]{1,0:T(8,128)(2,1)S(1)}, u32[]{:S(2)}, u32[]{:S(2)}) %collective-permute-start.36) | collective-permute-done | bytes 524320 | tf_op jit(solution)/shard_map/ppermute | solution.py:80
  170.6 4.8 %fusion.90 = (f32[128,512]{1,0:T(8,128)S(1)}, f32[128,512]{1,0:T(8,128)S(1)}) fusion(f32[128]{0:T(128)S(1)} %add_rsqrt_fusion.7, bf16[128,8192]{1,0:T(8,128)(2,1)S(1)} %constant_dynamic-update-slice_fusion.15, bf16[1,8192,512]{2,1,0:T(8,128)(2,1)} %param.14), kind=kOutput, calls=%fused_computation.186 | convolution fusion | flops 1073872896 | bytes 11010560 | tf_op jit(solution)/shard_map/dot_general | solution.py:225
  190.0 5.4 %fusion.17 = bf16[512,1024]{1,0:T(8,128)(2,1)} fusion(bf16[1,1024,1024]{2,1,0:T(8,128)(2,1)S(1)} %copy-done, bf16[1280,1024]{1,0:T(8,128)(2,1)} %constant_dynamic-update-slice_fusion, s32[1280]{0:T(1024)S(1)} %concatenate.74, s32[512]{0:T(512)S(1)} %select_bitcast_fusion), kind=kOutput, calls=%fused_computation.25 | convolution fusion | flops 2417623040 | bytes 5774336 | tf_op jit(solution)/shard_map/dot_general | solution.py:180
  213.8 4.9 %fusion.93 = (f32[64,512]{1,0:T(8,128)S(1)}, f32[64,512]{1,0:T(8,128)S(1)}) fusion(f32[64]{0:T(128)S(1)} %add_rsqrt_fusion.6, bf16[64,8192]{1,0:T(8,128)(2,1)S(1)} %constant_dynamic-update-slice_fusion.19, bf16[1,8192,512]{2,1,0:T(8,128)(2,1)} %param.14), kind=kOutput, calls=%fused_computation.189 | convolution fusion | flops 536936448 | bytes 9699584 | tf_op jit(solution)/shard_map/dot_general | solution.py:225
  219.6 4.5 %collective-permute-done.26 = bf16[256,256]{1,0:T(8,128)(2,1)S(1)} collective-permute-done((bf16[256,256]{1,0:T(8,128)(2,1)S(1)}, bf16[256,256]{1,0:T(8,128)(2,1)S(1)}, u32[]{:S(2)}, u32[]{:S(2)}) %collective-permute-start.26) | collective-permute-done | bytes 131104 | tf_op jit(solution)/shard_map/ppermute | solution.py:208
  227.5 5.0 %convolution_convert_fusion.2 = bf16[64,8192]{1,0:T(8,128)(2,1)S(1)} fusion(bf16[1,512,8192]{2,1,0:T(8,128)(2,1)} %param.16, bf16[8,8,4,128]{3,2,1,0:T(4,128)(2,1)S(1)} %bitcast.180), kind=kOutput, calls=%fused_computation.5 | convolution fusion | flops 537395200 | bytes 9502720 | tf_op jit(solution)/shard_map/dot_general | solution.py:257
  238.0 7.6 %convolution_convert_fusion = bf16[448,8192]{1,0:T(8,128)(2,1)S(1)} fusion(bf16[1,512,8192]{2,1,0:T(8,128)(2,1)} %param.16, bf16[56,8,4,128]{3,2,1,0:T(4,128)(2,1)S(1)} %bitcast.179), kind=kOutput, calls=%fused_computation.3 | convolution fusion | flops 3761766400 | bytes 16187392 | tf_op jit(solution)/shard_map/dot_general | solution.py:261
  248.0 12.5 %collective-permute-done.52 = bf16[32,8192]{1,0:T(8,128)(2,1)S(1)} collective-permute-done((bf16[32,8192]{1,0:T(8,128)(2,1)S(1)}, bf16[32,8192]{1,0:T(8,128)(2,1)S(1)}, u32[]{:S(2)}, u32[]{:S(2)}) %collective-permute-start.52) | collective-permute-done | bytes 524320 | tf_op jit(solution)/shard_map/ppermute | solution.py:83
  262.8 6.0 %collective-permute-done.46 = bf16[32,8192]{1,0:T(8,128)(2,1)S(1)} collective-permute-done((bf16[32,8192]{1,0:T(8,128)(2,1)S(1)}, bf16[32,8192]{1,0:T(8,128)(2,1)S(1)}, u32[]{:S(2)}, u32[]{:S(2)}) %collective-permute-start.46) | collective-permute-done | bytes 524320 | tf_op jit(solution)/shard_map/ppermute | solution.py:83
  270.7 8.8 %collective-permute-done.53 = bf16[32,8192]{1,0:T(8,128)(2,1)S(1)} collective-permute-done((bf16[32,8192]{1,0:T(8,128)(2,1)S(1)}, bf16[32,8192]{1,0:T(8,128)(2,1)S(1)}, u32[]{:S(2)}, u32[]{:S(2)}) %collective-permute-start.53) | collective-permute-done | bytes 524320 | tf_op jit(solution)/shard_map/ppermute | solution.py:83
  284.3 5.0 %collective-permute-done.44 = bf16[32,8192]{1,0:T(8,128)(2,1)S(1)} collective-permute-done((bf16[32,8192]{1,0:T(8,128)(2,1)S(1)}, bf16[32,8192]{1,0:T(8,128)(2,1)S(1)}, u32[]{:S(2)}, u32[]{:S(2)}) %collective-permute-start.44) | collective-permute-done | bytes 524320 | tf_op jit(solution)/shard_map/ppermute | solution.py:80
  291.3 3.6 %collective-permute-done.50 = bf16[32,8192]{1,0:T(8,128)(2,1)S(1)} collective-permute-done((bf16[32,8192]{1,0:T(8,128)(2,1)S(1)}, bf16[32,8192]{1,0:T(8,128)(2,1)S(1)}, u32[]{:S(2)}, u32[]{:S(2)}) %collective-permute-start.50) | collective-permute-done | bytes 524320 | tf_op jit(solution)/shard_map/ppermute | solution.py:80
  302.5 15.4 %collective-permute-done.39 = bf16[64,8192]{1,0:T(8,128)(2,1)S(1)} collective-permute-done((bf16[64,8192]{1,0:T(8,128)(2,1)S(1)}, bf16[64,8192]{1,0:T(8,128)(2,1)S(1)}, u32[]{:S(2)}, u32[]{:S(2)}) %collective-permute-start.39) | collective-permute-done | bytes 1048608 | tf_op jit(solution)/shard_map/ppermute | solution.py:99
  317.9 8.0 %collective-permute-done.45 = bf16[32,8192]{1,0:T(8,128)(2,1)S(1)} collective-permute-done((bf16[32,8192]{1,0:T(8,128)(2,1)S(1)}, bf16[32,8192]{1,0:T(8,128)(2,1)S(1)}, u32[]{:S(2)}, u32[]{:S(2)}) %collective-permute-start.45) | collective-permute-done | bytes 524320 | tf_op jit(solution)/shard_map/ppermute | solution.py:93
  326.0 5.6 %collective-permute-done.51 = bf16[32,8192]{1,0:T(8,128)(2,1)S(1)} collective-permute-done((bf16[32,8192]{1,0:T(8,128)(2,1)S(1)}, bf16[32,8192]{1,0:T(8,128)(2,1)S(1)}, u32[]{:S(2)}, u32[]{:S(2)}) %collective-permute-start.51) | collective-permute-done | bytes 524320 | tf_op jit(solution)/shard_map/ppermute | solution.py:93
  (235 shorter events, 136.9 us)
Async XLA Ops:
  2.4 80.9 %collective-permute-start.30 = (bf16[32,8192]{1,0:T(8,128)(2,1)}, bf16[32,8192]{1,0:T(8,128)(2,1)}, u32[]{:S(2)}, u32[]{:S(2)}) collective-permute-start(bf16[32,8192]{1,0:T(8,128)(2,1)} %get-tuple-element.90), channel_id=1, source_target_pairs={{2,0},{4,2},{6,4},{7,6},{5,7},{3,5},{1,3},{0,1},{10,8},{12,10},{14... | collective-permute-start | bytes 1572872 | tf_op jit(solution)/shard_map/ppermute | solution.py:83
  5.4 67.2 %collective-permute-start.28 = (bf16[32,8192]{1,0:T(8,128)(2,1)}, bf16[32,8192]{1,0:T(8,128)(2,1)}, u32[]{:S(2)}, u32[]{:S(2)}) collective-permute-start(bf16[32,8192]{1,0:T(8,128)(2,1)} %get-tuple-element.90), channel_id=1, source_target_pairs={{0,2},{2,4},{4,6},{6,7},{7,5},{5,3},{3,1},{1,0},{8,10},{10,12},{12... | collective-permute-start | bytes 1572872 | tf_op jit(solution)/shard_map/ppermute | solution.py:80
  30.8 34.9 %collective-permute-start.12 = (bf16[160,1024]{1,0:T(8,128)(2,1)}, bf16[160,1024]{1,0:T(8,128)(2,1)S(1)}, u32[]{:S(2)}, u32[]{:S(2)}) collective-permute-start(bf16[160,1024]{1,0:T(8,128)(2,1)} %get-tuple-element.65), channel_id=1, source_target_pairs={{2,0},{4,2},{6,4},{7,6},{5,7},{3,5},{1,3},{0,1},{10,8},{12,10},{14... | collective-permute-start | bytes 983048 | tf_op jit(solution)/shard_map/ppermute | solution.py:83
  32.8 33.0 %collective-permute-start.2 = (bf16[160,1024]{1,0:T(8,128)(2,1)}, bf16[160,1024]{1,0:T(8,128)(2,1)}, u32[]{:S(2)}, u32[]{:S(2)}) collective-permute-start(bf16[160,1024]{1,0:T(8,128)(2,1)} %get-tuple-element.67), channel_id=1, source_target_pairs={{0,2},{2,4},{4,6},{6,7},{7,5},{5,3},{3,1},{1,0},{8,10},{10,12},{12... | collective-permute-start | bytes 983048 | tf_op jit(solution)/shard_map/ppermute | solution.py:80
  32.8 37.4 %collective-permute-start.27 = (bf16[32,8192]{1,0:T(8,128)(2,1)}, bf16[32,8192]{1,0:T(8,128)(2,1)}, u32[]{:S(2)}, u32[]{:S(2)}) collective-permute-start(bf16[32,8192]{1,0:T(8,128)(2,1)} %get-tuple-element.91), channel_id=1, source_target_pairs={{0,2},{2,4},{4,6},{6,7},{7,5},{5,3},{3,1},{1,0},{8,10},{10,12},{12... | collective-permute-start | bytes 1572872 | tf_op jit(solution)/shard_map/ppermute | solution.py:80
  65.8 27.0 %collective-permute-start.9 = (bf16[160,1024]{1,0:T(8,128)(2,1)}, bf16[160,1024]{1,0:T(8,128)(2,1)}, u32[]{:S(2)}, u32[]{:S(2)}) collective-permute-start(bf16[160,1024]{1,0:T(8,128)(2,1)} %get-tuple-element.64), channel_id=1, source_target_pairs={{0,2},{2,4},{4,6},{6,7},{7,5},{5,3},{3,1},{1,0},{8,10},{10,12},{12... | collective-permute-start | bytes 983048 | tf_op jit(solution)/shard_map/ppermute | solution.py:80
  70.2 22.6 %collective-permute-start.6 = (bf16[160,1024]{1,0:T(8,128)(2,1)}, bf16[160,1024]{1,0:T(8,128)(2,1)}, u32[]{:S(2)}, u32[]{:S(2)}) collective-permute-start(bf16[160,1024]{1,0:T(8,128)(2,1)} %get-tuple-element.66), channel_id=1, source_target_pairs={{2,0},{4,2},{6,4},{7,6},{5,7},{3,5},{1,3},{0,1},{10,8},{12,10},{14... | collective-permute-start | bytes 983048 | tf_op jit(solution)/shard_map/ppermute | solution.py:83
  72.6 20.2 %collective-permute-start.13 = (bf16[160,1024]{1,0:T(8,128)(2,1)}, bf16[160,1024]{1,0:T(8,128)(2,1)}, u32[]{:S(2)}, u32[]{:S(2)}) collective-permute-start(bf16[160,1024]{1,0:T(8,128)(2,1)} %get-tuple-element.68), channel_id=1, source_target_pairs={{2,0},{4,2},{6,4},{7,6},{5,7},{3,5},{1,3},{0,1},{10,8},{12,10},{14... | collective-permute-start | bytes 983048 | tf_op jit(solution)/shard_map/ppermute | solution.py:83
  99.3 24.8 %collective-permute-start.31 = (bf16[32,8192]{1,0:T(8,128)(2,1)}, bf16[32,8192]{1,0:T(8,128)(2,1)S(1)}, u32[]{:S(2)}, u32[]{:S(2)}) collective-permute-start(bf16[32,8192]{1,0:T(8,128)(2,1)} %collective-permute-done.27), channel_id=1, source_target_pairs={{0,2},{2,4},{4,6},{6,7},{7,5},{5,3},{3,1},{1,0},{8,10},{10,12},{12... | collective-permute-start | bytes 1572872 | tf_op jit(solution)/shard_map/ppermute | solution.py:80
  105.9 32.6 %collective-permute-start.34 = (bf16[32,8192]{1,0:T(8,128)(2,1)}, bf16[32,8192]{1,0:T(8,128)(2,1)S(1)}, u32[]{:S(2)}, u32[]{:S(2)}) collective-permute-start(bf16[32,8192]{1,0:T(8,128)(2,1)} %collective-permute-done.30), channel_id=1, source_target_pairs={{2,0},{4,2},{6,4},{7,6},{5,7},{3,5},{1,3},{0,1},{10,8},{12,10},{14... | collective-permute-start | bytes 1572872 | tf_op jit(solution)/shard_map/ppermute | solution.py:83
  107.5 27.9 %collective-permute-start.32 = (bf16[32,8192]{1,0:T(8,128)(2,1)}, bf16[32,8192]{1,0:T(8,128)(2,1)S(1)}, u32[]{:S(2)}, u32[]{:S(2)}) collective-permute-start(bf16[32,8192]{1,0:T(8,128)(2,1)} %collective-permute-done.28), channel_id=1, source_target_pairs={{0,2},{2,4},{4,6},{6,7},{7,5},{5,3},{3,1},{1,0},{8,10},{10,12},{12... | collective-permute-start | bytes 1572872 | tf_op jit(solution)/shard_map/ppermute | solution.py:80
  114.5 22.5 %collective-permute-start.33 = (bf16[32,8192]{1,0:T(8,128)(2,1)S(1)}, bf16[32,8192]{1,0:T(8,128)(2,1)S(1)}, u32[]{:S(2)}, u32[]{:S(2)}) collective-permute-start(bf16[32,8192]{1,0:T(8,128)(2,1)S(1)} %collective-permute-done.29), channel_id=1, source_target_pairs={{2,0},{4,2},{6,4},{7,6},{5,7},{3,5},{1,3},{0,1},{10,8},{12,10},{14... | collective-permute-start | bytes 1572872 | tf_op jit(solution)/shard_map/ppermute | solution.py:83
  117.6 26.5 %collective-permute-start.8 = (bf16[160,1024]{1,0:T(8,128)(2,1)}, bf16[160,1024]{1,0:T(8,128)(2,1)}, u32[]{:S(2)}, u32[]{:S(2)}) collective-permute-start(bf16[160,1024]{1,0:T(8,128)(2,1)} %get-tuple-element.58), channel_id=1, source_target_pairs={{2,0},{4,2},{6,4},{7,6},{5,7},{3,5},{1,3},{0,1},{10,8},{12,10},{14... | collective-permute-start | bytes 983048 | tf_op jit(solution)/shard_map/ppermute | solution.py:83
  124.2 20.4 %collective-permute-start.5 = (bf16[160,1024]{1,0:T(8,128)(2,1)}, bf16[160,1024]{1,0:T(8,128)(2,1)}, u32[]{:S(2)}, u32[]{:S(2)}) collective-permute-start(bf16[160,1024]{1,0:T(8,128)(2,1)} %get-tuple-element.59), channel_id=1, source_target_pairs={{0,2},{2,4},{4,6},{6,7},{7,5},{5,3},{3,1},{1,0},{8,10},{10,12},{12... | collective-permute-start | bytes 983048 | tf_op jit(solution)/shard_map/ppermute | solution.py:80
  141.0 19.7 %collective-permute-start.35 = (bf16[32,8192]{1,0:T(8,128)(2,1)}, bf16[32,8192]{1,0:T(8,128)(2,1)S(1)}, u32[]{:S(2)}, u32[]{:S(2)}) collective-permute-start(bf16[32,8192]{1,0:T(8,128)(2,1)} %copy-done.6), channel_id=1, source_target_pairs={{0,2},{2,4},{4,6},{6,7},{7,5},{5,3},{3,1},{1,0},{8,10},{10,12},{12... | collective-permute-start | bytes 1572872 | tf_op jit(solution)/shard_map/ppermute | solution.py:80
  144.1 25.2 %collective-permute-start.38 = (bf16[32,8192]{1,0:T(8,128)(2,1)}, bf16[32,8192]{1,0:T(8,128)(2,1)S(1)}, u32[]{:S(2)}, u32[]{:S(2)}) collective-permute-start(bf16[32,8192]{1,0:T(8,128)(2,1)} %copy-done.5), channel_id=1, source_target_pairs={{2,0},{4,2},{6,4},{7,6},{5,7},{3,5},{1,3},{0,1},{10,8},{12,10},{14... | collective-permute-start | bytes 1572872 | tf_op jit(solution)/shard_map/ppermute | solution.py:83
  144.5 23.4 %collective-permute-start.36 = (bf16[32,8192]{1,0:T(8,128)(2,1)}, bf16[32,8192]{1,0:T(8,128)(2,1)S(1)}, u32[]{:S(2)}, u32[]{:S(2)}) collective-permute-start(bf16[32,8192]{1,0:T(8,128)(2,1)} %copy-done.7), channel_id=1, source_target_pairs={{0,2},{2,4},{4,6},{6,7},{7,5},{5,3},{3,1},{1,0},{8,10},{10,12},{12... | collective-permute-start | bytes 1572872 | tf_op jit(solution)/shard_map/ppermute | solution.py:80
  154.5 24.7 %collective-permute-start.16 = (bf16[320,1024]{1,0:T(8,128)(2,1)}, bf16[320,1024]{1,0:T(8,128)(2,1)}, u32[]{:S(2)}, u32[]{:S(2)}) collective-permute-start(bf16[320,1024]{1,0:T(8,128)(2,1)} %pad_maximum_fusion), channel_id=1, source_target_pairs={{0,8},{8,0},{16,24},{24,16},{1,9},{9,1},{17,25},{25,17},{2,10},{10... | collective-permute-start | bytes 1966088 | tf_op jit(solution)/shard_map/ppermute | solution.py:154
  247.8 21.0 %collective-permute-start.46 = (bf16[32,8192]{1,0:T(8,128)(2,1)S(1)}, bf16[32,8192]{1,0:T(8,128)(2,1)S(1)}, u32[]{:S(2)}, u32[]{:S(2)}) collective-permute-start(bf16[32,8192]{1,0:T(8,128)(2,1)S(1)} %get-tuple-element.54), channel_id=1, source_target_pairs={{2,0},{4,2},{6,4},{7,6},{5,7},{3,5},{1,3},{0,1},{10,8},{12,10},{14... | collective-permute-start | bytes 1572872 | tf_op jit(solution)/shard_map/ppermute | solution.py:83
  291.3 26.6 %collective-permute-start.39 = (bf16[64,8192]{1,0:T(8,128)(2,1)S(1)}, bf16[64,8192]{1,0:T(8,128)(2,1)S(1)}, u32[]{:S(2)}, u32[]{:S(2)}) collective-permute-start(bf16[64,8192]{1,0:T(8,128)(2,1)S(1)} %slice.139), channel_id=1, source_target_pairs={{0,8},{8,16},{16,24},{24,0},{1,9},{9,17},{17,25},{25,1},{2,10},{10... | collective-permute-start | bytes 3145736 | tf_op jit(solution)/shard_map/ppermute | solution.py:99
  297.4 20.5 %collective-permute-start.48 = (bf16[32,8192]{1,0:T(8,128)(2,1)S(1)}, bf16[32,8192]{1,0:T(8,128)(2,1)S(1)}, u32[]{:S(2)}, u32[]{:S(2)}) collective-permute-start(bf16[32,8192]{1,0:T(8,128)(2,1)S(1)} %get-tuple-element.47), channel_id=1, source_target_pairs={{2,8},{4,10},{6,12},{7,14},{5,15},{3,13},{1,11},{0,9},{10,16},{12,... | collective-permute-start | bytes 1572872 | tf_op jit(solution)/shard_map/ppermute | solution.py:96
  297.5 28.5 %collective-permute-start.45 = (bf16[32,8192]{1,0:T(8,128)(2,1)S(1)}, bf16[32,8192]{1,0:T(8,128)(2,1)S(1)}, u32[]{:S(2)}, u32[]{:S(2)}) collective-permute-start(bf16[32,8192]{1,0:T(8,128)(2,1)S(1)} %get-tuple-element.44), channel_id=1, source_target_pairs={{0,10},{2,12},{4,14},{6,15},{7,13},{5,11},{3,9},{1,8},{8,18},{10,2... | collective-permute-start | bytes 1572872 | tf_op jit(solution)/shard_map/ppermute | solution.py:93
  300.2 25.8 %collective-permute-start.55 = (bf16[32,8192]{1,0:T(8,128)(2,1)S(1)}, bf16[32,8192]{1,0:T(8,128)(2,1)S(1)}, u32[]{:S(2)}, u32[]{:S(2)}) collective-permute-start(bf16[32,8192]{1,0:T(8,128)(2,1)S(1)} %get-tuple-element.45), channel_id=1, source_target_pairs={{2,8},{4,10},{6,12},{7,14},{5,15},{3,13},{1,11},{0,9},{10,16},{12,... | collective-permute-start | bytes 1572872 | tf_op jit(solution)/shard_map/ppermute | solution.py:96
  300.2 31.3 %collective-permute-start.51 = (bf16[32,8192]{1,0:T(8,128)(2,1)S(1)}, bf16[32,8192]{1,0:T(8,128)(2,1)S(1)}, u32[]{:S(2)}, u32[]{:S(2)}) collective-permute-start(bf16[32,8192]{1,0:T(8,128)(2,1)S(1)} %get-tuple-element.46), channel_id=1, source_target_pairs={{0,10},{2,12},{4,14},{6,15},{7,13},{5,11},{3,9},{1,8},{8,18},{10,2... | collective-permute-start | bytes 1572872 | tf_op jit(solution)/shard_map/ppermute | solution.py:93
  (49 other events, 790.7 us)

commit v2 on v1

v2 whole, which is shorter than its diff:
```python
import math

import jax
import jax.numpy as jnp
import numpy as np
from jax import lax
from jax.experimental import pallas as pl
from jax.experimental.pallas import tpu as pltpu
from jax.sharding import PartitionSpec as P

HD = 128
HEADS = 32
KVH = 4
SAMP_SECTION = 4
TXT = 128
TT = 32
MAXT = 4
BLOCK = MAXT * TT
SLOTS = SAMP_SECTION * BLOCK
F32 = jnp.float32
BF16 = jnp.bfloat16
VMEM_LIMIT = 40 * 1024 * 1024


def ring_order(count):
    wide = 2 if count <= 8 else 4
    tall = count // wide
    if count < 4 or count % wide or tall % 2:
        return list(range(count))
    order = [row * wide for row in range(tall)]
    for turn, row in enumerate(reversed(range(tall))):
        columns = range(1, wide) if turn % 2 == 0 else range(wide - 1, 0, -1)
        order += [row * wide + column for column in columns]
    return order


def own_samples(tile_counts, section_table, section_id):
    samples_all = tile_counts.shape[0]
    sample_ids = jnp.arange(samples_all, dtype=jnp.int32)
    same_section = section_table[None, :] == section_table[:, None]
    before = sample_ids[None, :] < sample_ids[:, None]
    ranking = jnp.sum((same_section & before).astype(jnp.int32), axis=1)
    picked = (section_table[None, :] == section_id) & (
        ranking[None, :] == jnp.arange(SAMP_SECTION, dtype=jnp.int32)[:, None]
    )
    first_row = TT * jnp.sum(jnp.where(before, tile_counts[None, :], 0), axis=1)
    counts_own = jnp.sum(jnp.where(picked, tile_counts[None, :], 0), axis=1)
    starts_own = jnp.sum(jnp.where(picked, first_row[None, :], 0), axis=1)
    return starts_own, counts_own


def add(one, other):
    return (one.astype(F32) + other.astype(F32)).astype(BF16)


def params():
    return pltpu.CompilerParams(vmem_limit_bytes=VMEM_LIMIT)


def project(meta, feats, weight, order_len):
    rows, depth = feats.shape
    wide = weight.shape[1] // order_len

    def kernel(meta_ref, feats_ref, weight_ref, out_ref):
        out_ref[0] = jnp.dot(
            feats_ref[...], weight_ref[...], preferred_element_type=F32
        ).astype(BF16)

    return pl.pallas_call(
        kernel,
        grid_spec=pltpu.PrefetchScalarGridSpec(
            num_scalar_prefetch=1,
            grid=(order_len,),
            in_specs=[
                pl.BlockSpec((rows, depth), lambda i, meta: (0, 0)),
                pl.BlockSpec((depth, wide), lambda i, meta: (0, meta[i])),
            ],
            out_specs=pl.BlockSpec((1, rows, wide), lambda i, meta: (i, 0, 0)),
        ),
        out_shape=jax.ShapeDtypeStruct((order_len, rows, wide), BF16),
        compiler_params=params(),
        cost_estimate=pl.CostEstimate(
            flops=2 * rows * depth * weight.shape[1],
            bytes_accessed=2 * (depth + rows) * weight.shape[1],
            transcendentals=0,
        ),
        name="project",
    )(meta, feats, weight)


def key_values(meta, pieces, weight, order_len, section_count, sharing):
    feat_rows = pieces[0].shape[0]
    depth, width = weight.shape
    kv_rows = SLOTS // sharing
    half_width = width // 2
    count = len(pieces)

    def kernel(meta_ref, *refs):
        piece_refs, weight_ref, out_ref, kv_ref = refs[:count], refs[count], refs[-2], refs[-1]
        section = meta_ref[order_len + 1]
        slot = lax.broadcasted_iota(jnp.int32, (BLOCK, feat_rows), 0)
        packed = lax.broadcasted_iota(jnp.int32, (BLOCK, feat_rows), 1)
        for sample in range(SAMP_SECTION):
            start = meta_ref[order_len + 2 + sample]
            live = TT * meta_ref[order_len + 2 + SAMP_SECTION + sample]
            image = jnp.zeros((BLOCK, depth), F32)
            for index in range(count):
                step, swapped = index // 2, index % 2
                origin = lax.rem(section + (section_count - 2 * step), section_count)
                if swapped:
                    origin = origin + 1 - 2 * lax.rem(origin, 2)
                chosen = (slot < live) & (packed == slot + (start - origin * feat_rows))
                image += jnp.dot(
                    chosen.astype(F32).astype(BF16),
                    piece_refs[index][...],
                    preferred_element_type=F32,
                )
            kv_ref[sample * BLOCK : (sample + 1) * BLOCK, :] = jnp.dot(
                image.astype(BF16), weight_ref[...], preferred_element_type=F32
            ).astype(BF16)
        for index in range(order_len):
            target = meta_ref[index]
            row = pl.multiple_of(lax.rem(target, sharing) * kv_rows, kv_rows)
            column = pl.multiple_of(target // sharing * HD, HD)
            out_ref[index, :, :HD] = kv_ref[pl.ds(row, kv_rows), pl.ds(column, HD)]
            out_ref[index, :, HD:] = kv_ref[
                pl.ds(row, kv_rows), pl.ds(pl.multiple_of(column + half_width, HD), HD)
            ]

    whole = pl.BlockSpec(memory_space=pltpu.VMEM)
    return pl.pallas_call(
        kernel,
        in_specs=[pl.BlockSpec(memory_space=pltpu.SMEM)] + [whole] * (count + 1),
        out_specs=whole,
        out_shape=jax.ShapeDtypeStruct((order_len, kv_rows, 2 * HD), BF16),
        scratch_shapes=[pltpu.VMEM((SLOTS, width), BF16)],
        compiler_params=params(),
        cost_estimate=pl.CostEstimate(
            flops=2 * SLOTS * depth * (width + feat_rows * count),
            bytes_accessed=2 * depth * (width + feat_rows * count),
            transcendentals=0,
        ),
        name="key_values",
    )(meta, *pieces, weight)


def query(chunks, weight):
    rows = sum(chunk.shape[0] for chunk in chunks)
    depth, width = weight.shape
    wide = min(2 * HD, width)
    count = len(chunks)

    def kernel(*refs):
        chunk_refs, weight_ref, out_ref = refs[:count], refs[count], refs[count + 1]
        first = 0
        for chunk_ref in chunk_refs:
            size = chunk_ref.shape[0]
            chunk = chunk_ref[...]
            wider = chunk.astype(F32)
            scale = lax.rsqrt(jnp.mean(wider * wider, axis=-1, keepdims=True) + 1e-05)
            projected = jnp.dot(chunk, weight_ref[...], preferred_element_type=F32) * scale
            for head in range(wide // HD):
                one = projected[:, head * HD : (head + 1) * HD]
                one = one * lax.rsqrt(jnp.mean(one * one, axis=-1, keepdims=True) + 1e-06)
                out_ref[first : first + size, head * HD : (head + 1) * HD] = one.astype(BF16)
            first += size

    return pl.pallas_call(
        kernel,
        grid=(width // wide,),
        in_specs=[pl.BlockSpec(chunk.shape, lambda i: (0, 0)) for chunk in chunks]
        + [pl.BlockSpec((depth, wide), lambda i: (0, i))],
        out_specs=pl.BlockSpec((rows, wide), lambda i: (0, i)),
        out_shape=jax.ShapeDtypeStruct((rows, width), BF16),
        compiler_params=params(),
        cost_estimate=pl.CostEstimate(
            flops=2 * rows * depth * width,
            bytes_accessed=2 * depth * (width + rows),
            transcendentals=0,
        ),
        name="query",
    )(*chunks, weight)


def attend(meta, queries, kv_pieces, weight, indices, text_rows, order_len):
    rows, width = queries.shape
    heads = width // HD
    sharing = len(kv_pieces)
    kv_rows = SLOTS // sharing
    columns = weight.shape[1]
    wide = min(1024, columns)

    def kernel(meta_ref, query_ref, *refs):
        kv_refs, weight_ref, out_ref = refs[:sharing], refs[sharing], refs[sharing + 1]
        key_ref, value_ref, attended_ref = refs[sharing + 2 :]

        @pl.when(pl.program_id(0) == 0)
        def _():
            mine = lax.rem(meta_ref[order_len], sharing)
            for step in range(sharing):
                row = pl.multiple_of(
                    lax.rem(mine + sharing - step, sharing) * kv_rows, kv_rows
                )
                keys = kv_refs[step][:, :HD].astype(F32)
                keys = keys * lax.rsqrt(jnp.mean(keys * keys, axis=-1, keepdims=True) + 1e-06)
                key_ref[pl.ds(row, kv_rows), :] = keys.astype(BF16)
                value_ref[pl.ds(row, kv_rows), :] = kv_refs[step][:, HD:]
            for place, index in enumerate(indices):
                sample = meta_ref[index] * text_rows // TXT
                slots = pl.ds(pl.multiple_of(sample * BLOCK, BLOCK), BLOCK)
                live = TT * meta_ref[order_len + 2 + SAMP_SECTION + sample]
                first = place * text_rows
                own = query_ref[first : first + text_rows, :]
                stacked = jnp.concatenate(
                    [own[:, h * HD : (h + 1) * HD] for h in range(heads)], axis=0
                )
                scores = lax.dot_general(
                    stacked,
                    key_ref[slots, :],
                    (((1,), (1,)), ((), ())),
                    preferred_element_type=F32,
                ) * (1.0 / math.sqrt(HD))
                slot = lax.broadcasted_iota(jnp.int32, scores.shape, 1)
                raised = jnp.where(slot < live, jnp.exp(scores), 0.0)
                weights = (raised / jnp.sum(raised, axis=-1, keepdims=True)).astype(BF16)
                result = jnp.dot(
                    weights, value_ref[slots, :], preferred_element_type=F32
                ).astype(BF16)
                for h in range(heads):
                    attended_ref[first : first + text_rows, h * HD : (h + 1) * HD] = result[
                        h * text_rows : (h + 1) * text_rows
                    ]

        out_ref[...] = jnp.dot(
            attended_ref[...], weight_ref[...], preferred_element_type=F32
        ).astype(BF16)

    return pl.pallas_call(
        kernel,
        grid_spec=pltpu.PrefetchScalarGridSpec(
            num_scalar_prefetch=1,
            grid=(columns // wide,),
            in_specs=[pl.BlockSpec((rows, width), lambda i, meta: (0, 0))]
            + [pl.BlockSpec(piece.shape, lambda i, meta: (0, 0)) for piece in kv_pieces]
            + [pl.BlockSpec((width, wide), lambda i, meta: (0, i))],
            out_specs=pl.BlockSpec((rows, wide), lambda i, meta: (0, i)),
            scratch_shapes=[
                pltpu.VMEM((SLOTS, HD), BF16),
                pltpu.VMEM((SLOTS, HD), BF16),
                pltpu.VMEM((rows, width), BF16),
            ],
        ),
        out_shape=jax.ShapeDtypeStruct((rows, columns), BF16),
        compiler_params=params(),
        cost_estimate=pl.CostEstimate(
            flops=2 * rows * width * (columns + 2 * BLOCK),
            bytes_accessed=2 * columns * (width + rows),
            transcendentals=rows * heads * BLOCK,
        ),
        name="attend",
    )(meta, queries, *kv_pieces, weight)


def after(value, *others):
    return lax.optimization_barrier((value, *others))[0]


def local(
    mesh_shape,
    text_state,
    tile_feats,
    w_proj,
    w_query,
    w_kv,
    w_out,
    attn_gate,
    tile_counts,
    section_table,
):
    mp_count, section_count = mesh_shape["mp"], mesh_shape["section"]
    ring = ring_order(mp_count)
    far = mp_count // 2
    sharing = mp_count // KVH
    order = [far]
    for distance in range(far - 1, 0, -1):
        order += [-distance, distance]
    order.append(0)
    index_of = {offset: index for index, offset in enumerate(order)}
    index_of[-far] = 0
    table = np.array(
        [
            [ring[(ring.index(m) + offset) % mp_count] for offset in order] + [m, s]
            for s in range(section_count)
            for m in range(mp_count)
        ],
        np.int32,
    )
    device = lax.axis_index(("section", "mp"))
    places = lax.dynamic_slice(
        jnp.asarray(table), (device, 0), (1, mp_count + 2)
    ).reshape(-1)
    starts, counts = own_samples(tile_counts, section_table, places[mp_count + 1])
    meta = jnp.concatenate([places, starts, counts])

    up_pairs = [(ring[i], ring[(i + 1) % mp_count]) for i in range(mp_count)]
    down_pairs = [(target, source) for source, target in up_pairs]

    def up(value):
        return lax.ppermute(value, "mp", up_pairs)

    def down(value):
        return lax.ppermute(value, "mp", down_pairs)

    def across(pairs):
        return [
            (s * mp_count + a, ((s + 1) % section_count) * mp_count + b)
            for s in range(section_count)
            for a, b in pairs
        ]

    def up_across(value):
        return lax.ppermute(value, ("section", "mp"), across(up_pairs))

    def down_across(value):
        return lax.ppermute(value, ("section", "mp"), across(down_pairs))

    def to_next(value):
        return lax.ppermute(
            value, "section", [(s, (s + 1) % section_count) for s in range(section_count)]
        )

    def ring_sum(part, start_up, start_down, last_up=up, last_down=down):
        hops = []
        for start, sign, move, last in (
            (start_up, 1, up, last_up),
            (start_down, -1, down, last_down),
        ):
            running = part(sign * start)
            came = []
            for distance in range(start, 1, -1):
                came.append(move(running))
                running = add(came[-1], part(sign * (distance - 1)))
            came.append(last(running))
            hops.append(came)
        return hops

    text_own = text_state[0]
    text_rows = text_own.shape[0]
    parts = 2 if text_rows % 32 == 0 else 1
    cut = text_rows // parts
    halves = [text_own[i * cut : (i + 1) * cut] for i in range(parts)]
    reach = [(far, far - 1), (far - 1, far)][:parts]
    from_below, from_above = [halves], [halves]

    def text_round(distance, *first):
        below, above = [], []
        for part, (reach_up, reach_down) in enumerate(reach):
            if distance <= reach_up:
                below.append(up(after(from_below[-1][part], *first)))
            if distance <= reach_down:
                above.append(down(after(from_above[-1][part], *first)))
        from_below.append(below)
        from_above.append(above)

    text_round(1)

    image_part = project(meta, tile_feats, w_proj, mp_count)
    feat_rows = tile_feats.shape[0]
    image_rows = feat_rows // 2
    image_halves, image_hops = [], []
    for half, (start_up, start_down) in enumerate(((far, far - 1), (far - 1, far))):

        def image_block(offset, half=half):
            return image_part[
                index_of[offset], half * image_rows : (half + 1) * image_rows
            ]

        hops = ring_sum(image_block, start_up, start_down)
        image_hops += hops
        total = image_block(0).astype(F32) + hops[0][-1].astype(F32) + hops[1][-1].astype(F32)
        image_halves.append(total.astype(BF16))
    image_cols = jnp.concatenate(image_halves, axis=0)

    for distance in range(2, far + 1):
        text_round(distance, *([hops[-2] for hops in image_hops] if distance == 2 else []))
    text_next = to_next(text_own)
    gate_next = to_next(attn_gate)

    pieces = []
    moving = image_cols
    for step in range(section_count // 2):
        pieces += [
            moving,
            lax.ppermute(moving, "section", [(s, s ^ 1) for s in range(section_count)]),
        ]
        if step + 1 < section_count // 2:
            moving = lax.ppermute(
                moving,
                "section",
                [(s, (s + 2) % section_count) for s in range(section_count)],
            )

    kv_part = key_values(meta, pieces, w_kv[0], mp_count, section_count, sharing)

    def kv_block(offset):
        return kv_part[index_of[offset]]

    hops = ring_sum(kv_block, far, far - 1)
    kv_own = (
        kv_block(0).astype(F32) + hops[0][-1].astype(F32) + hops[1][-1].astype(F32)
    ).astype(BF16)
    kv_pieces = [kv_own]
    for step in range(1, sharing):
        pairs = [
            (m, m // sharing * sharing + (m % sharing + step) % sharing) for m in range(mp_count)
        ]
        kv_pieces.append(lax.ppermute(kv_own, "mp", pairs))

    weight_query, weight_out = w_query[0], w_out[0]
    near = []
    near_queries = []
    for distance in range(1, far):
        chunks = from_below[distance] + from_above[distance]
        near += [-distance, distance]
        if distance == 1:
            chunks = chunks + halves
            near.append(0)
        near_queries.append(query(chunks, weight_query))
    near_queries = jnp.concatenate(near_queries, axis=0)
    far_queries = query(from_below[far] + from_above[far], weight_query)
    far_part = attend(
        meta, far_queries, kv_pieces, weight_out, [index_of[far]], text_rows, mp_count
    )
    near_part = attend(
        meta,
        near_queries,
        kv_pieces,
        weight_out,
        [index_of[offset] for offset in near],
        text_rows,
        mp_count,
    )

    own_first = near.index(0) * text_rows
    own_next = to_next(near_part[own_first : own_first + text_rows])
    results = []
    for part, (start_up, start_down) in enumerate(reach):

        def out_block(offset, part=part):
            if abs(offset) == far:
                return far_part[part * cut : (part + 1) * cut]
            first = near.index(offset) * text_rows + part * cut
            return near_part[first : first + cut]

        hops = ring_sum(out_block, start_up, start_down, up_across, down_across)
        rows = slice(part * cut, (part + 1) * cut)
        branch = own_next[rows].astype(F32) + hops[0][-1].astype(F32) + hops[1][-1].astype(F32)
        results.append(
            (text_next[rows].astype(F32) + jnp.tanh(gate_next[0]) * branch).astype(BF16)
        )
    return jnp.concatenate(results, axis=0)[None]


def solution(mesh):
    mesh_shape = dict(mesh.shape)

    def body(*arrays):
        return local(mesh_shape, *arrays)

    return jax.shard_map(
        body,
        mesh=mesh,
        in_specs=(
            P("section", "mp", None),
            P("section", "mp"),
            P("mp", None),
            P("section", None, "mp"),
            P("section", "mp", None),
            P("section", "mp", None),
            P("section"),
            P(),
            P(),
        ),
        out_specs=P("section", "mp", None),
        check_vma=False,
    )
```

time: 335 us -> 293 us (0.87)
  Pallas kernels: 0 us -> 58 us
  matrix products: 47.9 us -> 0 us
  between operations: 38.3 us -> 1.08 us
  local copies, waits for them, and re-layouts: 30.6 us -> 6.16 us
  waiting for transfers between devices: 139 us -> 154 us
  other arithmetic: 22.8 us -> 8.7 us
  starting transfers between devices: 55.1 us -> 64 us
    pallas_call x0 -> x8, Pallas kernels: none -> 58 us  [the longest x4 27.7 us: query(): pl.pallas_call(kernel, grid=(width // wide,), in_specs=[pl.BlockSpec(chun...]
    dot_general x12 -> x0, matrix products: 47.9 us -> none  [the longest x4 15.5 us: query_of(): projected = jnp.dot(rows, weight_query, preferred_element_type=F32) * scale]
    ppermute x23, waiting for transfers between devices: 51 us -> 81.1 us  [up(): return lax.ppermute(value, 'mp', up_pairs)]
    ppermute x22, waiting for transfers between devices: 54 us -> 38 us  [down(): return lax.ppermute(value, 'mp', down_pairs)]
    ppermute x23, starting transfers between devices: 31.6 us -> 42.2 us  [up(): return lax.ppermute(value, 'mp', up_pairs)]
    ppermute x3, waiting for transfers between devices: 15.4 us -> 6.54 us  [to_next(): lax.ppermute(value, 'section', [(s, (s + 1) % section_count) for s in ran...]
    unnamed x48 -> x12, local copies, waits for them, and re-layouts: 13 us -> 4.5 us
    ppermute x1, waiting for transfers between devices: 0.01 us -> 8.04 us  [local(): lax.ppermute(moving, 'section', [(s, (s + 2) % section_count) for s in ra...]
  transfers between devices with their start and end apart: 56 -> 56, of which waited for: 31 -> 32; matrix products, arithmetic and copies ran while one was open for 23% -> 1% of each run, Pallas kernels for 0% -> 15%
where the time goes in v2:
time: 293 us; the launch traced here: 292 us
  waiting for transfers between devices  154 us (53%)
  starting transfers between devices  64 us (22%)
  Pallas kernels  58 us (20%)
  other arithmetic  8.7 us (3%)
  local copies, waits for them, and re-layouts  6.16 us (2%)
    ppermute x23, waiting for transfers between devices, up(): return lax.ppermute(value, 'mp', up_pairs)  81.1 us
    ppermute x23, starting transfers between devices, up(): return lax.ppermute(value, 'mp', up_pairs)  42.2 us
    ppermute x22, waiting for transfers between devices, down(): return lax.ppermute(value, 'mp', down_pairs)  38 us
    pallas_call x4, Pallas kernels, query(): pl.pallas_call(kernel, grid=(width // wide,), in_specs=[pl.BlockSpec(chun...  27.7 us
    ppermute x2, waiting for transfers between devices, up_across(): return lax.ppermute(value, ('section', 'mp'), across(up_pairs))  19.7 us
    pallas_call x2, Pallas kernels, attend(): pl.pallas_call(kernel, grid_spec=pltpu.PrefetchScalarGridSpec(num_scalar_...  14.5 us
    ppermute x22, starting transfers between devices, down(): return lax.ppermute(value, 'mp', down_pairs)  13.1 us
    pallas_call x1, Pallas kernels, project(): pl.pallas_call(kernel, grid_spec=pltpu.PrefetchScalarGridSpec(num_scalar_...  11.4 us
  transfers between devices with their start and end apart: 56, of which 32 were waited for; matrix products, arithmetic and copies ran while one was open for 1% of the time, Pallas kernels for 15%

profile of v2, /device:TPU:0, one launch (start us, length us, event | category | flops | bytes accessed | tf_op | source)
XLA Modules:
  0.0 292.3 jit_solution(9239766608572281228)
XLA Ops:
  6.3 11.4 %project.1 = bf16[8,320,1024]{2,1,0:T(8,128)(2,1)S(1)} custom-call(s32[18]{0:T(128)S(1)} %pad_add_fusion.meta_ref, bf16[320,960]{1,0:T(8,128)(2,1)S(1)} %copy-done.1, bf16[960,8192]{1,0:T(8,128)(2,1)} %weight_ref.1), custom_call_target="tpu_custom_call" | custom-call | flops 5033164800 | bytes 20971520 | tf_op jit(solution)/shard_map/project/pallas_call | solution.py:69
  22.8 5.7 %collective-permute-done.6 = bf16[160,1024]{1,0:T(8,128)(2,1)S(1)} collective-permute-done((bf16[160,1024]{1,0:T(8,128)(2,1)S(1)}, bf16[160,1024]{1,0:T(8,128)(2,1)S(1)}, u32[]{:S(2)}, u32[]{:S(2)}) %collective-permute-start.6) | collective-permute-done | bytes 327712 | tf_op jit(solution)/shard_map/ppermute | solution.py:309
  32.1 5.0 %collective-permute-done.9 = bf16[160,1024]{1,0:T(8,128)(2,1)S(1)} collective-permute-done((bf16[160,1024]{1,0:T(8,128)(2,1)S(1)}, bf16[160,1024]{1,0:T(8,128)(2,1)S(1)}, u32[]{:S(2)}, u32[]{:S(2)}) %collective-permute-start.9) | collective-permute-done | bytes 327712 | tf_op jit(solution)/shard_map/ppermute | solution.py:312
  57.7 5.6 %collective-permute-done.12 = bf16[160,1024]{1,0:T(8,128)(2,1)S(1)} collective-permute-done((bf16[160,1024]{1,0:T(8,128)(2,1)S(1)}, bf16[160,1024]{1,0:T(8,128)(2,1)S(1)}, u32[]{:S(2)}, u32[]{:S(2)}) %collective-permute-start.12) | collective-permute-done | bytes 327712 | tf_op jit(solution)/shard_map/ppermute | solution.py:309
  70.6 5.0 %collective-permute-done.26 = bf16[160,1024]{1,0:T(8,128)(2,1)S(1)} collective-permute-done((bf16[160,1024]{1,0:T(8,128)(2,1)S(1)}, bf16[160,1024]{1,0:T(8,128)(2,1)S(1)}, u32[]{:S(2)}, u32[]{:S(2)}) %collective-permute-start.26) | collective-permute-done | bytes 327712 | tf_op jit(solution)/shard_map/ppermute | solution.py:309
  82.1 8.0 %collective-permute-done.29.refs_2_ = bf16[320,1024]{1,0:T(8,128)(2,1)S(1)} collective-permute-done((bf16[320,1024]{1,0:T(8,128)(2,1)S(1)}, bf16[320,1024]{1,0:T(8,128)(2,1)S(1)}, u32[]{:S(2)}, u32[]{:S(2)}) %collective-permute-start.29) | collective-permute-done | bytes 655392 | tf_op jit(solution)/shard_map/ppermute | solution.py:397
  94.7 10.2 %collective-permute-done.3.refs_1_ = bf16[32,8192]{1,0:T(8,128)(2,1)S(1)} collective-permute-done((bf16[32,8192]{1,0:T(8,128)(2,1)S(1)}, bf16[32,8192]{1,0:T(8,128)(2,1)S(1)}, u32[]{:S(2)}, u32[]{:S(2)}) %collective-permute-start.3) | collective-permute-done | bytes 524320 | tf_op jit(solution)/shard_map/ppermute | solution.py:309
  108.8 7.4 %collective-permute-done.2.refs_0_ = bf16[32,8192]{1,0:T(8,128)(2,1)S(1)} collective-permute-done((bf16[32,8192]{1,0:T(8,128)(2,1)S(1)}, bf16[32,8192]{1,0:T(8,128)(2,1)S(1)}, u32[]{:S(2)}, u32[]{:S(2)}) %collective-permute-start.2) | collective-permute-done | bytes 524320 | tf_op jit(solution)/shard_map/ppermute | solution.py:309
  118.4 4.4 %key_values.1 = bf16[8,256,256]{2,1,0:T(8,128)(2,1)S(1)} custom-call(s32[18]{0:T(128)S(1)} %pad_add_fusion.meta_ref, bf16[320,1024]{1,0:T(8,128)(2,1)S(1)} %pad_maximum_fusion.refs_0_, bf16[320,1024]{1,0:T(8,128)(2,1)S(1)} %collective-permute-done.28.refs_1_, bf16[320,1024]{1,0:T(8,128)(2,1)S(1)} %collective-permute-done.29.refs_2_, ...), custom_call_target="tpu_custom_call" | custom-call | flops 2415919104 | bytes 4718592 | tf_op jit(solution)/shard_map/key_values/pallas_call | solution.py:131
  125.2 4.6 %collective-permute-done.19.refs_3_ = bf16[32,8192]{1,0:T(8,128)(2,1)S(1)} collective-permute-done((bf16[32,8192]{1,0:T(8,128)(2,1)S(1)}, bf16[32,8192]{1,0:T(8,128)(2,1)S(1)}, u32[]{:S(2)}, u32[]{:S(2)}) %collective-permute-start.19) | collective-permute-done | bytes 524320 | tf_op jit(solution)/shard_map/ppermute | solution.py:312
  129.8 8.8 %collective-permute-done.16.refs_0_ = bf16[32,8192]{1,0:T(8,128)(2,1)S(1)} collective-permute-done((bf16[32,8192]{1,0:T(8,128)(2,1)S(1)}, bf16[32,8192]{1,0:T(8,128)(2,1)S(1)}, u32[]{:S(2)}, u32[]{:S(2)}) %collective-permute-start.16) | collective-permute-done | bytes 524320 | tf_op jit(solution)/shard_map/ppermute | solution.py:309
  150.2 6.1 %collective-permute-done.32 = bf16[256,256]{1,0:T(8,128)(2,1)S(1)} collective-permute-done((bf16[256,256]{1,0:T(8,128)(2,1)S(1)}, bf16[256,256]{1,0:T(8,128)(2,1)S(1)}, u32[]{:S(2)}, u32[]{:S(2)}) %collective-permute-start.32) | collective-permute-done | bytes 131104 | tf_op jit(solution)/shard_map/ppermute | solution.py:309
  158.6 10.1 %query.4 = bf16[192,512]{1,0:T(8,128)(2,1)S(1)} custom-call(bf16[32,8192]{1,0:T(8,128)(2,1)S(1)} %collective-permute-done.2.refs_0_, bf16[32,8192]{1,0:T(8,128)(2,1)S(1)} %collective-permute-done.3.refs_1_, bf16[32,8192]{1,0:T(8,128)(2,1)S(1)} %collective-permute-done.4.refs_2_, bf16[32,8192]{1,0:T(8,128)(2,1)S(1)} %collective-permute-done.5.refs_3_, ...), custom_call_target="tpu_custom_call" | custom-call | flops 1610612736 | bytes 11534336 | tf_op jit(solution)/shard_map/query/pallas_call | solution.py:168
  173.8 6.9 %query.5 = bf16[128,512]{1,0:T(8,128)(2,1)S(1)} custom-call(bf16[32,8192]{1,0:T(8,128)(2,1)S(1)} %collective-permute-done.16.refs_0_, bf16[32,8192]{1,0:T(8,128)(2,1)S(1)} %collective-permute-done.17.refs_1_, bf16[32,8192]{1,0:T(8,128)(2,1)S(1)} %collective-permute-done.18.refs_2_, bf16[32,8192]{1,0:T(8,128)(2,1)S(1)} %collective-permute-done.19.refs_3_, ...), custom_call_target="tpu_custom_call" | custom-call | flops 1073741824 | bytes 10485760 | tf_op jit(solution)/shard_map/query/pallas_call | solution.py:168
  180.7 6.9 %query.6 = bf16[128,512]{1,0:T(8,128)(2,1)S(1)} custom-call(bf16[32,8192]{1,0:T(8,128)(2,1)S(1)} %collective-permute-done.20.refs_0_, bf16[32,8192]{1,0:T(8,128)(2,1)S(1)} %collective-permute-done.21.refs_1_, bf16[32,8192]{1,0:T(8,128)(2,1)S(1)} %collective-permute-done.22.refs_2_, bf16[32,8192]{1,0:T(8,128)(2,1)S(1)} %collective-permute-done.23.refs_3_, ...), custom_call_target="tpu_custom_call" | custom-call | flops 1073741824 | bytes 10485760 | tf_op jit(solution)/shard_map/query/pallas_call | solution.py:168
  196.1 4.2 %attend.3 = bf16[64,8192]{1,0:T(8,128)(2,1)S(1)} custom-call(s32[18]{0:T(128)S(1)} %pad_add_fusion.meta_ref, bf16[64,512]{1,0:T(8,128)(2,1)S(1)} %query.7.query_ref, bf16[256,256]{1,0:T(8,128)(2,1)S(1)} %fusion.20.refs_0_, bf16[256,256]{1,0:T(8,128)(2,1)S(1)} %collective-permute-done.38.refs_1_, bf16[512,8192]{1,0:T(8,128)(2,1)S(1)} %bitcast.123), custom_call_target="tpu_custom_call" | custom-call | flops 553648128 | bytes 9437184 | tf_op jit(solution)/shard_map/attend/pallas_call | solution.py:238
  202.5 10.3 %attend.2 = bf16[448,8192]{1,0:T(8,128)(2,1)S(1)} custom-call(s32[18]{0:T(128)S(1)} %pad_add_fusion.meta_ref, bf16[448,512]{1,0:T(8,128)(2,1)S(1)} %pad_maximum_fusion.1.query_ref, bf16[256,256]{1,0:T(8,128)(2,1)S(1)} %fusion.20.refs_0_, bf16[256,256]{1,0:T(8,128)(2,1)S(1)} %collective-permute-done.38.refs_1_, bf16[512,8192]{1,0:T(8,128)(2,1)} %bitcast.122), custom_call_target="tpu_custom_call" | custom-call | flops 3875536896 | bytes 15728640 | tf_op jit(solution)/shard_map/attend/pallas_call | solution.py:238
  217.3 10.5 %collective-permute-done.46 = bf16[32,8192]{1,0:T(8,128)(2,1)S(1)} collective-permute-done((bf16[32,8192]{1,0:T(8,128)(2,1)S(1)}, bf16[32,8192]{1,0:T(8,128)(2,1)S(1)}, u32[]{:S(2)}, u32[]{:S(2)}) %collective-permute-start.46) | collective-permute-done | bytes 524320 | tf_op jit(solution)/shard_map/ppermute | solution.py:312
  228.8 7.9 %collective-permute-done.43 = bf16[32,8192]{1,0:T(8,128)(2,1)S(1)} collective-permute-done((bf16[32,8192]{1,0:T(8,128)(2,1)S(1)}, bf16[32,8192]{1,0:T(8,128)(2,1)S(1)}, u32[]{:S(2)}, u32[]{:S(2)}) %collective-permute-start.43) | collective-permute-done | bytes 524320 | tf_op jit(solution)/shard_map/ppermute | solution.py:309
  241.4 10.7 %collective-permute-done.44 = bf16[32,8192]{1,0:T(8,128)(2,1)S(1)} collective-permute-done((bf16[32,8192]{1,0:T(8,128)(2,1)S(1)}, bf16[32,8192]{1,0:T(8,128)(2,1)S(1)}, u32[]{:S(2)}, u32[]{:S(2)}) %collective-permute-start.44) | collective-permute-done | bytes 524320 | tf_op jit(solution)/shard_map/ppermute | solution.py:309
  254.3 4.4 %collective-permute-done.50 = bf16[32,8192]{1,0:T(8,128)(2,1)S(1)} collective-permute-done((bf16[32,8192]{1,0:T(8,128)(2,1)S(1)}, bf16[32,8192]{1,0:T(8,128)(2,1)S(1)}, u32[]{:S(2)}, u32[]{:S(2)}) %collective-permute-start.50) | collective-permute-done | bytes 524320 | tf_op jit(solution)/shard_map/ppermute | solution.py:309
  264.4 6.5 %collective-permute-done.39 = bf16[64,8192]{1,0:T(8,128)(2,1)S(1)} collective-permute-done((bf16[64,8192]{1,0:T(8,128)(2,1)S(1)}, bf16[64,8192]{1,0:T(8,128)(2,1)S(1)}, u32[]{:S(2)}, u32[]{:S(2)}) %collective-permute-start.39) | collective-permute-done | bytes 1048608 | tf_op jit(solution)/shard_map/ppermute | solution.py:328
  270.9 12.4 %collective-permute-done.45 = bf16[32,8192]{1,0:T(8,128)(2,1)S(1)} collective-permute-done((bf16[32,8192]{1,0:T(8,128)(2,1)S(1)}, bf16[32,8192]{1,0:T(8,128)(2,1)S(1)}, u32[]{:S(2)}, u32[]{:S(2)}) %collective-permute-start.45) | collective-permute-done | bytes 524320 | tf_op jit(solution)/shard_map/ppermute | solution.py:322
  283.4 7.3 %collective-permute-done.51 = bf16[32,8192]{1,0:T(8,128)(2,1)S(1)} collective-permute-done((bf16[32,8192]{1,0:T(8,128)(2,1)S(1)}, bf16[32,8192]{1,0:T(8,128)(2,1)S(1)}, u32[]{:S(2)}, u32[]{:S(2)}) %collective-permute-start.51) | collective-permute-done | bytes 524320 | tf_op jit(solution)/shard_map/ppermute | solution.py:322
  (139 shorter events, 110.9 us)
Async XLA Ops:
  20.9 16.2 %collective-permute-start.9 = (bf16[160,1024]{1,0:T(8,128)(2,1)S(1)}, bf16[160,1024]{1,0:T(8,128)(2,1)S(1)}, u32[]{:S(2)}, u32[]{:S(2)}) collective-permute-start(bf16[160,1024]{1,0:T(8,128)(2,1)S(1)} %get-tuple-element.39), channel_id=1, source_target_pairs={{2,0},{4,2},{6,4},{7,6},{5,7},{3,5},{1,3},{0,1},{10,8},{12,10},{14... | collective-permute-start | bytes 983048 | tf_op jit(solution)/shard_map/ppermute | solution.py:312
  82.1 34.4 %collective-permute-start.28 = (bf16[320,1024]{1,0:T(8,128)(2,1)S(1)}, bf16[320,1024]{1,0:T(8,128)(2,1)S(1)}, u32[]{:S(2)}, u32[]{:S(2)}) collective-permute-start(bf16[320,1024]{1,0:T(8,128)(2,1)S(1)} %pad_maximum_fusion.refs_0_), channel_id=1, source_target_pairs={{0,8},{8,0},{16,24},{24,16},{1,9},{9,1},{17,25},{25,17},{2,10},{10... | collective-permute-start | bytes 1966088 | tf_op jit(solution)/shard_map/ppermute | solution.py:394
  90.2 28.2 %collective-permute-start.30 = (bf16[320,1024]{1,0:T(8,128)(2,1)S(1)}, bf16[320,1024]{1,0:T(8,128)(2,1)S(1)}, u32[]{:S(2)}, u32[]{:S(2)}) collective-permute-start(bf16[320,1024]{1,0:T(8,128)(2,1)S(1)} %collective-permute-done.29.refs_2_), channel_id=1, source_target_pairs={{0,8},{8,0},{16,24},{24,16},{1,9},{9,1},{17,25},{25,17},{2,10},{10... | collective-permute-start | bytes 1966088 | tf_op jit(solution)/shard_map/ppermute | solution.py:394
  92.4 23.7 %collective-permute-start.2 = (bf16[32,8192]{1,0:T(8,128)(2,1)S(1)}, bf16[32,8192]{1,0:T(8,128)(2,1)S(1)}, u32[]{:S(2)}, u32[]{:S(2)}) collective-permute-start(bf16[32,8192]{1,0:T(8,128)(2,1)S(1)} %get-tuple-element.52.refs_4_), channel_id=1, source_target_pairs={{0,2},{2,4},{4,6},{6,7},{7,5},{5,3},{3,1},{1,0},{8,10},{10,12},{12... | collective-permute-start | bytes 1572872 | tf_op jit(solution)/shard_map/ppermute | solution.py:309
  104.9 36.9 %collective-permute-start.18 = (bf16[32,8192]{1,0:T(8,128)(2,1)S(1)}, bf16[32,8192]{1,0:T(8,128)(2,1)S(1)}, u32[]{:S(2)}, u32[]{:S(2)}) collective-permute-start(bf16[32,8192]{1,0:T(8,128)(2,1)S(1)} %collective-permute-done.4.refs_2_), channel_id=1, source_target_pairs={{2,0},{4,2},{6,4},{7,6},{5,7},{3,5},{1,3},{0,1},{10,8},{12,10},{14... | collective-permute-start | bytes 1572872 | tf_op jit(solution)/shard_map/ppermute | solution.py:312
  107.0 36.7 %collective-permute-start.17 = (bf16[32,8192]{1,0:T(8,128)(2,1)S(1)}, bf16[32,8192]{1,0:T(8,128)(2,1)S(1)}, u32[]{:S(2)}, u32[]{:S(2)}) collective-permute-start(bf16[32,8192]{1,0:T(8,128)(2,1)S(1)} %collective-permute-done.3.refs_1_), channel_id=1, source_target_pairs={{0,2},{2,4},{4,6},{6,7},{7,5},{5,3},{3,1},{1,0},{8,10},{10,12},{12... | collective-permute-start | bytes 1572872 | tf_op jit(solution)/shard_map/ppermute | solution.py:309
  116.5 22.1 %collective-permute-start.16 = (bf16[32,8192]{1,0:T(8,128)(2,1)S(1)}, bf16[32,8192]{1,0:T(8,128)(2,1)S(1)}, u32[]{:S(2)}, u32[]{:S(2)}) collective-permute-start(bf16[32,8192]{1,0:T(8,128)(2,1)S(1)} %collective-permute-done.2.refs_0_), channel_id=1, source_target_pairs={{0,2},{2,4},{4,6},{6,7},{7,5},{5,3},{3,1},{1,0},{8,10},{10,12},{12... | collective-permute-start | bytes 1572872 | tf_op jit(solution)/shard_map/ppermute | solution.py:309
  122.8 18.6 %collective-permute-start.31 = (bf16[256,256]{1,0:T(8,128)(2,1)S(1)}, bf16[256,256]{1,0:T(8,128)(2,1)S(1)}, u32[]{:S(2)}, u32[]{:S(2)}) collective-permute-start(bf16[256,256]{1,0:T(8,128)(2,1)S(1)} %get-tuple-element.49), channel_id=1, source_target_pairs={{0,2},{2,4},{4,6},{6,7},{7,5},{5,3},{3,1},{1,0},{8,10},{10,12},{12... | collective-permute-start | bytes 393224 | tf_op jit(solution)/shard_map/ppermute | solution.py:309
  129.8 28.8 %collective-permute-start.23 = (bf16[32,8192]{1,0:T(8,128)(2,1)S(1)}, bf16[32,8192]{1,0:T(8,128)(2,1)S(1)}, u32[]{:S(2)}, u32[]{:S(2)}) collective-permute-start(bf16[32,8192]{1,0:T(8,128)(2,1)S(1)} %collective-permute-done.19.refs_3_), channel_id=1, source_target_pairs={{2,0},{4,2},{6,4},{7,6},{5,7},{3,5},{1,3},{0,1},{10,8},{12,10},{14... | collective-permute-start | bytes 1572872 | tf_op jit(solution)/shard_map/ppermute | solution.py:312
  138.6 30.1 %collective-permute-start.20 = (bf16[32,8192]{1,0:T(8,128)(2,1)S(1)}, bf16[32,8192]{1,0:T(8,128)(2,1)S(1)}, u32[]{:S(2)}, u32[]{:S(2)}) collective-permute-start(bf16[32,8192]{1,0:T(8,128)(2,1)S(1)} %collective-permute-done.16.refs_0_), channel_id=1, source_target_pairs={{0,2},{2,4},{4,6},{6,7},{7,5},{5,3},{3,1},{1,0},{8,10},{10,12},{12... | collective-permute-start | bytes 1572872 | tf_op jit(solution)/shard_map/ppermute | solution.py:309
  143.7 30.1 %collective-permute-start.22 = (bf16[32,8192]{1,0:T(8,128)(2,1)S(1)}, bf16[32,8192]{1,0:T(8,128)(2,1)S(1)}, u32[]{:S(2)}, u32[]{:S(2)}) collective-permute-start(bf16[32,8192]{1,0:T(8,128)(2,1)S(1)} %collective-permute-done.18.refs_2_), channel_id=1, source_target_pairs={{2,0},{4,2},{6,4},{7,6},{5,7},{3,5},{1,3},{0,1},{10,8},{12,10},{14... | collective-permute-start | bytes 1572872 | tf_op jit(solution)/shard_map/ppermute | solution.py:312
  147.3 33.4 %collective-permute-start.21 = (bf16[32,8192]{1,0:T(8,128)(2,1)S(1)}, bf16[32,8192]{1,0:T(8,128)(2,1)S(1)}, u32[]{:S(2)}, u32[]{:S(2)}) collective-permute-start(bf16[32,8192]{1,0:T(8,128)(2,1)S(1)} %collective-permute-done.17.refs_1_), channel_id=1, source_target_pairs={{0,2},{2,4},{4,6},{6,7},{7,5},{5,3},{3,1},{1,0},{8,10},{10,12},{12... | collective-permute-start | bytes 1572872 | tf_op jit(solution)/shard_map/ppermute | solution.py:309
  168.7 19.1 %collective-permute-start.41 = (bf16[32,8192]{1,0:T(8,128)(2,1)S(1)}, bf16[32,8192]{1,0:T(8,128)(2,1)S(1)}, u32[]{:S(2)}, u32[]{:S(2)}) collective-permute-start(bf16[32,8192]{1,0:T(8,128)(2,1)S(1)} %collective-permute-done.23.refs_3_), channel_id=1, source_target_pairs={{2,0},{4,2},{6,4},{7,6},{5,7},{3,5},{1,3},{0,1},{10,8},{12,10},{14... | collective-permute-start | bytes 1572872 | tf_op jit(solution)/shard_map/ppermute | solution.py:312
  169.1 18.7 %collective-permute-start.40 = (bf16[32,8192]{1,0:T(8,128)(2,1)S(1)}, bf16[32,8192]{1,0:T(8,128)(2,1)S(1)}, u32[]{:S(2)}, u32[]{:S(2)}) collective-permute-start(bf16[32,8192]{1,0:T(8,128)(2,1)S(1)} %collective-permute-done.20.refs_0_), channel_id=1, source_target_pairs={{0,2},{2,4},{4,6},{6,7},{7,5},{5,3},{3,1},{1,0},{8,10},{10,12},{12... | collective-permute-start | bytes 1572872 | tf_op jit(solution)/shard_map/ppermute | solution.py:309
  215.2 21.5 %collective-permute-start.43 = (bf16[32,8192]{1,0:T(8,128)(2,1)S(1)}, bf16[32,8192]{1,0:T(8,128)(2,1)S(1)}, u32[]{:S(2)}, u32[]{:S(2)}) collective-permute-start(bf16[32,8192]{1,0:T(8,128)(2,1)S(1)} %get-tuple-element.23), channel_id=1, source_target_pairs={{0,2},{2,4},{4,6},{6,7},{7,5},{5,3},{3,1},{1,0},{8,10},{10,12},{12... | collective-permute-start | bytes 1572872 | tf_op jit(solution)/shard_map/ppermute | solution.py:309
  217.2 19.5 %collective-permute-start.53 = (bf16[32,8192]{1,0:T(8,128)(2,1)S(1)}, bf16[32,8192]{1,0:T(8,128)(2,1)S(1)}, u32[]{:S(2)}, u32[]{:S(2)}) collective-permute-start(bf16[32,8192]{1,0:T(8,128)(2,1)S(1)} %get-tuple-element.24), channel_id=1, source_target_pairs={{2,0},{4,2},{6,4},{7,6},{5,7},{3,5},{1,3},{0,1},{10,8},{12,10},{14... | collective-permute-start | bytes 1572872 | tf_op jit(solution)/shard_map/ppermute | solution.py:312
  239.3 19.4 %collective-permute-start.50 = (bf16[32,8192]{1,0:T(8,128)(2,1)S(1)}, bf16[32,8192]{1,0:T(8,128)(2,1)S(1)}, u32[]{:S(2)}, u32[]{:S(2)}) collective-permute-start(bf16[32,8192]{1,0:T(8,128)(2,1)S(1)} %get-tuple-element.21), channel_id=1, source_target_pairs={{0,2},{2,4},{4,6},{6,7},{7,5},{5,3},{3,1},{1,0},{8,10},{10,12},{12... | collective-permute-start | bytes 1572872 | tf_op jit(solution)/shard_map/ppermute | solution.py:309
  240.2 18.5 %collective-permute-start.54 = (bf16[32,8192]{1,0:T(8,128)(2,1)S(1)}, bf16[32,8192]{1,0:T(8,128)(2,1)S(1)}, u32[]{:S(2)}, u32[]{:S(2)}) collective-permute-start(bf16[32,8192]{1,0:T(8,128)(2,1)S(1)} %get-tuple-element.20), channel_id=1, source_target_pairs={{2,0},{4,2},{6,4},{7,6},{5,7},{3,5},{1,3},{0,1},{10,8},{12,10},{14... | collective-permute-start | bytes 1572872 | tf_op jit(solution)/shard_map/ppermute | solution.py:312
  241.3 21.2 %collective-permute-start = (bf16[64,8192]{1,0:T(8,128)(2,1)S(1)}, bf16[64,8192]{1,0:T(8,128)(2,1)S(1)}, u32[]{:S(2)}, u32[]{:S(2)}) collective-permute-start(bf16[64,8192]{1,0:T(8,128)(2,1)S(1)} %bitcast.125), channel_id=1, source_target_pairs={{0,8},{8,16},{16,24},{24,0},{1,9},{9,17},{17,25},{25,1},{2,10},{10... | collective-permute-start | bytes 3145736 | tf_op jit(solution)/shard_map/ppermute | solution.py:328
  252.6 18.3 %collective-permute-start.39 = (bf16[64,8192]{1,0:T(8,128)(2,1)S(1)}, bf16[64,8192]{1,0:T(8,128)(2,1)S(1)}, u32[]{:S(2)}, u32[]{:S(2)}) collective-permute-start(bf16[64,8192]{1,0:T(8,128)(2,1)S(1)} %slice.218), channel_id=1, source_target_pairs={{0,8},{8,16},{16,24},{24,0},{1,9},{9,17},{17,25},{25,1},{2,10},{10... | collective-permute-start | bytes 3145736 | tf_op jit(solution)/shard_map/ppermute | solution.py:328
  259.2 24.1 %collective-permute-start.45 = (bf16[32,8192]{1,0:T(8,128)(2,1)S(1)}, bf16[32,8192]{1,0:T(8,128)(2,1)S(1)}, u32[]{:S(2)}, u32[]{:S(2)}) collective-permute-start(bf16[32,8192]{1,0:T(8,128)(2,1)S(1)} %get-tuple-element.15), channel_id=1, source_target_pairs={{0,10},{2,12},{4,14},{6,15},{7,13},{5,11},{3,9},{1,8},{8,18},{10,2... | collective-permute-start | bytes 1572872 | tf_op jit(solution)/shard_map/ppermute | solution.py:322
  259.3 24.1 %collective-permute-start.48 = (bf16[32,8192]{1,0:T(8,128)(2,1)S(1)}, bf16[32,8192]{1,0:T(8,128)(2,1)S(1)}, u32[]{:S(2)}, u32[]{:S(2)}) collective-permute-start(bf16[32,8192]{1,0:T(8,128)(2,1)S(1)} %get-tuple-element.18), channel_id=1, source_target_pairs={{2,8},{4,10},{6,12},{7,14},{5,15},{3,13},{1,11},{0,9},{10,16},{12,... | collective-permute-start | bytes 1572872 | tf_op jit(solution)/shard_map/ppermute | solution.py:325
  262.5 28.2 %collective-permute-start.51 = (bf16[32,8192]{1,0:T(8,128)(2,1)S(1)}, bf16[32,8192]{1,0:T(8,128)(2,1)S(1)}, u32[]{:S(2)}, u32[]{:S(2)}) collective-permute-start(bf16[32,8192]{1,0:T(8,128)(2,1)S(1)} %get-tuple-element.17), channel_id=1, source_target_pairs={{0,10},{2,12},{4,14},{6,15},{7,13},{5,11},{3,9},{1,8},{8,18},{10,2... | collective-permute-start | bytes 1572872 | tf_op jit(solution)/shard_map/ppermute | solution.py:322
  262.6 28.1 %collective-permute-start.55 = (bf16[32,8192]{1,0:T(8,128)(2,1)S(1)}, bf16[32,8192]{1,0:T(8,128)(2,1)S(1)}, u32[]{:S(2)}, u32[]{:S(2)}) collective-permute-start(bf16[32,8192]{1,0:T(8,128)(2,1)S(1)} %get-tuple-element.16), channel_id=1, source_target_pairs={{2,8},{4,10},{6,12},{7,14},{5,15},{3,13},{1,11},{0,9},{10,16},{12,... | collective-permute-start | bytes 1572872 | tf_op jit(solution)/shard_map/ppermute | solution.py:325
  (38 other events, 621.4 us)

commit v3 on v2

--- a/solution.py
+++ b/solution.py
@@ -57,11 +57,11 @@
     return pltpu.CompilerParams(vmem_limit_bytes=VMEM_LIMIT)
 
 
-def project(meta, feats, weight, order_len):
+def project(places, feats, weight, order_len, first, blocks):
     rows, depth = feats.shape
     wide = weight.shape[1] // order_len
 
-    def kernel(meta_ref, feats_ref, weight_ref, out_ref):
+    def kernel(places_ref, feats_ref, weight_ref, out_ref):
         out_ref[0] = jnp.dot(
             feats_ref[...], weight_ref[...], preferred_element_type=F32
         ).astype(BF16)
@@ -70,22 +70,22 @@
         kernel,
         grid_spec=pltpu.PrefetchScalarGridSpec(
             num_scalar_prefetch=1,
-            grid=(order_len,),
+            grid=(blocks,),
             in_specs=[
-                pl.BlockSpec((rows, depth), lambda i, meta: (0, 0)),
-                pl.BlockSpec((depth, wide), lambda i, meta: (0, meta[i])),
+                pl.BlockSpec((rows, depth), lambda i, places: (0, 0)),
+                pl.BlockSpec((depth, wide), lambda i, places: (0, places[first + i])),
             ],
-            out_specs=pl.BlockSpec((1, rows, wide), lambda i, meta: (i, 0, 0)),
-        ),
-        out_shape=jax.ShapeDtypeStruct((order_len, rows, wide), BF16),
+            out_specs=pl.BlockSpec((1, rows, wide), lambda i, places: (i, 0, 0)),
+        ),
+        out_shape=jax.ShapeDtypeStruct((blocks, rows, wide), BF16),
         compiler_params=params(),
         cost_estimate=pl.CostEstimate(
-            flops=2 * rows * depth * weight.shape[1],
-            bytes_accessed=2 * (depth + rows) * weight.shape[1],
+            flops=2 * rows * depth * wide * (blocks - 1),
+            bytes_accessed=2 * (depth + rows) * wide * (blocks - 1),
             transcendentals=0,
         ),
         name="project",
-    )(meta, feats, weight)
+    )(places, feats, weight)
 
 
 def key_values(meta, pieces, weight, order_len, section_count, sharing):
@@ -152,18 +152,27 @@
 
     def kernel(*refs):
         chunk_refs, weight_ref, out_ref = refs[:count], refs[count], refs[count + 1]
-        first = 0
-        for chunk_ref in chunk_refs:
-            size = chunk_ref.shape[0]
-            chunk = chunk_ref[...]
-            wider = chunk.astype(F32)
-            scale = lax.rsqrt(jnp.mean(wider * wider, axis=-1, keepdims=True) + 1e-05)
-            projected = jnp.dot(chunk, weight_ref[...], preferred_element_type=F32) * scale
-            for head in range(wide // HD):
-                one = projected[:, head * HD : (head + 1) * HD]
-                one = one * lax.rsqrt(jnp.mean(one * one, axis=-1, keepdims=True) + 1e-06)
-                out_ref[first : first + size, head * HD : (head + 1) * HD] = one.astype(BF16)
-            first += size
+        rows_ref, scale_ref = refs[count + 2 :]
+
+        @pl.when(pl.program_id(0) == 0)
+        def _():
+            first = 0
+            for chunk_ref in chunk_refs:
+                place = slice(first, first + chunk_ref.shape[0])
+                chunk = chunk_ref[...]
+                wider = chunk.astype(F32)
+                rows_ref[place, :] = chunk
+                scale_ref[place, :] = lax.rsqrt(
+                    jnp.mean(wider * wider, axis=-1, keepdims=True) + 1e-05
+                )
+                first += chunk_ref.shape[0]
+
+        projected = jnp.dot(rows_ref[...], weight_ref[...], preferred_element_type=F32)
+        projected = projected * scale_ref[...]
+        for head in range(wide // HD):
+            one = projected[:, head * HD : (head + 1) * HD]
+            one = one * lax.rsqrt(jnp.mean(one * one, axis=-1, keepdims=True) + 1e-06)
+            out_ref[:, head * HD : (head + 1) * HD] = one.astype(BF16)
 
     return pl.pallas_call(
         kernel,
@@ -172,6 +181,7 @@
         + [pl.BlockSpec((depth, wide), lambda i: (0, i))],
         out_specs=pl.BlockSpec((rows, wide), lambda i: (0, i)),
         out_shape=jax.ShapeDtypeStruct((rows, width), BF16),
+        scratch_shapes=[pltpu.VMEM((rows, depth), BF16), pltpu.VMEM((rows, 1), F32)],
         compiler_params=params(),
         cost_estimate=pl.CostEstimate(
             flops=2 * rows * depth * width,
@@ -329,7 +339,8 @@
             value, "section", [(s, (s + 1) % section_count) for s in range(section_count)]
         )
 
-    def ring_sum(part, start_up, start_down, last_up=up, last_down=down):
+    def ring_sum(part, start_up, start_down, last_up=up, last_down=down, tie=None):
+        tie = tie or (lambda left, value: value)
         hops = []
         for start, sign, move, last in (
             (start_up, 1, up, last_up),
@@ -338,9 +349,9 @@
             running = part(sign * start)
             came = []
             for distance in range(start, 1, -1):
-                came.append(move(running))
+                came.append(move(tie(distance, running)))
                 running = add(came[-1], part(sign * (distance - 1)))
-            came.append(last(running))
+            came.append(last(tie(1, running)))
             hops.append(came)
         return hops
 
@@ -348,43 +359,38 @@
     text_rows = text_own.shape[0]
     parts = 2 if text_rows % 32 == 0 else 1
     cut = text_rows // parts
-    halves = [text_own[i * cut : (i + 1) * cut] for i in range(parts)]
     reach = [(far, far - 1), (far - 1, far)][:parts]
-    from_below, from_above = [halves], [halves]
-
-    def text_round(distance, *first):
-        below, above = [], []
-        for part, (reach_up, reach_down) in enumerate(reach):
-            if distance <= reach_up:
-                below.append(up(after(from_below[-1][part], *first)))
-            if distance <= reach_down:
-                above.append(down(after(from_above[-1][part], *first)))
-        from_below.append(below)
-        from_above.append(above)
-
-    text_round(1)
-
-    image_part = project(meta, tile_feats, w_proj, mp_count)
+    text_next = to_next(text_own)
+    gate_next = to_next(attn_gate)
+    from_below, from_above = [text_own], [text_own]
+
+    def text_round(*first):
+        from_below.append(up(after(from_below[-1], *first)))
+        from_above.append(down(after(from_above[-1], *first)))
+
+    text_round()
+
+    image_far = project(places, tile_feats, w_proj, mp_count, 0, 1)
+    image_near = project(places, tile_feats, w_proj, mp_count, 1, mp_count - 1)
     feat_rows = tile_feats.shape[0]
     image_rows = feat_rows // 2
-    image_halves, image_hops = [], []
+    image_halves = []
     for half, (start_up, start_down) in enumerate(((far, far - 1), (far - 1, far))):
 
         def image_block(offset, half=half):
-            return image_part[
-                index_of[offset], half * image_rows : (half + 1) * image_rows
-            ]
-
-        hops = ring_sum(image_block, start_up, start_down)
-        image_hops += hops
+            index = index_of[offset]
+            rows = slice(half * image_rows, (half + 1) * image_rows)
+            return image_far[0, rows] if index == 0 else image_near[index - 1, rows]
+
+        def image_tie(left, value):
+            if left == far - 2:
+                return after(value, from_below[1], from_above[1], text_next, gate_next)
+            return value
+
+        hops = ring_sum(image_block, start_up, start_down, tie=image_tie)
         total = image_block(0).astype(F32) + hops[0][-1].astype(F32) + hops[1][-1].astype(F32)
         image_halves.append(total.astype(BF16))
     image_cols = jnp.concatenate(image_halves, axis=0)
-
-    for distance in range(2, far + 1):
-        text_round(distance, *([hops[-2] for hops in image_hops] if distance == 2 else []))
-    text_next = to_next(text_own)
-    gate_next = to_next(attn_gate)
 
     pieces = []
     moving = image_cols
@@ -400,7 +406,11 @@
                 [(s, (s + 2) % section_count) for s in range(section_count)],
             )
 
+    for distance in range(2, far):
+        text_round(*([image_cols] if distance == 2 else []))
     kv_part = key_values(meta, pieces, w_kv[0], mp_count, section_count, sharing)
+    if far > 2:
+        kv_part = after(kv_part, from_below[2], from_above[2])
 
     def kv_block(offset):
         return kv_part[index_of[offset]]
@@ -420,14 +430,17 @@
     near = []
     near_queries = []
     for distance in range(1, far):
-        chunks = from_below[distance] + from_above[distance]
+        chunks = [from_below[distance], from_above[distance]]
         near += [-distance, distance]
         if distance == 1:
-            chunks = chunks + halves
+            chunks.append(text_own)
             near.append(0)
         near_queries.append(query(chunks, weight_query))
     near_queries = jnp.concatenate(near_queries, axis=0)
-    far_queries = query(from_below[far] + from_above[far], weight_query)
+    far_chunks = [up(from_below[-1][:cut])]
+    if parts == 2:
+        far_chunks.append(down(from_above[-1][cut:]))
+    far_queries = query(far_chunks, weight_query)
     far_part = attend(
         meta, far_queries, kv_pieces, weight_out, [index_of[far]], text_rows, mp_count
     )
@@ -452,7 +465,10 @@
             first = near.index(offset) * text_rows + part * cut
             return near_part[first : first + cut]
 
-        hops = ring_sum(out_block, start_up, start_down, up_across, down_across)
+        def out_tie(left, value):
+            return after(value, own_next) if left == min(2, far - 1) else value
+
+        hops = ring_sum(out_block, start_up, start_down, up_across, down_across, out_tie)
         rows = slice(part * cut, (part + 1) * cut)
         branch = own_next[rows].astype(F32) + hops[0][-1].astype(F32) + hops[1][-1].astype(F32)
         results.append(

time: 293 us -> 273 us (0.932)
  starting transfers between devices: 64 us -> 47.2 us
  Pallas kernels: 58 us -> 44 us
  waiting for transfers between devices: 154 us -> 165 us
    ppermute x23 -> x20, starting transfers between devices: 42.2 us -> 26.3 us  [up(): return lax.ppermute(value, 'mp', up_pairs)]
    pallas_call x4, Pallas kernels: 27.7 us -> 11.9 us  [query(): pl.pallas_call(kernel, grid=(width // wide,), in_specs=[pl.BlockSpec(chun...]
    ppermute x22 -> x19, waiting for transfers between devices: 38 us -> 44.2 us  [down(): return lax.ppermute(value, 'mp', down_pairs)]
    ppermute x3, waiting for transfers between devices: 6.54 us -> 2.31 us  [to_next(): lax.ppermute(value, 'section', [(s, (s + 1) % section_count) for s in ran...]
    ppermute x23 -> x20, waiting for transfers between devices: 81.1 us -> 85.1 us  [up(): return lax.ppermute(value, 'mp', up_pairs)]
    unnamed x12 -> x22, local copies, waits for them, and re-layouts: 4.5 us -> 7.41 us
    ppermute x22 -> x19, starting transfers between devices: 13.1 us -> 15.5 us  [down(): return lax.ppermute(value, 'mp', down_pairs)]
    pallas_call x1 -> x2, Pallas kernels: 11.4 us -> 13.2 us  [project(): pl.pallas_call(kernel, grid_spec=pltpu.PrefetchScalarGridSpec(num_scalar_...]
  transfers between devices with their start and end apart: 56 -> 50, of which waited for: 32 -> 30; matrix products, arithmetic and copies ran while one was open for 1% -> 2% of each run, Pallas kernels for 15% -> 14%
where the time goes in v3:
time: 273 us; the launch traced here: 272 us
  waiting for transfers between devices  165 us (60%)
  starting transfers between devices  47.2 us (17%)
  Pallas kernels  44 us (16%)
  local copies, waits for them, and re-layouts  9.07 us (3%)
  other arithmetic  5.92 us (2%)
    ppermute x20, waiting for transfers between devices, up(): return lax.ppermute(value, 'mp', up_pairs)  85.1 us
    ppermute x19, waiting for transfers between devices, down(): return lax.ppermute(value, 'mp', down_pairs)  44.2 us
    ppermute x20, starting transfers between devices, up(): return lax.ppermute(value, 'mp', up_pairs)  26.3 us
    ppermute x2, waiting for transfers between devices, up_across(): return lax.ppermute(value, ('section', 'mp'), across(up_pairs))  21.2 us
    ppermute x19, starting transfers between devices, down(): return lax.ppermute(value, 'mp', down_pairs)  15.5 us
    pallas_call x2, Pallas kernels, attend(): pl.pallas_call(kernel, grid_spec=pltpu.PrefetchScalarGridSpec(num_scalar_...  14.5 us
    pallas_call x2, Pallas kernels, project(): pl.pallas_call(kernel, grid_spec=pltpu.PrefetchScalarGridSpec(num_scalar_...  13.2 us
    pallas_call x4, Pallas kernels, query(): pl.pallas_call(kernel, grid=(width // wide,), in_specs=[pl.BlockSpec(chun...  11.9 us
  transfers between devices with their start and end apart: 50, of which 30 were waited for; matrix products, arithmetic and copies ran while one was open for 2% of the time, Pallas kernels for 14%

profile of v3, /device:TPU:0, one launch (start us, length us, event | category | flops | bytes accessed | tf_op | source)
XLA Modules:
  0.0 272.2 jit_solution(14397559688298346888)
XLA Ops:
  0.0 3.0 %collective-permute-start.3 = (bf16[64,8192]{1,0:T(8,128)(2,1)}, bf16[64,8192]{1,0:T(8,128)(2,1)S(1)}, u32[]{:S(2)}, u32[]{:S(2)}) collective-permute-start(bf16[64,8192]{1,0:T(8,128)(2,1)} %bitcast.110), channel_id=1, source_target_pairs={{2,0},{4,2},{6,4},{7,6},{5,7},{3,5},{1,3},{0,1},{10,8},{12,10},{14... | collective-permute-start | bytes 3145736 | tf_op jit(solution)/shard_map/ppermute | solution.py:322
  9.9 10.3 %project.2 = bf16[7,320,1024]{2,1,0:T(8,128)(2,1)S(1)} custom-call(s32[10]{0:T(128)S(1)} %get-tuple-element.65.places_ref, bf16[320,960]{1,0:T(8,128)(2,1)S(1)} %copy-done.2, bf16[960,8192]{1,0:T(8,128)(2,1)} %weight_ref.3), custom_call_target="tpu_custom_call" | custom-call | flops 3774873600 | bytes 15728640 | tf_op jit(solution)/shard_map/project/pallas_call | solution.py:69
  20.2 14.6 %collective-permute-done.4 = bf16[160,1024]{1,0:T(8,128)(2,1)S(1)} collective-permute-done((bf16[160,1024]{1,0:T(8,128)(2,1)S(1)}, bf16[160,1024]{1,0:T(8,128)(2,1)S(1)}, u32[]{:S(2)}, u32[]{:S(2)}) %collective-permute-start.4) | collective-permute-done | bytes 327712 | tf_op jit(solution)/shard_map/ppermute | solution.py:319
  37.0 6.1 %collective-permute-done.8 = bf16[160,1024]{1,0:T(8,128)(2,1)S(1)} collective-permute-done((bf16[160,1024]{1,0:T(8,128)(2,1)S(1)}, bf16[160,1024]{1,0:T(8,128)(2,1)S(1)}, u32[]{:S(2)}, u32[]{:S(2)}) %collective-permute-start.8) | collective-permute-done | bytes 327712 | tf_op jit(solution)/shard_map/ppermute | solution.py:322
  49.8 5.3 %collective-permute-done.11 = bf16[160,1024]{1,0:T(8,128)(2,1)S(1)} collective-permute-done((bf16[160,1024]{1,0:T(8,128)(2,1)S(1)}, bf16[160,1024]{1,0:T(8,128)(2,1)S(1)}, u32[]{:S(2)}, u32[]{:S(2)}) %collective-permute-start.11) | collective-permute-done | bytes 327712 | tf_op jit(solution)/shard_map/ppermute | solution.py:319
  56.8 5.4 %collective-permute-done.9 = bf16[160,1024]{1,0:T(8,128)(2,1)S(1)} collective-permute-done((bf16[160,1024]{1,0:T(8,128)(2,1)S(1)}, bf16[160,1024]{1,0:T(8,128)(2,1)S(1)}, u32[]{:S(2)}, u32[]{:S(2)}) %collective-permute-start.9) | collective-permute-done | bytes 327712 | tf_op jit(solution)/shard_map/ppermute | solution.py:322
  66.8 6.6 %collective-permute-done.12 = bf16[160,1024]{1,0:T(8,128)(2,1)S(1)} collective-permute-done((bf16[160,1024]{1,0:T(8,128)(2,1)S(1)}, bf16[160,1024]{1,0:T(8,128)(2,1)S(1)}, u32[]{:S(2)}, u32[]{:S(2)}) %collective-permute-start.12) | collective-permute-done | bytes 327712 | tf_op jit(solution)/shard_map/ppermute | solution.py:319
  74.8 3.1 %collective-permute-done.7 = bf16[160,1024]{1,0:T(8,128)(2,1)S(1)} collective-permute-done((bf16[160,1024]{1,0:T(8,128)(2,1)S(1)}, bf16[160,1024]{1,0:T(8,128)(2,1)S(1)}, u32[]{:S(2)}, u32[]{:S(2)}) %collective-permute-start.7) | collective-permute-done | bytes 327712 | tf_op jit(solution)/shard_map/ppermute | solution.py:319
  82.3 5.9 %collective-permute-done.17 = bf16[160,1024]{1,0:T(8,128)(2,1)S(1)} collective-permute-done((bf16[160,1024]{1,0:T(8,128)(2,1)S(1)}, bf16[160,1024]{1,0:T(8,128)(2,1)S(1)}, u32[]{:S(2)}, u32[]{:S(2)}) %collective-permute-start.17) | collective-permute-done | bytes 327712 | tf_op jit(solution)/shard_map/ppermute | solution.py:322
  91.5 10.9 %collective-permute-done.23.refs_2_ = bf16[320,1024]{1,0:T(8,128)(2,1)S(1)} collective-permute-done((bf16[320,1024]{1,0:T(8,128)(2,1)S(1)}, bf16[320,1024]{1,0:T(8,128)(2,1)S(1)}, u32[]{:S(2)}, u32[]{:S(2)}) %collective-permute-start.23) | collective-permute-done | bytes 655392 | tf_op jit(solution)/shard_map/ppermute | solution.py:403
  104.5 4.4 %key_values.1 = bf16[8,256,256]{2,1,0:T(8,128)(2,1)S(1)} custom-call(s32[18]{0:T(128)S(1)} %pad_add_fusion.meta_ref, bf16[320,1024]{1,0:T(8,128)(2,1)S(1)} %pad_maximum_fusion.refs_0_, bf16[320,1024]{1,0:T(8,128)(2,1)S(1)} %collective-permute-done.22.refs_1_, bf16[320,1024]{1,0:T(8,128)(2,1)S(1)} %collective-permute-done.23.refs_2_, ...), custom_call_target="tpu_custom_call" | custom-call | flops 2415919104 | bytes 4718592 | tf_op jit(solution)/shard_map/key_values/pallas_call | solution.py:131
  114.5 4.3 %collective-permute-done.25 = bf16[256,256]{1,0:T(8,128)(2,1)S(1)} collective-permute-done((bf16[256,256]{1,0:T(8,128)(2,1)S(1)}, bf16[256,256]{1,0:T(8,128)(2,1)S(1)}, u32[]{:S(2)}, u32[]{:S(2)}) %collective-permute-start.25) | collective-permute-done | bytes 131104 | tf_op jit(solution)/shard_map/ppermute | solution.py:319
  127.5 19.1 %collective-permute-done.27 = bf16[256,256]{1,0:T(8,128)(2,1)S(1)} collective-permute-done((bf16[256,256]{1,0:T(8,128)(2,1)S(1)}, bf16[256,256]{1,0:T(8,128)(2,1)S(1)}, u32[]{:S(2)}, u32[]{:S(2)}) %collective-permute-start.27) | collective-permute-done | bytes 131104 | tf_op jit(solution)/shard_map/ppermute | solution.py:319
  148.7 3.5 %query.4 = bf16[192,512]{1,0:T(8,128)(2,1)S(1)} custom-call(bf16[64,8192]{1,0:T(8,128)(2,1)S(1)} %collective-permute-done.2.refs_0_, bf16[64,8192]{1,0:T(8,128)(2,1)S(1)} %collective-permute-done.3.refs_1_, bf16[64,8192]{1,0:T(8,128)(2,1)S(1)} %bitcast.113, bf16[8192,512]{1,0:T(8,128)(2,1)S(1)} %bitcast.102), custom_call_target="tpu_custom_call" | custom-call | flops 1610612736 | bytes 11534336 | tf_op jit(solution)/shard_map/query/pallas_call | solution.py:177
  160.9 10.3 %attend.2 = bf16[448,8192]{1,0:T(8,128)(2,1)S(1)} custom-call(s32[18]{0:T(128)S(1)} %pad_add_fusion.meta_ref, bf16[448,512]{1,0:T(8,128)(2,1)S(1)} %pad_maximum_fusion.1.query_ref, bf16[256,256]{1,0:T(8,128)(2,1)S(1)} %fusion.20.refs_0_, bf16[256,256]{1,0:T(8,128)(2,1)S(1)} %collective-permute-done.32.refs_1_, bf16[512,8192]{1,0:T(8,128)(2,1)} %bitcast.106), custom_call_target="tpu_custom_call" | custom-call | flops 3875536896 | bytes 15728640 | tf_op jit(solution)/shard_map/attend/pallas_call | solution.py:248
  177.0 3.4 %copy-done = bf16[1,512,8192]{2,1,0:T(8,128)(2,1)S(1)} copy-done((bf16[1,512,8192]{2,1,0:T(8,128)(2,1)S(1)}, bf16[1,512,8192]{2,1,0:T(8,128)(2,1)}, u32[]{:S(2)}) %copy-start) | copy-done | bytes 8388632
  180.3 4.2 %attend.3 = bf16[64,8192]{1,0:T(8,128)(2,1)S(1)} custom-call(s32[18]{0:T(128)S(1)} %pad_add_fusion.meta_ref, bf16[64,512]{1,0:T(8,128)(2,1)S(1)} %query.7.query_ref, bf16[256,256]{1,0:T(8,128)(2,1)S(1)} %fusion.20.refs_0_, bf16[256,256]{1,0:T(8,128)(2,1)S(1)} %collective-permute-done.32.refs_1_, bf16[512,8192]{1,0:T(8,128)(2,1)S(1)} %bitcast.107), custom_call_target="tpu_custom_call" | custom-call | flops 553648128 | bytes 9437184 | tf_op jit(solution)/shard_map/attend/pallas_call | solution.py:248
  188.9 10.7 %collective-permute-done.36 = bf16[32,8192]{1,0:T(8,128)(2,1)S(1)} collective-permute-done((bf16[32,8192]{1,0:T(8,128)(2,1)S(1)}, bf16[32,8192]{1,0:T(8,128)(2,1)S(1)}, u32[]{:S(2)}, u32[]{:S(2)}) %collective-permute-start.36) | collective-permute-done | bytes 524320 | tf_op jit(solution)/shard_map/ppermute | solution.py:319
  203.4 6.5 %collective-permute-done.40 = bf16[32,8192]{1,0:T(8,128)(2,1)S(1)} collective-permute-done((bf16[32,8192]{1,0:T(8,128)(2,1)S(1)}, bf16[32,8192]{1,0:T(8,128)(2,1)S(1)}, u32[]{:S(2)}, u32[]{:S(2)}) %collective-permute-start.40) | collective-permute-done | bytes 524320 | tf_op jit(solution)/shard_map/ppermute | solution.py:322
  209.9 4.3 %collective-permute-done.37 = bf16[32,8192]{1,0:T(8,128)(2,1)S(1)} collective-permute-done((bf16[32,8192]{1,0:T(8,128)(2,1)S(1)}, bf16[32,8192]{1,0:T(8,128)(2,1)S(1)}, u32[]{:S(2)}, u32[]{:S(2)}) %collective-permute-start.37) | collective-permute-done | bytes 524320 | tf_op jit(solution)/shard_map/ppermute | solution.py:319
  221.6 10.8 %collective-permute-done.38 = bf16[32,8192]{1,0:T(8,128)(2,1)S(1)} collective-permute-done((bf16[32,8192]{1,0:T(8,128)(2,1)S(1)}, bf16[32,8192]{1,0:T(8,128)(2,1)S(1)}, u32[]{:S(2)}, u32[]{:S(2)}) %collective-permute-start.38) | collective-permute-done | bytes 524320 | tf_op jit(solution)/shard_map/ppermute | solution.py:319
  234.2 9.5 %collective-permute-done.48 = bf16[32,8192]{1,0:T(8,128)(2,1)S(1)} collective-permute-done((bf16[32,8192]{1,0:T(8,128)(2,1)S(1)}, bf16[32,8192]{1,0:T(8,128)(2,1)S(1)}, u32[]{:S(2)}, u32[]{:S(2)}) %collective-permute-start.48) | collective-permute-done | bytes 524320 | tf_op jit(solution)/shard_map/ppermute | solution.py:322
  249.4 10.1 %collective-permute-done.39 = bf16[32,8192]{1,0:T(8,128)(2,1)S(1)} collective-permute-done((bf16[32,8192]{1,0:T(8,128)(2,1)S(1)}, bf16[32,8192]{1,0:T(8,128)(2,1)S(1)}, u32[]{:S(2)}, u32[]{:S(2)}) %collective-permute-start.39) | collective-permute-done | bytes 524320 | tf_op jit(solution)/shard_map/ppermute | solution.py:332
  259.4 11.1 %collective-permute-done.45 = bf16[32,8192]{1,0:T(8,128)(2,1)S(1)} collective-permute-done((bf16[32,8192]{1,0:T(8,128)(2,1)S(1)}, bf16[32,8192]{1,0:T(8,128)(2,1)S(1)}, u32[]{:S(2)}, u32[]{:S(2)}) %collective-permute-start.45) | collective-permute-done | bytes 524320 | tf_op jit(solution)/shard_map/ppermute | solution.py:332
  (141 shorter events, 87.8 us)
Async XLA Ops:
  0.0 47.7 %collective-permute-start.3 = (bf16[64,8192]{1,0:T(8,128)(2,1)}, bf16[64,8192]{1,0:T(8,128)(2,1)S(1)}, u32[]{:S(2)}, u32[]{:S(2)}) collective-permute-start(bf16[64,8192]{1,0:T(8,128)(2,1)} %bitcast.110), channel_id=1, source_target_pairs={{2,0},{4,2},{6,4},{7,6},{5,7},{3,5},{1,3},{0,1},{10,8},{12,10},{14... | collective-permute-start | bytes 3145736 | tf_op jit(solution)/shard_map/ppermute | solution.py:322
  3.0 44.7 %collective-permute-start.2 = (bf16[64,8192]{1,0:T(8,128)(2,1)}, bf16[64,8192]{1,0:T(8,128)(2,1)S(1)}, u32[]{:S(2)}, u32[]{:S(2)}) collective-permute-start(bf16[64,8192]{1,0:T(8,128)(2,1)} %bitcast.111), channel_id=1, source_target_pairs={{0,2},{2,4},{4,6},{6,7},{7,5},{5,3},{3,1},{1,0},{8,10},{10,12},{12... | collective-permute-start | bytes 3145736 | tf_op jit(solution)/shard_map/ppermute | solution.py:319
  3.0 44.7 %collective-permute-start = (bf16[64,8192]{1,0:T(8,128)(2,1)}, bf16[64,8192]{1,0:T(8,128)(2,1)S(1)}, u32[]{:S(2)}, u32[]{:S(2)}) collective-permute-start(bf16[64,8192]{1,0:T(8,128)(2,1)} %bitcast.112), channel_id=1, source_target_pairs={{0,8},{8,16},{16,24},{24,0},{1,9},{9,17},{17,25},{25,1},{2,10},{10... | collective-permute-start | bytes 3145736 | tf_op jit(solution)/shard_map/ppermute | solution.py:338
  7.8 27.0 %collective-permute-start.4 = (bf16[160,1024]{1,0:T(8,128)(2,1)S(1)}, bf16[160,1024]{1,0:T(8,128)(2,1)S(1)}, u32[]{:S(2)}, u32[]{:S(2)}) collective-permute-start(bf16[160,1024]{1,0:T(8,128)(2,1)S(1)} %get-tuple-element.63), channel_id=1, source_target_pairs={{0,2},{2,4},{4,6},{6,7},{7,5},{5,3},{3,1},{1,0},{8,10},{10,12},{12... | collective-permute-start | bytes 983048 | tf_op jit(solution)/shard_map/ppermute | solution.py:319
  9.9 26.6 %collective-permute-start.14 = (bf16[160,1024]{1,0:T(8,128)(2,1)S(1)}, bf16[160,1024]{1,0:T(8,128)(2,1)S(1)}, u32[]{:S(2)}, u32[]{:S(2)}) collective-permute-start(bf16[160,1024]{1,0:T(8,128)(2,1)S(1)} %get-tuple-element.64), channel_id=1, source_target_pairs={{2,0},{4,2},{6,4},{7,6},{5,7},{3,5},{1,3},{0,1},{10,8},{12,10},{14... | collective-permute-start | bytes 983048 | tf_op jit(solution)/shard_map/ppermute | solution.py:322
  88.5 22.5 %collective-permute-start.18 = (bf16[64,8192]{1,0:T(8,128)(2,1)S(1)}, bf16[64,8192]{1,0:T(8,128)(2,1)S(1)}, u32[]{:S(2)}, u32[]{:S(2)}) collective-permute-start(bf16[64,8192]{1,0:T(8,128)(2,1)S(1)} %collective-permute-done.2.refs_0_), channel_id=1, source_target_pairs={{0,2},{2,4},{4,6},{6,7},{7,5},{5,3},{3,1},{1,0},{8,10},{10,12},{12... | collective-permute-start | bytes 3145736 | tf_op jit(solution)/shard_map/ppermute | solution.py:319
  90.3 22.1 %collective-permute-start.19 = (bf16[64,8192]{1,0:T(8,128)(2,1)S(1)}, bf16[64,8192]{1,0:T(8,128)(2,1)S(1)}, u32[]{:S(2)}, u32[]{:S(2)}) collective-permute-start(bf16[64,8192]{1,0:T(8,128)(2,1)S(1)} %collective-permute-done.3.refs_1_), channel_id=1, source_target_pairs={{2,0},{4,2},{6,4},{7,6},{5,7},{3,5},{1,3},{0,1},{10,8},{12,10},{14... | collective-permute-start | bytes 3145736 | tf_op jit(solution)/shard_map/ppermute | solution.py:322
  120.5 35.4 %collective-permute-start.20 = (bf16[64,8192]{1,0:T(8,128)(2,1)S(1)}, bf16[64,8192]{1,0:T(8,128)(2,1)S(1)}, u32[]{:S(2)}, u32[]{:S(2)}) collective-permute-start(bf16[64,8192]{1,0:T(8,128)(2,1)S(1)} %collective-permute-done.18.refs_0_), channel_id=1, source_target_pairs={{0,2},{2,4},{4,6},{6,7},{7,5},{5,3},{3,1},{1,0},{8,10},{10,12},{12... | collective-permute-start | bytes 3145736 | tf_op jit(solution)/shard_map/ppermute | solution.py:319
  122.0 35.3 %collective-permute-start.21 = (bf16[64,8192]{1,0:T(8,128)(2,1)S(1)}, bf16[64,8192]{1,0:T(8,128)(2,1)S(1)}, u32[]{:S(2)}, u32[]{:S(2)}) collective-permute-start(bf16[64,8192]{1,0:T(8,128)(2,1)S(1)} %collective-permute-done.19.refs_1_), channel_id=1, source_target_pairs={{2,0},{4,2},{6,4},{7,6},{5,7},{3,5},{1,3},{0,1},{10,8},{12,10},{14... | collective-permute-start | bytes 3145736 | tf_op jit(solution)/shard_map/ppermute | solution.py:322
  125.4 21.2 %collective-permute-start.27 = (bf16[256,256]{1,0:T(8,128)(2,1)S(1)}, bf16[256,256]{1,0:T(8,128)(2,1)S(1)}, u32[]{:S(2)}, u32[]{:S(2)}) collective-permute-start(bf16[256,256]{1,0:T(8,128)(2,1)S(1)} %get-tuple-element.59), channel_id=1, source_target_pairs={{0,2},{2,4},{4,6},{6,7},{7,5},{5,3},{3,1},{1,0},{8,10},{10,12},{12... | collective-permute-start | bytes 393224 | tf_op jit(solution)/shard_map/ppermute | solution.py:319
  127.0 19.5 %collective-permute-start.30 = (bf16[256,256]{1,0:T(8,128)(2,1)S(1)}, bf16[256,256]{1,0:T(8,128)(2,1)S(1)}, u32[]{:S(2)}, u32[]{:S(2)}) collective-permute-start(bf16[256,256]{1,0:T(8,128)(2,1)S(1)} %get-tuple-element.60), channel_id=1, source_target_pairs={{2,0},{4,2},{6,4},{7,6},{5,7},{3,5},{1,3},{0,1},{10,8},{12,10},{14... | collective-permute-start | bytes 393224 | tf_op jit(solution)/shard_map/ppermute | solution.py:322
  155.9 18.2 %collective-permute-start.34 = (bf16[32,8192]{1,0:T(8,128)(2,1)S(1)}, bf16[32,8192]{1,0:T(8,128)(2,1)S(1)}, u32[]{:S(2)}, u32[]{:S(2)}) collective-permute-start(bf16[32,8192]{1,0:T(8,128)(2,1)S(1)} %slice.204), channel_id=1, source_target_pairs={{0,2},{2,4},{4,6},{6,7},{7,5},{5,3},{3,1},{1,0},{8,10},{10,12},{12... | collective-permute-start | bytes 1572872 | tf_op jit(solution)/shard_map/ppermute | solution.py:319
  157.3 16.8 %collective-permute-start.35 = (bf16[32,8192]{1,0:T(8,128)(2,1)S(1)}, bf16[32,8192]{1,0:T(8,128)(2,1)S(1)}, u32[]{:S(2)}, u32[]{:S(2)}) collective-permute-start(bf16[32,8192]{1,0:T(8,128)(2,1)S(1)} %slice.205), channel_id=1, source_target_pairs={{2,0},{4,2},{6,4},{7,6},{5,7},{3,5},{1,3},{0,1},{10,8},{12,10},{14... | collective-permute-start | bytes 1572872 | tf_op jit(solution)/shard_map/ppermute | solution.py:322
  184.7 14.9 %collective-permute-start.36 = (bf16[32,8192]{1,0:T(8,128)(2,1)S(1)}, bf16[32,8192]{1,0:T(8,128)(2,1)S(1)}, u32[]{:S(2)}, u32[]{:S(2)}) collective-permute-start(bf16[32,8192]{1,0:T(8,128)(2,1)S(1)} %get-tuple-element.55), channel_id=1, source_target_pairs={{0,2},{2,4},{4,6},{6,7},{7,5},{5,3},{3,1},{1,0},{8,10},{10,12},{12... | collective-permute-start | bytes 1572872 | tf_op jit(solution)/shard_map/ppermute | solution.py:319
  186.0 14.9 %collective-permute-start.46 = (bf16[32,8192]{1,0:T(8,128)(2,1)S(1)}, bf16[32,8192]{1,0:T(8,128)(2,1)S(1)}, u32[]{:S(2)}, u32[]{:S(2)}) collective-permute-start(bf16[32,8192]{1,0:T(8,128)(2,1)S(1)} %get-tuple-element.56), channel_id=1, source_target_pairs={{2,0},{4,2},{6,4},{7,6},{5,7},{3,5},{1,3},{0,1},{10,8},{12,10},{14... | collective-permute-start | bytes 1572872 | tf_op jit(solution)/shard_map/ppermute | solution.py:322
  186.8 23.1 %collective-permute-start.40 = (bf16[32,8192]{1,0:T(8,128)(2,1)S(1)}, bf16[32,8192]{1,0:T(8,128)(2,1)S(1)}, u32[]{:S(2)}, u32[]{:S(2)}) collective-permute-start(bf16[32,8192]{1,0:T(8,128)(2,1)S(1)} %get-tuple-element.39), channel_id=1, source_target_pairs={{2,0},{4,2},{6,4},{7,6},{5,7},{3,5},{1,3},{0,1},{10,8},{12,10},{14... | collective-permute-start | bytes 1572872 | tf_op jit(solution)/shard_map/ppermute | solution.py:322
  188.3 21.6 %collective-permute-start.43 = (bf16[32,8192]{1,0:T(8,128)(2,1)S(1)}, bf16[32,8192]{1,0:T(8,128)(2,1)S(1)}, u32[]{:S(2)}, u32[]{:S(2)}) collective-permute-start(bf16[32,8192]{1,0:T(8,128)(2,1)S(1)} %get-tuple-element.40), channel_id=1, source_target_pairs={{0,2},{2,4},{4,6},{6,7},{7,5},{5,3},{3,1},{1,0},{8,10},{10,12},{12... | collective-permute-start | bytes 1572872 | tf_op jit(solution)/shard_map/ppermute | solution.py:319
  219.3 14.9 %collective-permute-start.41 = (bf16[32,8192]{1,0:T(8,128)(2,1)S(1)}, bf16[32,8192]{1,0:T(8,128)(2,1)S(1)}, u32[]{:S(2)}, u32[]{:S(2)}) collective-permute-start(bf16[32,8192]{1,0:T(8,128)(2,1)S(1)} %get-tuple-element.24), channel_id=1, source_target_pairs={{2,0},{4,2},{6,4},{7,6},{5,7},{3,5},{1,3},{0,1},{10,8},{12,10},{14... | collective-permute-start | bytes 1572872 | tf_op jit(solution)/shard_map/ppermute | solution.py:322
  219.6 24.1 %collective-permute-start.48 = (bf16[32,8192]{1,0:T(8,128)(2,1)S(1)}, bf16[32,8192]{1,0:T(8,128)(2,1)S(1)}, u32[]{:S(2)}, u32[]{:S(2)}) collective-permute-start(bf16[32,8192]{1,0:T(8,128)(2,1)S(1)} %get-tuple-element.26), channel_id=1, source_target_pairs={{2,0},{4,2},{6,4},{7,6},{5,7},{3,5},{1,3},{0,1},{10,8},{12,10},{14... | collective-permute-start | bytes 1572872 | tf_op jit(solution)/shard_map/ppermute | solution.py:322
  220.3 23.4 %collective-permute-start.44 = (bf16[32,8192]{1,0:T(8,128)(2,1)S(1)}, bf16[32,8192]{1,0:T(8,128)(2,1)S(1)}, u32[]{:S(2)}, u32[]{:S(2)}) collective-permute-start(bf16[32,8192]{1,0:T(8,128)(2,1)S(1)} %get-tuple-element.25), channel_id=1, source_target_pairs={{0,2},{2,4},{4,6},{6,7},{7,5},{5,3},{3,1},{1,0},{8,10},{10,12},{12... | collective-permute-start | bytes 1572872 | tf_op jit(solution)/shard_map/ppermute | solution.py:319
  244.3 15.2 %collective-permute-start.39 = (bf16[32,8192]{1,0:T(8,128)(2,1)S(1)}, bf16[32,8192]{1,0:T(8,128)(2,1)S(1)}, u32[]{:S(2)}, u32[]{:S(2)}) collective-permute-start(bf16[32,8192]{1,0:T(8,128)(2,1)S(1)} %get-tuple-element.29), channel_id=1, source_target_pairs={{0,10},{2,12},{4,14},{6,15},{7,13},{5,11},{3,9},{1,8},{8,18},{10,2... | collective-permute-start | bytes 1572872 | tf_op jit(solution)/shard_map/ppermute | solution.py:332
  244.3 15.1 %collective-permute-start.49 = (bf16[32,8192]{1,0:T(8,128)(2,1)S(1)}, bf16[32,8192]{1,0:T(8,128)(2,1)S(1)}, u32[]{:S(2)}, u32[]{:S(2)}) collective-permute-start(bf16[32,8192]{1,0:T(8,128)(2,1)S(1)} %get-tuple-element.30), channel_id=1, source_target_pairs={{2,8},{4,10},{6,12},{7,14},{5,15},{3,13},{1,11},{0,9},{10,16},{12,... | collective-permute-start | bytes 1572872 | tf_op jit(solution)/shard_map/ppermute | solution.py:335
  245.6 25.0 %collective-permute-start.45 = (bf16[32,8192]{1,0:T(8,128)(2,1)S(1)}, bf16[32,8192]{1,0:T(8,128)(2,1)S(1)}, u32[]{:S(2)}, u32[]{:S(2)}) collective-permute-start(bf16[32,8192]{1,0:T(8,128)(2,1)S(1)} %get-tuple-element.31), channel_id=1, source_target_pairs={{0,10},{2,12},{4,14},{6,15},{7,13},{5,11},{3,9},{1,8},{8,18},{10,2... | collective-permute-start | bytes 1572872 | tf_op jit(solution)/shard_map/ppermute | solution.py:332
  246.6 24.0 %collective-permute-start.42 = (bf16[32,8192]{1,0:T(8,128)(2,1)S(1)}, bf16[32,8192]{1,0:T(8,128)(2,1)S(1)}, u32[]{:S(2)}, u32[]{:S(2)}) collective-permute-start(bf16[32,8192]{1,0:T(8,128)(2,1)S(1)} %get-tuple-element.32), channel_id=1, source_target_pairs={{2,8},{4,10},{6,12},{7,14},{5,15},{3,13},{1,11},{0,9},{10,16},{12,... | collective-permute-start | bytes 1572872 | tf_op jit(solution)/shard_map/ppermute | solution.py:335
  (37 other events, 583.3 us)

commit v4 on v3

--- a/solution.py
+++ b/solution.py
@@ -20,6 +20,8 @@
 F32 = jnp.float32
 BF16 = jnp.bfloat16
 VMEM_LIMIT = 40 * 1024 * 1024
+VMEM_MOST = 56 * 1024 * 1024
+VMEM_SMALL = 16 * 1024 * 1024
 
 
 def ring_order(count):
@@ -53,20 +55,83 @@
     return (one.astype(F32) + other.astype(F32)).astype(BF16)
 
 
-def params():
-    return pltpu.CompilerParams(vmem_limit_bytes=VMEM_LIMIT)
+def params(limit=VMEM_LIMIT):
+    return pltpu.CompilerParams(vmem_limit_bytes=limit)
+
+
+def total_of(groups):
+    parts, count = len(groups), len(groups[0])
+    part_rows, columns = groups[0][0].shape
+    rows = parts * part_rows
+    wide = columns // 4 if columns % 512 == 0 else columns
+
+    def kernel(*refs):
+        for part in range(parts):
+            total = refs[part * count][...].astype(F32)
+            for ref in refs[part * count + 1 : (part + 1) * count]:
+                total += ref[...].astype(F32)
+            refs[-1][part * part_rows : (part + 1) * part_rows, :] = total.astype(BF16)
+
+    return pl.pallas_call(
+        kernel,
+        grid=(columns // wide,),
+        in_specs=[pl.BlockSpec((part_rows, wide), lambda i: (0, i))] * (parts * count),
+        out_specs=pl.BlockSpec((rows, wide), lambda i: (0, i)),
+        out_shape=jax.ShapeDtypeStruct((rows, columns), BF16),
+        compiler_params=params(VMEM_SMALL),
+        name="total_of",
+    )(*[value for group in groups for value in group])
+
+
+def finish(gate, text, own, arrivals):
+    rows, columns = text.shape
+    parts = len(arrivals)
+    part_rows = rows // parts
+    wide = columns // 4
+    flat = [value for came in arrivals for value in came]
+    count = len(flat) // parts
+
+    def kernel(gate_ref, text_ref, own_ref, *refs):
+        factor = jnp.tanh(gate_ref[...])
+        for part in range(parts):
+            place = slice(part * part_rows, (part + 1) * part_rows)
+            branch = own_ref[place, :].astype(F32)
+            for ref in refs[part * count : (part + 1) * count]:
+                branch += ref[...].astype(F32)
+            refs[-1][0, place, :] = (text_ref[place, :].astype(F32) + factor * branch).astype(
+                BF16
+            )
+
+    return pl.pallas_call(
+        kernel,
+        grid=(columns // wide,),
+        in_specs=[pl.BlockSpec((1, 1), lambda i: (0, 0))]
+        + [pl.BlockSpec((rows, wide), lambda i: (0, i))] * 2
+        + [pl.BlockSpec((part_rows, wide), lambda i: (0, i))] * len(flat),
+        out_specs=pl.BlockSpec((1, rows, wide), lambda i: (0, 0, i)),
+        out_shape=jax.ShapeDtypeStruct((1, rows, columns), BF16),
+        compiler_params=params(VMEM_SMALL),
+        name="finish",
+    )(gate.reshape(1, 1), text, own, *flat)
 
 
 def project(places, feats, weight, order_len, first, blocks):
     rows, depth = feats.shape
+    half = rows // 2
     wide = weight.shape[1] // order_len
 
-    def kernel(places_ref, feats_ref, weight_ref, out_ref):
-        out_ref[0] = jnp.dot(
+    def kernel(places_ref, feats_ref, weight_ref, *out_refs):
+        product = jnp.dot(
             feats_ref[...], weight_ref[...], preferred_element_type=F32
         ).astype(BF16)
-
-    return pl.pallas_call(
+        for block in range(blocks):
+
+            @pl.when(pl.program_id(0) == block)
+            def _():
+                out_refs[2 * block][...] = product[:half]
+                out_refs[2 * block + 1][...] = product[half:]
+
+    halves = pl.pallas_call(
         kernel,
         grid_spec=pltpu.PrefetchScalarGridSpec(
             num_scalar_prefetch=1,
@@ -75,9 +140,9 @@
                 pl.BlockSpec((rows, depth), lambda i, places: (0, 0)),
                 pl.BlockSpec((depth, wide), lambda i, places: (0, places[first + i])),
             ],
-            out_specs=pl.BlockSpec((1, rows, wide), lambda i, places: (i, 0, 0)),
-        ),
-        out_shape=jax.ShapeDtypeStruct((blocks, rows, wide), BF16),
+            out_specs=[pl.BlockSpec((half, wide), lambda i, places: (0, 0))] * (2 * blocks),
+        ),
+        out_shape=[jax.ShapeDtypeStruct((half, wide), BF16)] * (2 * blocks),
         compiler_params=params(),
         cost_estimate=pl.CostEstimate(
             flops=2 * rows * depth * wide * (blocks - 1),
@@ -86,6 +151,7 @@
         ),
         name="project",
     )(places, feats, weight)
+    return [halves[2 * block : 2 * block + 2] for block in range(blocks)]
 
 
 def key_values(meta, pieces, weight, order_len, section_count, sharing):
@@ -96,7 +162,8 @@
     count = len(pieces)
 
     def kernel(meta_ref, *refs):
-        piece_refs, weight_ref, out_ref, kv_ref = refs[:count], refs[count], refs[-2], refs[-1]
+        piece_refs, weight_ref = refs[:count], refs[count]
+        out_refs, kv_ref = refs[count + 1 : -1], refs[-1]
         section = meta_ref[order_len + 1]
         slot = lax.broadcasted_iota(jnp.int32, (BLOCK, feat_rows), 0)
         packed = lax.broadcasted_iota(jnp.int32, (BLOCK, feat_rows), 1)
@@ -122,8 +189,8 @@
             target = meta_ref[index]
             row = pl.multiple_of(lax.rem(target, sharing) * kv_rows, kv_rows)
             column = pl.multiple_of(target // sharing * HD, HD)
-            out_ref[index, :, :HD] = kv_ref[pl.ds(row, kv_rows), pl.ds(column, HD)]
-            out_ref[index, :, HD:] = kv_ref[
+            out_refs[index][:, :HD] = kv_ref[pl.ds(row, kv_rows), pl.ds(column, HD)]
+            out_refs[index][:, HD:] = kv_ref[
                 pl.ds(row, kv_rows), pl.ds(pl.multiple_of(column + half_width, HD), HD)
             ]
 
@@ -131,8 +198,8 @@
     return pl.pallas_call(
         kernel,
         in_specs=[pl.BlockSpec(memory_space=pltpu.SMEM)] + [whole] * (count + 1),
-        out_specs=whole,
-        out_shape=jax.ShapeDtypeStruct((order_len, kv_rows, 2 * HD), BF16),
+        out_specs=[whole] * order_len,
+        out_shape=[jax.ShapeDtypeStruct((kv_rows, 2 * HD), BF16)] * order_len,
         scratch_shapes=[pltpu.VMEM((SLOTS, width), BF16)],
         compiler_params=params(),
         cost_estimate=pl.CostEstimate(
@@ -192,7 +259,8 @@
     )(*chunks, weight)
 
 
-def attend(meta, queries, kv_pieces, weight, indices, text_rows, order_len):
+def attend(meta, queries, kv_pieces, weight, indices, sizes, order_len):
+    text_rows = queries.shape[0] // len(indices)
     rows, width = queries.shape
     heads = width // HD
     sharing = len(kv_pieces)
@@ -201,8 +269,9 @@
     wide = min(1024, columns)
 
     def kernel(meta_ref, query_ref, *refs):
-        kv_refs, weight_ref, out_ref = refs[:sharing], refs[sharing], refs[sharing + 1]
-        key_ref, value_ref, attended_ref = refs[sharing + 2 :]
+        kv_refs, weight_ref = refs[:sharing], refs[sharing]
+        out_refs = refs[sharing + 1 : -3]
+        key_ref, value_ref, attended_ref = refs[-3:]
 
         @pl.when(pl.program_id(0) == 0)
         def _():
@@ -241,9 +310,13 @@
                         h * text_rows : (h + 1) * text_rows
                     ]
 
-        out_ref[...] = jnp.dot(
+        product = jnp.dot(
             attended_ref[...], weight_ref[...], preferred_element_type=F32
         ).astype(BF16)
+        first = 0
+        for out_ref, size in zip(out_refs, sizes):
+            out_ref[...] = product[first : first + size]
+            first += size
 
     return pl.pallas_call(
         kernel,
@@ -253,15 +326,15 @@
             in_specs=[pl.BlockSpec((rows, width), lambda i, meta: (0, 0))]
             + [pl.BlockSpec(piece.shape, lambda i, meta: (0, 0)) for piece in kv_pieces]
             + [pl.BlockSpec((width, wide), lambda i, meta: (0, i))],
-            out_specs=pl.BlockSpec((rows, wide), lambda i, meta: (0, i)),
+            out_specs=[pl.BlockSpec((size, wide), lambda i, meta: (0, i)) for size in sizes],
             scratch_shapes=[
                 pltpu.VMEM((SLOTS, HD), BF16),
                 pltpu.VMEM((SLOTS, HD), BF16),
                 pltpu.VMEM((rows, width), BF16),
             ],
         ),
-        out_shape=jax.ShapeDtypeStruct((rows, columns), BF16),
-        compiler_params=params(),
+        out_shape=[jax.ShapeDtypeStruct((size, columns), BF16) for size in sizes],
+        compiler_params=params(VMEM_MOST),
         cost_estimate=pl.CostEstimate(
             flops=2 * rows * width * (columns + 2 * BLOCK),
             bytes_accessed=2 * columns * (width + rows),
@@ -341,19 +414,16 @@
 
     def ring_sum(part, start_up, start_down, last_up=up, last_down=down, tie=None):
         tie = tie or (lambda left, value: value)
-        hops = []
+        arrived = []
         for start, sign, move, last in (
             (start_up, 1, up, last_up),
             (start_down, -1, down, last_down),
         ):
             running = part(sign * start)
-            came = []
             for distance in range(start, 1, -1):
-                came.append(move(tie(distance, running)))
-                running = add(came[-1], part(sign * (distance - 1)))
-            came.append(last(tie(1, running)))
-            hops.append(came)
-        return hops
+                running = add(move(tie(distance, running)), part(sign * (distance - 1)))
+            arrived.append(last(tie(1, running)))
+        return arrived
 
     text_own = text_state[0]
     text_rows = text_own.shape[0]
@@ -370,27 +440,25 @@
 
     text_round()
 
-    image_far = project(places, tile_feats, w_proj, mp_count, 0, 1)
-    image_near = project(places, tile_feats, w_proj, mp_count, 1, mp_count - 1)
-    feat_rows = tile_feats.shape[0]
-    image_rows = feat_rows // 2
-    image_halves = []
+    image_parts = project(places, tile_feats, w_proj, mp_count, 0, 1)
+    image_parts += project(places, tile_feats, w_proj, mp_count, 1, mp_count - 1)
+    image_arrivals = []
     for half, (start_up, start_down) in enumerate(((far, far - 1), (far - 1, far))):
 
         def image_block(offset, half=half):
-            index = index_of[offset]
-            rows = slice(half * image_rows, (half + 1) * image_rows)
-            return image_far[0, rows] if index == 0 else image_near[index - 1, rows]
+            return image_parts[index_of[offset]][half]
 
         def image_tie(left, value):
-            if left == far - 2:
-                return after(value, from_below[1], from_above[1], text_next, gate_next)
+            if left == min(2, far - 1):
+                return after(value, from_below[1], from_above[1])
+            if left == 1:
+                return after(value, text_next, gate_next)
             return value
 
-        hops = ring_sum(image_block, start_up, start_down, tie=image_tie)
-        total = image_block(0).astype(F32) + hops[0][-1].astype(F32) + hops[1][-1].astype(F32)
-        image_halves.append(total.astype(BF16))
-    image_cols = jnp.concatenate(image_halves, axis=0)
+        image_arrivals.append(
+            [image_block(0)] + ring_sum(image_block, start_up, start_down, tie=image_tie)
+        )
+    image_cols = total_of(image_arrivals)
 
     pieces = []
     moving = image_cols
@@ -408,17 +476,37 @@
 
     for distance in range(2, far):
         text_round(*([image_cols] if distance == 2 else []))
-    kv_part = key_values(meta, pieces, w_kv[0], mp_count, section_count, sharing)
+    far_chunks = [up(from_below[-1][:cut])]
+    if parts == 2:
+        far_chunks.append(down(from_above[-1][cut:]))
+
+    weight_query, weight_out = w_query[0], w_out[0]
+    near = [-1, 1, 0]
+    near_queries = [query([from_below[1], from_above[1], text_own], weight_query)]
+    kv_part = list(
+        key_values(
+            after(meta, near_queries[0]), pieces, w_kv[0], mp_count, section_count, sharing
+        )
+    )
     if far > 2:
-        kv_part = after(kv_part, from_below[2], from_above[2])
+        kv_part[0] = after(kv_part[0], from_below[2], from_above[2])
 
     def kv_block(offset):
         return kv_part[index_of[offset]]
 
-    hops = ring_sum(kv_block, far, far - 1)
+    def kv_tie(left, value):
+        if left == min(2, far - 1):
+            return after(value, *from_below[3:], *from_above[3:])
+        return value
+
+    came = ring_sum(kv_block, far, far - 1, tie=kv_tie)
     kv_own = (
-        kv_block(0).astype(F32) + hops[0][-1].astype(F32) + hops[1][-1].astype(F32)
+        kv_block(0).astype(F32) + came[0].astype(F32) + came[1].astype(F32)
     ).astype(BF16)
+    for distance in range(2, far):
+        near += [-distance, distance]
+        near_queries.append(query([from_below[distance], from_above[distance]], weight_query))
+    kv_own = after(kv_own, *far_chunks, *near_queries)
     kv_pieces = [kv_own]
     for step in range(1, sharing):
         pairs = [
@@ -426,55 +514,43 @@
         ]
         kv_pieces.append(lax.ppermute(kv_own, "mp", pairs))
 
-    weight_query, weight_out = w_query[0], w_out[0]
-    near = []
-    near_queries = []
-    for distance in range(1, far):
-        chunks = [from_below[distance], from_above[distance]]
-        near += [-distance, distance]
-        if distance == 1:
-            chunks.append(text_own)
-            near.append(0)
-        near_queries.append(query(chunks, weight_query))
     near_queries = jnp.concatenate(near_queries, axis=0)
-    far_chunks = [up(from_below[-1][:cut])]
-    if parts == 2:
-        far_chunks.append(down(from_above[-1][cut:]))
     far_queries = query(far_chunks, weight_query)
+    out_parts = {}
     far_part = attend(
-        meta, far_queries, kv_pieces, weight_out, [index_of[far]], text_rows, mp_count
+        meta, far_queries, kv_pieces, weight_out, [index_of[far]], [cut] * parts, mp_count
     )
+    out_parts[far] = out_parts[-far] = far_part
+    sizes = [size for o in near for size in ([cut] * parts if o else [text_rows])]
     near_part = attend(
         meta,
-        near_queries,
+        after(near_queries, *far_part),
         kv_pieces,
         weight_out,
         [index_of[offset] for offset in near],
-        text_rows,
+        sizes,
         mp_count,
     )
-
-    own_first = near.index(0) * text_rows
-    own_next = to_next(near_part[own_first : own_first + text_rows])
-    results = []
+    for offset in near:
+        count = parts if offset else 1
+        out_parts[offset], near_part = near_part[:count], near_part[count:]
+
+    own_next = to_next(out_parts[0][0])
+    branch_arrivals = []
     for part, (start_up, start_down) in enumerate(reach):
 
         def out_block(offset, part=part):
-            if abs(offset) == far:
-                return far_part[part * cut : (part + 1) * cut]
-            first = near.index(offset) * text_rows + part * cut
-            return near_part[first : first + cut]
-
-        def out_tie(left, value):
-            return after(value, own_next) if left == min(2, far - 1) else value
-
-        hops = ring_sum(out_block, start_up, start_down, up_across, down_across, out_tie)
-        rows = slice(part * cut, (part + 1) * cut)
-        branch = own_next[rows].astype(F32) + hops[0][-1].astype(F32) + hops[1][-1].astype(F32)
-        results.append(
-            (text_next[rows].astype(F32) + jnp.tanh(gate_next[0]) * branch).astype(BF16)
+            return out_parts[offset][part]
+
+        def out_tie(left, value, part=part):
+            if left == min(2, far - 1) and part == 0:
+                return after(value, own_next)
+            return value
+
+        branch_arrivals.append(
+            ring_sum(out_block, start_up, start_down, up_across, down_across, out_tie)
         )
-    return jnp.concatenate(results, axis=0)[None]
+    return finish(gate_next, text_next, own_next, branch_arrivals)
 
 
 def solution(mesh):

time: 273 us -> 275 us (level)
  waiting for transfers between devices: 165 us -> 147 us
  Pallas kernels: 44 us -> 54.7 us
  starting transfers between devices: 47.2 us -> 56.2 us
  other arithmetic: 5.92 us -> 10.7 us
  local copies, waits for them, and re-layouts: 9.07 us -> 5.34 us
    ppermute x2, waiting for transfers between devices: 21.2 us -> 0.01 us  [up_across(): return lax.ppermute(value, ('section', 'mp'), across(up_pairs))]
    ppermute x19, waiting for transfers between devices: 44.2 us -> 29.3 us  [down(): return lax.ppermute(value, 'mp', down_pairs)]
    ppermute x2, waiting for transfers between devices: 0.01 us -> 14.4 us  [down_across(): return lax.ppermute(value, ('section', 'mp'), across(down_pairs))]
    ppermute x20, starting transfers between devices: 26.3 us -> 12.1 us  [up(): return lax.ppermute(value, 'mp', up_pairs)]
    ppermute x19, starting transfers between devices: 15.5 us -> 29.6 us  [down(): return lax.ppermute(value, 'mp', down_pairs)]
    ppermute x2, starting transfers between devices: 3.4 us -> 9.92 us  [down_across(): return lax.ppermute(value, ('section', 'mp'), across(down_pairs))]
    pallas_call x2, Pallas kernels: 14.5 us -> 20.8 us  [attend(): pl.pallas_call(kernel, grid_spec=pltpu.PrefetchScalarGridSpec(num_scalar_...]
    convert_element_type x9 -> x25, other arithmetic: 2.41 us -> 8.65 us  [add(): return (one.astype(F32) + other.astype(F32)).astype(BF16)]
  transfers between devices with their start and end apart: 50 -> 50, of which waited for: 30 -> 25; matrix products, arithmetic and copies ran while one was open for 2% -> 4% of each run, Pallas kernels for 14% -> 15%
where the time goes in v4:
time: 275 us; the launch traced here: 274 us
  waiting for transfers between devices  147 us (53%)
  starting transfers between devices  56.2 us (20%)
  Pallas kernels  54.7 us (20%)
  other arithmetic  10.7 us (4%)
  local copies, waits for them, and re-layouts  5.34 us (2%)
    ppermute x20, waiting for transfers between devices, up(): return lax.ppermute(value, 'mp', up_pairs)  89.7 us
    ppermute x19, starting transfers between devices, down(): return lax.ppermute(value, 'mp', down_pairs)  29.6 us
    ppermute x19, waiting for transfers between devices, down(): return lax.ppermute(value, 'mp', down_pairs)  29.3 us
    pallas_call x2, Pallas kernels, attend(): pl.pallas_call(kernel, grid_spec=pltpu.PrefetchScalarGridSpec(num_scalar_...  20.8 us
    ppermute x2, waiting for transfers between devices, down_across(): return lax.ppermute(value, ('section', 'mp'), across(down_pairs))  14.4 us
    pallas_call x2, Pallas kernels, project(): pl.pallas_call(kernel, grid_spec=pltpu.PrefetchScalarGridSpec(num_scalar_...  14 us
    ppermute x1, waiting for transfers between devices, local(): lax.ppermute(moving, 'section', [(s, (s + 2) % section_count) for s in ra...  13.3 us
    ppermute x20, starting transfers between devices, up(): return lax.ppermute(value, 'mp', up_pairs)  12.1 us
  transfers between devices with their start and end apart: 50, of which 25 were waited for; matrix products, arithmetic and copies ran while one was open for 4% of the time, Pallas kernels for 15%

profile of v4, /device:TPU:0, one launch (start us, length us, event | category | flops | bytes accessed | tf_op | source)
XLA Modules:
  0.0 274.3 jit_solution(1758327869106828378)
XLA Ops:
  0.0 3.0 %collective-permute-start.3 = (bf16[64,8192]{1,0:T(8,128)(2,1)}, bf16[64,8192]{1,0:T(8,128)(2,1)S(1)}, u32[]{:S(2)}, u32[]{:S(2)}) collective-permute-start(bf16[64,8192]{1,0:T(8,128)(2,1)} %bitcast.14), channel_id=1, source_target_pairs={{2,0},{4,2},{6,4},{7,6},{5,7},{3,5},{1,3},{0,1},{10,8},{12,10},{14... | collective-permute-start | bytes 3145736 | tf_op jit(solution)/shard_map/ppermute | solution.py:395
  9.9 11.1 %project.2 = (bf16[160,1024]{1,0:T(8,128)(2,1)S(1)}, bf16[160,1024]{1,0:T(8,128)(2,1)S(1)}, bf16[160,1024]{1,0:T(8,128)(2,1)S(1)}, bf16[160,1024]{1,0:T(8,128)(2...) custom-call(s32[10]{0:T(128)S(1)} %get-tuple-element.121.places_ref,, ...), custom_call_target="tpu_custom_call" | custom-call | flops 3774873600 | bytes 15728640 | tf_op jit(solution)/shard_map/project/pallas_call | solution.py:134
  21.0 13.8 %collective-permute-done.4 = bf16[160,1024]{1,0:T(8,128)(2,1)S(1)} collective-permute-done((bf16[160,1024]{1,0:T(8,128)(2,1)S(1)}, bf16[160,1024]{1,0:T(8,128)(2,1)S(1)}, u32[]{:S(2)}, u32[]{:S(2)}) %collective-permute-start.4) | collective-permute-done | bytes 327712 | tf_op jit(solution)/shard_map/ppermute | solution.py:392
  37.1 6.0 %collective-permute-done.8 = bf16[160,1024]{1,0:T(8,128)(2,1)S(1)} collective-permute-done((bf16[160,1024]{1,0:T(8,128)(2,1)S(1)}, bf16[160,1024]{1,0:T(8,128)(2,1)S(1)}, u32[]{:S(2)}, u32[]{:S(2)}) %collective-permute-start.8) | collective-permute-done | bytes 327712 | tf_op jit(solution)/shard_map/ppermute | solution.py:395
  47.9 3.7 %collective-permute-done.11 = bf16[160,1024]{1,0:T(8,128)(2,1)S(1)} collective-permute-done((bf16[160,1024]{1,0:T(8,128)(2,1)S(1)}, bf16[160,1024]{1,0:T(8,128)(2,1)S(1)}, u32[]{:S(2)}, u32[]{:S(2)}) %collective-permute-start.11) | collective-permute-done | bytes 327712 | tf_op jit(solution)/shard_map/ppermute | solution.py:392
  53.9 4.6 %collective-permute-done.6 = bf16[160,1024]{1,0:T(8,128)(2,1)S(1)} collective-permute-done((bf16[160,1024]{1,0:T(8,128)(2,1)S(1)}, bf16[160,1024]{1,0:T(8,128)(2,1)S(1)}, u32[]{:S(2)}, u32[]{:S(2)}) %collective-permute-start.6) | collective-permute-done | bytes 327712 | tf_op jit(solution)/shard_map/ppermute | solution.py:392
  72.6 3.5 %collective-permute-done.10.refs_2_ = bf16[160,1024]{1,0:T(8,128)(2,1)S(1)} collective-permute-done((bf16[160,1024]{1,0:T(8,128)(2,1)S(1)}, bf16[160,1024]{1,0:T(8,128)(2,1)S(1)}, u32[]{:S(2)}, u32[]{:S(2)}) %collective-permute-start.10) | collective-permute-done | bytes 327712 | tf_op jit(solution)/shard_map/ppermute | solution.py:395
  76.1 3.5 %collective-permute-done.13.refs_4_ = bf16[160,1024]{1,0:T(8,128)(2,1)S(1)} collective-permute-done((bf16[160,1024]{1,0:T(8,128)(2,1)S(1)}, bf16[160,1024]{1,0:T(8,128)(2,1)S(1)}, u32[]{:S(2)}, u32[]{:S(2)}) %collective-permute-start.13) | collective-permute-done | bytes 327712 | tf_op jit(solution)/shard_map/ppermute | solution.py:392
  85.9 13.3 %collective-permute-done.25.refs_2_ = bf16[320,1024]{1,0:T(8,128)(2,1)S(1)} collective-permute-done((bf16[320,1024]{1,0:T(8,128)(2,1)S(1)}, bf16[320,1024]{1,0:T(8,128)(2,1)S(1)}, u32[]{:S(2)}, u32[]{:S(2)}) %collective-permute-start.25) | collective-permute-done | bytes 655392 | tf_op jit(solution)/shard_map/ppermute | solution.py:471
  100.9 6.8 %collective-permute-done.18.refs_0_ = bf16[64,8192]{1,0:T(8,128)(2,1)S(1)} collective-permute-done((bf16[64,8192]{1,0:T(8,128)(2,1)S(1)}, bf16[64,8192]{1,0:T(8,128)(2,1)S(1)}, u32[]{:S(2)}, u32[]{:S(2)}) %collective-permute-start.18) | collective-permute-done | bytes 1048608 | tf_op jit(solution)/shard_map/ppermute | solution.py:392
  109.8 3.5 %query.4 = bf16[192,512]{1,0:T(8,128)(2,1)S(1)} custom-call(bf16[64,8192]{1,0:T(8,128)(2,1)S(1)} %collective-permute-done.2.refs_0_, bf16[64,8192]{1,0:T(8,128)(2,1)S(1)} %collective-permute-done.3.refs_1_, bf16[64,8192]{1,0:T(8,128)(2,1)S(1)} %bitcast.17, bf16[8192,512]{1,0:T(8,128)(2,1)S(1)} %bitcast.10), custom_call_target="tpu_custom_call" | custom-call | flops 1610612736 | bytes 11534336 | tf_op jit(solution)/shard_map/query/pallas_call | solution.py:244
  114.9 4.4 %key_values.1 = (bf16[256,256]{1,0:T(8,128)(2,1)S(1)}, bf16[256,256]{1,0:T(8,128)(2,1)S(1)}, bf16[256,256]{1,0:T(8,128)(2,1)S(1)}, bf16[256,256]{1,0:T(8,128)(2,...) custom-call(s32[18]{0:T(128)S(1)} %pad_add_fusion.meta_ref, ...), custom_call_target="tpu_custom_call" | custom-call | flops 2415919104 | bytes 4718592 | tf_op jit(solution)/shard_map/key_values/pallas_call | solution.py:198
  119.8 13.9 %collective-permute-done.27 = bf16[256,256]{1,0:T(8,128)(2,1)S(1)} collective-permute-done((bf16[256,256]{1,0:T(8,128)(2,1)S(1)}, bf16[256,256]{1,0:T(8,128)(2,1)S(1)}, u32[]{:S(2)}, u32[]{:S(2)}) %collective-permute-start.27) | collective-permute-done | bytes 131104 | tf_op jit(solution)/shard_map/ppermute | solution.py:392
  135.9 4.2 %collective-permute-done.28 = bf16[256,256]{1,0:T(8,128)(2,1)S(1)} collective-permute-done((bf16[256,256]{1,0:T(8,128)(2,1)S(1)}, bf16[256,256]{1,0:T(8,128)(2,1)S(1)}, u32[]{:S(2)}, u32[]{:S(2)}) %collective-permute-start.28) | collective-permute-done | bytes 131104 | tf_op jit(solution)/shard_map/ppermute | solution.py:392
  163.4 9.0 %attend.2 = (bf16[32,8192]{1,0:T(8,128)(2,1)}, bf16[32,8192]{1,0:T(8,128)(2,1)}) custom-call(s32[18]{0:T(128)} %copy-done.3, bf16[64,512]{1,0:T(8,128)(2,1)} %copy-done.2, bf16[256,256]{1,0:T(8,128)(2,1)} %copy-done.5, bf16[256,256]{1,0:T(8,128)(2,1)} %copy-done.10, bf16[512,8192]{1,0:T(8,128)(2,1)} %bitcast.19), custom_call_target="tpu_custom_call" | custom-call | flops 553648128 | bytes 9437184 | tf_op jit(solution)/shard_map/attend/pallas_call | solution.py:321
  175.3 11.7 %attend.3 = (bf16[32,8192]{1,0:T(8,128)(2,1)}, bf16[32,8192]{1,0:T(8,128)(2,1)}, bf16[32,8192]{1,0:T(8,128)(2,1)}, bf16[32,8192]{1,0:T(8,128)(2,1)}, bf16[64,819...) custom-call(s32[18]{0:T(128)} %copy-done.3, ...), custom_call_target="tpu_custom_call" | custom-call | flops 3875536896 | bytes 15728640 | tf_op jit(solution)/shard_map/attend/pallas_call | solution.py:321
  190.4 10.8 %collective-permute-done.43 = bf16[32,8192]{1,0:T(8,128)(2,1)S(1)} collective-permute-done((bf16[32,8192]{1,0:T(8,128)(2,1)}, bf16[32,8192]{1,0:T(8,128)(2,1)S(1)}, u32[]{:S(2)}, u32[]{:S(2)}) %collective-permute-start.43) | collective-permute-done | bytes 524320 | tf_op jit(solution)/shard_map/ppermute | solution.py:392
  206.8 13.7 %collective-permute-done.44 = bf16[32,8192]{1,0:T(8,128)(2,1)S(1)} collective-permute-done((bf16[32,8192]{1,0:T(8,128)(2,1)S(1)}, bf16[32,8192]{1,0:T(8,128)(2,1)S(1)}, u32[]{:S(2)}, u32[]{:S(2)}) %collective-permute-start.44) | collective-permute-done | bytes 524320 | tf_op jit(solution)/shard_map/ppermute | solution.py:392
  225.3 11.7 %collective-permute-done.48 = bf16[32,8192]{1,0:T(8,128)(2,1)S(1)} collective-permute-done((bf16[32,8192]{1,0:T(8,128)(2,1)S(1)}, bf16[32,8192]{1,0:T(8,128)(2,1)S(1)}, u32[]{:S(2)}, u32[]{:S(2)}) %collective-permute-start.48) | collective-permute-done | bytes 524320 | tf_op jit(solution)/shard_map/ppermute | solution.py:395
  237.1 3.0 %collective-permute-start.49 = (bf16[32,8192]{1,0:T(8,128)(2,1)S(1)}, bf16[32,8192]{1,0:T(8,128)(2,1)S(1)}, u32[]{:S(2)}, u32[]{:S(2)}) collective-permute-start(bf16[32,8192]{1,0:T(8,128)(2,1)S(1)} %add_convert_fusion), channel_id=1, source_target_pairs={{2,8},{4,10},{6,12},{7,14},{5,15},{3,13},{1,11},{0,9},{10,16},{12,... | collective-permute-start | bytes 1572872 | tf_op jit(solution)/shard_map/ppermute | solution.py:408
  240.1 5.7 %collective-permute-done.38 = bf16[32,8192]{1,0:T(8,128)(2,1)S(1)} collective-permute-done((bf16[32,8192]{1,0:T(8,128)(2,1)S(1)}, bf16[32,8192]{1,0:T(8,128)(2,1)S(1)}, u32[]{:S(2)}, u32[]{:S(2)}) %collective-permute-start.38) | collective-permute-done | bytes 524320 | tf_op jit(solution)/shard_map/ppermute | solution.py:392
  250.0 6.9 %collective-permute-start.42 = (bf16[32,8192]{1,0:T(8,128)(2,1)S(1)}, bf16[32,8192]{1,0:T(8,128)(2,1)S(1)}, u32[]{:S(2)}, u32[]{:S(2)}) collective-permute-start(bf16[32,8192]{1,0:T(8,128)(2,1)S(1)} %add_convert_fusion.5), channel_id=1, source_target_pairs={{2,8},{4,10},{6,12},{7,14},{5,15},{3,13},{1,11},{0,9},{10,16},{12,... | collective-permute-start | bytes 1572872 | tf_op jit(solution)/shard_map/ppermute | solution.py:408
  257.0 3.7 %collective-permute-done.49.refs_3_ = bf16[32,8192]{1,0:T(8,128)(2,1)S(1)} collective-permute-done((bf16[32,8192]{1,0:T(8,128)(2,1)S(1)}, bf16[32,8192]{1,0:T(8,128)(2,1)S(1)}, u32[]{:S(2)}, u32[]{:S(2)}) %collective-permute-start.49) | collective-permute-done | bytes 524320 | tf_op jit(solution)/shard_map/ppermute | solution.py:408
  260.7 10.7 %collective-permute-done.42.refs_1_ = bf16[32,8192]{1,0:T(8,128)(2,1)S(1)} collective-permute-done((bf16[32,8192]{1,0:T(8,128)(2,1)S(1)}, bf16[32,8192]{1,0:T(8,128)(2,1)S(1)}, u32[]{:S(2)}, u32[]{:S(2)}) %collective-permute-start.42) | collective-permute-done | bytes 524320 | tf_op jit(solution)/shard_map/ppermute | solution.py:408
  (155 shorter events, 91.4 us)
Async XLA Ops:
  0.0 47.3 %collective-permute-start.3 = (bf16[64,8192]{1,0:T(8,128)(2,1)}, bf16[64,8192]{1,0:T(8,128)(2,1)S(1)}, u32[]{:S(2)}, u32[]{:S(2)}) collective-permute-start(bf16[64,8192]{1,0:T(8,128)(2,1)} %bitcast.14), channel_id=1, source_target_pairs={{2,0},{4,2},{6,4},{7,6},{5,7},{3,5},{1,3},{0,1},{10,8},{12,10},{14... | collective-permute-start | bytes 3145736 | tf_op jit(solution)/shard_map/ppermute | solution.py:395
  3.0 44.4 %collective-permute-start.2 = (bf16[64,8192]{1,0:T(8,128)(2,1)}, bf16[64,8192]{1,0:T(8,128)(2,1)S(1)}, u32[]{:S(2)}, u32[]{:S(2)}) collective-permute-start(bf16[64,8192]{1,0:T(8,128)(2,1)} %bitcast.15), channel_id=1, source_target_pairs={{0,2},{2,4},{4,6},{6,7},{7,5},{5,3},{3,1},{1,0},{8,10},{10,12},{12... | collective-permute-start | bytes 3145736 | tf_op jit(solution)/shard_map/ppermute | solution.py:392
  3.0 57.2 %collective-permute-start.1 = (bf16[64,8192]{1,0:T(8,128)(2,1)}, bf16[64,8192]{1,0:T(8,128)(2,1)S(1)}, u32[]{:S(2)}, u32[]{:S(2)}) collective-permute-start(bf16[64,8192]{1,0:T(8,128)(2,1)} %bitcast.16), channel_id=1, source_target_pairs={{0,8},{8,16},{16,24},{24,0},{1,9},{9,17},{17,25},{25,1},{2,10},{10... | collective-permute-start | bytes 3145736 | tf_op jit(solution)/shard_map/ppermute | solution.py:411
  7.7 27.1 %collective-permute-start.4 = (bf16[160,1024]{1,0:T(8,128)(2,1)S(1)}, bf16[160,1024]{1,0:T(8,128)(2,1)S(1)}, u32[]{:S(2)}, u32[]{:S(2)}) collective-permute-start(bf16[160,1024]{1,0:T(8,128)(2,1)S(1)} %get-tuple-element.63), channel_id=1, source_target_pairs={{0,2},{2,4},{4,6},{6,7},{7,5},{5,3},{3,1},{1,0},{8,10},{10,12},{12... | collective-permute-start | bytes 983048 | tf_op jit(solution)/shard_map/ppermute | solution.py:392
  9.8 26.7 %collective-permute-start.14 = (bf16[160,1024]{1,0:T(8,128)(2,1)S(1)}, bf16[160,1024]{1,0:T(8,128)(2,1)S(1)}, u32[]{:S(2)}, u32[]{:S(2)}) collective-permute-start(bf16[160,1024]{1,0:T(8,128)(2,1)S(1)} %get-tuple-element.80), channel_id=1, source_target_pairs={{2,0},{4,2},{6,4},{7,6},{5,7},{3,5},{1,3},{0,1},{10,8},{12,10},{14... | collective-permute-start | bytes 983048 | tf_op jit(solution)/shard_map/ppermute | solution.py:395
  83.1 16.2 %collective-permute-start.25 = (bf16[320,1024]{1,0:T(8,128)(2,1)S(1)}, bf16[320,1024]{1,0:T(8,128)(2,1)S(1)}, u32[]{:S(2)}, u32[]{:S(2)}) collective-permute-start(bf16[320,1024]{1,0:T(8,128)(2,1)S(1)} %total_of.1.refs_0_), channel_id=1, source_target_pairs={{0,16},{8,24},{16,0},{24,8},{1,17},{9,25},{17,1},{25,9},{2,18},{10... | collective-permute-start | bytes 1966088 | tf_op jit(solution)/shard_map/ppermute | solution.py:471
  83.7 24.0 %collective-permute-start.18 = (bf16[64,8192]{1,0:T(8,128)(2,1)S(1)}, bf16[64,8192]{1,0:T(8,128)(2,1)S(1)}, u32[]{:S(2)}, u32[]{:S(2)}) collective-permute-start(bf16[64,8192]{1,0:T(8,128)(2,1)S(1)} %collective-permute-done.2.refs_0_), channel_id=1, source_target_pairs={{0,2},{2,4},{4,6},{6,7},{7,5},{5,3},{3,1},{1,0},{8,10},{10,12},{12... | collective-permute-start | bytes 3145736 | tf_op jit(solution)/shard_map/ppermute | solution.py:392
  84.1 24.0 %collective-permute-start.19 = (bf16[64,8192]{1,0:T(8,128)(2,1)S(1)}, bf16[64,8192]{1,0:T(8,128)(2,1)S(1)}, u32[]{:S(2)}, u32[]{:S(2)}) collective-permute-start(bf16[64,8192]{1,0:T(8,128)(2,1)S(1)} %collective-permute-done.3.refs_1_), channel_id=1, source_target_pairs={{2,0},{4,2},{6,4},{7,6},{5,7},{3,5},{1,3},{0,1},{10,8},{12,10},{14... | collective-permute-start | bytes 3145736 | tf_op jit(solution)/shard_map/ppermute | solution.py:395
  85.8 27.5 %collective-permute-start.24 = (bf16[320,1024]{1,0:T(8,128)(2,1)S(1)}, bf16[320,1024]{1,0:T(8,128)(2,1)S(1)}, u32[]{:S(2)}, u32[]{:S(2)}) collective-permute-start(bf16[320,1024]{1,0:T(8,128)(2,1)S(1)} %total_of.1.refs_0_), channel_id=1, source_target_pairs={{0,8},{8,0},{16,24},{24,16},{1,9},{9,1},{17,25},{25,17},{2,10},{10... | collective-permute-start | bytes 1966088 | tf_op jit(solution)/shard_map/ppermute | solution.py:468
  107.7 32.4 %collective-permute-start.20 = (bf16[64,8192]{1,0:T(8,128)(2,1)S(1)}, bf16[64,8192]{1,0:T(8,128)(2,1)S(1)}, u32[]{:S(2)}, u32[]{:S(2)}) collective-permute-start(bf16[64,8192]{1,0:T(8,128)(2,1)S(1)} %collective-permute-done.18.refs_0_), channel_id=1, source_target_pairs={{0,2},{2,4},{4,6},{6,7},{7,5},{5,3},{3,1},{1,0},{8,10},{10,12},{12... | collective-permute-start | bytes 3145736 | tf_op jit(solution)/shard_map/ppermute | solution.py:392
  108.2 31.9 %collective-permute-start.21 = (bf16[64,8192]{1,0:T(8,128)(2,1)S(1)}, bf16[64,8192]{1,0:T(8,128)(2,1)S(1)}, u32[]{:S(2)}, u32[]{:S(2)}) collective-permute-start(bf16[64,8192]{1,0:T(8,128)(2,1)S(1)} %collective-permute-done.19.refs_1_), channel_id=1, source_target_pairs={{2,0},{4,2},{6,4},{7,6},{5,7},{3,5},{1,3},{0,1},{10,8},{12,10},{14... | collective-permute-start | bytes 3145736 | tf_op jit(solution)/shard_map/ppermute | solution.py:395
  140.7 16.4 %collective-permute-start.22 = (bf16[32,8192]{1,0:T(8,128)(2,1)S(1)}, bf16[32,8192]{1,0:T(8,128)(2,1)S(1)}, u32[]{:S(2)}, u32[]{:S(2)}) collective-permute-start(bf16[32,8192]{1,0:T(8,128)(2,1)S(1)} %slice.13), channel_id=1, source_target_pairs={{0,2},{2,4},{4,6},{6,7},{7,5},{5,3},{3,1},{1,0},{8,10},{10,12},{12... | collective-permute-start | bytes 1572872 | tf_op jit(solution)/shard_map/ppermute | solution.py:392
  172.4 16.8 %collective-permute-start.36 = (bf16[32,8192]{1,0:T(8,128)(2,1)}, bf16[32,8192]{1,0:T(8,128)(2,1)S(1)}, u32[]{:S(2)}, u32[]{:S(2)}) collective-permute-start(bf16[32,8192]{1,0:T(8,128)(2,1)} %get-tuple-element.101), channel_id=1, source_target_pairs={{0,2},{2,4},{4,6},{6,7},{7,5},{5,3},{3,1},{1,0},{8,10},{10,12},{12... | collective-permute-start | bytes 1572872 | tf_op jit(solution)/shard_map/ppermute | solution.py:392
  173.3 29.8 %collective-permute-start.46 = (bf16[32,8192]{1,0:T(8,128)(2,1)}, bf16[32,8192]{1,0:T(8,128)(2,1)S(1)}, u32[]{:S(2)}, u32[]{:S(2)}) collective-permute-start(bf16[32,8192]{1,0:T(8,128)(2,1)} %get-tuple-element.102), channel_id=1, source_target_pairs={{2,0},{4,2},{6,4},{7,6},{5,7},{3,5},{1,3},{0,1},{10,8},{12,10},{14... | collective-permute-start | bytes 1572872 | tf_op jit(solution)/shard_map/ppermute | solution.py:395
  187.1 18.6 %collective-permute-start.40 = (bf16[32,8192]{1,0:T(8,128)(2,1)}, bf16[32,8192]{1,0:T(8,128)(2,1)S(1)}, u32[]{:S(2)}, u32[]{:S(2)}) collective-permute-start(bf16[32,8192]{1,0:T(8,128)(2,1)} %get-tuple-element.109), channel_id=1, source_target_pairs={{2,0},{4,2},{6,4},{7,6},{5,7},{3,5},{1,3},{0,1},{10,8},{12,10},{14... | collective-permute-start | bytes 1572872 | tf_op jit(solution)/shard_map/ppermute | solution.py:395
  189.2 34.0 %collective-permute-start.35 = (bf16[64,8192]{1,0:T(8,128)(2,1)}, bf16[64,8192]{1,0:T(8,128)(2,1)S(1)}, u32[]{:S(2)}, u32[]{:S(2)}) collective-permute-start(bf16[64,8192]{1,0:T(8,128)(2,1)} %get-tuple-element.104), channel_id=1, source_target_pairs={{0,8},{8,16},{16,24},{24,0},{1,9},{9,17},{17,25},{25,1},{2,10},{10... | collective-permute-start | bytes 3145736 | tf_op jit(solution)/shard_map/ppermute | solution.py:411
  190.3 32.7 %collective-permute-start.37 = (bf16[32,8192]{1,0:T(8,128)(2,1)S(1)}, bf16[32,8192]{1,0:T(8,128)(2,1)S(1)}, u32[]{:S(2)}, u32[]{:S(2)}) collective-permute-start(bf16[32,8192]{1,0:T(8,128)(2,1)S(1)} %add_convert_fusion.9), channel_id=1, source_target_pairs={{0,2},{2,4},{4,6},{6,7},{7,5},{5,3},{3,1},{1,0},{8,10},{10,12},{12... | collective-permute-start | bytes 1572872 | tf_op jit(solution)/shard_map/ppermute | solution.py:392
  202.4 18.2 %collective-permute-start.44 = (bf16[32,8192]{1,0:T(8,128)(2,1)S(1)}, bf16[32,8192]{1,0:T(8,128)(2,1)S(1)}, u32[]{:S(2)}, u32[]{:S(2)}) collective-permute-start(bf16[32,8192]{1,0:T(8,128)(2,1)S(1)} %add_convert_fusion.4), channel_id=1, source_target_pairs={{0,2},{2,4},{4,6},{6,7},{7,5},{5,3},{3,1},{1,0},{8,10},{10,12},{12... | collective-permute-start | bytes 1572872 | tf_op jit(solution)/shard_map/ppermute | solution.py:392
  204.3 17.5 %collective-permute-start.47 = (bf16[32,8192]{1,0:T(8,128)(2,1)S(1)}, bf16[32,8192]{1,0:T(8,128)(2,1)S(1)}, u32[]{:S(2)}, u32[]{:S(2)}) collective-permute-start(bf16[32,8192]{1,0:T(8,128)(2,1)S(1)} %add_convert_fusion.2), channel_id=1, source_target_pairs={{2,0},{4,2},{6,4},{7,6},{5,7},{3,5},{1,3},{0,1},{10,8},{12,10},{14... | collective-permute-start | bytes 1572872 | tf_op jit(solution)/shard_map/ppermute | solution.py:395
  221.7 35.3 %collective-permute-start.45 = (bf16[32,8192]{1,0:T(8,128)(2,1)S(1)}, bf16[32,8192]{1,0:T(8,128)(2,1)S(1)}, u32[]{:S(2)}, u32[]{:S(2)}) collective-permute-start(bf16[32,8192]{1,0:T(8,128)(2,1)S(1)} %add_convert_fusion.3), channel_id=1, source_target_pairs={{0,10},{2,12},{4,14},{6,15},{7,13},{5,11},{3,9},{1,8},{8,18},{10,2... | collective-permute-start | bytes 1572872 | tf_op jit(solution)/shard_map/ppermute | solution.py:405
  223.2 22.6 %collective-permute-start.38 = (bf16[32,8192]{1,0:T(8,128)(2,1)S(1)}, bf16[32,8192]{1,0:T(8,128)(2,1)S(1)}, u32[]{:S(2)}, u32[]{:S(2)}) collective-permute-start(bf16[32,8192]{1,0:T(8,128)(2,1)S(1)} %add_convert_fusion.8), channel_id=1, source_target_pairs={{0,2},{2,4},{4,6},{6,7},{7,5},{5,3},{3,1},{1,0},{8,10},{10,12},{12... | collective-permute-start | bytes 1572872 | tf_op jit(solution)/shard_map/ppermute | solution.py:392
  225.2 24.7 %collective-permute-start.41 = (bf16[32,8192]{1,0:T(8,128)(2,1)S(1)}, bf16[32,8192]{1,0:T(8,128)(2,1)S(1)}, u32[]{:S(2)}, u32[]{:S(2)}) collective-permute-start(bf16[32,8192]{1,0:T(8,128)(2,1)S(1)} %add_convert_fusion.6), channel_id=1, source_target_pairs={{2,0},{4,2},{6,4},{7,6},{5,7},{3,5},{1,3},{0,1},{10,8},{12,10},{14... | collective-permute-start | bytes 1572872 | tf_op jit(solution)/shard_map/ppermute | solution.py:395
  237.1 23.6 %collective-permute-start.49 = (bf16[32,8192]{1,0:T(8,128)(2,1)S(1)}, bf16[32,8192]{1,0:T(8,128)(2,1)S(1)}, u32[]{:S(2)}, u32[]{:S(2)}) collective-permute-start(bf16[32,8192]{1,0:T(8,128)(2,1)S(1)} %add_convert_fusion), channel_id=1, source_target_pairs={{2,8},{4,10},{6,12},{7,14},{5,15},{3,13},{1,11},{0,9},{10,16},{12,... | collective-permute-start | bytes 1572872 | tf_op jit(solution)/shard_map/ppermute | solution.py:408
  250.0 21.4 %collective-permute-start.42 = (bf16[32,8192]{1,0:T(8,128)(2,1)S(1)}, bf16[32,8192]{1,0:T(8,128)(2,1)S(1)}, u32[]{:S(2)}, u32[]{:S(2)}) collective-permute-start(bf16[32,8192]{1,0:T(8,128)(2,1)S(1)} %add_convert_fusion.5), channel_id=1, source_target_pairs={{2,8},{4,10},{6,12},{7,14},{5,15},{3,13},{1,11},{0,9},{10,16},{12,... | collective-permute-start | bytes 1572872 | tf_op jit(solution)/shard_map/ppermute | solution.py:408
  (41 other events, 946.4 us)

commit v5 on v4

--- a/solution.py
+++ b/solution.py
@@ -20,6 +20,7 @@
 F32 = jnp.float32
 BF16 = jnp.bfloat16
 VMEM_LIMIT = 40 * 1024 * 1024
+QUICK = pl.CostEstimate(flops=1, bytes_accessed=1, transcendentals=0)
 VMEM_MOST = 56 * 1024 * 1024
 VMEM_SMALL = 16 * 1024 * 1024
 
@@ -63,7 +64,6 @@
     parts, count = len(groups), len(groups[0])
     part_rows, columns = groups[0][0].shape
     rows = parts * part_rows
-    wide = columns // 4 if columns % 512 == 0 else columns
 
     def kernel(*refs):
         for part in range(parts):
@@ -74,11 +74,11 @@
 
     return pl.pallas_call(
         kernel,
-        grid=(columns // wide,),
-        in_specs=[pl.BlockSpec((part_rows, wide), lambda i: (0, i))] * (parts * count),
-        out_specs=pl.BlockSpec((rows, wide), lambda i: (0, i)),
+        in_specs=[pl.BlockSpec(memory_space=pltpu.VMEM)] * (parts * count),
+        out_specs=pl.BlockSpec(memory_space=pltpu.VMEM),
         out_shape=jax.ShapeDtypeStruct((rows, columns), BF16),
         compiler_params=params(VMEM_SMALL),
+        cost_estimate=QUICK,
         name="total_of",
     )(*[value for group in groups for value in group])
 
@@ -87,7 +87,6 @@
     rows, columns = text.shape
     parts = len(arrivals)
     part_rows = rows // parts
-    wide = columns // 4
     flat = [value for came in arrivals for value in came]
     count = len(flat) // parts
 
@@ -104,13 +103,11 @@
 
     return pl.pallas_call(
         kernel,
-        grid=(columns // wide,),
-        in_specs=[pl.BlockSpec((1, 1), lambda i: (0, 0))]
-        + [pl.BlockSpec((rows, wide), lambda i: (0, i))] * 2
-        + [pl.BlockSpec((part_rows, wide), lambda i: (0, i))] * len(flat),
-        out_specs=pl.BlockSpec((1, rows, wide), lambda i: (0, 0, i)),
+        in_specs=[pl.BlockSpec(memory_space=pltpu.VMEM)] * (3 + len(flat)),
+        out_specs=pl.BlockSpec(memory_space=pltpu.VMEM),
         out_shape=jax.ShapeDtypeStruct((1, rows, columns), BF16),
         compiler_params=params(VMEM_SMALL),
+        cost_estimate=QUICK,
         name="finish",
     )(gate.reshape(1, 1), text, own, *flat)
 
@@ -145,8 +142,8 @@
         out_shape=[jax.ShapeDtypeStruct((half, wide), BF16)] * (2 * blocks),
         compiler_params=params(),
         cost_estimate=pl.CostEstimate(
-            flops=2 * rows * depth * wide * (blocks - 1),
-            bytes_accessed=2 * (depth + rows) * wide * (blocks - 1),
+            flops=2 * rows * depth * wide * blocks,
+            bytes_accessed=2 * (depth + rows) * wide * blocks,
             transcendentals=0,
         ),
         name="project",
@@ -202,11 +199,7 @@
         out_shape=[jax.ShapeDtypeStruct((kv_rows, 2 * HD), BF16)] * order_len,
         scratch_shapes=[pltpu.VMEM((SLOTS, width), BF16)],
         compiler_params=params(),
-        cost_estimate=pl.CostEstimate(
-            flops=2 * SLOTS * depth * (width + feat_rows * count),
-            bytes_accessed=2 * depth * (width + feat_rows * count),
-            transcendentals=0,
-        ),
+        cost_estimate=QUICK,
         name="key_values",
     )(meta, *pieces, weight)
 
@@ -250,11 +243,7 @@
         out_shape=jax.ShapeDtypeStruct((rows, width), BF16),
         scratch_shapes=[pltpu.VMEM((rows, depth), BF16), pltpu.VMEM((rows, 1), F32)],
         compiler_params=params(),
-        cost_estimate=pl.CostEstimate(
-            flops=2 * rows * depth * width,
-            bytes_accessed=2 * depth * (width + rows),
-            transcendentals=0,
-        ),
+        cost_estimate=QUICK,
         name="query",
     )(*chunks, weight)
 
@@ -270,20 +259,31 @@
 
     def kernel(meta_ref, query_ref, *refs):
         kv_refs, weight_ref = refs[:sharing], refs[sharing]
-        out_refs = refs[sharing + 1 : -3]
-        key_ref, value_ref, attended_ref = refs[-3:]
-
-        @pl.when(pl.program_id(0) == 0)
+        out_refs = refs[sharing + 1 : -5]
+        key_ref, value_ref, attended_ref, held_ref, sems = refs[-5:]
+        step = pl.program_id(0)
+
+        def fetch(index):
+            start = index * wide
+            return pltpu.make_async_copy(
+                weight_ref.at[:, pl.ds(pl.multiple_of(start, wide), wide)],
+                held_ref.at[index],
+                sems.at[index],
+            )
+
+        @pl.when(step == 0)
         def _():
+            for index in range(columns // wide):
+                fetch(index).start()
             mine = lax.rem(meta_ref[order_len], sharing)
-            for step in range(sharing):
+            for piece in range(sharing):
                 row = pl.multiple_of(
-                    lax.rem(mine + sharing - step, sharing) * kv_rows, kv_rows
+                    lax.rem(mine + sharing - piece, sharing) * kv_rows, kv_rows
                 )
-                keys = kv_refs[step][:, :HD].astype(F32)
+                keys = kv_refs[piece][:, :HD].astype(F32)
                 keys = keys * lax.rsqrt(jnp.mean(keys * keys, axis=-1, keepdims=True) + 1e-06)
                 key_ref[pl.ds(row, kv_rows), :] = keys.astype(BF16)
-                value_ref[pl.ds(row, kv_rows), :] = kv_refs[step][:, HD:]
+                value_ref[pl.ds(row, kv_rows), :] = kv_refs[piece][:, HD:]
             for place, index in enumerate(indices):
                 sample = meta_ref[index] * text_rows // TXT
                 slots = pl.ds(pl.multiple_of(sample * BLOCK, BLOCK), BLOCK)
@@ -310,8 +310,9 @@
                         h * text_rows : (h + 1) * text_rows
                     ]
 
+        fetch(step).wait()
         product = jnp.dot(
-            attended_ref[...], weight_ref[...], preferred_element_type=F32
+            attended_ref[...], held_ref[step], preferred_element_type=F32
         ).astype(BF16)
         first = 0
         for out_ref, size in zip(out_refs, sizes):
@@ -325,21 +326,19 @@
             grid=(columns // wide,),
             in_specs=[pl.BlockSpec((rows, width), lambda i, meta: (0, 0))]
             + [pl.BlockSpec(piece.shape, lambda i, meta: (0, 0)) for piece in kv_pieces]
-            + [pl.BlockSpec((width, wide), lambda i, meta: (0, i))],
+            + [pl.BlockSpec(memory_space=pl.ANY)],
             out_specs=[pl.BlockSpec((size, wide), lambda i, meta: (0, i)) for size in sizes],
             scratch_shapes=[
                 pltpu.VMEM((SLOTS, HD), BF16),
                 pltpu.VMEM((SLOTS, HD), BF16),
                 pltpu.VMEM((rows, width), BF16),
+                pltpu.VMEM((columns // wide, width, wide), BF16),
+                pltpu.SemaphoreType.DMA((columns // wide,)),
             ],
         ),
         out_shape=[jax.ShapeDtypeStruct((size, columns), BF16) for size in sizes],
         compiler_params=params(VMEM_MOST),
-        cost_estimate=pl.CostEstimate(
-            flops=2 * rows * width * (columns + 2 * BLOCK),
-            bytes_accessed=2 * columns * (width + rows),
-            transcendentals=rows * heads * BLOCK,
-        ),
+        cost_estimate=QUICK,
         name="attend",
     )(meta, queries, *kv_pieces, weight)
 
@@ -412,18 +411,25 @@
             value, "section", [(s, (s + 1) % section_count) for s in range(section_count)]
         )
 
-    def ring_sum(part, start_up, start_down, last_up=up, last_down=down, tie=None):
-        tie = tie or (lambda left, value: value)
-        arrived = []
-        for start, sign, move, last in (
-            (start_up, 1, up, last_up),
-            (start_down, -1, down, last_down),
-        ):
-            running = part(sign * start)
-            for distance in range(start, 1, -1):
-                running = add(move(tie(distance, running)), part(sign * (distance - 1)))
-            arrived.append(last(tie(1, running)))
-        return arrived
+    def ring_sums(chains, hold=lambda hop, value: value, turn=None):
+        running = [part(sign * distance) for part, distance, sign, _, _ in chains]
+        for hop in range(far):
+            for index, (part, distance, sign, move, last) in enumerate(chains):
+                left = distance - hop
+                if left == 1:
+                    running[index] = last(hold(hop, running[index]))
+                elif left > 1:
+                    came = move(hold(hop, running[index]))
+                    if turn is not None:
+                        came = after(came, turn)
+                    turn = running[index] = add(came, part(sign * (left - 1)))
+        return running
+
+    def both_ways(part, distance_up, distance_down, last_up=up, last_down=down):
+        return [
+            (part, distance_up, 1, up, last_up),
+            (part, distance_down, -1, down, last_down),
+        ]
 
     text_own = text_state[0]
     text_rows = text_own.shape[0]
@@ -442,23 +448,32 @@
 
     image_parts = project(places, tile_feats, w_proj, mp_count, 0, 1)
     image_parts += project(places, tile_feats, w_proj, mp_count, 1, mp_count - 1)
-    image_arrivals = []
-    for half, (start_up, start_down) in enumerate(((far, far - 1), (far - 1, far))):
-
-        def image_block(offset, half=half):
-            return image_parts[index_of[offset]][half]
-
-        def image_tie(left, value):
-            if left == min(2, far - 1):
-                return after(value, from_below[1], from_above[1])
-            if left == 1:
-                return after(value, text_next, gate_next)
-            return value
-
-        image_arrivals.append(
-            [image_block(0)] + ring_sum(image_block, start_up, start_down, tie=image_tie)
+    image_chains = [
+        chain
+        for half, distances in enumerate(((far, far - 1), (far - 1, far)))
+        for chain in both_ways(
+            lambda offset, half=half: image_parts[index_of[offset]][half], *distances
         )
-    image_cols = total_of(image_arrivals)
+    ]
+
+    def image_hold(hop, value):
+        if hop == min(2, far - 1):
+            return after(value, from_below[1], from_above[1])
+        if hop == far - 1:
+            return after(value, text_next, gate_next)
+        return value
+
+    turns = [0, 3, 1, 2]
+    came = ring_sums([image_chains[turn] for turn in turns], image_hold)
+    came = [came[turns.index(index)] for index in range(4)]
+    image_cols = total_of(
+        [[image_parts[index_of[0]][half], *came[2 * half : 2 * half + 2]] for half in range(2)]
+    )
+
+    text_round(image_cols)
+    weight_query, weight_out = w_query[0], w_out[0]
+    near = [-1, 1]
+    near_queries = [query([from_below[1], from_above[1]], weight_query)]
 
     pieces = []
     moving = image_cols
@@ -473,40 +488,31 @@
                 "section",
                 [(s, (s + 2) % section_count) for s in range(section_count)],
             )
-
-    for distance in range(2, far):
-        text_round(*([image_cols] if distance == 2 else []))
+            if step == 0:
+                moving = after(moving, near_queries[0])
+
+    kv_part = key_values(meta, pieces, w_kv[0], mp_count, section_count, sharing)
+
+    for distance in range(3, far):
+        text_round(*([kv_part[0]] if distance == 3 else []))
     far_chunks = [up(from_below[-1][:cut])]
     if parts == 2:
         far_chunks.append(down(from_above[-1][cut:]))
-
-    weight_query, weight_out = w_query[0], w_out[0]
-    near = [-1, 1, 0]
-    near_queries = [query([from_below[1], from_above[1], text_own], weight_query)]
-    kv_part = list(
-        key_values(
-            after(meta, near_queries[0]), pieces, w_kv[0], mp_count, section_count, sharing
-        )
-    )
-    if far > 2:
-        kv_part[0] = after(kv_part[0], from_below[2], from_above[2])
-
-    def kv_block(offset):
-        return kv_part[index_of[offset]]
-
-    def kv_tie(left, value):
-        if left == min(2, far - 1):
-            return after(value, *from_below[3:], *from_above[3:])
-        return value
-
-    came = ring_sum(kv_block, far, far - 1, tie=kv_tie)
-    kv_own = (
-        kv_block(0).astype(F32) + came[0].astype(F32) + came[1].astype(F32)
-    ).astype(BF16)
     for distance in range(2, far):
         near += [-distance, distance]
         near_queries.append(query([from_below[distance], from_above[distance]], weight_query))
-    kv_own = after(kv_own, *far_chunks, *near_queries)
+
+    def kv_hold(hop, value):
+        if hop == min(2, far - 1):
+            return after(value, *from_below[3:], *from_above[3:])
+        return value
+
+    came = ring_sums(both_ways(lambda offset: kv_part[index_of[offset]], far, far - 1), kv_hold)
+    kv_own = (
+        kv_part[index_of[0]].astype(F32) + came[0].astype(F32) + came[1].astype(F32)
+    ).astype(BF16)
+    near_queries = jnp.concatenate(near_queries, axis=0)
+    kv_own = after(kv_own, *far_chunks, near_queries)
     kv_pieces = [kv_own]
     for step in range(1, sharing):
         pairs = [
@@ -514,43 +520,46 @@
         ]
         kv_pieces.append(lax.ppermute(kv_own, "mp", pairs))
 
-    near_queries = jnp.concatenate(near_queries, axis=0)
-    far_queries = query(far_chunks, weight_query)
-    out_parts = {}
-    far_part = attend(
-        meta, far_queries, kv_pieces, weight_out, [index_of[far]], [cut] * parts, mp_count
-    )
-    out_parts[far] = out_parts[-far] = far_part
-    sizes = [size for o in near for size in ([cut] * parts if o else [text_rows])]
+    far_queries = query(far_chunks + [text_own], weight_query)
+    *far_part, own_part = attend(
+        meta,
+        far_queries,
+        kv_pieces,
+        weight_out,
+        [index_of[far], index_of[0]],
+        [cut] * parts + [text_rows],
+        mp_count,
+    )
     near_part = attend(
         meta,
-        after(near_queries, *far_part),
+        after(near_queries, own_part),
         kv_pieces,
         weight_out,
         [index_of[offset] for offset in near],
-        sizes,
+        [cut] * (parts * len(near)),
         mp_count,
     )
-    for offset in near:
-        count = parts if offset else 1
-        out_parts[offset], near_part = near_part[:count], near_part[count:]
-
-    own_next = to_next(out_parts[0][0])
-    branch_arrivals = []
-    for part, (start_up, start_down) in enumerate(reach):
-
-        def out_block(offset, part=part):
-            return out_parts[offset][part]
-
-        def out_tie(left, value, part=part):
-            if left == min(2, far - 1) and part == 0:
-                return after(value, own_next)
-            return value
-
-        branch_arrivals.append(
-            ring_sum(out_block, start_up, start_down, up_across, down_across, out_tie)
+    out_parts = {offset: near_part[parts * i :][:parts] for i, offset in enumerate(near)}
+    out_parts[far] = out_parts[-far] = far_part
+
+    own_next = to_next(own_part)
+    branch_chains = [
+        chain
+        for part, distances in enumerate(reach)
+        for chain in both_ways(
+            lambda offset, part=part: out_parts[offset][part],
+            *distances,
+            up_across,
+            down_across,
         )
-    return finish(gate_next, text_next, own_next, branch_arrivals)
+    ]
+
+    turns = [0, 3, 1, 2] if parts == 2 else [0, 1]
+    came = ring_sums([branch_chains[turn] for turn in turns], turn=own_next)
+    came = [came[turns.index(index)] for index in range(2 * parts)]
+    return finish(
+        gate_next, text_next, own_next, [came[2 * part : 2 * part + 2] for part in range(parts)]
+    )
 
 
 def solution(mesh):

time: 275 us -> 263 us (0.956)
  starting transfers between devices: 56.2 us -> 48.8 us
  Pallas kernels: 54.7 us -> 50.6 us
    ppermute x2, starting transfers between devices: 9.92 us -> 4.68 us  [down_across(): return lax.ppermute(value, ('section', 'mp'), across(down_pairs))]
    ppermute x19, waiting for transfers between devices: 29.3 us -> 34.3 us  [down(): return lax.ppermute(value, 'mp', down_pairs)]
    ppermute x20, waiting for transfers between devices: 89.7 us -> 86.4 us  [up(): return lax.ppermute(value, 'mp', up_pairs)]
    ppermute x1, waiting for transfers between devices: 13.3 us -> 10.3 us  [local(): lax.ppermute(moving, 'section', [(s, (s + 2) % section_count) for s in ra...]
  transfers between devices with their start and end apart: 50 -> 50, of which waited for: 25 -> 27; matrix products, arithmetic and copies ran while one was open for 4% -> 5% of each run, Pallas kernels for 15% -> 15%
where the time goes in v5:
time: 263 us
  waiting for transfers between devices  148 us (56%)
  Pallas kernels  50.6 us (19%)
  starting transfers between devices  48.8 us (19%)
  other arithmetic  10.6 us (4%)
  local copies, waits for them, and re-layouts  3.81 us (1%)
    ppermute x20, waiting for transfers between devices, up(): return lax.ppermute(value, 'mp', up_pairs)  86.4 us
    ppermute x19, waiting for transfers between devices, down(): return lax.ppermute(value, 'mp', down_pairs)  34.3 us
    ppermute x19, starting transfers between devices, down(): return lax.ppermute(value, 'mp', down_pairs)  30.1 us
    pallas_call x2, Pallas kernels, attend(): pl.pallas_call(kernel, grid_spec=pltpu.PrefetchScalarGridSpec(num_scalar_...  18.1 us
    pallas_call x2, Pallas kernels, project(): pl.pallas_call(kernel, grid_spec=pltpu.PrefetchScalarGridSpec(num_scalar_...  14 us
    ppermute x2, waiting for transfers between devices, down_across(): return lax.ppermute(value, ('section', 'mp'), across(down_pairs))  13.6 us
    ppermute x20, starting transfers between devices, up(): return lax.ppermute(value, 'mp', up_pairs)  11.2 us
    pallas_call x4, Pallas kernels, query(): pl.pallas_call(kernel, grid=(width // wide,), in_specs=[pl.BlockSpec(chun...  11.1 us
  transfers between devices with their start and end apart: 50, of which 27 were waited for; matrix products, arithmetic and copies ran while one was open for 5% of the time, Pallas kernels for 15%

profile of v5, /device:TPU:0, one launch (start us, length us, event | category | flops | bytes accessed | tf_op | source)
XLA Modules:
  0.0 262.7 jit_solution(15506277945841817645)
XLA Ops:
  0.0 3.0 %collective-permute-start.8 = (bf16[64,8192]{1,0:T(8,128)(2,1)}, bf16[64,8192]{1,0:T(8,128)(2,1)S(1)}, u32[]{:S(2)}, u32[]{:S(2)}) collective-permute-start(bf16[64,8192]{1,0:T(8,128)(2,1)} %bitcast.15), channel_id=1, source_target_pairs={{2,0},{4,2},{6,4},{7,6},{5,7},{3,5},{1,3},{0,1},{10,8},{12,10},{14... | collective-permute-start | bytes 3145736 | tf_op jit(solution)/shard_map/ppermute | solution.py:394
  9.9 11.1 %project.2 = (bf16[160,1024]{1,0:T(8,128)(2,1)S(1)}, bf16[160,1024]{1,0:T(8,128)(2,1)S(1)}, bf16[160,1024]{1,0:T(8,128)(2,1)S(1)}, bf16[160,1024]{1,0:T(8,128)(2...) custom-call(s32[10]{0:T(128)S(1)} %get-tuple-element.161.places_ref,, ...), custom_call_target="tpu_custom_call" | custom-call | flops 4404019200 | bytes 18350080 | tf_op jit(solution)/shard_map/project/pallas_call | solution.py:131
  21.0 13.8 %collective-permute-done.3 = bf16[160,1024]{1,0:T(8,128)(2,1)S(1)} collective-permute-done((bf16[160,1024]{1,0:T(8,128)(2,1)S(1)}, bf16[160,1024]{1,0:T(8,128)(2,1)S(1)}, u32[]{:S(2)}, u32[]{:S(2)}) %collective-permute-start.3) | collective-permute-done | bytes 327712 | tf_op jit(solution)/shard_map/ppermute | solution.py:391
  37.1 6.0 %collective-permute-done.6 = bf16[160,1024]{1,0:T(8,128)(2,1)S(1)} collective-permute-done((bf16[160,1024]{1,0:T(8,128)(2,1)S(1)}, bf16[160,1024]{1,0:T(8,128)(2,1)S(1)}, u32[]{:S(2)}, u32[]{:S(2)}) %collective-permute-start.6) | collective-permute-done | bytes 327712 | tf_op jit(solution)/shard_map/ppermute | solution.py:394
  47.3 4.3 %collective-permute-done.4 = bf16[160,1024]{1,0:T(8,128)(2,1)S(1)} collective-permute-done((bf16[160,1024]{1,0:T(8,128)(2,1)S(1)}, bf16[160,1024]{1,0:T(8,128)(2,1)S(1)}, u32[]{:S(2)}, u32[]{:S(2)}) %collective-permute-start.4) | collective-permute-done | bytes 327712 | tf_op jit(solution)/shard_map/ppermute | solution.py:391
  53.9 5.9 %collective-permute-done.11 = bf16[160,1024]{1,0:T(8,128)(2,1)S(1)} collective-permute-done((bf16[160,1024]{1,0:T(8,128)(2,1)S(1)}, bf16[160,1024]{1,0:T(8,128)(2,1)S(1)}, u32[]{:S(2)}, u32[]{:S(2)}) %collective-permute-start.11) | collective-permute-done | bytes 327712 | tf_op jit(solution)/shard_map/ppermute | solution.py:394
  62.8 7.1 %collective-permute-done.9 = bf16[160,1024]{1,0:T(8,128)(2,1)S(1)} collective-permute-done((bf16[160,1024]{1,0:T(8,128)(2,1)S(1)}, bf16[160,1024]{1,0:T(8,128)(2,1)S(1)}, u32[]{:S(2)}, u32[]{:S(2)}) %collective-permute-start.9) | collective-permute-done | bytes 327712 | tf_op jit(solution)/shard_map/ppermute | solution.py:391
  73.7 3.1 %collective-permute-done.15.refs_4_ = bf16[160,1024]{1,0:T(8,128)(2,1)S(1)} collective-permute-done((bf16[160,1024]{1,0:T(8,128)(2,1)S(1)}, bf16[160,1024]{1,0:T(8,128)(2,1)S(1)}, u32[]{:S(2)}, u32[]{:S(2)}) %collective-permute-start.15) | collective-permute-done | bytes 327712 | tf_op jit(solution)/shard_map/ppermute | solution.py:391
  76.9 3.4 %collective-permute-done.14.refs_2_ = bf16[160,1024]{1,0:T(8,128)(2,1)S(1)} collective-permute-done((bf16[160,1024]{1,0:T(8,128)(2,1)S(1)}, bf16[160,1024]{1,0:T(8,128)(2,1)S(1)}, u32[]{:S(2)}, u32[]{:S(2)}) %collective-permute-start.14) | collective-permute-done | bytes 327712 | tf_op jit(solution)/shard_map/ppermute | solution.py:394
  80.2 3.6 %collective-permute-done.13.refs_1_ = bf16[160,1024]{1,0:T(8,128)(2,1)S(1)} collective-permute-done((bf16[160,1024]{1,0:T(8,128)(2,1)S(1)}, bf16[160,1024]{1,0:T(8,128)(2,1)S(1)}, u32[]{:S(2)}, u32[]{:S(2)}) %collective-permute-start.13) | collective-permute-done | bytes 327712 | tf_op jit(solution)/shard_map/ppermute | solution.py:391
  83.9 3.4 %collective-permute-done.17.refs_5_ = bf16[160,1024]{1,0:T(8,128)(2,1)S(1)} collective-permute-done((bf16[160,1024]{1,0:T(8,128)(2,1)S(1)}, bf16[160,1024]{1,0:T(8,128)(2,1)S(1)}, u32[]{:S(2)}, u32[]{:S(2)}) %collective-permute-start.17) | collective-permute-done | bytes 327712 | tf_op jit(solution)/shard_map/ppermute | solution.py:394
  94.1 10.3 %collective-permute-done.20.refs_2_ = bf16[320,1024]{1,0:T(8,128)(2,1)S(1)} collective-permute-done((bf16[320,1024]{1,0:T(8,128)(2,1)S(1)}, bf16[320,1024]{1,0:T(8,128)(2,1)S(1)}, u32[]{:S(2)}, u32[]{:S(2)}) %collective-permute-start.20) | collective-permute-done | bytes 655392 | tf_op jit(solution)/shard_map/ppermute | solution.py:486
  106.4 4.4 %key_values.1 = (bf16[256,256]{1,0:T(8,128)(2,1)S(1)}, bf16[256,256]{1,0:T(8,128)(2,1)S(1)}, bf16[256,256]{1,0:T(8,128)(2,1)S(1)}, bf16[256,256]{1,0:T(8,128)(2,...) custom-call(s32[18]{0:T(128)S(1)} %pad_add_fusion.meta_ref, ...), custom_call_target="tpu_custom_call" | custom-call | flops 1 | bytes 1 | tf_op jit(solution)/shard_map/key_values/pallas_call | solution.py:195
  116.9 22.4 %collective-permute-done.27 = bf16[256,256]{1,0:T(8,128)(2,1)S(1)} collective-permute-done((bf16[256,256]{1,0:T(8,128)(2,1)S(1)}, bf16[256,256]{1,0:T(8,128)(2,1)S(1)}, u32[]{:S(2)}, u32[]{:S(2)}) %collective-permute-start.27) | collective-permute-done | bytes 131104 | tf_op jit(solution)/shard_map/ppermute | solution.py:391
  141.5 3.4 %collective-permute-done.28 = bf16[256,256]{1,0:T(8,128)(2,1)S(1)} collective-permute-done((bf16[256,256]{1,0:T(8,128)(2,1)S(1)}, bf16[256,256]{1,0:T(8,128)(2,1)S(1)}, u32[]{:S(2)}, u32[]{:S(2)}) %collective-permute-start.28) | collective-permute-done | bytes 131104 | tf_op jit(solution)/shard_map/ppermute | solution.py:391
  158.9 3.6 %collective-permute-done.32 = bf16[256,256]{1,0:T(8,128)(2,1)S(1)} collective-permute-done((bf16[256,256]{1,0:T(8,128)(2,1)S(1)}, bf16[256,256]{1,0:T(8,128)(2,1)S(1)}, u32[]{:S(2)}, u32[]{:S(2)}) %collective-permute-start.32) | collective-permute-done | bytes 131104 | tf_op jit(solution)/shard_map/ppermute | solution.py:391
  168.3 7.9 %attend.2 = (bf16[32,8192]{1,0:T(8,128)(2,1)}, bf16[32,8192]{1,0:T(8,128)(2,1)}, bf16[64,8192]{1,0:T(8,128)(2,1)}) custom-call(s32[18]{0:T(128)} %copy-done.4, bf16[128,512]{1,0:T(8,128)(2,1)} %copy-done.3, bf16[256,256]{1,0:T(8,128)(2,1)} %copy-done.5, bf16[256,256]{1,0:T(8,128)(2,1)} %copy-done.6, bf16[512,8192]{1,0:T(8,128)(2,1)} %bitcast.19), custom_call_target="tpu_custom_call" | custom-call | flops 1 | bytes 1 | tf_op jit(solution)/shard_map/attend/pallas_call | solution.py:322
  178.3 10.2 %attend.3 = (bf16[32,8192]{1,0:T(8,128)(2,1)}, bf16[32,8192]{1,0:T(8,128)(2,1)}, bf16[32,8192]{1,0:T(8,128)(2,1)}, bf16[32,8192]{1,0:T(8,128)(2,1)}, bf16[32,819...) custom-call(s32[18]{0:T(128)} %copy-done.4, ...), custom_call_target="tpu_custom_call" | custom-call | flops 1 | bytes 1 | tf_op jit(solution)/shard_map/attend/pallas_call | solution.py:322
  195.2 8.4 %collective-permute-done.39 = bf16[32,8192]{1,0:T(8,128)(2,1)S(1)} collective-permute-done((bf16[32,8192]{1,0:T(8,128)(2,1)}, bf16[32,8192]{1,0:T(8,128)(2,1)S(1)}, u32[]{:S(2)}, u32[]{:S(2)}) %collective-permute-start.39) | collective-permute-done | bytes 524320 | tf_op jit(solution)/shard_map/ppermute | solution.py:394
  208.0 6.2 %collective-permute-done.37 = bf16[32,8192]{1,0:T(8,128)(2,1)S(1)} collective-permute-done((bf16[32,8192]{1,0:T(8,128)(2,1)S(1)}, bf16[32,8192]{1,0:T(8,128)(2,1)S(1)}, u32[]{:S(2)}, u32[]{:S(2)}) %collective-permute-start.37) | collective-permute-done | bytes 524320 | tf_op jit(solution)/shard_map/ppermute | solution.py:391
  218.7 7.3 %collective-permute-done.43 = bf16[32,8192]{1,0:T(8,128)(2,1)S(1)} collective-permute-done((bf16[32,8192]{1,0:T(8,128)(2,1)S(1)}, bf16[32,8192]{1,0:T(8,128)(2,1)S(1)}, u32[]{:S(2)}, u32[]{:S(2)}) %collective-permute-start.43) | collective-permute-done | bytes 524320 | tf_op jit(solution)/shard_map/ppermute | solution.py:394
  230.1 12.3 %collective-permute-done.41 = bf16[32,8192]{1,0:T(8,128)(2,1)S(1)} collective-permute-done((bf16[32,8192]{1,0:T(8,128)(2,1)S(1)}, bf16[32,8192]{1,0:T(8,128)(2,1)S(1)}, u32[]{:S(2)}, u32[]{:S(2)}) %collective-permute-start.41) | collective-permute-done | bytes 524320 | tf_op jit(solution)/shard_map/ppermute | solution.py:391
  245.8 4.0 %collective-permute-done.46.refs_1_ = bf16[32,8192]{1,0:T(8,128)(2,1)S(1)} collective-permute-done((bf16[32,8192]{1,0:T(8,128)(2,1)S(1)}, bf16[32,8192]{1,0:T(8,128)(2,1)S(1)}, u32[]{:S(2)}, u32[]{:S(2)}) %collective-permute-start.46) | collective-permute-done | bytes 524320 | tf_op jit(solution)/shard_map/ppermute | solution.py:407
  249.8 9.5 %collective-permute-done.49.refs_3_ = bf16[32,8192]{1,0:T(8,128)(2,1)S(1)} collective-permute-done((bf16[32,8192]{1,0:T(8,128)(2,1)S(1)}, bf16[32,8192]{1,0:T(8,128)(2,1)S(1)}, u32[]{:S(2)}, u32[]{:S(2)}) %collective-permute-start.49) | collective-permute-done | bytes 524320 | tf_op jit(solution)/shard_map/ppermute | solution.py:407
  (155 shorter events, 87.6 us)
Async XLA Ops:
  0.0 59.7 %collective-permute-start.8 = (bf16[64,8192]{1,0:T(8,128)(2,1)}, bf16[64,8192]{1,0:T(8,128)(2,1)S(1)}, u32[]{:S(2)}, u32[]{:S(2)}) collective-permute-start(bf16[64,8192]{1,0:T(8,128)(2,1)} %bitcast.15), channel_id=1, source_target_pairs={{2,0},{4,2},{6,4},{7,6},{5,7},{3,5},{1,3},{0,1},{10,8},{12,10},{14... | collective-permute-start | bytes 3145736 | tf_op jit(solution)/shard_map/ppermute | solution.py:394
  3.0 56.8 %collective-permute-start.2 = (bf16[64,8192]{1,0:T(8,128)(2,1)}, bf16[64,8192]{1,0:T(8,128)(2,1)S(1)}, u32[]{:S(2)}, u32[]{:S(2)}) collective-permute-start(bf16[64,8192]{1,0:T(8,128)(2,1)} %bitcast.16), channel_id=1, source_target_pairs={{0,2},{2,4},{4,6},{6,7},{7,5},{5,3},{3,1},{1,0},{8,10},{10,12},{12... | collective-permute-start | bytes 3145736 | tf_op jit(solution)/shard_map/ppermute | solution.py:391
  3.0 68.6 %collective-permute-start.1 = (bf16[64,8192]{1,0:T(8,128)(2,1)}, bf16[64,8192]{1,0:T(8,128)(2,1)S(1)}, u32[]{:S(2)}, u32[]{:S(2)}) collective-permute-start(bf16[64,8192]{1,0:T(8,128)(2,1)} %bitcast.17), channel_id=1, source_target_pairs={{0,8},{8,16},{16,24},{24,0},{1,9},{9,17},{17,25},{25,1},{2,10},{10... | collective-permute-start | bytes 3145736 | tf_op jit(solution)/shard_map/ppermute | solution.py:410
  7.7 27.1 %collective-permute-start.3 = (bf16[160,1024]{1,0:T(8,128)(2,1)S(1)}, bf16[160,1024]{1,0:T(8,128)(2,1)S(1)}, u32[]{:S(2)}, u32[]{:S(2)}) collective-permute-start(bf16[160,1024]{1,0:T(8,128)(2,1)S(1)} %get-tuple-element.83), channel_id=1, source_target_pairs={{0,2},{2,4},{4,6},{6,7},{7,5},{5,3},{3,1},{1,0},{8,10},{10,12},{12... | collective-permute-start | bytes 983048 | tf_op jit(solution)/shard_map/ppermute | solution.py:391
  9.8 26.7 %collective-permute-start.7 = (bf16[160,1024]{1,0:T(8,128)(2,1)S(1)}, bf16[160,1024]{1,0:T(8,128)(2,1)S(1)}, u32[]{:S(2)}, u32[]{:S(2)}) collective-permute-start(bf16[160,1024]{1,0:T(8,128)(2,1)S(1)} %get-tuple-element.87), channel_id=1, source_target_pairs={{2,0},{4,2},{6,4},{7,6},{5,7},{3,5},{1,3},{0,1},{10,8},{12,10},{14... | collective-permute-start | bytes 983048 | tf_op jit(solution)/shard_map/ppermute | solution.py:394
  87.5 16.8 %collective-permute-start.20 = (bf16[320,1024]{1,0:T(8,128)(2,1)S(1)}, bf16[320,1024]{1,0:T(8,128)(2,1)S(1)}, u32[]{:S(2)}, u32[]{:S(2)}) collective-permute-start(bf16[320,1024]{1,0:T(8,128)(2,1)S(1)} %total_of.1.refs_0_), channel_id=1, source_target_pairs={{0,16},{8,24},{16,0},{24,8},{1,17},{9,25},{17,1},{25,9},{2,18},{10... | collective-permute-start | bytes 1966088 | tf_op jit(solution)/shard_map/ppermute | solution.py:486
  88.2 24.6 %collective-permute-start.18 = (bf16[64,8192]{1,0:T(8,128)(2,1)S(1)}, bf16[64,8192]{1,0:T(8,128)(2,1)S(1)}, u32[]{:S(2)}, u32[]{:S(2)}) collective-permute-start(bf16[64,8192]{1,0:T(8,128)(2,1)S(1)} %collective-permute-done.2.refs_0_), channel_id=1, source_target_pairs={{0,2},{2,4},{4,6},{6,7},{7,5},{5,3},{3,1},{1,0},{8,10},{10,12},{12... | collective-permute-start | bytes 3145736 | tf_op jit(solution)/shard_map/ppermute | solution.py:391
  88.4 24.7 %collective-permute-start.24 = (bf16[64,8192]{1,0:T(8,128)(2,1)S(1)}, bf16[64,8192]{1,0:T(8,128)(2,1)S(1)}, u32[]{:S(2)}, u32[]{:S(2)}) collective-permute-start(bf16[64,8192]{1,0:T(8,128)(2,1)S(1)} %collective-permute-done.8.refs_1_), channel_id=1, source_target_pairs={{2,0},{4,2},{6,4},{7,6},{5,7},{3,5},{1,3},{0,1},{10,8},{12,10},{14... | collective-permute-start | bytes 3145736 | tf_op jit(solution)/shard_map/ppermute | solution.py:394
  112.8 32.1 %collective-permute-start.22 = (bf16[64,8192]{1,0:T(8,128)(2,1)S(1)}, bf16[64,8192]{1,0:T(8,128)(2,1)S(1)}, u32[]{:S(2)}, u32[]{:S(2)}) collective-permute-start(bf16[64,8192]{1,0:T(8,128)(2,1)S(1)} %collective-permute-done.18.refs_0_), channel_id=1, source_target_pairs={{0,2},{2,4},{4,6},{6,7},{7,5},{5,3},{3,1},{1,0},{8,10},{10,12},{12... | collective-permute-start | bytes 3145736 | tf_op jit(solution)/shard_map/ppermute | solution.py:391
  113.1 31.8 %collective-permute-start.25 = (bf16[64,8192]{1,0:T(8,128)(2,1)S(1)}, bf16[64,8192]{1,0:T(8,128)(2,1)S(1)}, u32[]{:S(2)}, u32[]{:S(2)}) collective-permute-start(bf16[64,8192]{1,0:T(8,128)(2,1)S(1)} %collective-permute-done.24.refs_1_), channel_id=1, source_target_pairs={{2,0},{4,2},{6,4},{7,6},{5,7},{3,5},{1,3},{0,1},{10,8},{12,10},{14... | collective-permute-start | bytes 3145736 | tf_op jit(solution)/shard_map/ppermute | solution.py:394
  114.8 24.4 %collective-permute-start.27 = (bf16[256,256]{1,0:T(8,128)(2,1)S(1)}, bf16[256,256]{1,0:T(8,128)(2,1)S(1)}, u32[]{:S(2)}, u32[]{:S(2)}) collective-permute-start(bf16[256,256]{1,0:T(8,128)(2,1)S(1)} %get-tuple-element.115), channel_id=1, source_target_pairs={{0,2},{2,4},{4,6},{6,7},{7,5},{5,3},{3,1},{1,0},{8,10},{10,12},{12... | collective-permute-start | bytes 393224 | tf_op jit(solution)/shard_map/ppermute | solution.py:391
  115.1 24.7 %collective-permute-start.29 = (bf16[256,256]{1,0:T(8,128)(2,1)S(1)}, bf16[256,256]{1,0:T(8,128)(2,1)S(1)}, u32[]{:S(2)}, u32[]{:S(2)}) collective-permute-start(bf16[256,256]{1,0:T(8,128)(2,1)S(1)} %get-tuple-element.121), channel_id=1, source_target_pairs={{2,0},{4,2},{6,4},{7,6},{5,7},{3,5},{1,3},{0,1},{10,8},{12,10},{14... | collective-permute-start | bytes 393224 | tf_op jit(solution)/shard_map/ppermute | solution.py:394
  145.8 16.8 %collective-permute-start.23 = (bf16[32,8192]{1,0:T(8,128)(2,1)S(1)}, bf16[32,8192]{1,0:T(8,128)(2,1)S(1)}, u32[]{:S(2)}, u32[]{:S(2)}) collective-permute-start(bf16[32,8192]{1,0:T(8,128)(2,1)S(1)} %slice.13), channel_id=1, source_target_pairs={{0,2},{2,4},{4,6},{6,7},{7,5},{5,3},{3,1},{1,0},{8,10},{10,12},{12... | collective-permute-start | bytes 1572872 | tf_op jit(solution)/shard_map/ppermute | solution.py:391
  176.6 15.6 %collective-permute-start.40 = (bf16[32,8192]{1,0:T(8,128)(2,1)}, bf16[32,8192]{1,0:T(8,128)(2,1)S(1)}, u32[]{:S(2)}, u32[]{:S(2)}) collective-permute-start(bf16[32,8192]{1,0:T(8,128)(2,1)} %get-tuple-element.140), channel_id=1, source_target_pairs={{2,0},{4,2},{6,4},{7,6},{5,7},{3,5},{1,3},{0,1},{10,8},{12,10},{14... | collective-permute-start | bytes 1572872 | tf_op jit(solution)/shard_map/ppermute | solution.py:394
  188.6 18.0 %collective-permute-start.38 = (bf16[32,8192]{1,0:T(8,128)(2,1)}, bf16[32,8192]{1,0:T(8,128)(2,1)S(1)}, u32[]{:S(2)}, u32[]{:S(2)}) collective-permute-start(bf16[32,8192]{1,0:T(8,128)(2,1)} %get-tuple-element.138), channel_id=1, source_target_pairs={{0,2},{2,4},{4,6},{6,7},{7,5},{5,3},{3,1},{1,0},{8,10},{10,12},{12... | collective-permute-start | bytes 1572872 | tf_op jit(solution)/shard_map/ppermute | solution.py:391
  191.9 22.4 %collective-permute-start.37 = (bf16[32,8192]{1,0:T(8,128)(2,1)S(1)}, bf16[32,8192]{1,0:T(8,128)(2,1)S(1)}, u32[]{:S(2)}, u32[]{:S(2)}) collective-permute-start(bf16[32,8192]{1,0:T(8,128)(2,1)S(1)} %add_convert_fusion.9), channel_id=1, source_target_pairs={{0,2},{2,4},{4,6},{6,7},{7,5},{5,3},{3,1},{1,0},{8,10},{10,12},{12... | collective-permute-start | bytes 1572872 | tf_op jit(solution)/shard_map/ppermute | solution.py:391
  193.4 22.4 %collective-permute-start.44 = (bf16[32,8192]{1,0:T(8,128)(2,1)S(1)}, bf16[32,8192]{1,0:T(8,128)(2,1)S(1)}, u32[]{:S(2)}, u32[]{:S(2)}) collective-permute-start(bf16[32,8192]{1,0:T(8,128)(2,1)S(1)} %add_convert_fusion.8), channel_id=1, source_target_pairs={{2,0},{4,2},{6,4},{7,6},{5,7},{3,5},{1,3},{0,1},{10,8},{12,10},{14... | collective-permute-start | bytes 1572872 | tf_op jit(solution)/shard_map/ppermute | solution.py:394
  204.7 21.3 %collective-permute-start.43 = (bf16[32,8192]{1,0:T(8,128)(2,1)S(1)}, bf16[32,8192]{1,0:T(8,128)(2,1)S(1)}, u32[]{:S(2)}, u32[]{:S(2)}) collective-permute-start(bf16[32,8192]{1,0:T(8,128)(2,1)S(1)} %add_convert_fusion.7), channel_id=1, source_target_pairs={{2,0},{4,2},{6,4},{7,6},{5,7},{3,5},{1,3},{0,1},{10,8},{12,10},{14... | collective-permute-start | bytes 1572872 | tf_op jit(solution)/shard_map/ppermute | solution.py:394
  207.8 20.6 %collective-permute-start.42 = (bf16[32,8192]{1,0:T(8,128)(2,1)S(1)}, bf16[32,8192]{1,0:T(8,128)(2,1)S(1)}, u32[]{:S(2)}, u32[]{:S(2)}) collective-permute-start(bf16[32,8192]{1,0:T(8,128)(2,1)S(1)} %add_convert_fusion.6), channel_id=1, source_target_pairs={{0,2},{2,4},{4,6},{6,7},{7,5},{5,3},{3,1},{1,0},{8,10},{10,12},{12... | collective-permute-start | bytes 1572872 | tf_op jit(solution)/shard_map/ppermute | solution.py:391
  215.4 26.9 %collective-permute-start.41 = (bf16[32,8192]{1,0:T(8,128)(2,1)S(1)}, bf16[32,8192]{1,0:T(8,128)(2,1)S(1)}, u32[]{:S(2)}, u32[]{:S(2)}) collective-permute-start(bf16[32,8192]{1,0:T(8,128)(2,1)S(1)} %add_convert_fusion.5), channel_id=1, source_target_pairs={{0,2},{2,4},{4,6},{6,7},{7,5},{5,3},{3,1},{1,0},{8,10},{10,12},{12... | collective-permute-start | bytes 1572872 | tf_op jit(solution)/shard_map/ppermute | solution.py:391
  216.9 25.5 %collective-permute-start.48 = (bf16[32,8192]{1,0:T(8,128)(2,1)S(1)}, bf16[32,8192]{1,0:T(8,128)(2,1)S(1)}, u32[]{:S(2)}, u32[]{:S(2)}) collective-permute-start(bf16[32,8192]{1,0:T(8,128)(2,1)S(1)} %add_convert_fusion.4), channel_id=1, source_target_pairs={{2,0},{4,2},{6,4},{7,6},{5,7},{3,5},{1,3},{0,1},{10,8},{12,10},{14... | collective-permute-start | bytes 1572872 | tf_op jit(solution)/shard_map/ppermute | solution.py:394
  226.2 23.6 %collective-permute-start.46 = (bf16[32,8192]{1,0:T(8,128)(2,1)S(1)}, bf16[32,8192]{1,0:T(8,128)(2,1)S(1)}, u32[]{:S(2)}, u32[]{:S(2)}) collective-permute-start(bf16[32,8192]{1,0:T(8,128)(2,1)S(1)} %add_convert_fusion.3), channel_id=1, source_target_pairs={{2,8},{4,10},{6,12},{7,14},{5,15},{3,13},{1,11},{0,9},{10,16},{12,... | collective-permute-start | bytes 1572872 | tf_op jit(solution)/shard_map/ppermute | solution.py:407
  228.4 17.3 %collective-permute-start.47 = (bf16[32,8192]{1,0:T(8,128)(2,1)S(1)}, bf16[32,8192]{1,0:T(8,128)(2,1)S(1)}, u32[]{:S(2)}, u32[]{:S(2)}) collective-permute-start(bf16[32,8192]{1,0:T(8,128)(2,1)S(1)} %add_convert_fusion.2), channel_id=1, source_target_pairs={{0,10},{2,12},{4,14},{6,15},{7,13},{5,11},{3,9},{1,8},{8,18},{10,2... | collective-permute-start | bytes 1572872 | tf_op jit(solution)/shard_map/ppermute | solution.py:404
  242.6 16.7 %collective-permute-start.49 = (bf16[32,8192]{1,0:T(8,128)(2,1)S(1)}, bf16[32,8192]{1,0:T(8,128)(2,1)S(1)}, u32[]{:S(2)}, u32[]{:S(2)}) collective-permute-start(bf16[32,8192]{1,0:T(8,128)(2,1)S(1)} %add_convert_fusion), channel_id=1, source_target_pairs={{2,8},{4,10},{6,12},{7,14},{5,15},{3,13},{1,11},{0,9},{10,16},{12,... | collective-permute-start | bytes 1572872 | tf_op jit(solution)/shard_map/ppermute | solution.py:407
  (41 other events, 864.5 us)

commit v6 on v5

--- a/solution.py
+++ b/solution.py
@@ -19,9 +19,8 @@
 SLOTS = SAMP_SECTION * BLOCK
 F32 = jnp.float32
 BF16 = jnp.bfloat16
-VMEM_LIMIT = 40 * 1024 * 1024
+VMEM_LIMIT = 24 * 1024 * 1024
 QUICK = pl.CostEstimate(flops=1, bytes_accessed=1, transcendentals=0)
-VMEM_MOST = 56 * 1024 * 1024
 VMEM_SMALL = 16 * 1024 * 1024
 
 
@@ -85,31 +84,16 @@
 
 def finish(gate, text, own, arrivals):
     rows, columns = text.shape
-    parts = len(arrivals)
-    part_rows = rows // parts
-    flat = [value for came in arrivals for value in came]
-    count = len(flat) // parts
-
-    def kernel(gate_ref, text_ref, own_ref, *refs):
-        factor = jnp.tanh(gate_ref[...])
-        for part in range(parts):
-            place = slice(part * part_rows, (part + 1) * part_rows)
-            branch = own_ref[place, :].astype(F32)
-            for ref in refs[part * count : (part + 1) * count]:
-                branch += ref[...].astype(F32)
-            refs[-1][0, place, :] = (text_ref[place, :].astype(F32) + factor * branch).astype(
-                BF16
-            )
-
-    return pl.pallas_call(
-        kernel,
-        in_specs=[pl.BlockSpec(memory_space=pltpu.VMEM)] * (3 + len(flat)),
-        out_specs=pl.BlockSpec(memory_space=pltpu.VMEM),
-        out_shape=jax.ShapeDtypeStruct((1, rows, columns), BF16),
-        compiler_params=params(VMEM_SMALL),
-        cost_estimate=QUICK,
-        name="finish",
-    )(gate.reshape(1, 1), text, own, *flat)
+    part_rows = rows // len(arrivals)
+    result = jnp.zeros((1, rows, columns), BF16)
+    for part, came in enumerate(arrivals):
+        place = slice(part * part_rows, (part + 1) * part_rows)
+        branch = own[place].astype(F32)
+        for value in came:
+            branch = branch + value.astype(F32)
+        part_out = (text[place].astype(F32) + jnp.tanh(gate[0]) * branch).astype(BF16)
+        result = lax.dynamic_update_slice(result, part_out[None], (0, part * part_rows, 0))
+    return result
 
 
 def project(places, feats, weight, order_len, first, blocks):
@@ -140,7 +124,7 @@
             out_specs=[pl.BlockSpec((half, wide), lambda i, places: (0, 0))] * (2 * blocks),
         ),
         out_shape=[jax.ShapeDtypeStruct((half, wide), BF16)] * (2 * blocks),
-        compiler_params=params(),
+        compiler_params=params(56 * 1024 * 1024),
         cost_estimate=pl.CostEstimate(
             flops=2 * rows * depth * wide * blocks,
             bytes_accessed=2 * (depth + rows) * wide * blocks,
@@ -256,6 +240,7 @@
     kv_rows = SLOTS // sharing
     columns = weight.shape[1]
     wide = min(1024, columns)
+    tall = min(64, width)
 
     def kernel(meta_ref, query_ref, *refs):
         kv_refs, weight_ref = refs[:sharing], refs[sharing]
@@ -264,16 +249,14 @@
         step = pl.program_id(0)
 
         def fetch(index):
-            start = index * wide
+            place = pl.ds(index * tall, tall)
             return pltpu.make_async_copy(
-                weight_ref.at[:, pl.ds(pl.multiple_of(start, wide), wide)],
-                held_ref.at[index],
-                sems.at[index],
+                weight_ref.at[place, :], held_ref.at[place, :], sems.at[index]
             )
 
         @pl.when(step == 0)
         def _():
-            for index in range(columns // wide):
+            for index in range(width // tall):
                 fetch(index).start()
             mine = lax.rem(meta_ref[order_len], sharing)
             for piece in range(sharing):
@@ -309,10 +292,13 @@
                     attended_ref[first : first + text_rows, h * HD : (h + 1) * HD] = result[
                         h * text_rows : (h + 1) * text_rows
                     ]
-
-        fetch(step).wait()
+            for index in range(width // tall):
+                fetch(index).wait()
+
         product = jnp.dot(
-            attended_ref[...], held_ref[step], preferred_element_type=F32
+            attended_ref[...],
+            held_ref[:, pl.ds(pl.multiple_of(step * wide, wide), wide)],
+            preferred_element_type=F32,
         ).astype(BF16)
         first = 0
         for out_ref, size in zip(out_refs, sizes):
@@ -332,13 +318,17 @@
                 pltpu.VMEM((SLOTS, HD), BF16),
                 pltpu.VMEM((SLOTS, HD), BF16),
                 pltpu.VMEM((rows, width), BF16),
-                pltpu.VMEM((columns // wide, width, wide), BF16),
-                pltpu.SemaphoreType.DMA((columns // wide,)),
+                pltpu.VMEM((width, columns), BF16),
+                pltpu.SemaphoreType.DMA((width // tall,)),
             ],
         ),
         out_shape=[jax.ShapeDtypeStruct((size, columns), BF16) for size in sizes],
-        compiler_params=params(VMEM_MOST),
-        cost_estimate=QUICK,
+        compiler_params=params(),
+        cost_estimate=pl.CostEstimate(
+            flops=8 * rows * width * columns,
+            bytes_accessed=8 * width * columns,
+            transcendentals=rows * heads * BLOCK,
+        ),
         name="attend",
     )(meta, queries, *kv_pieces, weight)
 
@@ -457,10 +447,8 @@
     ]
 
     def image_hold(hop, value):
-        if hop == min(2, far - 1):
-            return after(value, from_below[1], from_above[1])
-        if hop == far - 1:
-            return after(value, text_next, gate_next)
+        if hop == 1:
+            return after(value, from_below[1], from_above[1], text_next)
         return value
 
     turns = [0, 3, 1, 2]
@@ -495,15 +483,12 @@
 
     for distance in range(3, far):
         text_round(*([kv_part[0]] if distance == 3 else []))
-    far_chunks = [up(from_below[-1][:cut])]
-    if parts == 2:
-        far_chunks.append(down(from_above[-1][cut:]))
     for distance in range(2, far):
         near += [-distance, distance]
         near_queries.append(query([from_below[distance], from_above[distance]], weight_query))
 
     def kv_hold(hop, value):
-        if hop == min(2, far - 1):
+        if hop == far - 1:
             return after(value, *from_below[3:], *from_above[3:])
         return value
 
@@ -511,8 +496,7 @@
     kv_own = (
         kv_part[index_of[0]].astype(F32) + came[0].astype(F32) + came[1].astype(F32)
     ).astype(BF16)
-    near_queries = jnp.concatenate(near_queries, axis=0)
-    kv_own = after(kv_own, *far_chunks, near_queries)
+    kv_own = after(kv_own, gate_next, *near_queries)
     kv_pieces = [kv_own]
     for step in range(1, sharing):
         pairs = [
@@ -520,26 +504,40 @@
         ]
         kv_pieces.append(lax.ppermute(kv_own, "mp", pairs))
 
-    far_queries = query(far_chunks + [text_own], weight_query)
-    *far_part, own_part = attend(
-        meta,
-        far_queries,
-        kv_pieces,
-        weight_out,
-        [index_of[far], index_of[0]],
-        [cut] * parts + [text_rows],
-        mp_count,
-    )
-    near_part = attend(
-        meta,
-        after(near_queries, own_part),
-        kv_pieces,
-        weight_out,
-        [index_of[offset] for offset in near],
-        [cut] * (parts * len(near)),
-        mp_count,
-    )
-    out_parts = {offset: near_part[parts * i :][:parts] for i, offset in enumerate(near)}
+    far_chunks = [up(after(from_below[-1], kv_own)[:cut])]
+    if parts == 2:
+        far_chunks.append(down(after(from_above[-1], kv_own)[cut:]))
+
+    def attend_to(offsets, queries, sizes):
+        return attend(
+            meta,
+            queries,
+            kv_pieces,
+            weight_out,
+            [index_of[offset] for offset in offsets],
+            sizes,
+            mp_count,
+        )
+
+    first, first_queries = near[-2:] + [0], [near_queries[-1], query([text_own], weight_query)]
+    rest, rest_queries = near[:-2], near_queries[:-1]
+    *first_part, own_part = attend_to(
+        first,
+        jnp.concatenate(first_queries, axis=0),
+        [cut] * (parts * (len(first) - 1)) + [text_rows],
+    )
+    far_part = attend_to(
+        [far], after(query(far_chunks, weight_query), own_part), [cut] * parts
+    )
+    rest_part = attend_to(
+        rest,
+        after(jnp.concatenate(rest_queries, axis=0), far_part[0]),
+        [cut] * (parts * len(rest)),
+    )
+    near_part = list(first_part) + list(rest_part)
+    out_parts = {
+        offset: near_part[parts * i :][:parts] for i, offset in enumerate(first[:-1] + rest)
+    }
     out_parts[far] = out_parts[-far] = far_part
 
     own_next = to_next(own_part)
@@ -554,7 +552,7 @@
         )
     ]
 
-    turns = [0, 3, 1, 2] if parts == 2 else [0, 1]
+    turns = [1, 2, 0, 3] if parts == 2 else [0, 1]
     came = ring_sums([branch_chains[turn] for turn in turns], turn=own_next)
     came = [came[turns.index(index)] for index in range(2 * parts)]
     return finish(

time: 263 us -> 250 us (0.951)
  waiting for transfers between devices: 148 us -> 135 us
  other arithmetic: 10.6 us -> 7.19 us
  starting transfers between devices: 48.8 us -> 52.1 us
    ppermute x1, waiting for transfers between devices: 10.3 us -> 3.74 us  [local(): lax.ppermute(moving, 'section', [(s, (s + 2) % section_count) for s in ra...]
    ppermute x2, starting transfers between devices: 4.68 us -> 0.11 us  [down_across(): return lax.ppermute(value, ('section', 'mp'), across(down_pairs))]
    convert_element_type x25, other arithmetic: 8.6 us -> 4.31 us  [add(): return (one.astype(F32) + other.astype(F32)).astype(BF16)]
    ppermute x20, starting transfers between devices: 11.2 us -> 14.9 us  [up(): return lax.ppermute(value, 'mp', up_pairs)]
    pallas_call x2, Pallas kernels: 14 us -> 17.1 us  [project(): pl.pallas_call(kernel, grid_spec=pltpu.PrefetchScalarGridSpec(num_scalar_...]
    pallas_call x4 -> x5, Pallas kernels: 11.1 us -> 14 us  [query(): pl.pallas_call(kernel, grid=(width // wide,), in_specs=[pl.BlockSpec(chun...]
    ppermute x19, starting transfers between devices: 30.1 us -> 27.3 us  [down(): return lax.ppermute(value, 'mp', down_pairs)]
    pallas_call x1 -> x0, Pallas kernels: 2.73 us -> none  [finish(): pl.pallas_call(kernel, in_specs=[pl.BlockSpec(memory_space=pltpu.VMEM)] *...]
  transfers between devices with their start and end apart: 50 -> 50, of which waited for: 27 -> 26; matrix products, arithmetic and copies ran while one was open for 5% -> 3% of each run, Pallas kernels for 15% -> 21%
where the time goes in v6:
time: 250 us; the launch traced here: 249 us
  waiting for transfers between devices  135 us (54%)
  starting transfers between devices  52.1 us (21%)
  Pallas kernels  51.9 us (21%)
  other arithmetic  7.19 us (3%)
    ppermute x20, waiting for transfers between devices, up(): return lax.ppermute(value, 'mp', up_pairs)  84.8 us
    ppermute x19, waiting for transfers between devices, down(): return lax.ppermute(value, 'mp', down_pairs)  32.9 us
    ppermute x19, starting transfers between devices, down(): return lax.ppermute(value, 'mp', down_pairs)  27.3 us
    pallas_call x2, Pallas kernels, project(): pl.pallas_call(kernel, grid_spec=pltpu.PrefetchScalarGridSpec(num_scalar_...  17.1 us
    pallas_call x3, Pallas kernels, attend(): pl.pallas_call(kernel, grid_spec=pltpu.PrefetchScalarGridSpec(num_scalar_...  16.1 us
    ppermute x20, starting transfers between devices, up(): return lax.ppermute(value, 'mp', up_pairs)  14.9 us
    pallas_call x5, Pallas kernels, query(): pl.pallas_call(kernel, grid=(width // wide,), in_specs=[pl.BlockSpec(chun...  14 us
    ppermute x2, waiting for transfers between devices, down_across(): return lax.ppermute(value, ('section', 'mp'), across(down_pairs))  12.1 us
  transfers between devices with their start and end apart: 50, of which 26 were waited for; matrix products, arithmetic and copies ran while one was open for 3% of the time, Pallas kernels for 21%

profile of v6, /device:TPU:0, one launch (start us, length us, event | category | flops | bytes accessed | tf_op | source)
XLA Modules:
  0.0 249.2 jit_solution(8294153026178727969)
XLA Ops:
  0.0 3.0 %collective-permute-start.4 = (bf16[64,8192]{1,0:T(8,128)(2,1)}, bf16[64,8192]{1,0:T(8,128)(2,1)S(1)}, u32[]{:S(2)}, u32[]{:S(2)}) collective-permute-start(bf16[64,8192]{1,0:T(8,128)(2,1)} %bitcast.23), channel_id=1, source_target_pairs={{2,0},{4,2},{6,4},{7,6},{5,7},{3,5},{1,3},{0,1},{10,8},{12,10},{14... | collective-permute-start | bytes 3145736 | tf_op jit(solution)/shard_map/ppermute | solution.py:384
  4.2 4.0 %project.3 = (bf16[160,1024]{1,0:T(8,128)(2,1)}, bf16[160,1024]{1,0:T(8,128)(2,1)}) custom-call(s32[10]{0:T(128)} %get-tuple-element.163.places_ref, bf16[320,960]{1,0:T(8,128)(2,1)} %feats_ref.3, bf16[960,8192]{1,0:T(8,128)(2,1)} %weight_ref.3), custom_call_target="tpu_custom_call" | custom-call | flops 629145600 | bytes 2621440 | tf_op jit(solution)/shard_map/project/pallas_call | solution.py:115
  10.3 13.1 %project.2 = (bf16[160,1024]{1,0:T(8,128)(2,1)}, bf16[160,1024]{1,0:T(8,128)(2,1)}, bf16[160,1024]{1,0:T(8,128)(2,1)}, bf16[160,1024]{1,0:T(8,128)(2,1)}, bf16[1...) custom-call(s32[10]{0:T(128)} %get-tuple-element.163.places_ref, ...), custom_call_target="tpu_custom_call" | custom-call | flops 4404019200 | bytes 18350080 | tf_op jit(solution)/shard_map/project/pallas_call | solution.py:115
  23.4 11.4 %collective-permute-done.3 = bf16[160,1024]{1,0:T(8,128)(2,1)S(1)} collective-permute-done((bf16[160,1024]{1,0:T(8,128)(2,1)}, bf16[160,1024]{1,0:T(8,128)(2,1)S(1)}, u32[]{:S(2)}, u32[]{:S(2)}) %collective-permute-start.3) | collective-permute-done | bytes 327712 | tf_op jit(solution)/shard_map/ppermute | solution.py:381
  39.1 4.2 %collective-permute-done.7 = bf16[160,1024]{1,0:T(8,128)(2,1)S(1)} collective-permute-done((bf16[160,1024]{1,0:T(8,128)(2,1)}, bf16[160,1024]{1,0:T(8,128)(2,1)S(1)}, u32[]{:S(2)}, u32[]{:S(2)}) %collective-permute-start.7) | collective-permute-done | bytes 327712 | tf_op jit(solution)/shard_map/ppermute | solution.py:384
  44.1 3.6 %collective-permute-done.6 = bf16[160,1024]{1,0:T(8,128)(2,1)S(1)} collective-permute-done((bf16[160,1024]{1,0:T(8,128)(2,1)}, bf16[160,1024]{1,0:T(8,128)(2,1)S(1)}, u32[]{:S(2)}, u32[]{:S(2)}) %collective-permute-start.6) | collective-permute-done | bytes 327712 | tf_op jit(solution)/shard_map/ppermute | solution.py:381
  51.5 3.2 %collective-permute-done.5 = bf16[160,1024]{1,0:T(8,128)(2,1)S(1)} collective-permute-done((bf16[160,1024]{1,0:T(8,128)(2,1)S(1)}, bf16[160,1024]{1,0:T(8,128)(2,1)S(1)}, u32[]{:S(2)}, u32[]{:S(2)}) %collective-permute-start.5) | collective-permute-done | bytes 327712 | tf_op jit(solution)/shard_map/ppermute | solution.py:381
  54.9 3.1 %collective-permute-done.12 = bf16[160,1024]{1,0:T(8,128)(2,1)S(1)} collective-permute-done((bf16[160,1024]{1,0:T(8,128)(2,1)S(1)}, bf16[160,1024]{1,0:T(8,128)(2,1)S(1)}, u32[]{:S(2)}, u32[]{:S(2)}) %collective-permute-start.12) | collective-permute-done | bytes 327712 | tf_op jit(solution)/shard_map/ppermute | solution.py:384
  60.1 4.9 %collective-permute-done.11 = bf16[160,1024]{1,0:T(8,128)(2,1)S(1)} collective-permute-done((bf16[160,1024]{1,0:T(8,128)(2,1)S(1)}, bf16[160,1024]{1,0:T(8,128)(2,1)S(1)}, u32[]{:S(2)}, u32[]{:S(2)}) %collective-permute-start.11) | collective-permute-done | bytes 327712 | tf_op jit(solution)/shard_map/ppermute | solution.py:384
  68.9 3.2 %collective-permute-done.16 = bf16[160,1024]{1,0:T(8,128)(2,1)S(1)} collective-permute-done((bf16[160,1024]{1,0:T(8,128)(2,1)S(1)}, bf16[160,1024]{1,0:T(8,128)(2,1)S(1)}, u32[]{:S(2)}, u32[]{:S(2)}) %collective-permute-start.16) | collective-permute-done | bytes 327712 | tf_op jit(solution)/shard_map/ppermute | solution.py:384
  74.3 3.1 %collective-permute-done.15.refs_4_ = bf16[160,1024]{1,0:T(8,128)(2,1)S(1)} collective-permute-done((bf16[160,1024]{1,0:T(8,128)(2,1)S(1)}, bf16[160,1024]{1,0:T(8,128)(2,1)S(1)}, u32[]{:S(2)}, u32[]{:S(2)}) %collective-permute-start.15) | collective-permute-done | bytes 327712 | tf_op jit(solution)/shard_map/ppermute | solution.py:381
  77.4 3.5 %collective-permute-done.17.refs_5_ = bf16[160,1024]{1,0:T(8,128)(2,1)S(1)} collective-permute-done((bf16[160,1024]{1,0:T(8,128)(2,1)S(1)}, bf16[160,1024]{1,0:T(8,128)(2,1)S(1)}, u32[]{:S(2)}, u32[]{:S(2)}) %collective-permute-start.17) | collective-permute-done | bytes 327712 | tf_op jit(solution)/shard_map/ppermute | solution.py:384
  90.0 3.7 %collective-permute-done.20.refs_2_ = bf16[320,1024]{1,0:T(8,128)(2,1)S(1)} collective-permute-done((bf16[320,1024]{1,0:T(8,128)(2,1)S(1)}, bf16[320,1024]{1,0:T(8,128)(2,1)S(1)}, u32[]{:S(2)}, u32[]{:S(2)}) %collective-permute-start.20) | collective-permute-done | bytes 655392 | tf_op jit(solution)/shard_map/ppermute | solution.py:474
  95.9 4.4 %key_values.1 = (bf16[256,256]{1,0:T(8,128)(2,1)S(1)}, bf16[256,256]{1,0:T(8,128)(2,1)S(1)}, bf16[256,256]{1,0:T(8,128)(2,1)S(1)}, bf16[256,256]{1,0:T(8,128)(2,...) custom-call(s32[18]{0:T(128)S(1)} %pad_add_fusion.meta_ref, ...), custom_call_target="tpu_custom_call" | custom-call | flops 1 | bytes 1 | tf_op jit(solution)/shard_map/key_values/pallas_call | solution.py:179
  109.7 22.1 %collective-permute-done.26 = bf16[256,256]{1,0:T(8,128)(2,1)S(1)} collective-permute-done((bf16[256,256]{1,0:T(8,128)(2,1)S(1)}, bf16[256,256]{1,0:T(8,128)(2,1)S(1)}, u32[]{:S(2)}, u32[]{:S(2)}) %collective-permute-start.26) | collective-permute-done | bytes 131104 | tf_op jit(solution)/shard_map/ppermute | solution.py:381
  150.7 5.5 %attend.3 = (bf16[32,8192]{1,0:T(8,128)(2,1)S(1)}, bf16[32,8192]{1,0:T(8,128)(2,1)S(1)}, bf16[32,8192]{1,0:T(8,128)(2,1)S(1)}, bf16[32,8192]{1,0:T(8,128)(2,1)S(1)}, bf16[64,8192]{1,0:T(8,128)(2,1)S(1)}) custom-call(s32[18]{0:T(128)S(1)} %pad_add_fusion.meta_ref, bf16[192,512]{1,0:T(8,128)(2,1)S(1)} %pad_maximum_fusion.2.query_ref, ...), custom_call_target="tpu_custom_call" | custom-call | flops 6442450944 | bytes 33554432 | tf_op jit(solution)/shard_map/attend/pallas_call | solution.py:308
  158.9 4.5 %collective-permute-done.34.refs_0_ = bf16[32,8192]{1,0:T(8,128)(2,1)S(1)} collective-permute-done((bf16[32,8192]{1,0:T(8,128)(2,1)S(1)}, bf16[32,8192]{1,0:T(8,128)(2,1)S(1)}, u32[]{:S(2)}, u32[]{:S(2)}) %collective-permute-start.34) | collective-permute-done | bytes 524320 | tf_op jit(solution)/shard_map/ppermute | solution.py:381
  168.0 4.3 %attend.4 = (bf16[32,8192]{1,0:T(8,128)(2,1)S(1)}, bf16[32,8192]{1,0:T(8,128)(2,1)S(1)}) custom-call(s32[18]{0:T(128)S(1)} %pad_add_fusion.meta_ref, bf16[64,512]{1,0:T(8,128)(2,1)S(1)} %query.9.query_ref, bf16[256,256]{1,0:T(8,128)(2,1)S(1)} %add_convert_fusion.22.refs_0_, bf16[256,256]{1,0:T(8,128)(2,1)S(1)} %collective-permute-done.32.refs_1_, ...), custom_call_target="tpu_custom_call" | custom-call | flops 2147483648 | bytes 33554432 | tf_op jit(solution)/shard_map/attend/pallas_call | solution.py:308
  174.5 6.2 %attend.5 = (bf16[32,8192]{1,0:T(8,128)(2,1)S(1)}, bf16[32,8192]{1,0:T(8,128)(2,1)S(1)}, bf16[32,8192]{1,0:T(8,128)(2,1)S(1)}, bf16[32,8192]{1,0:T(8,128)(2,1)S(...) custom-call(s32[18]{0:T(128)S(1)} %pad_add_fusion.meta_ref, ...), custom_call_target="tpu_custom_call" | custom-call | flops 8589934592 | bytes 33554432 | tf_op jit(solution)/shard_map/attend/pallas_call | solution.py:308
  183.1 4.1 %collective-permute-done.36 = bf16[32,8192]{1,0:T(8,128)(2,1)S(1)} collective-permute-done((bf16[32,8192]{1,0:T(8,128)(2,1)S(1)}, bf16[32,8192]{1,0:T(8,128)(2,1)S(1)}, u32[]{:S(2)}, u32[]{:S(2)}) %collective-permute-start.36) | collective-permute-done | bytes 524320 | tf_op jit(solution)/shard_map/ppermute | solution.py:381
  189.6 10.6 %collective-permute-done.41 = bf16[32,8192]{1,0:T(8,128)(2,1)S(1)} collective-permute-done((bf16[32,8192]{1,0:T(8,128)(2,1)S(1)}, bf16[32,8192]{1,0:T(8,128)(2,1)S(1)}, u32[]{:S(2)}, u32[]{:S(2)}) %collective-permute-start.41) | collective-permute-done | bytes 524320 | tf_op jit(solution)/shard_map/ppermute | solution.py:384
  202.9 11.2 %collective-permute-done.39 = bf16[32,8192]{1,0:T(8,128)(2,1)S(1)} collective-permute-done((bf16[32,8192]{1,0:T(8,128)(2,1)S(1)}, bf16[32,8192]{1,0:T(8,128)(2,1)S(1)}, u32[]{:S(2)}, u32[]{:S(2)}) %collective-permute-start.39) | collective-permute-done | bytes 524320 | tf_op jit(solution)/shard_map/ppermute | solution.py:381
  216.5 14.5 %collective-permute-done.43 = bf16[32,8192]{1,0:T(8,128)(2,1)S(1)} collective-permute-done((bf16[32,8192]{1,0:T(8,128)(2,1)S(1)}, bf16[32,8192]{1,0:T(8,128)(2,1)S(1)}, u32[]{:S(2)}, u32[]{:S(2)}) %collective-permute-start.43) | collective-permute-done | bytes 524320 | tf_op jit(solution)/shard_map/ppermute | solution.py:381
  235.3 12.1 %collective-permute-done.49 = bf16[32,8192]{1,0:T(8,128)(2,1)S(1)} collective-permute-done((bf16[32,8192]{1,0:T(8,128)(2,1)S(1)}, bf16[32,8192]{1,0:T(8,128)(2,1)S(1)}, u32[]{:S(2)}, u32[]{:S(2)}) %collective-permute-start.49) | collective-permute-done | bytes 524320 | tf_op jit(solution)/shard_map/ppermute | solution.py:397
  (165 shorter events, 84.3 us)
Async XLA Ops:
  0.0 43.3 %collective-permute-start.4 = (bf16[64,8192]{1,0:T(8,128)(2,1)}, bf16[64,8192]{1,0:T(8,128)(2,1)S(1)}, u32[]{:S(2)}, u32[]{:S(2)}) collective-permute-start(bf16[64,8192]{1,0:T(8,128)(2,1)} %bitcast.23), channel_id=1, source_target_pairs={{2,0},{4,2},{6,4},{7,6},{5,7},{3,5},{1,3},{0,1},{10,8},{12,10},{14... | collective-permute-start | bytes 3145736 | tf_op jit(solution)/shard_map/ppermute | solution.py:384
  3.0 40.3 %collective-permute-start.2 = (bf16[64,8192]{1,0:T(8,128)(2,1)}, bf16[64,8192]{1,0:T(8,128)(2,1)S(1)}, u32[]{:S(2)}, u32[]{:S(2)}) collective-permute-start(bf16[64,8192]{1,0:T(8,128)(2,1)} %bitcast.24), channel_id=1, source_target_pairs={{0,2},{2,4},{4,6},{6,7},{7,5},{5,3},{3,1},{1,0},{8,10},{10,12},{12... | collective-permute-start | bytes 3145736 | tf_op jit(solution)/shard_map/ppermute | solution.py:381
  3.0 40.3 %collective-permute-start = (bf16[64,8192]{1,0:T(8,128)(2,1)}, bf16[64,8192]{1,0:T(8,128)(2,1)S(1)}, u32[]{:S(2)}, u32[]{:S(2)}) collective-permute-start(bf16[64,8192]{1,0:T(8,128)(2,1)} %bitcast.25), channel_id=1, source_target_pairs={{0,8},{8,16},{16,24},{24,0},{1,9},{9,17},{17,25},{25,1},{2,10},{10... | collective-permute-start | bytes 3145736 | tf_op jit(solution)/shard_map/ppermute | solution.py:400
  8.3 26.5 %collective-permute-start.3 = (bf16[160,1024]{1,0:T(8,128)(2,1)}, bf16[160,1024]{1,0:T(8,128)(2,1)S(1)}, u32[]{:S(2)}, u32[]{:S(2)}) collective-permute-start(bf16[160,1024]{1,0:T(8,128)(2,1)} %get-tuple-element.83), channel_id=1, source_target_pairs={{0,2},{2,4},{4,6},{6,7},{7,5},{5,3},{3,1},{1,0},{8,10},{10,12},{12... | collective-permute-start | bytes 983048 | tf_op jit(solution)/shard_map/ppermute | solution.py:381
  10.3 27.2 %collective-permute-start.8 = (bf16[160,1024]{1,0:T(8,128)(2,1)}, bf16[160,1024]{1,0:T(8,128)(2,1)S(1)}, u32[]{:S(2)}, u32[]{:S(2)}) collective-permute-start(bf16[160,1024]{1,0:T(8,128)(2,1)} %get-tuple-element.88), channel_id=1, source_target_pairs={{2,0},{4,2},{6,4},{7,6},{5,7},{3,5},{1,3},{0,1},{10,8},{12,10},{14... | collective-permute-start | bytes 983048 | tf_op jit(solution)/shard_map/ppermute | solution.py:384
  49.4 17.7 %collective-permute-start.10 = (bf16[160,1024]{1,0:T(8,128)(2,1)S(1)}, bf16[160,1024]{1,0:T(8,128)(2,1)S(1)}, u32[]{:S(2)}, u32[]{:S(2)}) collective-permute-start(bf16[160,1024]{1,0:T(8,128)(2,1)S(1)} %add_convert_fusion.18), channel_id=1, source_target_pairs={{0,2},{2,4},{4,6},{6,7},{7,5},{5,3},{3,1},{1,0},{8,10},{10,12},{12... | collective-permute-start | bytes 983048 | tf_op jit(solution)/shard_map/ppermute | solution.py:381
  49.9 15.1 %collective-permute-start.11 = (bf16[160,1024]{1,0:T(8,128)(2,1)S(1)}, bf16[160,1024]{1,0:T(8,128)(2,1)S(1)}, u32[]{:S(2)}, u32[]{:S(2)}) collective-permute-start(bf16[160,1024]{1,0:T(8,128)(2,1)S(1)} %add_convert_fusion.19), channel_id=1, source_target_pairs={{2,0},{4,2},{6,4},{7,6},{5,7},{3,5},{1,3},{0,1},{10,8},{12,10},{14... | collective-permute-start | bytes 983048 | tf_op jit(solution)/shard_map/ppermute | solution.py:384
  84.2 20.1 %collective-permute-start.18 = (bf16[64,8192]{1,0:T(8,128)(2,1)S(1)}, bf16[64,8192]{1,0:T(8,128)(2,1)S(1)}, u32[]{:S(2)}, u32[]{:S(2)}) collective-permute-start(bf16[64,8192]{1,0:T(8,128)(2,1)S(1)} %collective-permute-done.2.refs_0_), channel_id=1, source_target_pairs={{0,2},{2,4},{4,6},{6,7},{7,5},{5,3},{3,1},{1,0},{8,10},{10,12},{12... | collective-permute-start | bytes 3145736 | tf_op jit(solution)/shard_map/ppermute | solution.py:381
  84.3 20.0 %collective-permute-start.23 = (bf16[64,8192]{1,0:T(8,128)(2,1)S(1)}, bf16[64,8192]{1,0:T(8,128)(2,1)S(1)}, u32[]{:S(2)}, u32[]{:S(2)}) collective-permute-start(bf16[64,8192]{1,0:T(8,128)(2,1)S(1)} %collective-permute-done.4.refs_1_), channel_id=1, source_target_pairs={{2,0},{4,2},{6,4},{7,6},{5,7},{3,5},{1,3},{0,1},{10,8},{12,10},{14... | collective-permute-start | bytes 3145736 | tf_op jit(solution)/shard_map/ppermute | solution.py:384
  104.3 33.3 %collective-permute-start.22 = (bf16[64,8192]{1,0:T(8,128)(2,1)S(1)}, bf16[64,8192]{1,0:T(8,128)(2,1)S(1)}, u32[]{:S(2)}, u32[]{:S(2)}) collective-permute-start(bf16[64,8192]{1,0:T(8,128)(2,1)S(1)} %collective-permute-done.18.refs_0_), channel_id=1, source_target_pairs={{0,2},{2,4},{4,6},{6,7},{7,5},{5,3},{3,1},{1,0},{8,10},{10,12},{12... | collective-permute-start | bytes 3145736 | tf_op jit(solution)/shard_map/ppermute | solution.py:381
  104.3 33.3 %collective-permute-start.24 = (bf16[64,8192]{1,0:T(8,128)(2,1)S(1)}, bf16[64,8192]{1,0:T(8,128)(2,1)S(1)}, u32[]{:S(2)}, u32[]{:S(2)}) collective-permute-start(bf16[64,8192]{1,0:T(8,128)(2,1)S(1)} %collective-permute-done.23.refs_1_), channel_id=1, source_target_pairs={{2,0},{4,2},{6,4},{7,6},{5,7},{3,5},{1,3},{0,1},{10,8},{12,10},{14... | collective-permute-start | bytes 3145736 | tf_op jit(solution)/shard_map/ppermute | solution.py:384
  107.1 24.7 %collective-permute-start.26 = (bf16[256,256]{1,0:T(8,128)(2,1)S(1)}, bf16[256,256]{1,0:T(8,128)(2,1)S(1)}, u32[]{:S(2)}, u32[]{:S(2)}) collective-permute-start(bf16[256,256]{1,0:T(8,128)(2,1)S(1)} %add_convert_fusion.27), channel_id=1, source_target_pairs={{0,2},{2,4},{4,6},{6,7},{7,5},{5,3},{3,1},{1,0},{8,10},{10,12},{12... | collective-permute-start | bytes 393224 | tf_op jit(solution)/shard_map/ppermute | solution.py:381
  107.6 24.4 %collective-permute-start.29 = (bf16[256,256]{1,0:T(8,128)(2,1)S(1)}, bf16[256,256]{1,0:T(8,128)(2,1)S(1)}, u32[]{:S(2)}, u32[]{:S(2)}) collective-permute-start(bf16[256,256]{1,0:T(8,128)(2,1)S(1)} %add_convert_fusion.26), channel_id=1, source_target_pairs={{2,0},{4,2},{6,4},{7,6},{5,7},{3,5},{1,3},{0,1},{10,8},{12,10},{14... | collective-permute-start | bytes 393224 | tf_op jit(solution)/shard_map/ppermute | solution.py:384
  156.3 24.4 %collective-permute-start.33 = (bf16[64,8192]{1,0:T(8,128)(2,1)S(1)}, bf16[64,8192]{1,0:T(8,128)(2,1)S(1)}, u32[]{:S(2)}, u32[]{:S(2)}) collective-permute-start(bf16[64,8192]{1,0:T(8,128)(2,1)S(1)} %get-tuple-element.130), channel_id=1, source_target_pairs={{0,8},{8,16},{16,24},{24,0},{1,9},{9,17},{17,25},{25,1},{2,10},{10... | collective-permute-start | bytes 3145736 | tf_op jit(solution)/shard_map/ppermute | solution.py:400
  156.9 24.3 %collective-permute-start.37 = (bf16[32,8192]{1,0:T(8,128)(2,1)S(1)}, bf16[32,8192]{1,0:T(8,128)(2,1)S(1)}, u32[]{:S(2)}, u32[]{:S(2)}) collective-permute-start(bf16[32,8192]{1,0:T(8,128)(2,1)S(1)} %get-tuple-element.135), channel_id=1, source_target_pairs={{0,2},{2,4},{4,6},{6,7},{7,5},{5,3},{3,1},{1,0},{8,10},{10,12},{12... | collective-permute-start | bytes 1572872 | tf_op jit(solution)/shard_map/ppermute | solution.py:381
  158.6 22.1 %collective-permute-start.38 = (bf16[32,8192]{1,0:T(8,128)(2,1)S(1)}, bf16[32,8192]{1,0:T(8,128)(2,1)S(1)}, u32[]{:S(2)}, u32[]{:S(2)}) collective-permute-start(bf16[32,8192]{1,0:T(8,128)(2,1)S(1)} %get-tuple-element.136), channel_id=1, source_target_pairs={{2,0},{4,2},{6,4},{7,6},{5,7},{3,5},{1,3},{0,1},{10,8},{12,10},{14... | collective-permute-start | bytes 1572872 | tf_op jit(solution)/shard_map/ppermute | solution.py:384
  180.9 19.4 %collective-permute-start.41 = (bf16[32,8192]{1,0:T(8,128)(2,1)S(1)}, bf16[32,8192]{1,0:T(8,128)(2,1)S(1)}, u32[]{:S(2)}, u32[]{:S(2)}) collective-permute-start(bf16[32,8192]{1,0:T(8,128)(2,1)S(1)} %add_convert_fusion.11), channel_id=1, source_target_pairs={{2,0},{4,2},{6,4},{7,6},{5,7},{3,5},{1,3},{0,1},{10,8},{12,10},{14... | collective-permute-start | bytes 1572872 | tf_op jit(solution)/shard_map/ppermute | solution.py:384
  181.3 19.1 %collective-permute-start.40 = (bf16[32,8192]{1,0:T(8,128)(2,1)S(1)}, bf16[32,8192]{1,0:T(8,128)(2,1)S(1)}, u32[]{:S(2)}, u32[]{:S(2)}) collective-permute-start(bf16[32,8192]{1,0:T(8,128)(2,1)S(1)} %add_convert_fusion.10), channel_id=1, source_target_pairs={{0,2},{2,4},{4,6},{6,7},{7,5},{5,3},{3,1},{1,0},{8,10},{10,12},{12... | collective-permute-start | bytes 1572872 | tf_op jit(solution)/shard_map/ppermute | solution.py:381
  187.4 26.7 %collective-permute-start.39 = (bf16[32,8192]{1,0:T(8,128)(2,1)S(1)}, bf16[32,8192]{1,0:T(8,128)(2,1)S(1)}, u32[]{:S(2)}, u32[]{:S(2)}) collective-permute-start(bf16[32,8192]{1,0:T(8,128)(2,1)S(1)} %add_convert_fusion.9), channel_id=1, source_target_pairs={{0,2},{2,4},{4,6},{6,7},{7,5},{5,3},{3,1},{1,0},{8,10},{10,12},{12... | collective-permute-start | bytes 1572872 | tf_op jit(solution)/shard_map/ppermute | solution.py:381
  189.3 24.9 %collective-permute-start.44 = (bf16[32,8192]{1,0:T(8,128)(2,1)S(1)}, bf16[32,8192]{1,0:T(8,128)(2,1)S(1)}, u32[]{:S(2)}, u32[]{:S(2)}) collective-permute-start(bf16[32,8192]{1,0:T(8,128)(2,1)S(1)} %add_convert_fusion.8), channel_id=1, source_target_pairs={{2,0},{4,2},{6,4},{7,6},{5,7},{3,5},{1,3},{0,1},{10,8},{12,10},{14... | collective-permute-start | bytes 1572872 | tf_op jit(solution)/shard_map/ppermute | solution.py:384
  200.4 34.8 %collective-permute-start.46 = (bf16[32,8192]{1,0:T(8,128)(2,1)S(1)}, bf16[32,8192]{1,0:T(8,128)(2,1)S(1)}, u32[]{:S(2)}, u32[]{:S(2)}) collective-permute-start(bf16[32,8192]{1,0:T(8,128)(2,1)S(1)} %add_convert_fusion.7), channel_id=1, source_target_pairs={{2,8},{4,10},{6,12},{7,14},{5,15},{3,13},{1,11},{0,9},{10,16},{12,... | collective-permute-start | bytes 1572872 | tf_op jit(solution)/shard_map/ppermute | solution.py:397
  200.6 34.6 %collective-permute-start.47 = (bf16[32,8192]{1,0:T(8,128)(2,1)S(1)}, bf16[32,8192]{1,0:T(8,128)(2,1)S(1)}, u32[]{:S(2)}, u32[]{:S(2)}) collective-permute-start(bf16[32,8192]{1,0:T(8,128)(2,1)S(1)} %add_convert_fusion.6), channel_id=1, source_target_pairs={{0,10},{2,12},{4,14},{6,15},{7,13},{5,11},{3,9},{1,8},{8,18},{10,2... | collective-permute-start | bytes 1572872 | tf_op jit(solution)/shard_map/ppermute | solution.py:394
  214.2 16.7 %collective-permute-start.43 = (bf16[32,8192]{1,0:T(8,128)(2,1)S(1)}, bf16[32,8192]{1,0:T(8,128)(2,1)S(1)}, u32[]{:S(2)}, u32[]{:S(2)}) collective-permute-start(bf16[32,8192]{1,0:T(8,128)(2,1)S(1)} %add_convert_fusion.5), channel_id=1, source_target_pairs={{0,2},{2,4},{4,6},{6,7},{7,5},{5,3},{3,1},{1,0},{8,10},{10,12},{12... | collective-permute-start | bytes 1572872 | tf_op jit(solution)/shard_map/ppermute | solution.py:381
  214.4 18.0 %collective-permute-start.48 = (bf16[32,8192]{1,0:T(8,128)(2,1)S(1)}, bf16[32,8192]{1,0:T(8,128)(2,1)S(1)}, u32[]{:S(2)}, u32[]{:S(2)}) collective-permute-start(bf16[32,8192]{1,0:T(8,128)(2,1)S(1)} %add_convert_fusion.4), channel_id=1, source_target_pairs={{2,0},{4,2},{6,4},{7,6},{5,7},{3,5},{1,3},{0,1},{10,8},{12,10},{14... | collective-permute-start | bytes 1572872 | tf_op jit(solution)/shard_map/ppermute | solution.py:384
  (44 other events, 630.5 us)

commit v7 on v6

--- a/solution.py
+++ b/solution.py
@@ -83,17 +83,23 @@
 
 
 def finish(gate, text, own, arrivals):
-    rows, columns = text.shape
-    part_rows = rows // len(arrivals)
-    result = jnp.zeros((1, rows, columns), BF16)
+    part_rows = text.shape[0] // len(arrivals)
+    results = []
     for part, came in enumerate(arrivals):
-        place = slice(part * part_rows, (part + 1) * part_rows)
-        branch = own[place].astype(F32)
-        for value in came:
-            branch = branch + value.astype(F32)
-        part_out = (text[place].astype(F32) + jnp.tanh(gate[0]) * branch).astype(BF16)
-        result = lax.dynamic_update_slice(result, part_out[None], (0, part * part_rows, 0))
-    return result
+        pieces = max(len(values) for values in came)
+        piece_rows = part_rows // pieces
+        for piece in range(pieces):
+            first = part * part_rows + piece * piece_rows
+            place = slice(first, first + piece_rows)
+            branch = own[place].astype(F32)
+            for values in came:
+                if len(values) == pieces:
+                    value = values[piece]
+                else:
+                    value = values[0][piece * piece_rows : (piece + 1) * piece_rows]
+                branch = branch + value.astype(F32)
+            results.append((text[place].astype(F32) + jnp.tanh(gate[0]) * branch).astype(BF16))
+    return jnp.concatenate(results, axis=0)[None]
 
 
 def project(places, feats, weight, order_len, first, blocks):
@@ -227,7 +233,11 @@
         out_shape=jax.ShapeDtypeStruct((rows, width), BF16),
         scratch_shapes=[pltpu.VMEM((rows, depth), BF16), pltpu.VMEM((rows, 1), F32)],
         compiler_params=params(),
-        cost_estimate=QUICK,
+        cost_estimate=pl.CostEstimate(
+            flops=2 * rows * depth * width,
+            bytes_accessed=2 * depth * (width + rows),
+            transcendentals=0,
+        ),
         name="query",
     )(*chunks, weight)
 
@@ -334,6 +344,8 @@
 
 
 def after(value, *others):
+    if not others:
+        return value
     return lax.optimization_barrier((value, *others))[0]
 
 
@@ -401,18 +413,34 @@
             value, "section", [(s, (s + 1) % section_count) for s in range(section_count)]
         )
 
-    def ring_sums(chains, hold=lambda hop, value: value, turn=None):
-        running = [part(sign * distance) for part, distance, sign, _, _ in chains]
+    def ring_sums(chains, hold=lambda left, value: value, turn=(), fine=False):
+        running = [[part(sign * distance)] for part, distance, sign, _, _ in chains]
+        ended = []
         for hop in range(far):
+            moved = [[] for _ in chains]
             for index, (part, distance, sign, move, last) in enumerate(chains):
                 left = distance - hop
+                sent = [hold(left, value) for value in running[index]]
                 if left == 1:
-                    running[index] = last(hold(hop, running[index]))
+                    running[index] = [last(value) for value in sent]
+                    if fine and distance < far:
+                        ended.append(running[index][0])
                 elif left > 1:
-                    came = move(hold(hop, running[index]))
-                    if turn is not None:
-                        came = after(came, turn)
-                    turn = running[index] = add(came, part(sign * (left - 1)))
+                    plus = [part(sign * (left - 1))]
+                    if left == 2 and fine and distance == far > 2:
+                        rows = plus[0].shape[0] // 2
+                        sent, plus = (
+                            [value[0][:rows], value[0][rows:]]
+                            for value in ([after(sent[0], *ended)], plus)
+                        )
+                    moved[index] = list(zip([move(value) for value in sent], plus))
+                    running[index] = []
+            for piece in range(max(len(values) for values in moved)):
+                for index, values in enumerate(moved):
+                    if piece < len(values):
+                        came, own = values[piece]
+                        turn = [add(after(came, *turn), own)]
+                        running[index] += turn
         return running
 
     def both_ways(part, distance_up, distance_down, last_up=up, last_down=down):
@@ -446,22 +474,26 @@
         )
     ]
 
-    def image_hold(hop, value):
-        if hop == 1:
-            return after(value, from_below[1], from_above[1], text_next)
-        return value
+    def image_hold(left, value):
+        return after(value, text_next) if left == 1 else value
 
     turns = [0, 3, 1, 2]
-    came = ring_sums([image_chains[turn] for turn in turns], image_hold)
-    came = [came[turns.index(index)] for index in range(4)]
+    came = ring_sums(
+        [image_chains[turn] for turn in turns],
+        image_hold,
+        turn=[gate_next, from_below[1], from_above[1]],
+    )
+    came = [came[turns.index(index)][0] for index in range(4)]
     image_cols = total_of(
         [[image_parts[index_of[0]][half], *came[2 * half : 2 * half + 2]] for half in range(2)]
     )
 
     text_round(image_cols)
     weight_query, weight_out = w_query[0], w_out[0]
-    near = [-1, 1]
-    near_queries = [query([from_below[1], from_above[1]], weight_query)]
+    queries = {
+        0: query([text_own], weight_query),
+        1: query([from_below[1], from_above[1]], weight_query),
+    }
 
     pieces = []
     moving = image_cols
@@ -477,32 +509,53 @@
                 [(s, (s + 2) % section_count) for s in range(section_count)],
             )
             if step == 0:
-                moving = after(moving, near_queries[0])
+                moving = after(moving, queries[0], queries[1])
 
     kv_part = key_values(meta, pieces, w_kv[0], mp_count, section_count, sharing)
 
     for distance in range(3, far):
         text_round(*([kv_part[0]] if distance == 3 else []))
-    for distance in range(2, far):
-        near += [-distance, distance]
-        near_queries.append(query([from_below[distance], from_above[distance]], weight_query))
-
-    def kv_hold(hop, value):
-        if hop == far - 1:
+    if far > 2:
+        queries[far - 1] = query([from_below[far - 1], from_above[far - 1]], weight_query)
+
+    def kv_hold(left, value):
+        if left == 1:
             return after(value, *from_below[3:], *from_above[3:])
         return value
 
-    came = ring_sums(both_ways(lambda offset: kv_part[index_of[offset]], far, far - 1), kv_hold)
-    kv_own = (
-        kv_part[index_of[0]].astype(F32) + came[0].astype(F32) + came[1].astype(F32)
-    ).astype(BF16)
-    kv_own = after(kv_own, gate_next, *near_queries)
-    kv_pieces = [kv_own]
-    for step in range(1, sharing):
-        pairs = [
+    def within(step):
+        return [
             (m, m // sharing * sharing + (m % sharing + step) % sharing) for m in range(mp_count)
         ]
-        kv_pieces.append(lax.ppermute(kv_own, "mp", pairs))
+
+    def last_to_both(move, pairs):
+        partner = dict(within(1))
+        other = [(source, partner[target]) for source, target in pairs]
+        if sharing != 2:
+            return lambda value: [move(value)]
+        return lambda value: [move(value), lax.ppermute(value, "mp", other)]
+
+    own_kv = [kv_part[index_of[0]]]
+    if sharing == 2:
+        own_kv.append(lax.ppermute(own_kv[0], "mp", within(1)))
+    came = ring_sums(
+        both_ways(
+            lambda offset: kv_part[index_of[offset]],
+            far,
+            far - 1,
+            last_to_both(up, up_pairs),
+            last_to_both(down, down_pairs),
+        ),
+        kv_hold,
+    )
+    kv_pieces = [
+        (own.astype(F32) + above.astype(F32) + below.astype(F32)).astype(BF16)
+        for own, above, below in zip(own_kv, came[0][0], came[1][0])
+    ]
+    kv_own = kv_pieces[0] = after(kv_pieces[0], queries[far - 1])
+    if sharing != 2:
+        for step in range(1, sharing):
+            kv_pieces.append(lax.ppermute(kv_own, "mp", within(step)))
 
     far_chunks = [up(after(from_below[-1], kv_own)[:cut])]
     if parts == 2:
@@ -519,20 +572,21 @@
             mp_count,
         )
 
-    first, first_queries = near[-2:] + [0], [near_queries[-1], query([text_own], weight_query)]
-    rest, rest_queries = near[:-2], near_queries[:-1]
+    first = [1 - far, far - 1, 0]
     *first_part, own_part = attend_to(
         first,
-        jnp.concatenate(first_queries, axis=0),
-        [cut] * (parts * (len(first) - 1)) + [text_rows],
-    )
-    far_part = attend_to(
-        [far], after(query(far_chunks, weight_query), own_part), [cut] * parts
-    )
+        jnp.concatenate([queries[far - 1], queries[0]], axis=0),
+        [cut] * (2 * parts) + [text_rows],
+    )
+    rest = [sign * distance for distance in range(1, far - 1) for sign in (-1, 1)]
+    for distance in range(2, far - 1):
+        below = after(from_below[distance], own_part)
+        queries[distance] = query([below, from_above[distance]], weight_query)
+    rest_queries = jnp.concatenate([queries[distance] for distance in range(1, far - 1)], axis=0)
+    far_queries = query(far_chunks, weight_query)
+    far_part = attend_to([far], after(far_queries, rest_queries, own_part), [cut] * parts)
     rest_part = attend_to(
-        rest,
-        after(jnp.concatenate(rest_queries, axis=0), far_part[0]),
-        [cut] * (parts * len(rest)),
+        rest, after(rest_queries, far_part[0]), [cut] * (parts * len(rest))
     )
     near_part = list(first_part) + list(rest_part)
     out_parts = {
@@ -553,7 +607,7 @@
     ]
 
     turns = [1, 2, 0, 3] if parts == 2 else [0, 1]
-    came = ring_sums([branch_chains[turn] for turn in turns], turn=own_next)
+    came = ring_sums([branch_chains[turn] for turn in turns], turn=[own_next], fine=parts == 2)
     came = [came[turns.index(index)] for index in range(2 * parts)]
     return finish(
         gate_next, text_next, own_next, [came[2 * part : 2 * part + 2] for part in range(parts)]

time: 250 us -> 252 us (level)
  starting transfers between devices: 52.1 us -> 59.5 us
  waiting for transfers between devices: 135 us -> 129 us
    ppermute x19 -> x20, waiting for transfers between devices: 32.9 us -> 25.6 us  [down(): return lax.ppermute(value, 'mp', down_pairs)]
    ppermute x2 -> x3, waiting for transfers between devices: 0.19 us -> 7.13 us  [up_across(): return lax.ppermute(value, ('section', 'mp'), across(up_pairs))]
    ppermute x20 -> x21, starting transfers between devices: 14.9 us -> 20.5 us  [up(): return lax.ppermute(value, 'mp', up_pairs)]
    ppermute x2 -> x3, waiting for transfers between devices: 12.1 us -> 6.8 us  [down_across(): return lax.ppermute(value, ('section', 'mp'), across(down_pairs))]
    ppermute x2 -> x3, starting transfers between devices: 4.28 us -> 0.92 us  [up_across(): return lax.ppermute(value, ('section', 'mp'), across(up_pairs))]
    ppermute x19 -> x20, starting transfers between devices: 27.3 us -> 29.1 us  [down(): return lax.ppermute(value, 'mp', down_pairs)]
    ppermute x20 -> x21, waiting for transfers between devices: 84.8 us -> 84.1 us  [up(): return lax.ppermute(value, 'mp', up_pairs)]
  transfers between devices with their start and end apart: 50 -> 56, of which waited for: 26 -> 28; matrix products, arithmetic and copies ran while one was open for 3% -> 3% of each run, Pallas kernels for 21% -> 21%
where the time goes in v7:
time: 252 us; the launch traced here: 251 us
  waiting for transfers between devices  129 us (51%)
  starting transfers between devices  59.5 us (24%)
  Pallas kernels  52.1 us (21%)
  other arithmetic  7.35 us (3%)
    ppermute x21, waiting for transfers between devices, up(): return lax.ppermute(value, 'mp', up_pairs)  84.1 us
    ppermute x20, starting transfers between devices, down(): return lax.ppermute(value, 'mp', down_pairs)  29.1 us
    ppermute x20, waiting for transfers between devices, down(): return lax.ppermute(value, 'mp', down_pairs)  25.6 us
    ppermute x21, starting transfers between devices, up(): return lax.ppermute(value, 'mp', up_pairs)  20.5 us
    pallas_call x2, Pallas kernels, project(): pl.pallas_call(kernel, grid_spec=pltpu.PrefetchScalarGridSpec(num_scalar_...  17.3 us
    pallas_call x3, Pallas kernels, attend(): pl.pallas_call(kernel, grid_spec=pltpu.PrefetchScalarGridSpec(num_scalar_...  16.1 us
    pallas_call x5, Pallas kernels, query(): pl.pallas_call(kernel, grid=(width // wide,), in_specs=[pl.BlockSpec(chun...  14 us
    ppermute x3, waiting for transfers between devices, up_across(): return lax.ppermute(value, ('section', 'mp'), across(up_pairs))  7.13 us
  transfers between devices with their start and end apart: 56, of which 28 were waited for; matrix products, arithmetic and copies ran while one was open for 3% of the time, Pallas kernels for 21%

profile of v7, /device:TPU:0, one launch (start us, length us, event | category | flops | bytes accessed | tf_op | source)
XLA Modules:
  0.0 251.5 jit_solution(6547193076402468289)
XLA Ops:
  4.2 4.1 %project.3 = (bf16[160,1024]{1,0:T(8,128)(2,1)}, bf16[160,1024]{1,0:T(8,128)(2,1)}) custom-call(s32[10]{0:T(128)} %get-tuple-element.185.places_ref, bf16[320,960]{1,0:T(8,128)(2,1)} %feats_ref.3, bf16[960,8192]{1,0:T(8,128)(2,1)} %weight_ref.3), custom_call_target="tpu_custom_call" | custom-call | flops 629145600 | bytes 2621440 | tf_op jit(solution)/shard_map/project/pallas_call | solution.py:121
  10.3 13.2 %project.2 = (bf16[160,1024]{1,0:T(8,128)(2,1)}, bf16[160,1024]{1,0:T(8,128)(2,1)}, bf16[160,1024]{1,0:T(8,128)(2,1)}, bf16[160,1024]{1,0:T(8,128)(2,1)}, bf16[1...) custom-call(s32[10]{0:T(128)} %get-tuple-element.185.places_ref, ...), custom_call_target="tpu_custom_call" | custom-call | flops 4404019200 | bytes 18350080 | tf_op jit(solution)/shard_map/project/pallas_call | solution.py:121
  25.1 9.7 %collective-permute-done.3 = bf16[160,1024]{1,0:T(8,128)(2,1)S(1)} collective-permute-done((bf16[160,1024]{1,0:T(8,128)(2,1)}, bf16[160,1024]{1,0:T(8,128)(2,1)S(1)}, u32[]{:S(2)}, u32[]{:S(2)}) %collective-permute-start.3) | collective-permute-done | bytes 327712 | tf_op jit(solution)/shard_map/ppermute | solution.py:393
  41.2 4.9 %collective-permute-done.7 = bf16[160,1024]{1,0:T(8,128)(2,1)S(1)} collective-permute-done((bf16[160,1024]{1,0:T(8,128)(2,1)}, bf16[160,1024]{1,0:T(8,128)(2,1)S(1)}, u32[]{:S(2)}, u32[]{:S(2)}) %collective-permute-start.7) | collective-permute-done | bytes 327712 | tf_op jit(solution)/shard_map/ppermute | solution.py:396
  48.4 4.3 %collective-permute-done.5 = bf16[160,1024]{1,0:T(8,128)(2,1)S(1)} collective-permute-done((bf16[160,1024]{1,0:T(8,128)(2,1)S(1)}, bf16[160,1024]{1,0:T(8,128)(2,1)S(1)}, u32[]{:S(2)}, u32[]{:S(2)}) %collective-permute-start.5) | collective-permute-done | bytes 327712 | tf_op jit(solution)/shard_map/ppermute | solution.py:393
  55.1 5.0 %collective-permute-done.11 = bf16[160,1024]{1,0:T(8,128)(2,1)S(1)} collective-permute-done((bf16[160,1024]{1,0:T(8,128)(2,1)S(1)}, bf16[160,1024]{1,0:T(8,128)(2,1)S(1)}, u32[]{:S(2)}, u32[]{:S(2)}) %collective-permute-start.11) | collective-permute-done | bytes 327712 | tf_op jit(solution)/shard_map/ppermute | solution.py:396
  62.4 4.3 %collective-permute-done.9 = bf16[160,1024]{1,0:T(8,128)(2,1)S(1)} collective-permute-done((bf16[160,1024]{1,0:T(8,128)(2,1)S(1)}, bf16[160,1024]{1,0:T(8,128)(2,1)S(1)}, u32[]{:S(2)}, u32[]{:S(2)}) %collective-permute-start.9) | collective-permute-done | bytes 327712 | tf_op jit(solution)/shard_map/ppermute | solution.py:393
  69.3 4.5 %collective-permute-done.15.refs_4_ = bf16[160,1024]{1,0:T(8,128)(2,1)S(1)} collective-permute-done((bf16[160,1024]{1,0:T(8,128)(2,1)S(1)}, bf16[160,1024]{1,0:T(8,128)(2,1)S(1)}, u32[]{:S(2)}, u32[]{:S(2)}) %collective-permute-start.15) | collective-permute-done | bytes 327712 | tf_op jit(solution)/shard_map/ppermute | solution.py:393
  74.1 4.3 %collective-permute-done.13.refs_1_ = bf16[160,1024]{1,0:T(8,128)(2,1)S(1)} collective-permute-done((bf16[160,1024]{1,0:T(8,128)(2,1)S(1)}, bf16[160,1024]{1,0:T(8,128)(2,1)S(1)}, u32[]{:S(2)}, u32[]{:S(2)}) %collective-permute-start.13) | collective-permute-done | bytes 327712 | tf_op jit(solution)/shard_map/ppermute | solution.py:393
  89.1 4.4 %collective-permute-done.20.refs_2_ = bf16[320,1024]{1,0:T(8,128)(2,1)S(1)} collective-permute-done((bf16[320,1024]{1,0:T(8,128)(2,1)S(1)}, bf16[320,1024]{1,0:T(8,128)(2,1)S(1)}, u32[]{:S(2)}, u32[]{:S(2)}) %collective-permute-start.20) | collective-permute-done | bytes 655392 | tf_op jit(solution)/shard_map/ppermute | solution.py:506
  95.6 4.4 %key_values.1 = (bf16[256,256]{1,0:T(8,128)(2,1)S(1)}, bf16[256,256]{1,0:T(8,128)(2,1)S(1)}, bf16[256,256]{1,0:T(8,128)(2,1)S(1)}, bf16[256,256]{1,0:T(8,128)(2,...) custom-call(s32[18]{0:T(128)S(1)} %pad_add_fusion.meta_ref, ...), custom_call_target="tpu_custom_call" | custom-call | flops 1 | bytes 1 | tf_op jit(solution)/shard_map/key_values/pallas_call | solution.py:185
  109.1 25.3 %collective-permute-done.26 = bf16[256,256]{1,0:T(8,128)(2,1)S(1)} collective-permute-done((bf16[256,256]{1,0:T(8,128)(2,1)S(1)}, bf16[256,256]{1,0:T(8,128)(2,1)S(1)}, u32[]{:S(2)}, u32[]{:S(2)}) %collective-permute-start.26) | collective-permute-done | bytes 131104 | tf_op jit(solution)/shard_map/ppermute | solution.py:393
  134.5 4.9 %collective-permute-done.28 = bf16[256,256]{1,0:T(8,128)(2,1)S(1)} collective-permute-done((bf16[256,256]{1,0:T(8,128)(2,1)S(1)}, bf16[256,256]{1,0:T(8,128)(2,1)S(1)}, u32[]{:S(2)}, u32[]{:S(2)}) %collective-permute-start.28) | collective-permute-done | bytes 131104 | tf_op jit(solution)/shard_map/ppermute | solution.py:393
  141.7 3.6 %collective-permute-start.30 = (bf16[256,256]{1,0:T(8,128)(2,1)S(1)}, bf16[256,256]{1,0:T(8,128)(2,1)S(1)}, u32[]{:S(2)}, u32[]{:S(2)}) collective-permute-start(bf16[256,256]{1,0:T(8,128)(2,1)S(1)} %add_convert_fusion.28), channel_id=1, source_target_pairs={{0,2},{2,4},{4,6},{6,7},{7,5},{5,3},{3,1},{1,0},{8,10},{10,12},{12... | collective-permute-start | bytes 393224 | tf_op jit(solution)/shard_map/ppermute | solution.py:393
  146.0 4.8 %collective-permute-start.31 = (bf16[256,256]{1,0:T(8,128)(2,1)S(1)}, bf16[256,256]{1,0:T(8,128)(2,1)S(1)}, u32[]{:S(2)}, u32[]{:S(2)}) collective-permute-start(bf16[256,256]{1,0:T(8,128)(2,1)S(1)} %add_convert_fusion.29), channel_id=1, source_target_pairs={{2,0},{4,2},{6,4},{7,6},{5,7},{3,5},{1,3},{0,1},{10,8},{12,10},{14... | collective-permute-start | bytes 393224 | tf_op jit(solution)/shard_map/ppermute | solution.py:396
  156.9 5.6 %attend.3 = (bf16[32,8192]{1,0:T(8,128)(2,1)S(1)}, bf16[32,8192]{1,0:T(8,128)(2,1)S(1)}, bf16[32,8192]{1,0:T(8,128)(2,1)S(1)}, bf16[32,8192]{1,0:T(8,128)(2,1)S(1)}, bf16[64,8192]{1,0:T(8,128)(2,1)S(1)}) custom-call(s32[18]{0:T(128)S(1)} %pad_add_fusion.meta_ref, bf16[192,512]{1,0:T(8,128)(2,1)S(1)} %pad_maximum_fusion.1.query_ref, ...), custom_call_target="tpu_custom_call" | custom-call | flops 6442450944 | bytes 33554432 | tf_op jit(solution)/shard_map/attend/pallas_call | solution.py:318
  170.4 4.3 %attend.4 = (bf16[32,8192]{1,0:T(8,128)(2,1)S(1)}, bf16[32,8192]{1,0:T(8,128)(2,1)S(1)}) custom-call(s32[18]{0:T(128)S(1)} %pad_add_fusion.meta_ref, bf16[64,512]{1,0:T(8,128)(2,1)S(1)} %query.8.query_ref, bf16[256,256]{1,0:T(8,128)(2,1)S(1)} %add_convert_fusion.27.refs_0_, bf16[256,256]{1,0:T(8,128)(2,1)S(1)} %add_convert_fusion.26.refs_1_, ...), custom_call_target="tpu_custom_call" | custom-call | flops 2147483648 | bytes 33554432 | tf_op jit(solution)/shard_map/attend/pallas_call | solution.py:318
  176.8 6.2 %attend.5 = (bf16[32,8192]{1,0:T(8,128)(2,1)S(1)}, bf16[32,8192]{1,0:T(8,128)(2,1)S(1)}, bf16[32,8192]{1,0:T(8,128)(2,1)S(1)}, bf16[32,8192]{1,0:T(8,128)(2,1)S(...) custom-call(s32[18]{0:T(128)S(1)} %pad_add_fusion.meta_ref, ...), custom_call_target="tpu_custom_call" | custom-call | flops 8589934592 | bytes 33554432 | tf_op jit(solution)/shard_map/attend/pallas_call | solution.py:318
  185.5 4.1 %collective-permute-done.38 = bf16[32,8192]{1,0:T(8,128)(2,1)S(1)} collective-permute-done((bf16[32,8192]{1,0:T(8,128)(2,1)S(1)}, bf16[32,8192]{1,0:T(8,128)(2,1)S(1)}, u32[]{:S(2)}, u32[]{:S(2)}) %collective-permute-start.38) | collective-permute-done | bytes 524320 | tf_op jit(solution)/shard_map/ppermute | solution.py:393
  192.0 8.9 %collective-permute-done.43 = bf16[32,8192]{1,0:T(8,128)(2,1)S(1)} collective-permute-done((bf16[32,8192]{1,0:T(8,128)(2,1)S(1)}, bf16[32,8192]{1,0:T(8,128)(2,1)S(1)}, u32[]{:S(2)}, u32[]{:S(2)}) %collective-permute-start.43) | collective-permute-done | bytes 524320 | tf_op jit(solution)/shard_map/ppermute | solution.py:396
  202.0 14.5 %collective-permute-done.41 = bf16[32,8192]{1,0:T(8,128)(2,1)S(1)} collective-permute-done((bf16[32,8192]{1,0:T(8,128)(2,1)S(1)}, bf16[32,8192]{1,0:T(8,128)(2,1)S(1)}, u32[]{:S(2)}, u32[]{:S(2)}) %collective-permute-start.41) | collective-permute-done | bytes 524320 | tf_op jit(solution)/shard_map/ppermute | solution.py:393
  227.1 5.1 %collective-permute-done.47 = bf16[16,8192]{1,0:T(8,128)(2,1)S(1)} collective-permute-done((bf16[16,8192]{1,0:T(8,128)(2,1)S(1)}, bf16[16,8192]{1,0:T(8,128)(2,1)S(1)}, u32[]{:S(2)}, u32[]{:S(2)}) %collective-permute-start.47) | collective-permute-done | bytes 262176 | tf_op jit(solution)/shard_map/ppermute | solution.py:393
  242.0 4.0 %collective-permute-done.52 = bf16[16,8192]{1,0:T(8,128)(2,1)S(1)} collective-permute-done((bf16[16,8192]{1,0:T(8,128)(2,1)S(1)}, bf16[16,8192]{1,0:T(8,128)(2,1)S(1)}, u32[]{:S(2)}, u32[]{:S(2)}) %collective-permute-start.52) | collective-permute-done | bytes 262176 | tf_op jit(solution)/shard_map/ppermute | solution.py:406
  246.0 3.8 %collective-permute-done.55 = bf16[16,8192]{1,0:T(8,128)(2,1)S(1)} collective-permute-done((bf16[16,8192]{1,0:T(8,128)(2,1)S(1)}, bf16[16,8192]{1,0:T(8,128)(2,1)S(1)}, u32[]{:S(2)}, u32[]{:S(2)}) %collective-permute-start.55) | collective-permute-done | bytes 262176 | tf_op jit(solution)/shard_map/ppermute | solution.py:409
  (182 shorter events, 92.0 us)
Async XLA Ops:
  0.0 35.2 %collective-permute-start.4 = (bf16[64,8192]{1,0:T(8,128)(2,1)}, bf16[64,8192]{1,0:T(8,128)(2,1)S(1)}, u32[]{:S(2)}, u32[]{:S(2)}) collective-permute-start(bf16[64,8192]{1,0:T(8,128)(2,1)} %bitcast.21), channel_id=1, source_target_pairs={{2,0},{4,2},{6,4},{7,6},{5,7},{3,5},{1,3},{0,1},{10,8},{12,10},{14... | collective-permute-start | bytes 3145736 | tf_op jit(solution)/shard_map/ppermute | solution.py:396
  3.0 33.9 %collective-permute-start.2 = (bf16[64,8192]{1,0:T(8,128)(2,1)}, bf16[64,8192]{1,0:T(8,128)(2,1)S(1)}, u32[]{:S(2)}, u32[]{:S(2)}) collective-permute-start(bf16[64,8192]{1,0:T(8,128)(2,1)} %bitcast.22), channel_id=1, source_target_pairs={{0,2},{2,4},{4,6},{6,7},{7,5},{5,3},{3,1},{1,0},{8,10},{10,12},{12... | collective-permute-start | bytes 3145736 | tf_op jit(solution)/shard_map/ppermute | solution.py:393
  3.0 20.5 %collective-permute-start.1 = (f32[1]{0:T(128)}, f32[1]{0:T(128)}, u32[]{:S(2)}, u32[]{:S(2)}) collective-permute-start(f32[1]{0:T(128)} %param.16), channel_id=1, source_target_pairs={{0,8},{8,16},{16,24},{24,0},{1,9},{9,17},{17,25},{25,1},{2,10},{10... | collective-permute-start | bytes 20 | tf_op jit(solution)/shard_map/ppermute | solution.py:412
  8.3 26.5 %collective-permute-start.3 = (bf16[160,1024]{1,0:T(8,128)(2,1)}, bf16[160,1024]{1,0:T(8,128)(2,1)S(1)}, u32[]{:S(2)}, u32[]{:S(2)}) collective-permute-start(bf16[160,1024]{1,0:T(8,128)(2,1)} %get-tuple-element.90), channel_id=1, source_target_pairs={{0,2},{2,4},{4,6},{6,7},{7,5},{5,3},{3,1},{1,0},{8,10},{10,12},{12... | collective-permute-start | bytes 983048 | tf_op jit(solution)/shard_map/ppermute | solution.py:393
  10.3 28.0 %collective-permute-start.8 = (bf16[160,1024]{1,0:T(8,128)(2,1)}, bf16[160,1024]{1,0:T(8,128)(2,1)S(1)}, u32[]{:S(2)}, u32[]{:S(2)}) collective-permute-start(bf16[160,1024]{1,0:T(8,128)(2,1)} %get-tuple-element.95), channel_id=1, source_target_pairs={{2,0},{4,2},{6,4},{7,6},{5,7},{3,5},{1,3},{0,1},{10,8},{12,10},{14... | collective-permute-start | bytes 983048 | tf_op jit(solution)/shard_map/ppermute | solution.py:396
  23.6 36.7 %collective-permute-start = (bf16[64,8192]{1,0:T(8,128)(2,1)S(1)}, bf16[64,8192]{1,0:T(8,128)(2,1)S(1)}, u32[]{:S(2)}, u32[]{:S(2)}) collective-permute-start(bf16[64,8192]{1,0:T(8,128)(2,1)S(1)} %bitcast.23), channel_id=1, source_target_pairs={{0,8},{8,16},{16,24},{24,0},{1,9},{9,17},{17,25},{25,1},{2,10},{10... | collective-permute-start | bytes 3145736 | tf_op jit(solution)/shard_map/ppermute | solution.py:412
  81.1 22.9 %collective-permute-start.18 = (bf16[64,8192]{1,0:T(8,128)(2,1)S(1)}, bf16[64,8192]{1,0:T(8,128)(2,1)S(1)}, u32[]{:S(2)}, u32[]{:S(2)}) collective-permute-start(bf16[64,8192]{1,0:T(8,128)(2,1)S(1)} %collective-permute-done.2.refs_0_), channel_id=1, source_target_pairs={{0,2},{2,4},{4,6},{6,7},{7,5},{5,3},{3,1},{1,0},{8,10},{10,12},{12... | collective-permute-start | bytes 3145736 | tf_op jit(solution)/shard_map/ppermute | solution.py:393
  82.8 23.3 %collective-permute-start.23 = (bf16[64,8192]{1,0:T(8,128)(2,1)S(1)}, bf16[64,8192]{1,0:T(8,128)(2,1)S(1)}, u32[]{:S(2)}, u32[]{:S(2)}) collective-permute-start(bf16[64,8192]{1,0:T(8,128)(2,1)S(1)} %collective-permute-done.4.refs_1_), channel_id=1, source_target_pairs={{2,0},{4,2},{6,4},{7,6},{5,7},{3,5},{1,3},{0,1},{10,8},{12,10},{14... | collective-permute-start | bytes 3145736 | tf_op jit(solution)/shard_map/ppermute | solution.py:396
  102.1 54.7 %collective-permute-start.32 = (bf16[256,256]{1,0:T(8,128)(2,1)S(1)}, bf16[256,256]{1,0:T(8,128)(2,1)S(1)}, u32[]{:S(2)}, u32[]{:S(2)}) collective-permute-start(bf16[256,256]{1,0:T(8,128)(2,1)S(1)} %get-tuple-element.125), channel_id=1, source_target_pairs={{0,1},{1,0},{2,3},{3,2},{4,5},{5,4},{6,7},{7,6},{8,9},{9,8},{10,11... | collective-permute-start | bytes 393224 | tf_op jit(solution)/shard_map/ppermute | solution.py:540
  104.1 35.4 %collective-permute-start.22 = (bf16[64,8192]{1,0:T(8,128)(2,1)S(1)}, bf16[64,8192]{1,0:T(8,128)(2,1)S(1)}, u32[]{:S(2)}, u32[]{:S(2)}) collective-permute-start(bf16[64,8192]{1,0:T(8,128)(2,1)S(1)} %collective-permute-done.18.refs_0_), channel_id=1, source_target_pairs={{0,2},{2,4},{4,6},{6,7},{7,5},{5,3},{3,1},{1,0},{8,10},{10,12},{12... | collective-permute-start | bytes 3145736 | tf_op jit(solution)/shard_map/ppermute | solution.py:393
  106.0 33.5 %collective-permute-start.24 = (bf16[64,8192]{1,0:T(8,128)(2,1)S(1)}, bf16[64,8192]{1,0:T(8,128)(2,1)S(1)}, u32[]{:S(2)}, u32[]{:S(2)}) collective-permute-start(bf16[64,8192]{1,0:T(8,128)(2,1)S(1)} %collective-permute-done.23.refs_1_), channel_id=1, source_target_pairs={{2,0},{4,2},{6,4},{7,6},{5,7},{3,5},{1,3},{0,1},{10,8},{12,10},{14... | collective-permute-start | bytes 3145736 | tf_op jit(solution)/shard_map/ppermute | solution.py:396
  106.9 27.5 %collective-permute-start.26 = (bf16[256,256]{1,0:T(8,128)(2,1)S(1)}, bf16[256,256]{1,0:T(8,128)(2,1)S(1)}, u32[]{:S(2)}, u32[]{:S(2)}) collective-permute-start(bf16[256,256]{1,0:T(8,128)(2,1)S(1)} %add_convert_fusion.32), channel_id=1, source_target_pairs={{0,2},{2,4},{4,6},{6,7},{7,5},{5,3},{3,1},{1,0},{8,10},{10,12},{12... | collective-permute-start | bytes 393224 | tf_op jit(solution)/shard_map/ppermute | solution.py:393
  108.9 25.5 %collective-permute-start.29 = (bf16[256,256]{1,0:T(8,128)(2,1)S(1)}, bf16[256,256]{1,0:T(8,128)(2,1)S(1)}, u32[]{:S(2)}, u32[]{:S(2)}) collective-permute-start(bf16[256,256]{1,0:T(8,128)(2,1)S(1)} %add_convert_fusion.31), channel_id=1, source_target_pairs={{2,0},{4,2},{6,4},{7,6},{5,7},{3,5},{1,3},{0,1},{10,8},{12,10},{14... | collective-permute-start | bytes 393224 | tf_op jit(solution)/shard_map/ppermute | solution.py:396
  139.5 17.4 %collective-permute-start.33 = (bf16[256,256]{1,0:T(8,128)(2,1)S(1)}, bf16[256,256]{1,0:T(8,128)(2,1)S(1)}, u32[]{:S(2)}, u32[]{:S(2)}) collective-permute-start(bf16[256,256]{1,0:T(8,128)(2,1)S(1)} %add_convert_fusion.28), channel_id=1, source_target_pairs={{0,3},{2,5},{4,7},{6,6},{7,4},{5,2},{3,0},{1,1},{8,11},{10,13},{12... | collective-permute-start | bytes 393224 | tf_op jit(solution)/shard_map/ppermute | solution.py:536
  162.5 20.5 %collective-permute-start.35 = (bf16[64,8192]{1,0:T(8,128)(2,1)S(1)}, bf16[64,8192]{1,0:T(8,128)(2,1)S(1)}, u32[]{:S(2)}, u32[]{:S(2)}) collective-permute-start(bf16[64,8192]{1,0:T(8,128)(2,1)S(1)} %get-tuple-element.139), channel_id=1, source_target_pairs={{0,8},{8,16},{16,24},{24,0},{1,9},{9,17},{17,25},{25,1},{2,10},{10... | collective-permute-start | bytes 3145736 | tf_op jit(solution)/shard_map/ppermute | solution.py:412
  162.6 22.6 %collective-permute-start.39 = (bf16[32,8192]{1,0:T(8,128)(2,1)S(1)}, bf16[32,8192]{1,0:T(8,128)(2,1)S(1)}, u32[]{:S(2)}, u32[]{:S(2)}) collective-permute-start(bf16[32,8192]{1,0:T(8,128)(2,1)S(1)} %get-tuple-element.145), channel_id=1, source_target_pairs={{0,2},{2,4},{4,6},{6,7},{7,5},{5,3},{3,1},{1,0},{8,10},{10,12},{12... | collective-permute-start | bytes 1572872 | tf_op jit(solution)/shard_map/ppermute | solution.py:393
  162.6 20.4 %collective-permute-start.40 = (bf16[32,8192]{1,0:T(8,128)(2,1)S(1)}, bf16[32,8192]{1,0:T(8,128)(2,1)S(1)}, u32[]{:S(2)}, u32[]{:S(2)}) collective-permute-start(bf16[32,8192]{1,0:T(8,128)(2,1)S(1)} %get-tuple-element.146), channel_id=1, source_target_pairs={{2,0},{4,2},{6,4},{7,6},{5,7},{3,5},{1,3},{0,1},{10,8},{12,10},{14... | collective-permute-start | bytes 1572872 | tf_op jit(solution)/shard_map/ppermute | solution.py:396
  174.8 15.0 %collective-permute-start.44 = (bf16[32,8192]{1,0:T(8,128)(2,1)S(1)}, bf16[32,8192]{1,0:T(8,128)(2,1)S(1)}, u32[]{:S(2)}, u32[]{:S(2)}) collective-permute-start(bf16[32,8192]{1,0:T(8,128)(2,1)S(1)} %get-tuple-element.154), channel_id=1, source_target_pairs={{2,0},{4,2},{6,4},{7,6},{5,7},{3,5},{1,3},{0,1},{10,8},{12,10},{14... | collective-permute-start | bytes 1572872 | tf_op jit(solution)/shard_map/ppermute | solution.py:396
  183.2 17.7 %collective-permute-start.43 = (bf16[32,8192]{1,0:T(8,128)(2,1)S(1)}, bf16[32,8192]{1,0:T(8,128)(2,1)S(1)}, u32[]{:S(2)}, u32[]{:S(2)}) collective-permute-start(bf16[32,8192]{1,0:T(8,128)(2,1)S(1)} %add_convert_fusion.7), channel_id=1, source_target_pairs={{2,0},{4,2},{6,4},{7,6},{5,7},{3,5},{1,3},{0,1},{10,8},{12,10},{14... | collective-permute-start | bytes 1572872 | tf_op jit(solution)/shard_map/ppermute | solution.py:396
  185.3 15.7 %collective-permute-start.42 = (bf16[32,8192]{1,0:T(8,128)(2,1)S(1)}, bf16[32,8192]{1,0:T(8,128)(2,1)S(1)}, u32[]{:S(2)}, u32[]{:S(2)}) collective-permute-start(bf16[32,8192]{1,0:T(8,128)(2,1)S(1)} %add_convert_fusion.6), channel_id=1, source_target_pairs={{0,2},{2,4},{4,6},{6,7},{7,5},{5,3},{3,1},{1,0},{8,10},{10,12},{12... | collective-permute-start | bytes 1572872 | tf_op jit(solution)/shard_map/ppermute | solution.py:393
  189.7 26.8 %collective-permute-start.41 = (bf16[32,8192]{1,0:T(8,128)(2,1)S(1)}, bf16[32,8192]{1,0:T(8,128)(2,1)S(1)}, u32[]{:S(2)}, u32[]{:S(2)}) collective-permute-start(bf16[32,8192]{1,0:T(8,128)(2,1)S(1)} %add_convert_fusion.5), channel_id=1, source_target_pairs={{0,2},{2,4},{4,6},{6,7},{7,5},{5,3},{3,1},{1,0},{8,10},{10,12},{12... | collective-permute-start | bytes 1572872 | tf_op jit(solution)/shard_map/ppermute | solution.py:393
  189.9 26.7 %collective-permute-start.48 = (bf16[32,8192]{1,0:T(8,128)(2,1)S(1)}, bf16[32,8192]{1,0:T(8,128)(2,1)S(1)}, u32[]{:S(2)}, u32[]{:S(2)}) collective-permute-start(bf16[32,8192]{1,0:T(8,128)(2,1)S(1)} %add_convert_fusion.4), channel_id=1, source_target_pairs={{2,0},{4,2},{6,4},{7,6},{5,7},{3,5},{1,3},{0,1},{10,8},{12,10},{14... | collective-permute-start | bytes 1572872 | tf_op jit(solution)/shard_map/ppermute | solution.py:396
  201.0 21.9 %collective-permute-start.45 = (bf16[32,8192]{1,0:T(8,128)(2,1)S(1)}, bf16[32,8192]{1,0:T(8,128)(2,1)S(1)}, u32[]{:S(2)}, u32[]{:S(2)}) collective-permute-start(bf16[32,8192]{1,0:T(8,128)(2,1)S(1)} %add_convert_fusion.3), channel_id=1, source_target_pairs={{2,8},{4,10},{6,12},{7,14},{5,15},{3,13},{1,11},{0,9},{10,16},{12,... | collective-permute-start | bytes 1572872 | tf_op jit(solution)/shard_map/ppermute | solution.py:409
  201.2 18.7 %collective-permute-start.46 = (bf16[32,8192]{1,0:T(8,128)(2,1)S(1)}, bf16[32,8192]{1,0:T(8,128)(2,1)S(1)}, u32[]{:S(2)}, u32[]{:S(2)}) collective-permute-start(bf16[32,8192]{1,0:T(8,128)(2,1)S(1)} %add_convert_fusion.2), channel_id=1, source_target_pairs={{0,10},{2,12},{4,14},{6,15},{7,13},{5,11},{3,9},{1,8},{8,18},{10,2... | collective-permute-start | bytes 1572872 | tf_op jit(solution)/shard_map/ppermute | solution.py:406
  (50 other events, 699.5 us)

commit v8 on v6

--- a/solution.py
+++ b/solution.py
@@ -80,20 +80,6 @@
         cost_estimate=QUICK,
         name="total_of",
     )(*[value for group in groups for value in group])
-
-
-def finish(gate, text, own, arrivals):
-    rows, columns = text.shape
-    part_rows = rows // len(arrivals)
-    result = jnp.zeros((1, rows, columns), BF16)
-    for part, came in enumerate(arrivals):
-        place = slice(part * part_rows, (part + 1) * part_rows)
-        branch = own[place].astype(F32)
-        for value in came:
-            branch = branch + value.astype(F32)
-        part_out = (text[place].astype(F32) + jnp.tanh(gate[0]) * branch).astype(BF16)
-        result = lax.dynamic_update_slice(result, part_out[None], (0, part * part_rows, 0))
-    return result
 
 
 def project(places, feats, weight, order_len, first, blocks):
@@ -227,7 +213,11 @@
         out_shape=jax.ShapeDtypeStruct((rows, width), BF16),
         scratch_shapes=[pltpu.VMEM((rows, depth), BF16), pltpu.VMEM((rows, 1), F32)],
         compiler_params=params(),
-        cost_estimate=QUICK,
+        cost_estimate=pl.CostEstimate(
+            flops=2 * rows * depth * width,
+            bytes_accessed=2 * depth * (width + rows),
+            transcendentals=0,
+        ),
         name="query",
     )(*chunks, weight)
 
@@ -334,6 +324,8 @@
 
 
 def after(value, *others):
+    if not others:
+        return value
     return lax.optimization_barrier((value, *others))[0]
 
 
@@ -401,24 +393,23 @@
             value, "section", [(s, (s + 1) % section_count) for s in range(section_count)]
         )
 
-    def ring_sums(chains, hold=lambda hop, value: value, turn=None):
+    def ring_sums(chains, hold=lambda left, value: value, turn=()):
         running = [part(sign * distance) for part, distance, sign, _, _ in chains]
         for hop in range(far):
             for index, (part, distance, sign, move, last) in enumerate(chains):
                 left = distance - hop
                 if left == 1:
-                    running[index] = last(hold(hop, running[index]))
+                    running[index] = last(hold(left, running[index]))
                 elif left > 1:
-                    came = move(hold(hop, running[index]))
-                    if turn is not None:
-                        came = after(came, turn)
-                    turn = running[index] = add(came, part(sign * (left - 1)))
+                    came = after(move(hold(left, running[index])), *turn)
+                    running[index] = add(came, part(sign * (left - 1)))
+                    turn = [running[index]]
         return running
 
     def both_ways(part, distance_up, distance_down, last_up=up, last_down=down):
         return [
-            (part, distance_up, 1, up, last_up),
-            (part, distance_down, -1, down, last_down),
+            (part, distance_up, 1, up, last_up if distance_up == far else up),
+            (part, distance_down, -1, down, last_down if distance_down == far else down),
         ]
 
     text_own = text_state[0]
@@ -446,13 +437,15 @@
         )
     ]
 
-    def image_hold(hop, value):
-        if hop == 1:
-            return after(value, from_below[1], from_above[1], text_next)
-        return value
+    def image_hold(left, value):
+        return after(value, text_next) if left == 1 else value
 
     turns = [0, 3, 1, 2]
-    came = ring_sums([image_chains[turn] for turn in turns], image_hold)
+    came = ring_sums(
+        [image_chains[turn] for turn in turns],
+        image_hold,
+        turn=[gate_next, from_below[1], from_above[1]],
+    )
     came = [came[turns.index(index)] for index in range(4)]
     image_cols = total_of(
         [[image_parts[index_of[0]][half], *came[2 * half : 2 * half + 2]] for half in range(2)]
@@ -460,8 +453,10 @@
 
     text_round(image_cols)
     weight_query, weight_out = w_query[0], w_out[0]
-    near = [-1, 1]
-    near_queries = [query([from_below[1], from_above[1]], weight_query)]
+    queries = {
+        0: query([text_own], weight_query),
+        1: query([from_below[1], from_above[1]], weight_query),
+    }
 
     pieces = []
     moving = image_cols
@@ -477,26 +472,34 @@
                 [(s, (s + 2) % section_count) for s in range(section_count)],
             )
             if step == 0:
-                moving = after(moving, near_queries[0])
+                moving = after(moving, queries[0], queries[1])
 
     kv_part = key_values(meta, pieces, w_kv[0], mp_count, section_count, sharing)
 
-    for distance in range(3, far):
+    for distance in range(3, far - 1):
         text_round(*([kv_part[0]] if distance == 3 else []))
-    for distance in range(2, far):
-        near += [-distance, distance]
-        near_queries.append(query([from_below[distance], from_above[distance]], weight_query))
-
-    def kv_hold(hop, value):
-        if hop == far - 1:
-            return after(value, *from_below[3:], *from_above[3:])
-        return value
+    below, above = (after(value[-1], kv_part[0]) for value in (from_below, from_above))
+    low = slice(text_rows - cut, text_rows)
+    onward = [up(below[:cut]), down(above[low])]
+    sent, behind = [], []
+
+    def kv_hold(left, value):
+        sent.append(value)
+        if len(sent) == 4 and parts == 2:
+            behind.append(up(after(below[cut:], sent[2])))
+            behind.append(down(after(above[: text_rows - cut], sent[3])))
+        if left == min(2, far - 1):
+            return after(value, *onward)
+        return after(value, *behind) if left == 1 else value
 
     came = ring_sums(both_ways(lambda offset: kv_part[index_of[offset]], far, far - 1), kv_hold)
     kv_own = (
         kv_part[index_of[0]].astype(F32) + came[0].astype(F32) + came[1].astype(F32)
     ).astype(BF16)
-    kv_own = after(kv_own, gate_next, *near_queries)
+    if far > 2:
+        last_chunks = [onward[0], *behind, onward[1]]
+        queries[far - 1] = query(last_chunks, weight_query)
+        kv_own = after(kv_own, queries[far - 1])
     kv_pieces = [kv_own]
     for step in range(1, sharing):
         pairs = [
@@ -504,43 +507,31 @@
         ]
         kv_pieces.append(lax.ppermute(kv_own, "mp", pairs))
 
-    far_chunks = [up(after(from_below[-1], kv_own)[:cut])]
+    far_chunks = [up(after(onward[0], kv_own))]
     if parts == 2:
-        far_chunks.append(down(after(from_above[-1], kv_own)[cut:]))
-
-    def attend_to(offsets, queries, sizes):
-        return attend(
-            meta,
-            queries,
-            kv_pieces,
-            weight_out,
-            [index_of[offset] for offset in offsets],
-            sizes,
-            mp_count,
-        )
-
-    first, first_queries = near[-2:] + [0], [near_queries[-1], query([text_own], weight_query)]
-    rest, rest_queries = near[:-2], near_queries[:-1]
-    *first_part, own_part = attend_to(
-        first,
-        jnp.concatenate(first_queries, axis=0),
-        [cut] * (parts * (len(first) - 1)) + [text_rows],
-    )
-    far_part = attend_to(
-        [far], after(query(far_chunks, weight_query), own_part), [cut] * parts
-    )
-    rest_part = attend_to(
-        rest,
-        after(jnp.concatenate(rest_queries, axis=0), far_part[0]),
-        [cut] * (parts * len(rest)),
-    )
+        far_chunks.append(down(after(onward[1], kv_own)))
+
+    def attend_to(offsets, rows):
+        indices = [index_of[offset] for offset in offsets]
+        sizes = [cut] * (parts * len(offsets))
+        return attend(meta, rows, kv_pieces, weight_out, indices, sizes, mp_count)
+
+    first = [1 - far, far - 1]
+    first_part = attend_to(first, queries[far - 1])
+    rest = [0] + [sign * distance for distance in range(1, far - 1) for sign in (-1, 1)]
+    for distance in range(2, far - 1):
+        below = after(from_below[distance], first_part[0])
+        queries[distance] = query([below, from_above[distance]], weight_query)
+    rest_queries = jnp.concatenate([queries[distance] for distance in range(far - 1)], axis=0)
+    far_queries = after(query(far_chunks, weight_query), rest_queries, first_part[0])
+    far_part = attend_to([far], far_queries)
+    rest_part = attend_to(rest, after(rest_queries, far_part[0]))
     near_part = list(first_part) + list(rest_part)
     out_parts = {
-        offset: near_part[parts * i :][:parts] for i, offset in enumerate(first[:-1] + rest)
+        offset: near_part[parts * i :][:parts] for i, offset in enumerate(first + rest)
     }
     out_parts[far] = out_parts[-far] = far_part
 
-    own_next = to_next(own_part)
     branch_chains = [
         chain
         for part, distances in enumerate(reach)
@@ -551,13 +542,24 @@
             down_across,
         )
     ]
-
-    turns = [1, 2, 0, 3] if parts == 2 else [0, 1]
-    came = ring_sums([branch_chains[turn] for turn in turns], turn=own_next)
+    turns = [1, 2, 0, 3] if parts == 2 else [1, 0]
+    came = ring_sums([branch_chains[turn] for turn in turns])
     came = [came[turns.index(index)] for index in range(2 * parts)]
-    return finish(
-        gate_next, text_next, own_next, [came[2 * part : 2 * part + 2] for part in range(parts)]
+    near_came = [came[1], came[2]] if parts == 2 else [came[1]]
+    far_came = [came[0], came[3]] if parts == 2 else [came[0]]
+    own_next = to_next(
+        jnp.concatenate(
+            [add(out_parts[0][part], near_came[part]) for part in range(parts)], axis=0
+        )
     )
+    results = []
+    for part in range(parts):
+        place = slice(part * cut, (part + 1) * cut)
+        branch = own_next[place].astype(F32) + far_came[part].astype(F32)
+        results.append(
+            (text_next[place].astype(F32) + jnp.tanh(gate_next[0]) * branch).astype(BF16)
+        )
+    return jnp.concatenate(results, axis=0)[None]
 
 
 def solution(mesh):

time: 250 us -> 257 us (1.028)
  waiting for transfers between devices: 135 us -> 140 us
    ppermute x20 -> x22, waiting for transfers between devices: 84.8 us -> 61 us  [up(): return lax.ppermute(value, 'mp', up_pairs)]
    ppermute x19 -> x21, waiting for transfers between devices: 32.9 us -> 55.6 us  [down(): return lax.ppermute(value, 'mp', down_pairs)]
    ppermute x20 -> x22, starting transfers between devices: 14.9 us -> 20.5 us  [up(): return lax.ppermute(value, 'mp', up_pairs)]
    ppermute x2 -> x1, waiting for transfers between devices: 0.19 us -> 4.65 us  [up_across(): return lax.ppermute(value, ('section', 'mp'), across(up_pairs))]
    ppermute x1, waiting for transfers between devices: 0.01 us -> 3.47 us  [local(): kv_pieces.append(lax.ppermute(kv_own, 'mp', pairs))]
    ppermute x2 -> x1, waiting for transfers between devices: 12.1 us -> 10.6 us  [down_across(): return lax.ppermute(value, ('section', 'mp'), across(down_pairs))]
    ppermute x19 -> x21, starting transfers between devices: 27.3 us -> 26.3 us  [down(): return lax.ppermute(value, 'mp', down_pairs)]
  transfers between devices with their start and end apart: 50 -> 52, of which waited for: 26 -> 31; matrix products, arithmetic and copies ran while one was open for 3% -> 3% of each run, Pallas kernels for 21% -> 20%
where the time goes in v8:
time: 257 us
  waiting for transfers between devices  140 us (54%)
  starting transfers between devices  53.6 us (21%)
  Pallas kernels  52.1 us (20%)
  other arithmetic  7.36 us (3%)
    ppermute x22, waiting for transfers between devices, up(): return lax.ppermute(value, 'mp', up_pairs)  61 us
    ppermute x21, waiting for transfers between devices, down(): return lax.ppermute(value, 'mp', down_pairs)  55.6 us
    ppermute x21, starting transfers between devices, down(): return lax.ppermute(value, 'mp', down_pairs)  26.3 us
    ppermute x22, starting transfers between devices, up(): return lax.ppermute(value, 'mp', up_pairs)  20.5 us
    pallas_call x2, Pallas kernels, project(): pl.pallas_call(kernel, grid_spec=pltpu.PrefetchScalarGridSpec(num_scalar_...  17.2 us
    pallas_call x3, Pallas kernels, attend(): pl.pallas_call(kernel, grid_spec=pltpu.PrefetchScalarGridSpec(num_scalar_...  16.1 us
    pallas_call x5, Pallas kernels, query(): pl.pallas_call(kernel, grid=(width // wide,), in_specs=[pl.BlockSpec(chun...  14 us
    ppermute x1, waiting for transfers between devices, down_across(): return lax.ppermute(value, ('section', 'mp'), across(down_pairs))  10.6 us
  transfers between devices with their start and end apart: 52, of which 31 were waited for; matrix products, arithmetic and copies ran while one was open for 3% of the time, Pallas kernels for 20%

profile of v8, /device:TPU:0, one launch (start us, length us, event | category | flops | bytes accessed | tf_op | source)
XLA Modules:
  0.0 256.6 jit_solution(9846271889510219999)
XLA Ops:
  4.3 4.1 %project.3 = (bf16[160,1024]{1,0:T(8,128)(2,1)}, bf16[160,1024]{1,0:T(8,128)(2,1)}) custom-call(s32[10]{0:T(128)} %get-tuple-element.181.places_ref, bf16[320,960]{1,0:T(8,128)(2,1)} %feats_ref.3, bf16[960,8192]{1,0:T(8,128)(2,1)} %weight_ref.3), custom_call_target="tpu_custom_call" | custom-call | flops 629145600 | bytes 2621440 | tf_op jit(solution)/shard_map/project/pallas_call | solution.py:101
  10.4 13.2 %project.2 = (bf16[160,1024]{1,0:T(8,128)(2,1)}, bf16[160,1024]{1,0:T(8,128)(2,1)}, bf16[160,1024]{1,0:T(8,128)(2,1)}, bf16[160,1024]{1,0:T(8,128)(2,1)}, bf16[1...) custom-call(s32[10]{0:T(128)} %get-tuple-element.181.places_ref, ...), custom_call_target="tpu_custom_call" | custom-call | flops 4404019200 | bytes 18350080 | tf_op jit(solution)/shard_map/project/pallas_call | solution.py:101
  25.1 9.7 %collective-permute-done.4 = bf16[160,1024]{1,0:T(8,128)(2,1)S(1)} collective-permute-done((bf16[160,1024]{1,0:T(8,128)(2,1)}, bf16[160,1024]{1,0:T(8,128)(2,1)S(1)}, u32[]{:S(2)}, u32[]{:S(2)}) %collective-permute-start.4) | collective-permute-done | bytes 327712 | tf_op jit(solution)/shard_map/ppermute | solution.py:373
  41.2 4.9 %collective-permute-done.7 = bf16[160,1024]{1,0:T(8,128)(2,1)S(1)} collective-permute-done((bf16[160,1024]{1,0:T(8,128)(2,1)}, bf16[160,1024]{1,0:T(8,128)(2,1)S(1)}, u32[]{:S(2)}, u32[]{:S(2)}) %collective-permute-start.7) | collective-permute-done | bytes 327712 | tf_op jit(solution)/shard_map/ppermute | solution.py:376
  48.4 4.3 %collective-permute-done.5 = bf16[160,1024]{1,0:T(8,128)(2,1)S(1)} collective-permute-done((bf16[160,1024]{1,0:T(8,128)(2,1)S(1)}, bf16[160,1024]{1,0:T(8,128)(2,1)S(1)}, u32[]{:S(2)}, u32[]{:S(2)}) %collective-permute-start.5) | collective-permute-done | bytes 327712 | tf_op jit(solution)/shard_map/ppermute | solution.py:373
  55.1 5.0 %collective-permute-done.11 = bf16[160,1024]{1,0:T(8,128)(2,1)S(1)} collective-permute-done((bf16[160,1024]{1,0:T(8,128)(2,1)S(1)}, bf16[160,1024]{1,0:T(8,128)(2,1)S(1)}, u32[]{:S(2)}, u32[]{:S(2)}) %collective-permute-start.11) | collective-permute-done | bytes 327712 | tf_op jit(solution)/shard_map/ppermute | solution.py:376
  62.4 4.3 %collective-permute-done.9 = bf16[160,1024]{1,0:T(8,128)(2,1)S(1)} collective-permute-done((bf16[160,1024]{1,0:T(8,128)(2,1)S(1)}, bf16[160,1024]{1,0:T(8,128)(2,1)S(1)}, u32[]{:S(2)}, u32[]{:S(2)}) %collective-permute-start.9) | collective-permute-done | bytes 327712 | tf_op jit(solution)/shard_map/ppermute | solution.py:373
  69.3 4.5 %collective-permute-done.15.refs_4_ = bf16[160,1024]{1,0:T(8,128)(2,1)S(1)} collective-permute-done((bf16[160,1024]{1,0:T(8,128)(2,1)S(1)}, bf16[160,1024]{1,0:T(8,128)(2,1)S(1)}, u32[]{:S(2)}, u32[]{:S(2)}) %collective-permute-start.15) | collective-permute-done | bytes 327712 | tf_op jit(solution)/shard_map/ppermute | solution.py:373
  74.1 4.3 %collective-permute-done.13.refs_1_ = bf16[160,1024]{1,0:T(8,128)(2,1)S(1)} collective-permute-done((bf16[160,1024]{1,0:T(8,128)(2,1)S(1)}, bf16[160,1024]{1,0:T(8,128)(2,1)S(1)}, u32[]{:S(2)}, u32[]{:S(2)}) %collective-permute-start.13) | collective-permute-done | bytes 327712 | tf_op jit(solution)/shard_map/ppermute | solution.py:373
  88.6 4.9 %collective-permute-done.20.refs_2_ = bf16[320,1024]{1,0:T(8,128)(2,1)S(1)} collective-permute-done((bf16[320,1024]{1,0:T(8,128)(2,1)S(1)}, bf16[320,1024]{1,0:T(8,128)(2,1)S(1)}, u32[]{:S(2)}, u32[]{:S(2)}) %collective-permute-start.20) | collective-permute-done | bytes 655392 | tf_op jit(solution)/shard_map/ppermute | solution.py:469
  95.6 4.4 %key_values.1 = (bf16[256,256]{1,0:T(8,128)(2,1)S(1)}, bf16[256,256]{1,0:T(8,128)(2,1)S(1)}, bf16[256,256]{1,0:T(8,128)(2,1)S(1)}, bf16[256,256]{1,0:T(8,128)(2,...) custom-call(s32[18]{0:T(128)S(1)} %pad_add_fusion.meta_ref, ...), custom_call_target="tpu_custom_call" | custom-call | flops 1 | bytes 1 | tf_op jit(solution)/shard_map/key_values/pallas_call | solution.py:165
  105.3 15.1 %collective-permute-done.25.refs_1_ = bf16[64,8192]{1,0:T(8,128)(2,1)S(1)} collective-permute-done((bf16[64,8192]{1,0:T(8,128)(2,1)S(1)}, bf16[64,8192]{1,0:T(8,128)(2,1)S(1)}, u32[]{:S(2)}, u32[]{:S(2)}) %collective-permute-start.25) | collective-permute-done | bytes 1048608 | tf_op jit(solution)/shard_map/ppermute | solution.py:376
  128.1 7.2 %collective-permute-done.28.refs_3_ = bf16[32,8192]{1,0:T(8,128)(2,1)S(1)} collective-permute-done((bf16[32,8192]{1,0:T(8,128)(2,1)S(1)}, bf16[32,8192]{1,0:T(8,128)(2,1)S(1)}, u32[]{:S(2)}, u32[]{:S(2)}) %collective-permute-start.28) | collective-permute-done | bytes 524320 | tf_op jit(solution)/shard_map/ppermute | solution.py:376
  137.5 10.6 %collective-permute-done.31 = bf16[256,256]{1,0:T(8,128)(2,1)S(1)} collective-permute-done((bf16[256,256]{1,0:T(8,128)(2,1)S(1)}, bf16[256,256]{1,0:T(8,128)(2,1)S(1)}, u32[]{:S(2)}, u32[]{:S(2)}) %collective-permute-start.31) | collective-permute-done | bytes 131104 | tf_op jit(solution)/shard_map/ppermute | solution.py:376
  160.9 4.8 %attend.3 = (bf16[32,8192]{1,0:T(8,128)(2,1)S(1)}, bf16[32,8192]{1,0:T(8,128)(2,1)S(1)}, bf16[32,8192]{1,0:T(8,128)(2,1)S(1)}, bf16[32,8192]{1,0:T(8,128)(2,1)S(1)}) custom-call(s32[18]{0:T(128)S(1)} %pad_add_fusion.meta_ref, bf16[128,512]{1,0:T(8,128)(2,1)S(1)} %query.7.query_ref, bf16[256,256]{1,0:T(8,128)(2,1)S(1)} %add_convert_fusion.24.refs_0_, ...), custom_call_target="tpu_custom_call" | custom-call | flops 4294967296 | bytes 33554432 | tf_op jit(solution)/shard_map/attend/pallas_call | solution.py:298
  174.9 4.3 %attend.4 = (bf16[32,8192]{1,0:T(8,128)(2,1)S(1)}, bf16[32,8192]{1,0:T(8,128)(2,1)S(1)}) custom-call(s32[18]{0:T(128)S(1)} %pad_add_fusion.meta_ref, bf16[64,512]{1,0:T(8,128)(2,1)S(1)} %query.9.query_ref, bf16[256,256]{1,0:T(8,128)(2,1)S(1)} %add_convert_fusion.24.refs_0_, bf16[256,256]{1,0:T(8,128)(2,1)S(1)} %collective-permute-done.34.refs_1_, ...), custom_call_target="tpu_custom_call" | custom-call | flops 2147483648 | bytes 33554432 | tf_op jit(solution)/shard_map/attend/pallas_call | solution.py:298
  181.3 7.0 %attend.5 = (bf16[32,8192]{1,0:T(8,128)(2,1)S(1)}, bf16[32,8192]{1,0:T(8,128)(2,1)S(1)}, bf16[32,8192]{1,0:T(8,128)(2,1)S(1)}, bf16[32,8192]{1,0:T(8,128)(2,1)S(...) custom-call(s32[18]{0:T(128)S(1)} %pad_add_fusion.meta_ref, ...), custom_call_target="tpu_custom_call" | custom-call | flops 10737418240 | bytes 33554432 | tf_op jit(solution)/shard_map/attend/pallas_call | solution.py:298
  190.7 3.8 %collective-permute-done.40 = bf16[32,8192]{1,0:T(8,128)(2,1)S(1)} collective-permute-done((bf16[32,8192]{1,0:T(8,128)(2,1)S(1)}, bf16[32,8192]{1,0:T(8,128)(2,1)S(1)}, u32[]{:S(2)}, u32[]{:S(2)}) %collective-permute-start.40) | collective-permute-done | bytes 524320 | tf_op jit(solution)/shard_map/ppermute | solution.py:373
  197.0 9.3 %collective-permute-done.38 = bf16[32,8192]{1,0:T(8,128)(2,1)S(1)} collective-permute-done((bf16[32,8192]{1,0:T(8,128)(2,1)S(1)}, bf16[32,8192]{1,0:T(8,128)(2,1)S(1)}, u32[]{:S(2)}, u32[]{:S(2)}) %collective-permute-start.38) | collective-permute-done | bytes 524320 | tf_op jit(solution)/shard_map/ppermute | solution.py:376
  208.7 8.4 %collective-permute-done.46 = bf16[32,8192]{1,0:T(8,128)(2,1)S(1)} collective-permute-done((bf16[32,8192]{1,0:T(8,128)(2,1)S(1)}, bf16[32,8192]{1,0:T(8,128)(2,1)S(1)}, u32[]{:S(2)}, u32[]{:S(2)}) %collective-permute-start.46) | collective-permute-done | bytes 524320 | tf_op jit(solution)/shard_map/ppermute | solution.py:373
  219.4 8.8 %collective-permute-done.44 = bf16[32,8192]{1,0:T(8,128)(2,1)S(1)} collective-permute-done((bf16[32,8192]{1,0:T(8,128)(2,1)S(1)}, bf16[32,8192]{1,0:T(8,128)(2,1)S(1)}, u32[]{:S(2)}, u32[]{:S(2)}) %collective-permute-start.44) | collective-permute-done | bytes 524320 | tf_op jit(solution)/shard_map/ppermute | solution.py:373
  229.0 7.1 %collective-permute-done.47 = bf16[32,8192]{1,0:T(8,128)(2,1)S(1)} collective-permute-done((bf16[32,8192]{1,0:T(8,128)(2,1)S(1)}, bf16[32,8192]{1,0:T(8,128)(2,1)S(1)}, u32[]{:S(2)}, u32[]{:S(2)}) %collective-permute-start.47) | collective-permute-done | bytes 524320 | tf_op jit(solution)/shard_map/ppermute | solution.py:373
  239.8 10.6 %collective-permute-done.51 = bf16[32,8192]{1,0:T(8,128)(2,1)S(1)} collective-permute-done((bf16[32,8192]{1,0:T(8,128)(2,1)S(1)}, bf16[32,8192]{1,0:T(8,128)(2,1)S(1)}, u32[]{:S(2)}, u32[]{:S(2)}) %collective-permute-start.51) | collective-permute-done | bytes 524320 | tf_op jit(solution)/shard_map/ppermute | solution.py:389
  250.4 4.6 %collective-permute-done.49 = bf16[32,8192]{1,0:T(8,128)(2,1)S(1)} collective-permute-done((bf16[32,8192]{1,0:T(8,128)(2,1)S(1)}, bf16[32,8192]{1,0:T(8,128)(2,1)S(1)}, u32[]{:S(2)}, u32[]{:S(2)}) %collective-permute-start.49) | collective-permute-done | bytes 524320 | tf_op jit(solution)/shard_map/ppermute | solution.py:386
  (171 shorter events, 90.0 us)
Async XLA Ops:
  0.0 35.2 %collective-permute-start.3 = (bf16[64,8192]{1,0:T(8,128)(2,1)}, bf16[64,8192]{1,0:T(8,128)(2,1)S(1)}, u32[]{:S(2)}, u32[]{:S(2)}) collective-permute-start(bf16[64,8192]{1,0:T(8,128)(2,1)} %bitcast.21), channel_id=1, source_target_pairs={{2,0},{4,2},{6,4},{7,6},{5,7},{3,5},{1,3},{0,1},{10,8},{12,10},{14... | collective-permute-start | bytes 3145736 | tf_op jit(solution)/shard_map/ppermute | solution.py:376
  3.0 33.9 %collective-permute-start.2 = (bf16[64,8192]{1,0:T(8,128)(2,1)}, bf16[64,8192]{1,0:T(8,128)(2,1)S(1)}, u32[]{:S(2)}, u32[]{:S(2)}) collective-permute-start(bf16[64,8192]{1,0:T(8,128)(2,1)} %bitcast.22), channel_id=1, source_target_pairs={{0,2},{2,4},{4,6},{6,7},{7,5},{5,3},{3,1},{1,0},{8,10},{10,12},{12... | collective-permute-start | bytes 3145736 | tf_op jit(solution)/shard_map/ppermute | solution.py:373
  3.0 20.5 %collective-permute-start.1 = (f32[1]{0:T(128)}, f32[1]{0:T(128)}, u32[]{:S(2)}, u32[]{:S(2)}) collective-permute-start(f32[1]{0:T(128)} %param.16), channel_id=1, source_target_pairs={{0,8},{8,16},{16,24},{24,0},{1,9},{9,17},{17,25},{25,1},{2,10},{10... | collective-permute-start | bytes 20 | tf_op jit(solution)/shard_map/ppermute | solution.py:392
  8.3 26.5 %collective-permute-start.4 = (bf16[160,1024]{1,0:T(8,128)(2,1)}, bf16[160,1024]{1,0:T(8,128)(2,1)S(1)}, u32[]{:S(2)}, u32[]{:S(2)}) collective-permute-start(bf16[160,1024]{1,0:T(8,128)(2,1)} %get-tuple-element.90), channel_id=1, source_target_pairs={{0,2},{2,4},{4,6},{6,7},{7,5},{5,3},{3,1},{1,0},{8,10},{10,12},{12... | collective-permute-start | bytes 983048 | tf_op jit(solution)/shard_map/ppermute | solution.py:373
  10.4 28.0 %collective-permute-start.8 = (bf16[160,1024]{1,0:T(8,128)(2,1)}, bf16[160,1024]{1,0:T(8,128)(2,1)S(1)}, u32[]{:S(2)}, u32[]{:S(2)}) collective-permute-start(bf16[160,1024]{1,0:T(8,128)(2,1)} %get-tuple-element.95), channel_id=1, source_target_pairs={{2,0},{4,2},{6,4},{7,6},{5,7},{3,5},{1,3},{0,1},{10,8},{12,10},{14... | collective-permute-start | bytes 983048 | tf_op jit(solution)/shard_map/ppermute | solution.py:376
  23.6 36.7 %collective-permute-start = (bf16[64,8192]{1,0:T(8,128)(2,1)S(1)}, bf16[64,8192]{1,0:T(8,128)(2,1)S(1)}, u32[]{:S(2)}, u32[]{:S(2)}) collective-permute-start(bf16[64,8192]{1,0:T(8,128)(2,1)S(1)} %bitcast.23), channel_id=1, source_target_pairs={{0,8},{8,16},{16,24},{24,0},{1,9},{9,17},{17,25},{25,1},{2,10},{10... | collective-permute-start | bytes 3145736 | tf_op jit(solution)/shard_map/ppermute | solution.py:392
  81.0 22.3 %collective-permute-start.18 = (bf16[64,8192]{1,0:T(8,128)(2,1)S(1)}, bf16[64,8192]{1,0:T(8,128)(2,1)S(1)}, u32[]{:S(2)}, u32[]{:S(2)}) collective-permute-start(bf16[64,8192]{1,0:T(8,128)(2,1)S(1)} %collective-permute-done.2.refs_0_), channel_id=1, source_target_pairs={{0,2},{2,4},{4,6},{6,7},{7,5},{5,3},{3,1},{1,0},{8,10},{10,12},{12... | collective-permute-start | bytes 3145736 | tf_op jit(solution)/shard_map/ppermute | solution.py:373
  94.4 26.0 %collective-permute-start.25 = (bf16[64,8192]{1,0:T(8,128)(2,1)S(1)}, bf16[64,8192]{1,0:T(8,128)(2,1)S(1)}, u32[]{:S(2)}, u32[]{:S(2)}) collective-permute-start(bf16[64,8192]{1,0:T(8,128)(2,1)S(1)} %collective-permute-done.3.refs_1_), channel_id=1, source_target_pairs={{2,0},{4,2},{6,4},{7,6},{5,7},{3,5},{1,3},{0,1},{10,8},{12,10},{14... | collective-permute-start | bytes 3145736 | tf_op jit(solution)/shard_map/ppermute | solution.py:376
  100.0 23.1 %collective-permute-start.26 = (bf16[256,256]{1,0:T(8,128)(2,1)S(1)}, bf16[256,256]{1,0:T(8,128)(2,1)S(1)}, u32[]{:S(2)}, u32[]{:S(2)}) collective-permute-start(bf16[256,256]{1,0:T(8,128)(2,1)S(1)} %get-tuple-element.127), channel_id=1, source_target_pairs={{2,0},{4,2},{6,4},{7,6},{5,7},{3,5},{1,3},{0,1},{10,8},{12,10},{14... | collective-permute-start | bytes 393224 | tf_op jit(solution)/shard_map/ppermute | solution.py:376
  101.6 20.0 %collective-permute-start.23 = (bf16[256,256]{1,0:T(8,128)(2,1)S(1)}, bf16[256,256]{1,0:T(8,128)(2,1)S(1)}, u32[]{:S(2)}, u32[]{:S(2)}) collective-permute-start(bf16[256,256]{1,0:T(8,128)(2,1)S(1)} %get-tuple-element.121), channel_id=1, source_target_pairs={{0,2},{2,4},{4,6},{6,7},{7,5},{5,3},{3,1},{1,0},{8,10},{10,12},{12... | collective-permute-start | bytes 393224 | tf_op jit(solution)/shard_map/ppermute | solution.py:373
  103.4 24.7 %collective-permute-start.22 = (bf16[32,8192]{1,0:T(8,128)(2,1)S(1)}, bf16[32,8192]{1,0:T(8,128)(2,1)S(1)}, u32[]{:S(2)}, u32[]{:S(2)}) collective-permute-start(bf16[32,8192]{1,0:T(8,128)(2,1)S(1)} %get-tuple-element.180), channel_id=1, source_target_pairs={{0,2},{2,4},{4,6},{6,7},{7,5},{5,3},{3,1},{1,0},{8,10},{10,12},{12... | collective-permute-start | bytes 1572872 | tf_op jit(solution)/shard_map/ppermute | solution.py:373
  123.1 25.0 %collective-permute-start.24 = (bf16[32,8192]{1,0:T(8,128)(2,1)S(1)}, bf16[32,8192]{1,0:T(8,128)(2,1)S(1)}, u32[]{:S(2)}, u32[]{:S(2)}) collective-permute-start(bf16[32,8192]{1,0:T(8,128)(2,1)S(1)} %get-tuple-element.124), channel_id=1, source_target_pairs={{0,2},{2,4},{4,6},{6,7},{7,5},{5,3},{3,1},{1,0},{8,10},{10,12},{12... | collective-permute-start | bytes 1572872 | tf_op jit(solution)/shard_map/ppermute | solution.py:373
  124.2 23.9 %collective-permute-start.27 = (bf16[32,8192]{1,0:T(8,128)(2,1)S(1)}, bf16[32,8192]{1,0:T(8,128)(2,1)S(1)}, u32[]{:S(2)}, u32[]{:S(2)}) collective-permute-start(bf16[32,8192]{1,0:T(8,128)(2,1)S(1)} %get-tuple-element.130), channel_id=1, source_target_pairs={{2,0},{4,2},{6,4},{7,6},{5,7},{3,5},{1,3},{0,1},{10,8},{12,10},{14... | collective-permute-start | bytes 1572872 | tf_op jit(solution)/shard_map/ppermute | solution.py:376
  165.7 22.6 %collective-permute-start.37 = (bf16[32,8192]{1,0:T(8,128)(2,1)S(1)}, bf16[32,8192]{1,0:T(8,128)(2,1)S(1)}, u32[]{:S(2)}, u32[]{:S(2)}) collective-permute-start(bf16[32,8192]{1,0:T(8,128)(2,1)S(1)} %get-tuple-element.143), channel_id=1, source_target_pairs={{2,0},{4,2},{6,4},{7,6},{5,7},{3,5},{1,3},{0,1},{10,8},{12,10},{14... | collective-permute-start | bytes 1572872 | tf_op jit(solution)/shard_map/ppermute | solution.py:376
  166.7 22.7 %collective-permute-start.41 = (bf16[32,8192]{1,0:T(8,128)(2,1)S(1)}, bf16[32,8192]{1,0:T(8,128)(2,1)S(1)}, u32[]{:S(2)}, u32[]{:S(2)}) collective-permute-start(bf16[32,8192]{1,0:T(8,128)(2,1)S(1)} %get-tuple-element.153), channel_id=1, source_target_pairs={{0,2},{2,4},{4,6},{6,7},{7,5},{5,3},{3,1},{1,0},{8,10},{10,12},{12... | collective-permute-start | bytes 1572872 | tf_op jit(solution)/shard_map/ppermute | solution.py:373
  189.6 18.1 %collective-permute-start.43 = (bf16[32,8192]{1,0:T(8,128)(2,1)S(1)}, bf16[32,8192]{1,0:T(8,128)(2,1)S(1)}, u32[]{:S(2)}, u32[]{:S(2)}) collective-permute-start(bf16[32,8192]{1,0:T(8,128)(2,1)S(1)} %add_convert_fusion.12), channel_id=1, source_target_pairs={{0,2},{2,4},{4,6},{6,7},{7,5},{5,3},{3,1},{1,0},{8,10},{10,12},{12... | collective-permute-start | bytes 1572872 | tf_op jit(solution)/shard_map/ppermute | solution.py:373
  194.7 22.3 %collective-permute-start.46 = (bf16[32,8192]{1,0:T(8,128)(2,1)S(1)}, bf16[32,8192]{1,0:T(8,128)(2,1)S(1)}, u32[]{:S(2)}, u32[]{:S(2)}) collective-permute-start(bf16[32,8192]{1,0:T(8,128)(2,1)S(1)} %add_convert_fusion.11), channel_id=1, source_target_pairs={{0,2},{2,4},{4,6},{6,7},{7,5},{5,3},{3,1},{1,0},{8,10},{10,12},{12... | collective-permute-start | bytes 1572872 | tf_op jit(solution)/shard_map/ppermute | solution.py:373
  195.2 22.3 %collective-permute-start.48 = (bf16[32,8192]{1,0:T(8,128)(2,1)S(1)}, bf16[32,8192]{1,0:T(8,128)(2,1)S(1)}, u32[]{:S(2)}, u32[]{:S(2)}) collective-permute-start(bf16[32,8192]{1,0:T(8,128)(2,1)S(1)} %add_convert_fusion.10), channel_id=1, source_target_pairs={{2,0},{4,2},{6,4},{7,6},{5,7},{3,5},{1,3},{0,1},{10,8},{12,10},{14... | collective-permute-start | bytes 1572872 | tf_op jit(solution)/shard_map/ppermute | solution.py:376
  206.4 22.3 %collective-permute-start.42 = (bf16[32,8192]{1,0:T(8,128)(2,1)S(1)}, bf16[32,8192]{1,0:T(8,128)(2,1)S(1)}, u32[]{:S(2)}, u32[]{:S(2)}) collective-permute-start(bf16[32,8192]{1,0:T(8,128)(2,1)S(1)} %add_convert_fusion.9), channel_id=1, source_target_pairs={{2,0},{4,2},{6,4},{7,6},{5,7},{3,5},{1,3},{0,1},{10,8},{12,10},{14... | collective-permute-start | bytes 1572872 | tf_op jit(solution)/shard_map/ppermute | solution.py:376
  207.8 20.5 %collective-permute-start.44 = (bf16[32,8192]{1,0:T(8,128)(2,1)S(1)}, bf16[32,8192]{1,0:T(8,128)(2,1)S(1)}, u32[]{:S(2)}, u32[]{:S(2)}) collective-permute-start(bf16[32,8192]{1,0:T(8,128)(2,1)S(1)} %add_convert_fusion.7), channel_id=1, source_target_pairs={{0,2},{2,4},{4,6},{6,7},{7,5},{5,3},{3,1},{1,0},{8,10},{10,12},{12... | collective-permute-start | bytes 1572872 | tf_op jit(solution)/shard_map/ppermute | solution.py:373
  217.2 19.0 %collective-permute-start.47 = (bf16[32,8192]{1,0:T(8,128)(2,1)S(1)}, bf16[32,8192]{1,0:T(8,128)(2,1)S(1)}, u32[]{:S(2)}, u32[]{:S(2)}) collective-permute-start(bf16[32,8192]{1,0:T(8,128)(2,1)S(1)} %add_convert_fusion.5), channel_id=1, source_target_pairs={{0,2},{2,4},{4,6},{6,7},{7,5},{5,3},{3,1},{1,0},{8,10},{10,12},{12... | collective-permute-start | bytes 1572872 | tf_op jit(solution)/shard_map/ppermute | solution.py:373
  217.6 18.6 %collective-permute-start.50 = (bf16[32,8192]{1,0:T(8,128)(2,1)S(1)}, bf16[32,8192]{1,0:T(8,128)(2,1)S(1)}, u32[]{:S(2)}, u32[]{:S(2)}) collective-permute-start(bf16[32,8192]{1,0:T(8,128)(2,1)S(1)} %add_convert_fusion.4), channel_id=1, source_target_pairs={{2,0},{4,2},{6,4},{7,6},{5,7},{3,5},{1,3},{0,1},{10,8},{12,10},{14... | collective-permute-start | bytes 1572872 | tf_op jit(solution)/shard_map/ppermute | solution.py:376
  228.9 26.1 %collective-permute-start.45 = (bf16[64,8192]{1,0:T(8,128)(2,1)S(1)}, bf16[64,8192]{1,0:T(8,128)(2,1)S(1)}, u32[]{:S(2)}, u32[]{:S(2)}) collective-permute-start(bf16[64,8192]{1,0:T(8,128)(2,1)S(1)} %pad_maximum_fusion), channel_id=1, source_target_pairs={{0,8},{8,16},{16,24},{24,0},{1,9},{9,17},{17,25},{25,1},{2,10},{10... | collective-permute-start | bytes 3145736 | tf_op jit(solution)/shard_map/ppermute | solution.py:392
  236.5 18.6 %collective-permute-start.49 = (bf16[32,8192]{1,0:T(8,128)(2,1)S(1)}, bf16[32,8192]{1,0:T(8,128)(2,1)S(1)}, u32[]{:S(2)}, u32[]{:S(2)}) collective-permute-start(bf16[32,8192]{1,0:T(8,128)(2,1)S(1)} %add_convert_fusion.3), channel_id=1, source_target_pairs={{0,10},{2,12},{4,14},{6,15},{7,13},{5,11},{3,9},{1,8},{8,18},{10,2... | collective-permute-start | bytes 1572872 | tf_op jit(solution)/shard_map/ppermute | solution.py:386
  (46 other events, 681.2 us)

commit v9 on v8

--- a/solution.py
+++ b/solution.py
@@ -222,7 +222,7 @@
     )(*chunks, weight)
 
 
-def attend(meta, queries, kv_pieces, weight, indices, sizes, order_len):
+def attend(meta, queries, kv_pieces, weight, indices, sizes, shard_rows, order_len):
     text_rows = queries.shape[0] // len(indices)
     rows, width = queries.shape
     heads = width // HD
@@ -258,7 +258,7 @@
                 key_ref[pl.ds(row, kv_rows), :] = keys.astype(BF16)
                 value_ref[pl.ds(row, kv_rows), :] = kv_refs[piece][:, HD:]
             for place, index in enumerate(indices):
-                sample = meta_ref[index] * text_rows // TXT
+                sample = meta_ref[index] * shard_rows // TXT
                 slots = pl.ds(pl.multiple_of(sample * BLOCK, BLOCK), BLOCK)
                 live = TT * meta_ref[order_len + 2 + SAMP_SECTION + sample]
                 first = place * text_rows
@@ -408,8 +408,8 @@
 
     def both_ways(part, distance_up, distance_down, last_up=up, last_down=down):
         return [
-            (part, distance_up, 1, up, last_up if distance_up == far else up),
-            (part, distance_down, -1, down, last_down if distance_down == far else down),
+            (part, distance_up, 1, up, last_up),
+            (part, distance_down, -1, down, last_down),
         ]
 
     text_own = text_state[0]
@@ -481,25 +481,22 @@
     below, above = (after(value[-1], kv_part[0]) for value in (from_below, from_above))
     low = slice(text_rows - cut, text_rows)
     onward = [up(below[:cut]), down(above[low])]
-    sent, behind = [], []
+    far_chunks = [up(onward[0])]
+    if parts == 2:
+        far_chunks.append(down(onward[1]))
 
     def kv_hold(left, value):
-        sent.append(value)
-        if len(sent) == 4 and parts == 2:
-            behind.append(up(after(below[cut:], sent[2])))
-            behind.append(down(after(above[: text_rows - cut], sent[3])))
-        if left == min(2, far - 1):
-            return after(value, *onward)
-        return after(value, *behind) if left == 1 else value
-
-    came = ring_sums(both_ways(lambda offset: kv_part[index_of[offset]], far, far - 1), kv_hold)
+        return after(value, *onward) if left == min(2, far - 1) else value
+
+    came = ring_sums(
+        both_ways(lambda offset: kv_part[index_of[offset]], far, far - 1),
+        kv_hold,
+        turn=[from_below[2], from_above[2]] if far > 2 else [],
+    )
     kv_own = (
         kv_part[index_of[0]].astype(F32) + came[0].astype(F32) + came[1].astype(F32)
     ).astype(BF16)
-    if far > 2:
-        last_chunks = [onward[0], *behind, onward[1]]
-        queries[far - 1] = query(last_chunks, weight_query)
-        kv_own = after(kv_own, queries[far - 1])
+    kv_own = after(kv_own, *far_chunks)
     kv_pieces = [kv_own]
     for step in range(1, sharing):
         pairs = [
@@ -507,30 +504,37 @@
         ]
         kv_pieces.append(lax.ppermute(kv_own, "mp", pairs))
 
-    far_chunks = [up(after(onward[0], kv_own))]
+    behind = []
     if parts == 2:
-        far_chunks.append(down(after(onward[1], kv_own)))
-
-    def attend_to(offsets, rows):
+        behind = [up(after(below, kv_own)[cut:]), down(after(above, kv_own)[:cut])]
+
+    def attend_to(offsets, rows, sizes):
         indices = [index_of[offset] for offset in offsets]
-        sizes = [cut] * (parts * len(offsets))
-        return attend(meta, rows, kv_pieces, weight_out, indices, sizes, mp_count)
-
-    first = [1 - far, far - 1]
-    first_part = attend_to(first, queries[far - 1])
-    rest = [0] + [sign * distance for distance in range(1, far - 1) for sign in (-1, 1)]
-    for distance in range(2, far - 1):
-        below = after(from_below[distance], first_part[0])
-        queries[distance] = query([below, from_above[distance]], weight_query)
-    rest_queries = jnp.concatenate([queries[distance] for distance in range(far - 1)], axis=0)
-    far_queries = after(query(far_chunks, weight_query), rest_queries, first_part[0])
-    far_part = attend_to([far], far_queries)
-    rest_part = attend_to(rest, after(rest_queries, far_part[0]))
-    near_part = list(first_part) + list(rest_part)
-    out_parts = {
-        offset: near_part[parts * i :][:parts] for i, offset in enumerate(first + rest)
-    }
-    out_parts[far] = out_parts[-far] = far_part
+        return attend(meta, rows, kv_pieces, weight_out, indices, sizes, text_rows, mp_count)
+
+    last = far - 1
+    near = [sign * distance for distance in range(1, last) for sign in (-1, 1)]
+    out_parts = {offset: [None] * parts for offset in [last, -last]}
+    first = [far] * parts + [-last, last]
+    first_queries = query(far_chunks + onward, weight_query)
+    first_part = attend_to(first, first_queries, [cut] * len(first))
+    out_parts[far] = out_parts[-far] = first_part[:parts]
+    out_parts[-last][0], out_parts[last][parts - 1] = first_part[parts:]
+    ready = first_part[0]
+    for distance in range(2, last):
+        rows = [after(from_below[distance], ready), from_above[distance]]
+        queries[distance] = query(rows, weight_query)
+    rest_queries = jnp.concatenate([queries[distance] for distance in range(last)], axis=0)
+    if parts == 2:
+        behind_queries = after(query(behind, weight_query), rest_queries, ready)
+        behind_part = attend_to([-last, last], behind_queries, [cut] * 2)
+        out_parts[-last][1], out_parts[last][0] = behind_part
+        ready = behind_part[0]
+    sizes = [text_rows] + [cut] * (parts * len(near))
+    own_part, *near_part = attend_to([0] + near, after(rest_queries, ready), sizes)
+    for index, offset in enumerate(near):
+        out_parts[offset] = near_part[parts * index :][:parts]
+    own_next = to_next(own_part)
 
     branch_chains = [
         chain
@@ -542,20 +546,21 @@
             down_across,
         )
     ]
-    turns = [1, 2, 0, 3] if parts == 2 else [1, 0]
-    came = ring_sums([branch_chains[turn] for turn in turns])
+
+    def branch_hold(left, value):
+        if left == 1:
+            return after(value, own_next)
+        return after(value, *behind) if left == last else value
+
+    turns = [0, 3, 1, 2] if parts == 2 else [0, 1]
+    came = ring_sums([branch_chains[turn] for turn in turns], branch_hold)
     came = [came[turns.index(index)] for index in range(2 * parts)]
-    near_came = [came[1], came[2]] if parts == 2 else [came[1]]
-    far_came = [came[0], came[3]] if parts == 2 else [came[0]]
-    own_next = to_next(
-        jnp.concatenate(
-            [add(out_parts[0][part], near_came[part]) for part in range(parts)], axis=0
-        )
-    )
     results = []
     for part in range(parts):
         place = slice(part * cut, (part + 1) * cut)
-        branch = own_next[place].astype(F32) + far_came[part].astype(F32)
+        branch = own_next[place].astype(F32)
+        for value in came[2 * part : 2 * part + 2]:
+            branch = branch + value.astype(F32)
         results.append(
             (text_next[place].astype(F32) + jnp.tanh(gate_next[0]) * branch).astype(BF16)
         )

time: 257 us -> 238 us (0.926)
  waiting for transfers between devices: 140 us -> 126 us
  starting transfers between devices: 53.6 us -> 48.9 us
    ppermute x21 -> x20, waiting for transfers between devices: 55.6 us -> 31.8 us  [down(): return lax.ppermute(value, 'mp', down_pairs)]
    ppermute x22 -> x21, waiting for transfers between devices: 61 us -> 72.3 us  [up(): return lax.ppermute(value, 'mp', up_pairs)]
    ppermute x1 -> x2, waiting for transfers between devices: 4.65 us -> 9.42 us  [up_across(): return lax.ppermute(value, ('section', 'mp'), across(up_pairs))]
    ppermute x1 -> x2, waiting for transfers between devices: 10.6 us -> 6.11 us  [down_across(): return lax.ppermute(value, ('section', 'mp'), across(down_pairs))]
    ppermute x21 -> x20, starting transfers between devices: 26.3 us -> 22.3 us  [down(): return lax.ppermute(value, 'mp', down_pairs)]
    ppermute x1, waiting for transfers between devices: 3.47 us -> 0.6 us  [local(): kv_pieces.append(lax.ppermute(kv_own, 'mp', pairs))]
    ppermute x22 -> x21, starting transfers between devices: 20.5 us -> 22.2 us  [up(): return lax.ppermute(value, 'mp', up_pairs)]
  transfers between devices with their start and end apart: 52 -> 52, of which waited for: 31 -> 26; matrix products, arithmetic and copies ran while one was open for 3% -> 3% of each run, Pallas kernels for 20% -> 22%
where the time goes in v9:
time: 238 us
  waiting for transfers between devices  126 us (53%)
  Pallas kernels  52.7 us (22%)
  starting transfers between devices  48.9 us (21%)
  other arithmetic  7.28 us (3%)
    ppermute x21, waiting for transfers between devices, up(): return lax.ppermute(value, 'mp', up_pairs)  72.3 us
    ppermute x20, waiting for transfers between devices, down(): return lax.ppermute(value, 'mp', down_pairs)  31.8 us
    ppermute x20, starting transfers between devices, down(): return lax.ppermute(value, 'mp', down_pairs)  22.3 us
    ppermute x21, starting transfers between devices, up(): return lax.ppermute(value, 'mp', up_pairs)  22.2 us
    pallas_call x2, Pallas kernels, project(): pl.pallas_call(kernel, grid_spec=pltpu.PrefetchScalarGridSpec(num_scalar_...  17.2 us
    pallas_call x3, Pallas kernels, attend(): pl.pallas_call(kernel, grid_spec=pltpu.PrefetchScalarGridSpec(num_scalar_...  16.8 us
    pallas_call x5, Pallas kernels, query(): pl.pallas_call(kernel, grid=(width // wide,), in_specs=[pl.BlockSpec(chun...  14 us
    ppermute x2, waiting for transfers between devices, up_across(): return lax.ppermute(value, ('section', 'mp'), across(up_pairs))  9.42 us
  transfers between devices with their start and end apart: 52, of which 26 were waited for; matrix products, arithmetic and copies ran while one was open for 3% of the time, Pallas kernels for 22%

profile of v9, /device:TPU:0, one launch (start us, length us, event | category | flops | bytes accessed | tf_op | source)
XLA Modules:
  0.0 237.9 jit_solution(14119915596598047431)
XLA Ops:
  0.0 3.0 %collective-permute-start.3 = (bf16[64,8192]{1,0:T(8,128)(2,1)}, bf16[64,8192]{1,0:T(8,128)(2,1)S(1)}, u32[]{:S(2)}, u32[]{:S(2)}) collective-permute-start(bf16[64,8192]{1,0:T(8,128)(2,1)} %bitcast.21), channel_id=1, source_target_pairs={{2,0},{4,2},{6,4},{7,6},{5,7},{3,5},{1,3},{0,1},{10,8},{12,10},{14... | collective-permute-start | bytes 3145736 | tf_op jit(solution)/shard_map/ppermute | solution.py:376
  4.3 4.0 %project.3 = (bf16[160,1024]{1,0:T(8,128)(2,1)}, bf16[160,1024]{1,0:T(8,128)(2,1)}) custom-call(s32[10]{0:T(128)} %get-tuple-element.185.places_ref, bf16[320,960]{1,0:T(8,128)(2,1)} %feats_ref.3, bf16[960,8192]{1,0:T(8,128)(2,1)} %weight_ref.3), custom_call_target="tpu_custom_call" | custom-call | flops 629145600 | bytes 2621440 | tf_op jit(solution)/shard_map/project/pallas_call | solution.py:101
  10.4 13.2 %project.2 = (bf16[160,1024]{1,0:T(8,128)(2,1)}, bf16[160,1024]{1,0:T(8,128)(2,1)}, bf16[160,1024]{1,0:T(8,128)(2,1)}, bf16[160,1024]{1,0:T(8,128)(2,1)}, bf16[1...) custom-call(s32[10]{0:T(128)} %get-tuple-element.185.places_ref, ...), custom_call_target="tpu_custom_call" | custom-call | flops 4404019200 | bytes 18350080 | tf_op jit(solution)/shard_map/project/pallas_call | solution.py:101
  25.2 9.7 %collective-permute-done.4 = bf16[160,1024]{1,0:T(8,128)(2,1)S(1)} collective-permute-done((bf16[160,1024]{1,0:T(8,128)(2,1)}, bf16[160,1024]{1,0:T(8,128)(2,1)S(1)}, u32[]{:S(2)}, u32[]{:S(2)}) %collective-permute-start.4) | collective-permute-done | bytes 327712 | tf_op jit(solution)/shard_map/ppermute | solution.py:373
  41.2 4.9 %collective-permute-done.7 = bf16[160,1024]{1,0:T(8,128)(2,1)S(1)} collective-permute-done((bf16[160,1024]{1,0:T(8,128)(2,1)}, bf16[160,1024]{1,0:T(8,128)(2,1)S(1)}, u32[]{:S(2)}, u32[]{:S(2)}) %collective-permute-start.7) | collective-permute-done | bytes 327712 | tf_op jit(solution)/shard_map/ppermute | solution.py:376
  48.4 4.3 %collective-permute-done.5 = bf16[160,1024]{1,0:T(8,128)(2,1)S(1)} collective-permute-done((bf16[160,1024]{1,0:T(8,128)(2,1)S(1)}, bf16[160,1024]{1,0:T(8,128)(2,1)S(1)}, u32[]{:S(2)}, u32[]{:S(2)}) %collective-permute-start.5) | collective-permute-done | bytes 327712 | tf_op jit(solution)/shard_map/ppermute | solution.py:373
  55.1 5.0 %collective-permute-done.11 = bf16[160,1024]{1,0:T(8,128)(2,1)S(1)} collective-permute-done((bf16[160,1024]{1,0:T(8,128)(2,1)S(1)}, bf16[160,1024]{1,0:T(8,128)(2,1)S(1)}, u32[]{:S(2)}, u32[]{:S(2)}) %collective-permute-start.11) | collective-permute-done | bytes 327712 | tf_op jit(solution)/shard_map/ppermute | solution.py:376
  62.4 4.3 %collective-permute-done.9 = bf16[160,1024]{1,0:T(8,128)(2,1)S(1)} collective-permute-done((bf16[160,1024]{1,0:T(8,128)(2,1)S(1)}, bf16[160,1024]{1,0:T(8,128)(2,1)S(1)}, u32[]{:S(2)}, u32[]{:S(2)}) %collective-permute-start.9) | collective-permute-done | bytes 327712 | tf_op jit(solution)/shard_map/ppermute | solution.py:373
  69.3 4.5 %collective-permute-done.15.refs_4_ = bf16[160,1024]{1,0:T(8,128)(2,1)S(1)} collective-permute-done((bf16[160,1024]{1,0:T(8,128)(2,1)S(1)}, bf16[160,1024]{1,0:T(8,128)(2,1)S(1)}, u32[]{:S(2)}, u32[]{:S(2)}) %collective-permute-start.15) | collective-permute-done | bytes 327712 | tf_op jit(solution)/shard_map/ppermute | solution.py:373
  74.1 4.3 %collective-permute-done.13.refs_1_ = bf16[160,1024]{1,0:T(8,128)(2,1)S(1)} collective-permute-done((bf16[160,1024]{1,0:T(8,128)(2,1)S(1)}, bf16[160,1024]{1,0:T(8,128)(2,1)S(1)}, u32[]{:S(2)}, u32[]{:S(2)}) %collective-permute-start.13) | collective-permute-done | bytes 327712 | tf_op jit(solution)/shard_map/ppermute | solution.py:373
  89.1 4.4 %collective-permute-done.20.refs_2_ = bf16[320,1024]{1,0:T(8,128)(2,1)S(1)} collective-permute-done((bf16[320,1024]{1,0:T(8,128)(2,1)S(1)}, bf16[320,1024]{1,0:T(8,128)(2,1)S(1)}, u32[]{:S(2)}, u32[]{:S(2)}) %collective-permute-start.20) | collective-permute-done | bytes 655392 | tf_op jit(solution)/shard_map/ppermute | solution.py:469
  95.6 4.4 %key_values.1 = (bf16[256,256]{1,0:T(8,128)(2,1)S(1)}, bf16[256,256]{1,0:T(8,128)(2,1)S(1)}, bf16[256,256]{1,0:T(8,128)(2,1)S(1)}, bf16[256,256]{1,0:T(8,128)(2,...) custom-call(s32[18]{0:T(128)S(1)} %pad_add_fusion.meta_ref, ...), custom_call_target="tpu_custom_call" | custom-call | flops 1 | bytes 1 | tf_op jit(solution)/shard_map/key_values/pallas_call | solution.py:165
  101.2 8.3 %collective-permute-done.18.refs_0_ = bf16[64,8192]{1,0:T(8,128)(2,1)S(1)} collective-permute-done((bf16[64,8192]{1,0:T(8,128)(2,1)S(1)}, bf16[64,8192]{1,0:T(8,128)(2,1)S(1)}, u32[]{:S(2)}, u32[]{:S(2)}) %collective-permute-start.18) | collective-permute-done | bytes 1048608 | tf_op jit(solution)/shard_map/ppermute | solution.py:373
  114.2 8.9 %collective-permute-done.29 = bf16[256,256]{1,0:T(8,128)(2,1)S(1)} collective-permute-done((bf16[256,256]{1,0:T(8,128)(2,1)S(1)}, bf16[256,256]{1,0:T(8,128)(2,1)S(1)}, u32[]{:S(2)}, u32[]{:S(2)}) %collective-permute-start.29) | collective-permute-done | bytes 131104 | tf_op jit(solution)/shard_map/ppermute | solution.py:376
  133.7 9.0 %collective-permute-done.32 = bf16[256,256]{1,0:T(8,128)(2,1)S(1)} collective-permute-done((bf16[256,256]{1,0:T(8,128)(2,1)S(1)}, bf16[256,256]{1,0:T(8,128)(2,1)S(1)}, u32[]{:S(2)}, u32[]{:S(2)}) %collective-permute-start.32) | collective-permute-done | bytes 131104 | tf_op jit(solution)/shard_map/ppermute | solution.py:373
  148.5 5.3 %attend.3 = (bf16[32,8192]{1,0:T(8,128)(2,1)S(1)}, bf16[32,8192]{1,0:T(8,128)(2,1)S(1)}, bf16[32,8192]{1,0:T(8,128)(2,1)S(1)}, bf16[32,8192]{1,0:T(8,128)(2,1)S(1)}) custom-call(s32[18]{0:T(128)S(1)} %pad_add_fusion.meta_ref, bf16[128,512]{1,0:T(8,128)(2,1)S(1)} %query.7.query_ref, bf16[256,256]{1,0:T(8,128)(2,1)S(1)} %add_convert_fusion.22.refs_0_, ...), custom_call_target="tpu_custom_call" | custom-call | flops 4294967296 | bytes 33554432 | tf_op jit(solution)/shard_map/attend/pallas_call | solution.py:298
  159.8 2.8 %query.9.query_ref = bf16[64,512]{1,0:T(8,128)(2,1)S(1)} custom-call(bf16[32,8192]{1,0:T(8,128)(2,1)S(1)} %collective-permute-done.35.refs_0_, bf16[32,8192]{1,0:T(8,128)(2,1)S(1)} %collective-permute-done.36.refs_1_, bf16[8192,512]{1,0:T(8,128)(2,1)S(1)} %bitcast.14), custom_call_target="tpu_custom_call" | custom-call | flops 536870912 | bytes 9437184 | tf_op jit(solution)/shard_map/query/pallas_call | solution.py:207
  164.7 4.5 %attend.4 = (bf16[32,8192]{1,0:T(8,128)(2,1)S(1)}, bf16[32,8192]{1,0:T(8,128)(2,1)S(1)}) custom-call(s32[18]{0:T(128)S(1)} %pad_add_fusion.meta_ref, bf16[64,512]{1,0:T(8,128)(2,1)S(1)} %query.9.query_ref, bf16[256,256]{1,0:T(8,128)(2,1)S(1)} %add_convert_fusion.22.refs_0_, bf16[256,256]{1,0:T(8,128)(2,1)S(1)} %collective-permute-done.34.refs_1_, ...), custom_call_target="tpu_custom_call" | custom-call | flops 2147483648 | bytes 33554432 | tf_op jit(solution)/shard_map/attend/pallas_call | solution.py:298
  169.3 6.9 %attend.5 = (bf16[64,8192]{1,0:T(8,128)(2,1)S(1)}, bf16[32,8192]{1,0:T(8,128)(2,1)S(1)}, bf16[32,8192]{1,0:T(8,128)(2,1)S(1)}, bf16[32,8192]{1,0:T(8,128)(2,1)S(...) custom-call(s32[18]{0:T(128)S(1)} %pad_add_fusion.meta_ref, ...), custom_call_target="tpu_custom_call" | custom-call | flops 10737418240 | bytes 33554432 | tf_op jit(solution)/shard_map/attend/pallas_call | solution.py:298
  181.1 10.3 %collective-permute-done.39 = bf16[32,8192]{1,0:T(8,128)(2,1)S(1)} collective-permute-done((bf16[32,8192]{1,0:T(8,128)(2,1)S(1)}, bf16[32,8192]{1,0:T(8,128)(2,1)S(1)}, u32[]{:S(2)}, u32[]{:S(2)}) %collective-permute-start.39) | collective-permute-done | bytes 524320 | tf_op jit(solution)/shard_map/ppermute | solution.py:373
  193.8 9.7 %collective-permute-done.45 = bf16[32,8192]{1,0:T(8,128)(2,1)S(1)} collective-permute-done((bf16[32,8192]{1,0:T(8,128)(2,1)S(1)}, bf16[32,8192]{1,0:T(8,128)(2,1)S(1)}, u32[]{:S(2)}, u32[]{:S(2)}) %collective-permute-start.45) | collective-permute-done | bytes 524320 | tf_op jit(solution)/shard_map/ppermute | solution.py:376
  203.9 14.9 %collective-permute-done.43 = bf16[32,8192]{1,0:T(8,128)(2,1)S(1)} collective-permute-done((bf16[32,8192]{1,0:T(8,128)(2,1)S(1)}, bf16[32,8192]{1,0:T(8,128)(2,1)S(1)}, u32[]{:S(2)}, u32[]{:S(2)}) %collective-permute-start.43) | collective-permute-done | bytes 524320 | tf_op jit(solution)/shard_map/ppermute | solution.py:373
  220.7 5.5 %collective-permute-done.48 = bf16[32,8192]{1,0:T(8,128)(2,1)S(1)} collective-permute-done((bf16[32,8192]{1,0:T(8,128)(2,1)S(1)}, bf16[32,8192]{1,0:T(8,128)(2,1)S(1)}, u32[]{:S(2)}, u32[]{:S(2)}) %collective-permute-start.48) | collective-permute-done | bytes 524320 | tf_op jit(solution)/shard_map/ppermute | solution.py:389
  226.2 9.4 %collective-permute-done.47 = bf16[32,8192]{1,0:T(8,128)(2,1)S(1)} collective-permute-done((bf16[32,8192]{1,0:T(8,128)(2,1)S(1)}, bf16[32,8192]{1,0:T(8,128)(2,1)S(1)}, u32[]{:S(2)}, u32[]{:S(2)}) %collective-permute-start.47) | collective-permute-done | bytes 524320 | tf_op jit(solution)/shard_map/ppermute | solution.py:386
  (170 shorter events, 75.2 us)
Async XLA Ops:
  0.0 35.2 %collective-permute-start.3 = (bf16[64,8192]{1,0:T(8,128)(2,1)}, bf16[64,8192]{1,0:T(8,128)(2,1)S(1)}, u32[]{:S(2)}, u32[]{:S(2)}) collective-permute-start(bf16[64,8192]{1,0:T(8,128)(2,1)} %bitcast.21), channel_id=1, source_target_pairs={{2,0},{4,2},{6,4},{7,6},{5,7},{3,5},{1,3},{0,1},{10,8},{12,10},{14... | collective-permute-start | bytes 3145736 | tf_op jit(solution)/shard_map/ppermute | solution.py:376
  3.0 33.9 %collective-permute-start.2 = (bf16[64,8192]{1,0:T(8,128)(2,1)}, bf16[64,8192]{1,0:T(8,128)(2,1)S(1)}, u32[]{:S(2)}, u32[]{:S(2)}) collective-permute-start(bf16[64,8192]{1,0:T(8,128)(2,1)} %bitcast.22), channel_id=1, source_target_pairs={{0,2},{2,4},{4,6},{6,7},{7,5},{5,3},{3,1},{1,0},{8,10},{10,12},{12... | collective-permute-start | bytes 3145736 | tf_op jit(solution)/shard_map/ppermute | solution.py:373
  3.0 20.6 %collective-permute-start.1 = (f32[1]{0:T(128)}, f32[1]{0:T(128)}, u32[]{:S(2)}, u32[]{:S(2)}) collective-permute-start(f32[1]{0:T(128)} %param.16), channel_id=1, source_target_pairs={{0,8},{8,16},{16,24},{24,0},{1,9},{9,17},{17,25},{25,1},{2,10},{10... | collective-permute-start | bytes 20 | tf_op jit(solution)/shard_map/ppermute | solution.py:392
  8.4 26.5 %collective-permute-start.4 = (bf16[160,1024]{1,0:T(8,128)(2,1)}, bf16[160,1024]{1,0:T(8,128)(2,1)S(1)}, u32[]{:S(2)}, u32[]{:S(2)}) collective-permute-start(bf16[160,1024]{1,0:T(8,128)(2,1)} %get-tuple-element.94), channel_id=1, source_target_pairs={{0,2},{2,4},{4,6},{6,7},{7,5},{5,3},{3,1},{1,0},{8,10},{10,12},{12... | collective-permute-start | bytes 983048 | tf_op jit(solution)/shard_map/ppermute | solution.py:373
  10.4 28.0 %collective-permute-start.8 = (bf16[160,1024]{1,0:T(8,128)(2,1)}, bf16[160,1024]{1,0:T(8,128)(2,1)S(1)}, u32[]{:S(2)}, u32[]{:S(2)}) collective-permute-start(bf16[160,1024]{1,0:T(8,128)(2,1)} %get-tuple-element.99), channel_id=1, source_target_pairs={{2,0},{4,2},{6,4},{7,6},{5,7},{3,5},{1,3},{0,1},{10,8},{12,10},{14... | collective-permute-start | bytes 983048 | tf_op jit(solution)/shard_map/ppermute | solution.py:376
  23.6 36.7 %collective-permute-start = (bf16[64,8192]{1,0:T(8,128)(2,1)S(1)}, bf16[64,8192]{1,0:T(8,128)(2,1)S(1)}, u32[]{:S(2)}, u32[]{:S(2)}) collective-permute-start(bf16[64,8192]{1,0:T(8,128)(2,1)S(1)} %bitcast.23), channel_id=1, source_target_pairs={{0,8},{8,16},{16,24},{24,0},{1,9},{9,17},{17,25},{25,1},{2,10},{10... | collective-permute-start | bytes 3145736 | tf_op jit(solution)/shard_map/ppermute | solution.py:392
  83.8 25.7 %collective-permute-start.18 = (bf16[64,8192]{1,0:T(8,128)(2,1)S(1)}, bf16[64,8192]{1,0:T(8,128)(2,1)S(1)}, u32[]{:S(2)}, u32[]{:S(2)}) collective-permute-start(bf16[64,8192]{1,0:T(8,128)(2,1)S(1)} %collective-permute-done.2.refs_0_), channel_id=1, source_target_pairs={{0,2},{2,4},{4,6},{6,7},{7,5},{5,3},{3,1},{1,0},{8,10},{10,12},{12... | collective-permute-start | bytes 3145736 | tf_op jit(solution)/shard_map/ppermute | solution.py:373
  85.5 26.1 %collective-permute-start.24 = (bf16[64,8192]{1,0:T(8,128)(2,1)S(1)}, bf16[64,8192]{1,0:T(8,128)(2,1)S(1)}, u32[]{:S(2)}, u32[]{:S(2)}) collective-permute-start(bf16[64,8192]{1,0:T(8,128)(2,1)S(1)} %collective-permute-done.3.refs_1_), channel_id=1, source_target_pairs={{2,0},{4,2},{6,4},{7,6},{5,7},{3,5},{1,3},{0,1},{10,8},{12,10},{14... | collective-permute-start | bytes 3145736 | tf_op jit(solution)/shard_map/ppermute | solution.py:376
  126.0 16.8 %collective-permute-start.23 = (bf16[32,8192]{1,0:T(8,128)(2,1)S(1)}, bf16[32,8192]{1,0:T(8,128)(2,1)S(1)}, u32[]{:S(2)}, u32[]{:S(2)}) collective-permute-start(bf16[32,8192]{1,0:T(8,128)(2,1)S(1)} %collective-permute-done.22.refs_2_), channel_id=1, source_target_pairs={{0,2},{2,4},{4,6},{6,7},{7,5},{5,3},{3,1},{1,0},{8,10},{10,12},{12... | collective-permute-start | bytes 1572872 | tf_op jit(solution)/shard_map/ppermute | solution.py:373
  143.0 15.7 %collective-permute-start.36 = (bf16[32,8192]{1,0:T(8,128)(2,1)S(1)}, bf16[32,8192]{1,0:T(8,128)(2,1)S(1)}, u32[]{:S(2)}, u32[]{:S(2)}) collective-permute-start(bf16[32,8192]{1,0:T(8,128)(2,1)S(1)} %slice.33), channel_id=1, source_target_pairs={{2,0},{4,2},{6,4},{7,6},{5,7},{3,5},{1,3},{0,1},{10,8},{12,10},{14... | collective-permute-start | bytes 1572872 | tf_op jit(solution)/shard_map/ppermute | solution.py:376
  153.8 22.5 %collective-permute-start.38 = (bf16[32,8192]{1,0:T(8,128)(2,1)S(1)}, bf16[32,8192]{1,0:T(8,128)(2,1)S(1)}, u32[]{:S(2)}, u32[]{:S(2)}) collective-permute-start(bf16[32,8192]{1,0:T(8,128)(2,1)S(1)} %get-tuple-element.144), channel_id=1, source_target_pairs={{0,2},{2,4},{4,6},{6,7},{7,5},{5,3},{3,1},{1,0},{8,10},{10,12},{12... | collective-permute-start | bytes 1572872 | tf_op jit(solution)/shard_map/ppermute | solution.py:373
  154.6 21.8 %collective-permute-start.42 = (bf16[32,8192]{1,0:T(8,128)(2,1)S(1)}, bf16[32,8192]{1,0:T(8,128)(2,1)S(1)}, u32[]{:S(2)}, u32[]{:S(2)}) collective-permute-start(bf16[32,8192]{1,0:T(8,128)(2,1)S(1)} %get-tuple-element.158), channel_id=1, source_target_pairs={{2,0},{4,2},{6,4},{7,6},{5,7},{3,5},{1,3},{0,1},{10,8},{12,10},{14... | collective-permute-start | bytes 1572872 | tf_op jit(solution)/shard_map/ppermute | solution.py:376
  162.7 16.0 %collective-permute-start.41 = (bf16[32,8192]{1,0:T(8,128)(2,1)S(1)}, bf16[32,8192]{1,0:T(8,128)(2,1)S(1)}, u32[]{:S(2)}, u32[]{:S(2)}) collective-permute-start(bf16[32,8192]{1,0:T(8,128)(2,1)S(1)} %get-tuple-element.157), channel_id=1, source_target_pairs={{2,0},{4,2},{6,4},{7,6},{5,7},{3,5},{1,3},{0,1},{10,8},{12,10},{14... | collective-permute-start | bytes 1572872 | tf_op jit(solution)/shard_map/ppermute | solution.py:376
  163.1 16.2 %collective-permute-start.40 = (bf16[32,8192]{1,0:T(8,128)(2,1)S(1)}, bf16[32,8192]{1,0:T(8,128)(2,1)S(1)}, u32[]{:S(2)}, u32[]{:S(2)}) collective-permute-start(bf16[32,8192]{1,0:T(8,128)(2,1)S(1)} %get-tuple-element.155), channel_id=1, source_target_pairs={{0,2},{2,4},{4,6},{6,7},{7,5},{5,3},{3,1},{1,0},{8,10},{10,12},{12... | collective-permute-start | bytes 1572872 | tf_op jit(solution)/shard_map/ppermute | solution.py:373
  176.2 27.5 %collective-permute-start.37 = (bf16[64,8192]{1,0:T(8,128)(2,1)S(1)}, bf16[64,8192]{1,0:T(8,128)(2,1)S(1)}, u32[]{:S(2)}, u32[]{:S(2)}) collective-permute-start(bf16[64,8192]{1,0:T(8,128)(2,1)S(1)} %get-tuple-element.151), channel_id=1, source_target_pairs={{0,8},{8,16},{16,24},{24,0},{1,9},{9,17},{17,25},{25,1},{2,10},{10... | collective-permute-start | bytes 3145736 | tf_op jit(solution)/shard_map/ppermute | solution.py:392
  177.4 15.0 %collective-permute-start.46 = (bf16[32,8192]{1,0:T(8,128)(2,1)S(1)}, bf16[32,8192]{1,0:T(8,128)(2,1)S(1)}, u32[]{:S(2)}, u32[]{:S(2)}) collective-permute-start(bf16[32,8192]{1,0:T(8,128)(2,1)S(1)} %add_convert_fusion.10), channel_id=1, source_target_pairs={{2,0},{4,2},{6,4},{7,6},{5,7},{3,5},{1,3},{0,1},{10,8},{12,10},{14... | collective-permute-start | bytes 1572872 | tf_op jit(solution)/shard_map/ppermute | solution.py:376
  178.8 24.7 %collective-permute-start.45 = (bf16[32,8192]{1,0:T(8,128)(2,1)S(1)}, bf16[32,8192]{1,0:T(8,128)(2,1)S(1)}, u32[]{:S(2)}, u32[]{:S(2)}) collective-permute-start(bf16[32,8192]{1,0:T(8,128)(2,1)S(1)} %add_convert_fusion.9), channel_id=1, source_target_pairs={{2,0},{4,2},{6,4},{7,6},{5,7},{3,5},{1,3},{0,1},{10,8},{12,10},{14... | collective-permute-start | bytes 1572872 | tf_op jit(solution)/shard_map/ppermute | solution.py:376
  179.4 24.2 %collective-permute-start.44 = (bf16[32,8192]{1,0:T(8,128)(2,1)S(1)}, bf16[32,8192]{1,0:T(8,128)(2,1)S(1)}, u32[]{:S(2)}, u32[]{:S(2)}) collective-permute-start(bf16[32,8192]{1,0:T(8,128)(2,1)S(1)} %add_convert_fusion.8), channel_id=1, source_target_pairs={{0,2},{2,4},{4,6},{6,7},{7,5},{5,3},{3,1},{1,0},{8,10},{10,12},{12... | collective-permute-start | bytes 1572872 | tf_op jit(solution)/shard_map/ppermute | solution.py:373
  191.5 27.2 %collective-permute-start.43 = (bf16[32,8192]{1,0:T(8,128)(2,1)S(1)}, bf16[32,8192]{1,0:T(8,128)(2,1)S(1)}, u32[]{:S(2)}, u32[]{:S(2)}) collective-permute-start(bf16[32,8192]{1,0:T(8,128)(2,1)S(1)} %add_convert_fusion.7), channel_id=1, source_target_pairs={{0,2},{2,4},{4,6},{6,7},{7,5},{5,3},{3,1},{1,0},{8,10},{10,12},{12... | collective-permute-start | bytes 1572872 | tf_op jit(solution)/shard_map/ppermute | solution.py:373
  192.5 26.4 %collective-permute-start.50 = (bf16[32,8192]{1,0:T(8,128)(2,1)S(1)}, bf16[32,8192]{1,0:T(8,128)(2,1)S(1)}, u32[]{:S(2)}, u32[]{:S(2)}) collective-permute-start(bf16[32,8192]{1,0:T(8,128)(2,1)S(1)} %add_convert_fusion.6), channel_id=1, source_target_pairs={{2,0},{4,2},{6,4},{7,6},{5,7},{3,5},{1,3},{0,1},{10,8},{12,10},{14... | collective-permute-start | bytes 1572872 | tf_op jit(solution)/shard_map/ppermute | solution.py:376
  203.7 22.4 %collective-permute-start.48 = (bf16[32,8192]{1,0:T(8,128)(2,1)S(1)}, bf16[32,8192]{1,0:T(8,128)(2,1)S(1)}, u32[]{:S(2)}, u32[]{:S(2)}) collective-permute-start(bf16[32,8192]{1,0:T(8,128)(2,1)S(1)} %add_convert_fusion.5), channel_id=1, source_target_pairs={{2,8},{4,10},{6,12},{7,14},{5,15},{3,13},{1,11},{0,9},{10,16},{12,... | collective-permute-start | bytes 1572872 | tf_op jit(solution)/shard_map/ppermute | solution.py:389
  203.8 22.4 %collective-permute-start.49 = (bf16[32,8192]{1,0:T(8,128)(2,1)S(1)}, bf16[32,8192]{1,0:T(8,128)(2,1)S(1)}, u32[]{:S(2)}, u32[]{:S(2)}) collective-permute-start(bf16[32,8192]{1,0:T(8,128)(2,1)S(1)} %add_convert_fusion.4), channel_id=1, source_target_pairs={{0,10},{2,12},{4,14},{6,15},{7,13},{5,11},{3,9},{1,8},{8,18},{10,2... | collective-permute-start | bytes 1572872 | tf_op jit(solution)/shard_map/ppermute | solution.py:386
  219.0 16.6 %collective-permute-start.47 = (bf16[32,8192]{1,0:T(8,128)(2,1)S(1)}, bf16[32,8192]{1,0:T(8,128)(2,1)S(1)}, u32[]{:S(2)}, u32[]{:S(2)}) collective-permute-start(bf16[32,8192]{1,0:T(8,128)(2,1)S(1)} %add_convert_fusion.3), channel_id=1, source_target_pairs={{0,10},{2,12},{4,14},{6,15},{7,13},{5,11},{3,9},{1,8},{8,18},{10,2... | collective-permute-start | bytes 1572872 | tf_op jit(solution)/shard_map/ppermute | solution.py:386
  219.1 17.2 %collective-permute-start.51 = (bf16[32,8192]{1,0:T(8,128)(2,1)S(1)}, bf16[32,8192]{1,0:T(8,128)(2,1)S(1)}, u32[]{:S(2)}, u32[]{:S(2)}) collective-permute-start(bf16[32,8192]{1,0:T(8,128)(2,1)S(1)} %add_convert_fusion.1), channel_id=1, source_target_pairs={{2,8},{4,10},{6,12},{7,14},{5,15},{3,13},{1,11},{0,9},{10,16},{12,... | collective-permute-start | bytes 1572872 | tf_op jit(solution)/shard_map/ppermute | solution.py:389
  (46 other events, 658.8 us)

commit v10 on v9

--- a/solution.py
+++ b/solution.py
@@ -437,14 +437,12 @@
         )
     ]
 
-    def image_hold(left, value):
-        return after(value, text_next) if left == 1 else value
+    weight_query, weight_out = w_query[0], w_out[0]
+    queries = [query([text_own, from_below[1], from_above[1]], weight_query)]
 
     turns = [0, 3, 1, 2]
     came = ring_sums(
-        [image_chains[turn] for turn in turns],
-        image_hold,
-        turn=[gate_next, from_below[1], from_above[1]],
+        [image_chains[turn] for turn in turns], turn=[gate_next, queries[0]]
     )
     came = [came[turns.index(index)] for index in range(4)]
     image_cols = total_of(
@@ -452,12 +450,6 @@
     )
 
     text_round(image_cols)
-    weight_query, weight_out = w_query[0], w_out[0]
-    queries = {
-        0: query([text_own], weight_query),
-        1: query([from_below[1], from_above[1]], weight_query),
-    }
-
     pieces = []
     moving = image_cols
     for step in range(section_count // 2):
@@ -471,8 +463,6 @@
                 "section",
                 [(s, (s + 2) % section_count) for s in range(section_count)],
             )
-            if step == 0:
-                moving = after(moving, queries[0], queries[1])
 
     kv_part = key_values(meta, pieces, w_kv[0], mp_count, section_count, sharing)
 
@@ -523,15 +513,15 @@
     ready = first_part[0]
     for distance in range(2, last):
         rows = [after(from_below[distance], ready), from_above[distance]]
-        queries[distance] = query(rows, weight_query)
-    rest_queries = jnp.concatenate([queries[distance] for distance in range(last)], axis=0)
+        queries.append(query(rows, weight_query))
+    rest_queries = jnp.concatenate(queries, axis=0)
     if parts == 2:
         behind_queries = after(query(behind, weight_query), rest_queries, ready)
         behind_part = attend_to([-last, last], behind_queries, [cut] * 2)
         out_parts[-last][1], out_parts[last][0] = behind_part
         ready = behind_part[0]
     sizes = [text_rows] + [cut] * (parts * len(near))
-    own_part, *near_part = attend_to([0] + near, after(rest_queries, ready), sizes)
+    own_part, *near_part = attend_to([0] + near, after(rest_queries, ready, text_next), sizes)
     for index, offset in enumerate(near):
         out_parts[offset] = near_part[parts * index :][:parts]
     own_next = to_next(own_part)

time: 238 us -> 236 us (level)
  waiting for transfers between devices: 126 us -> 119 us
  starting transfers between devices: 48.9 us -> 54.2 us
  local copies, waits for them, and re-layouts: 2.08 us -> 5.41 us
    ppermute x21, waiting for transfers between devices: 72.3 us -> 56.9 us  [up(): return lax.ppermute(value, 'mp', up_pairs)]
    ppermute x20, starting transfers between devices: 22.3 us -> 29.4 us  [down(): return lax.ppermute(value, 'mp', down_pairs)]
    ppermute x21, starting transfers between devices: 22.2 us -> 15.6 us  [up(): return lax.ppermute(value, 'mp', up_pairs)]
    ppermute x1, waiting for transfers between devices: 4.38 us -> 10.8 us  [local(): lax.ppermute(moving, 'section', [(s, (s + 2) % section_count) for s in ra...]
    ppermute x20, waiting for transfers between devices: 31.8 us -> 35.5 us  [down(): return lax.ppermute(value, 'mp', down_pairs)]
    ppermute x2, starting transfers between devices: 1.07 us -> 4.52 us  [down_across(): return lax.ppermute(value, ('section', 'mp'), across(down_pairs))]
    unnamed x36 -> x44, local copies, waits for them, and re-layouts: 0.08 us -> 3.47 us
    pallas_call x5 -> x4, Pallas kernels: 14 us -> 11.9 us  [query(): pl.pallas_call(kernel, grid=(width // wide,), in_specs=[pl.BlockSpec(chun...]
  transfers between devices with their start and end apart: 52 -> 52, of which waited for: 26 -> 24; matrix products, arithmetic and copies ran while one was open for 3% -> 2% of each run, Pallas kernels for 22% -> 21%
where the time goes in v10:
time: 236 us; the launch traced here: 235 us
  waiting for transfers between devices  119 us (50%)
  starting transfers between devices  54.2 us (23%)
  Pallas kernels  50.6 us (21%)
  local copies, waits for them, and re-layouts  5.41 us (2%)
  other arithmetic  5.34 us (2%)
    ppermute x21, waiting for transfers between devices, up(): return lax.ppermute(value, 'mp', up_pairs)  56.9 us
    ppermute x20, waiting for transfers between devices, down(): return lax.ppermute(value, 'mp', down_pairs)  35.5 us
    ppermute x20, starting transfers between devices, down(): return lax.ppermute(value, 'mp', down_pairs)  29.4 us
    pallas_call x2, Pallas kernels, project(): pl.pallas_call(kernel, grid_spec=pltpu.PrefetchScalarGridSpec(num_scalar_...  17.3 us
    pallas_call x3, Pallas kernels, attend(): pl.pallas_call(kernel, grid_spec=pltpu.PrefetchScalarGridSpec(num_scalar_...  16.8 us
    ppermute x21, starting transfers between devices, up(): return lax.ppermute(value, 'mp', up_pairs)  15.6 us
    pallas_call x4, Pallas kernels, query(): pl.pallas_call(kernel, grid=(width // wide,), in_specs=[pl.BlockSpec(chun...  11.9 us
    ppermute x1, waiting for transfers between devices, local(): lax.ppermute(moving, 'section', [(s, (s + 2) % section_count) for s in ra...  10.8 us
  transfers between devices with their start and end apart: 52, of which 24 were waited for; matrix products, arithmetic and copies ran while one was open for 2% of the time, Pallas kernels for 21%

profile of v10, /device:TPU:0, one launch (start us, length us, event | category | flops | bytes accessed | tf_op | source)
XLA Modules:
  0.0 235.3 jit_solution(6734676413537190617)
XLA Ops:
  0.0 3.0 %collective-permute-start.3 = (bf16[64,8192]{1,0:T(8,128)(2,1)}, bf16[64,8192]{1,0:T(8,128)(2,1)S(1)}, u32[]{:S(2)}, u32[]{:S(2)}) collective-permute-start(bf16[64,8192]{1,0:T(8,128)(2,1)} %bitcast.22), channel_id=1, source_target_pairs={{2,0},{4,2},{6,4},{7,6},{5,7},{3,5},{1,3},{0,1},{10,8},{12,10},{14... | collective-permute-start | bytes 3145736 | tf_op jit(solution)/shard_map/ppermute | solution.py:376
  4.2 4.1 %project.3 = (bf16[160,1024]{1,0:T(8,128)(2,1)}, bf16[160,1024]{1,0:T(8,128)(2,1)}) custom-call(s32[10]{0:T(128)} %get-tuple-element.175.places_ref, bf16[320,960]{1,0:T(8,128)(2,1)} %feats_ref.3, bf16[960,8192]{1,0:T(8,128)(2,1)} %weight_ref.3), custom_call_target="tpu_custom_call" | custom-call | flops 629145600 | bytes 2621440 | tf_op jit(solution)/shard_map/project/pallas_call | solution.py:101
  10.3 13.2 %project.2 = (bf16[160,1024]{1,0:T(8,128)(2,1)}, bf16[160,1024]{1,0:T(8,128)(2,1)}, bf16[160,1024]{1,0:T(8,128)(2,1)}, bf16[160,1024]{1,0:T(8,128)(2,1)}, bf16[1...) custom-call(s32[10]{0:T(128)} %get-tuple-element.175.places_ref, ...), custom_call_target="tpu_custom_call" | custom-call | flops 4404019200 | bytes 18350080 | tf_op jit(solution)/shard_map/project/pallas_call | solution.py:101
  23.6 3.7 %collective-permute-done.3.refs_2_ = bf16[64,8192]{1,0:T(8,128)(2,1)S(1)} collective-permute-done((bf16[64,8192]{1,0:T(8,128)(2,1)}, bf16[64,8192]{1,0:T(8,128)(2,1)S(1)}, u32[]{:S(2)}, u32[]{:S(2)}) %collective-permute-start.3) | collective-permute-done | bytes 1048608 | tf_op jit(solution)/shard_map/ppermute | solution.py:376
  30.8 3.4 %copy-done = bf16[1,8192,512]{2,1,0:T(8,128)(2,1)S(1)} copy-done((bf16[1,8192,512]{2,1,0:T(8,128)(2,1)S(1)}, bf16[1,8192,512]{2,1,0:T(8,128)(2,1)}, u32[]{:S(2)}) %copy-start) | copy-done | bytes 8388632
  34.2 3.5 %query.4 = bf16[192,512]{1,0:T(8,128)(2,1)S(1)} custom-call(bf16[64,8192]{1,0:T(8,128)(2,1)S(1)} %bitcast.24, bf16[64,8192]{1,0:T(8,128)(2,1)S(1)} %collective-permute-done.2.refs_1_, bf16[64,8192]{1,0:T(8,128)(2,1)S(1)} %collective-permute-done.3.refs_2_, bf16[8192,512]{1,0:T(8,128)(2,1)S(1)} %bitcast.10), custom_call_target="tpu_custom_call" | custom-call | flops 1610612736 | bytes 11534336 | tf_op jit(solution)/shard_map/query/pallas_call | solution.py:207
  43.7 6.6 %collective-permute-done.5 = bf16[160,1024]{1,0:T(8,128)(2,1)S(1)} collective-permute-done((bf16[160,1024]{1,0:T(8,128)(2,1)S(1)}, bf16[160,1024]{1,0:T(8,128)(2,1)S(1)}, u32[]{:S(2)}, u32[]{:S(2)}) %collective-permute-start.5) | collective-permute-done | bytes 327712 | tf_op jit(solution)/shard_map/ppermute | solution.py:373
  52.7 3.6 %collective-permute-done.11 = bf16[160,1024]{1,0:T(8,128)(2,1)S(1)} collective-permute-done((bf16[160,1024]{1,0:T(8,128)(2,1)S(1)}, bf16[160,1024]{1,0:T(8,128)(2,1)S(1)}, u32[]{:S(2)}, u32[]{:S(2)}) %collective-permute-start.11) | collective-permute-done | bytes 327712 | tf_op jit(solution)/shard_map/ppermute | solution.py:376
  58.6 5.7 %collective-permute-done.9 = bf16[160,1024]{1,0:T(8,128)(2,1)S(1)} collective-permute-done((bf16[160,1024]{1,0:T(8,128)(2,1)S(1)}, bf16[160,1024]{1,0:T(8,128)(2,1)S(1)}, u32[]{:S(2)}, u32[]{:S(2)}) %collective-permute-start.9) | collective-permute-done | bytes 327712 | tf_op jit(solution)/shard_map/ppermute | solution.py:373
  66.7 4.7 %collective-permute-done.15.refs_4_ = bf16[160,1024]{1,0:T(8,128)(2,1)S(1)} collective-permute-done((bf16[160,1024]{1,0:T(8,128)(2,1)S(1)}, bf16[160,1024]{1,0:T(8,128)(2,1)S(1)}, u32[]{:S(2)}, u32[]{:S(2)}) %collective-permute-start.15) | collective-permute-done | bytes 327712 | tf_op jit(solution)/shard_map/ppermute | solution.py:373
  71.4 4.1 %collective-permute-done.17.refs_5_ = bf16[160,1024]{1,0:T(8,128)(2,1)S(1)} collective-permute-done((bf16[160,1024]{1,0:T(8,128)(2,1)S(1)}, bf16[160,1024]{1,0:T(8,128)(2,1)S(1)}, u32[]{:S(2)}, u32[]{:S(2)}) %collective-permute-start.17) | collective-permute-done | bytes 327712 | tf_op jit(solution)/shard_map/ppermute | solution.py:376
  81.7 10.8 %collective-permute-done.20.refs_2_ = bf16[320,1024]{1,0:T(8,128)(2,1)S(1)} collective-permute-done((bf16[320,1024]{1,0:T(8,128)(2,1)S(1)}, bf16[320,1024]{1,0:T(8,128)(2,1)S(1)}, u32[]{:S(2)}, u32[]{:S(2)}) %collective-permute-start.20) | collective-permute-done | bytes 655392 | tf_op jit(solution)/shard_map/ppermute | solution.py:461
  94.7 4.4 %key_values.1 = (bf16[256,256]{1,0:T(8,128)(2,1)S(1)}, bf16[256,256]{1,0:T(8,128)(2,1)S(1)}, bf16[256,256]{1,0:T(8,128)(2,1)S(1)}, bf16[256,256]{1,0:T(8,128)(2,...) custom-call(s32[18]{0:T(128)S(1)} %pad_add_fusion.meta_ref, ...), custom_call_target="tpu_custom_call" | custom-call | flops 1 | bytes 1 | tf_op jit(solution)/shard_map/key_values/pallas_call | solution.py:165
  106.8 10.8 %collective-permute-done.29 = bf16[256,256]{1,0:T(8,128)(2,1)S(1)} collective-permute-done((bf16[256,256]{1,0:T(8,128)(2,1)S(1)}, bf16[256,256]{1,0:T(8,128)(2,1)S(1)}, u32[]{:S(2)}, u32[]{:S(2)}) %collective-permute-start.29) | collective-permute-done | bytes 131104 | tf_op jit(solution)/shard_map/ppermute | solution.py:376
  129.3 9.5 %collective-permute-done.32 = bf16[256,256]{1,0:T(8,128)(2,1)S(1)} collective-permute-done((bf16[256,256]{1,0:T(8,128)(2,1)S(1)}, bf16[256,256]{1,0:T(8,128)(2,1)S(1)}, u32[]{:S(2)}, u32[]{:S(2)}) %collective-permute-start.32) | collective-permute-done | bytes 131104 | tf_op jit(solution)/shard_map/ppermute | solution.py:373
  145.6 5.3 %attend.3 = (bf16[32,8192]{1,0:T(8,128)(2,1)S(1)}, bf16[32,8192]{1,0:T(8,128)(2,1)S(1)}, bf16[32,8192]{1,0:T(8,128)(2,1)S(1)}, bf16[32,8192]{1,0:T(8,128)(2,1)S(1)}) custom-call(s32[18]{0:T(128)S(1)} %pad_add_fusion.meta_ref, bf16[128,512]{1,0:T(8,128)(2,1)S(1)} %query.5.query_ref, bf16[256,256]{1,0:T(8,128)(2,1)S(1)} %add_convert_fusion.22.refs_0_, ...), custom_call_target="tpu_custom_call" | custom-call | flops 4294967296 | bytes 33554432 | tf_op jit(solution)/shard_map/attend/pallas_call | solution.py:298
  161.6 4.5 %attend.4 = (bf16[32,8192]{1,0:T(8,128)(2,1)S(1)}, bf16[32,8192]{1,0:T(8,128)(2,1)S(1)}) custom-call(s32[18]{0:T(128)S(1)} %pad_add_fusion.meta_ref, bf16[64,512]{1,0:T(8,128)(2,1)S(1)} %query.7.query_ref, bf16[256,256]{1,0:T(8,128)(2,1)S(1)} %add_convert_fusion.22.refs_0_, bf16[256,256]{1,0:T(8,128)(2,1)S(1)} %collective-permute-done.34.refs_1_, ...), custom_call_target="tpu_custom_call" | custom-call | flops 2147483648 | bytes 33554432 | tf_op jit(solution)/shard_map/attend/pallas_call | solution.py:298
  166.1 6.9 %attend.5 = (bf16[64,8192]{1,0:T(8,128)(2,1)S(1)}, bf16[32,8192]{1,0:T(8,128)(2,1)S(1)}, bf16[32,8192]{1,0:T(8,128)(2,1)S(1)}, bf16[32,8192]{1,0:T(8,128)(2,1)S(...) custom-call(s32[18]{0:T(128)S(1)} %pad_add_fusion.meta_ref, ...), custom_call_target="tpu_custom_call" | custom-call | flops 10737418240 | bytes 33554432 | tf_op jit(solution)/shard_map/attend/pallas_call | solution.py:298
  177.9 9.8 %collective-permute-done.39 = bf16[32,8192]{1,0:T(8,128)(2,1)S(1)} collective-permute-done((bf16[32,8192]{1,0:T(8,128)(2,1)S(1)}, bf16[32,8192]{1,0:T(8,128)(2,1)S(1)}, u32[]{:S(2)}, u32[]{:S(2)}) %collective-permute-start.39) | collective-permute-done | bytes 524320 | tf_op jit(solution)/shard_map/ppermute | solution.py:373
  190.1 9.9 %collective-permute-done.45 = bf16[32,8192]{1,0:T(8,128)(2,1)S(1)} collective-permute-done((bf16[32,8192]{1,0:T(8,128)(2,1)S(1)}, bf16[32,8192]{1,0:T(8,128)(2,1)S(1)}, u32[]{:S(2)}, u32[]{:S(2)}) %collective-permute-start.45) | collective-permute-done | bytes 524320 | tf_op jit(solution)/shard_map/ppermute | solution.py:376
  203.2 12.5 %collective-permute-done.43 = bf16[32,8192]{1,0:T(8,128)(2,1)S(1)} collective-permute-done((bf16[32,8192]{1,0:T(8,128)(2,1)S(1)}, bf16[32,8192]{1,0:T(8,128)(2,1)S(1)}, u32[]{:S(2)}, u32[]{:S(2)}) %collective-permute-start.43) | collective-permute-done | bytes 524320 | tf_op jit(solution)/shard_map/ppermute | solution.py:373
  216.1 2.9 %collective-permute-start.51 = (bf16[32,8192]{1,0:T(8,128)(2,1)S(1)}, bf16[32,8192]{1,0:T(8,128)(2,1)S(1)}, u32[]{:S(2)}, u32[]{:S(2)}) collective-permute-start(bf16[32,8192]{1,0:T(8,128)(2,1)S(1)} %add_convert_fusion.1), channel_id=1, source_target_pairs={{2,8},{4,10},{6,12},{7,14},{5,15},{3,13},{1,11},{0,9},{10,16},{12,... | collective-permute-start | bytes 1572872 | tf_op jit(solution)/shard_map/ppermute | solution.py:389
  219.6 2.8 %collective-permute-done.48 = bf16[32,8192]{1,0:T(8,128)(2,1)S(1)} collective-permute-done((bf16[32,8192]{1,0:T(8,128)(2,1)S(1)}, bf16[32,8192]{1,0:T(8,128)(2,1)S(1)}, u32[]{:S(2)}, u32[]{:S(2)}) %collective-permute-start.48) | collective-permute-done | bytes 524320 | tf_op jit(solution)/shard_map/ppermute | solution.py:389
  222.5 8.8 %collective-permute-done.47 = bf16[32,8192]{1,0:T(8,128)(2,1)S(1)} collective-permute-done((bf16[32,8192]{1,0:T(8,128)(2,1)S(1)}, bf16[32,8192]{1,0:T(8,128)(2,1)S(1)}, u32[]{:S(2)}, u32[]{:S(2)}) %collective-permute-start.47) | collective-permute-done | bytes 524320 | tf_op jit(solution)/shard_map/ppermute | solution.py:386
  (178 shorter events, 79.5 us)
Async XLA Ops:
  0.0 27.2 %collective-permute-start.3 = (bf16[64,8192]{1,0:T(8,128)(2,1)}, bf16[64,8192]{1,0:T(8,128)(2,1)S(1)}, u32[]{:S(2)}, u32[]{:S(2)}) collective-permute-start(bf16[64,8192]{1,0:T(8,128)(2,1)} %bitcast.22), channel_id=1, source_target_pairs={{2,0},{4,2},{6,4},{7,6},{5,7},{3,5},{1,3},{0,1},{10,8},{12,10},{14... | collective-permute-start | bytes 3145736 | tf_op jit(solution)/shard_map/ppermute | solution.py:376
  3.0 26.3 %collective-permute-start.2 = (bf16[64,8192]{1,0:T(8,128)(2,1)}, bf16[64,8192]{1,0:T(8,128)(2,1)S(1)}, u32[]{:S(2)}, u32[]{:S(2)}) collective-permute-start(bf16[64,8192]{1,0:T(8,128)(2,1)} %bitcast.23), channel_id=1, source_target_pairs={{0,2},{2,4},{4,6},{6,7},{7,5},{5,3},{3,1},{1,0},{8,10},{10,12},{12... | collective-permute-start | bytes 3145736 | tf_op jit(solution)/shard_map/ppermute | solution.py:373
  3.0 34.7 %collective-permute-start.1 = (f32[1]{0:T(128)}, f32[1]{0:T(128)}, u32[]{:S(2)}, u32[]{:S(2)}) collective-permute-start(f32[1]{0:T(128)} %param.16), channel_id=1, source_target_pairs={{0,8},{8,16},{16,24},{24,0},{1,9},{9,17},{17,25},{25,1},{2,10},{10... | collective-permute-start | bytes 20 | tf_op jit(solution)/shard_map/ppermute | solution.py:392
  8.3 29.5 %collective-permute-start.4 = (bf16[160,1024]{1,0:T(8,128)(2,1)}, bf16[160,1024]{1,0:T(8,128)(2,1)S(1)}, u32[]{:S(2)}, u32[]{:S(2)}) collective-permute-start(bf16[160,1024]{1,0:T(8,128)(2,1)} %get-tuple-element.89), channel_id=1, source_target_pairs={{0,2},{2,4},{4,6},{6,7},{7,5},{5,3},{3,1},{1,0},{8,10},{10,12},{12... | collective-permute-start | bytes 983048 | tf_op jit(solution)/shard_map/ppermute | solution.py:373
  10.3 28.1 %collective-permute-start.8 = (bf16[160,1024]{1,0:T(8,128)(2,1)}, bf16[160,1024]{1,0:T(8,128)(2,1)S(1)}, u32[]{:S(2)}, u32[]{:S(2)}) collective-permute-start(bf16[160,1024]{1,0:T(8,128)(2,1)} %get-tuple-element.94), channel_id=1, source_target_pairs={{2,0},{4,2},{6,4},{7,6},{5,7},{3,5},{1,3},{0,1},{10,8},{12,10},{14... | collective-permute-start | bytes 983048 | tf_op jit(solution)/shard_map/ppermute | solution.py:376
  27.2 16.2 %collective-permute-start.6 = (bf16[160,1024]{1,0:T(8,128)(2,1)}, bf16[160,1024]{1,0:T(8,128)(2,1)S(1)}, u32[]{:S(2)}, u32[]{:S(2)}) collective-permute-start(bf16[160,1024]{1,0:T(8,128)(2,1)} %get-tuple-element.92), channel_id=1, source_target_pairs={{0,2},{2,4},{4,6},{6,7},{7,5},{5,3},{3,1},{1,0},{8,10},{10,12},{12... | collective-permute-start | bytes 983048 | tf_op jit(solution)/shard_map/ppermute | solution.py:373
  78.8 23.7 %collective-permute-start.18 = (bf16[64,8192]{1,0:T(8,128)(2,1)S(1)}, bf16[64,8192]{1,0:T(8,128)(2,1)S(1)}, u32[]{:S(2)}, u32[]{:S(2)}) collective-permute-start(bf16[64,8192]{1,0:T(8,128)(2,1)S(1)} %collective-permute-done.2.refs_1_), channel_id=1, source_target_pairs={{0,2},{2,4},{4,6},{6,7},{7,5},{5,3},{3,1},{1,0},{8,10},{10,12},{12... | collective-permute-start | bytes 3145736 | tf_op jit(solution)/shard_map/ppermute | solution.py:373
  79.3 23.6 %collective-permute-start.24 = (bf16[64,8192]{1,0:T(8,128)(2,1)S(1)}, bf16[64,8192]{1,0:T(8,128)(2,1)S(1)}, u32[]{:S(2)}, u32[]{:S(2)}) collective-permute-start(bf16[64,8192]{1,0:T(8,128)(2,1)S(1)} %collective-permute-done.3.refs_2_), channel_id=1, source_target_pairs={{2,0},{4,2},{6,4},{7,6},{5,7},{3,5},{1,3},{0,1},{10,8},{12,10},{14... | collective-permute-start | bytes 3145736 | tf_op jit(solution)/shard_map/ppermute | solution.py:376
  102.5 16.5 %collective-permute-start.22 = (bf16[32,8192]{1,0:T(8,128)(2,1)S(1)}, bf16[32,8192]{1,0:T(8,128)(2,1)S(1)}, u32[]{:S(2)}, u32[]{:S(2)}) collective-permute-start(bf16[32,8192]{1,0:T(8,128)(2,1)S(1)} %slice.30), channel_id=1, source_target_pairs={{0,2},{2,4},{4,6},{6,7},{7,5},{5,3},{3,1},{1,0},{8,10},{10,12},{12... | collective-permute-start | bytes 1572872 | tf_op jit(solution)/shard_map/ppermute | solution.py:373
  102.9 16.1 %collective-permute-start.25 = (bf16[32,8192]{1,0:T(8,128)(2,1)S(1)}, bf16[32,8192]{1,0:T(8,128)(2,1)S(1)}, u32[]{:S(2)}, u32[]{:S(2)}) collective-permute-start(bf16[32,8192]{1,0:T(8,128)(2,1)S(1)} %slice.31), channel_id=1, source_target_pairs={{2,0},{4,2},{6,4},{7,6},{5,7},{3,5},{1,3},{0,1},{10,8},{12,10},{14... | collective-permute-start | bytes 1572872 | tf_op jit(solution)/shard_map/ppermute | solution.py:376
  121.2 17.7 %collective-permute-start.23 = (bf16[32,8192]{1,0:T(8,128)(2,1)S(1)}, bf16[32,8192]{1,0:T(8,128)(2,1)S(1)}, u32[]{:S(2)}, u32[]{:S(2)}) collective-permute-start(bf16[32,8192]{1,0:T(8,128)(2,1)S(1)} %collective-permute-done.22.refs_2_), channel_id=1, source_target_pairs={{0,2},{2,4},{4,6},{6,7},{7,5},{5,3},{3,1},{1,0},{8,10},{10,12},{12... | collective-permute-start | bytes 1572872 | tf_op jit(solution)/shard_map/ppermute | solution.py:373
  121.7 17.2 %collective-permute-start.26 = (bf16[32,8192]{1,0:T(8,128)(2,1)S(1)}, bf16[32,8192]{1,0:T(8,128)(2,1)S(1)}, u32[]{:S(2)}, u32[]{:S(2)}) collective-permute-start(bf16[32,8192]{1,0:T(8,128)(2,1)S(1)} %collective-permute-done.25.refs_3_), channel_id=1, source_target_pairs={{2,0},{4,2},{6,4},{7,6},{5,7},{3,5},{1,3},{0,1},{10,8},{12,10},{14... | collective-permute-start | bytes 1572872 | tf_op jit(solution)/shard_map/ppermute | solution.py:376
  129.3 36.8 %collective-permute-start = (bf16[64,8192]{1,0:T(8,128)(2,1)S(1)}, bf16[64,8192]{1,0:T(8,128)(2,1)S(1)}, u32[]{:S(2)}, u32[]{:S(2)}) collective-permute-start(bf16[64,8192]{1,0:T(8,128)(2,1)S(1)} %bitcast.25), channel_id=1, source_target_pairs={{0,8},{8,16},{16,24},{24,0},{1,9},{9,17},{17,25},{25,1},{2,10},{10... | collective-permute-start | bytes 3145736 | tf_op jit(solution)/shard_map/ppermute | solution.py:392
  150.9 22.2 %collective-permute-start.38 = (bf16[32,8192]{1,0:T(8,128)(2,1)S(1)}, bf16[32,8192]{1,0:T(8,128)(2,1)S(1)}, u32[]{:S(2)}, u32[]{:S(2)}) collective-permute-start(bf16[32,8192]{1,0:T(8,128)(2,1)S(1)} %get-tuple-element.134), channel_id=1, source_target_pairs={{0,2},{2,4},{4,6},{6,7},{7,5},{5,3},{3,1},{1,0},{8,10},{10,12},{12... | collective-permute-start | bytes 1572872 | tf_op jit(solution)/shard_map/ppermute | solution.py:373
  152.5 20.7 %collective-permute-start.42 = (bf16[32,8192]{1,0:T(8,128)(2,1)S(1)}, bf16[32,8192]{1,0:T(8,128)(2,1)S(1)}, u32[]{:S(2)}, u32[]{:S(2)}) collective-permute-start(bf16[32,8192]{1,0:T(8,128)(2,1)S(1)} %get-tuple-element.148), channel_id=1, source_target_pairs={{2,0},{4,2},{6,4},{7,6},{5,7},{3,5},{1,3},{0,1},{10,8},{12,10},{14... | collective-permute-start | bytes 1572872 | tf_op jit(solution)/shard_map/ppermute | solution.py:376
  160.5 17.1 %collective-permute-start.40 = (bf16[32,8192]{1,0:T(8,128)(2,1)S(1)}, bf16[32,8192]{1,0:T(8,128)(2,1)S(1)}, u32[]{:S(2)}, u32[]{:S(2)}) collective-permute-start(bf16[32,8192]{1,0:T(8,128)(2,1)S(1)} %get-tuple-element.145), channel_id=1, source_target_pairs={{0,2},{2,4},{4,6},{6,7},{7,5},{5,3},{3,1},{1,0},{8,10},{10,12},{12... | collective-permute-start | bytes 1572872 | tf_op jit(solution)/shard_map/ppermute | solution.py:373
  173.0 27.2 %collective-permute-start.37 = (bf16[64,8192]{1,0:T(8,128)(2,1)S(1)}, bf16[64,8192]{1,0:T(8,128)(2,1)S(1)}, u32[]{:S(2)}, u32[]{:S(2)}) collective-permute-start(bf16[64,8192]{1,0:T(8,128)(2,1)S(1)} %get-tuple-element.141), channel_id=1, source_target_pairs={{0,8},{8,16},{16,24},{24,0},{1,9},{9,17},{17,25},{25,1},{2,10},{10... | collective-permute-start | bytes 3145736 | tf_op jit(solution)/shard_map/ppermute | solution.py:392
  175.6 24.4 %collective-permute-start.45 = (bf16[32,8192]{1,0:T(8,128)(2,1)S(1)}, bf16[32,8192]{1,0:T(8,128)(2,1)S(1)}, u32[]{:S(2)}, u32[]{:S(2)}) collective-permute-start(bf16[32,8192]{1,0:T(8,128)(2,1)S(1)} %add_convert_fusion.9), channel_id=1, source_target_pairs={{2,0},{4,2},{6,4},{7,6},{5,7},{3,5},{1,3},{0,1},{10,8},{12,10},{14... | collective-permute-start | bytes 1572872 | tf_op jit(solution)/shard_map/ppermute | solution.py:376
  177.7 22.4 %collective-permute-start.44 = (bf16[32,8192]{1,0:T(8,128)(2,1)S(1)}, bf16[32,8192]{1,0:T(8,128)(2,1)S(1)}, u32[]{:S(2)}, u32[]{:S(2)}) collective-permute-start(bf16[32,8192]{1,0:T(8,128)(2,1)S(1)} %add_convert_fusion.8), channel_id=1, source_target_pairs={{0,2},{2,4},{4,6},{6,7},{7,5},{5,3},{3,1},{1,0},{8,10},{10,12},{12... | collective-permute-start | bytes 1572872 | tf_op jit(solution)/shard_map/ppermute | solution.py:373
  187.8 27.9 %collective-permute-start.43 = (bf16[32,8192]{1,0:T(8,128)(2,1)S(1)}, bf16[32,8192]{1,0:T(8,128)(2,1)S(1)}, u32[]{:S(2)}, u32[]{:S(2)}) collective-permute-start(bf16[32,8192]{1,0:T(8,128)(2,1)S(1)} %add_convert_fusion.7), channel_id=1, source_target_pairs={{0,2},{2,4},{4,6},{6,7},{7,5},{5,3},{3,1},{1,0},{8,10},{10,12},{12... | collective-permute-start | bytes 1572872 | tf_op jit(solution)/shard_map/ppermute | solution.py:373
  188.9 27.0 %collective-permute-start.50 = (bf16[32,8192]{1,0:T(8,128)(2,1)S(1)}, bf16[32,8192]{1,0:T(8,128)(2,1)S(1)}, u32[]{:S(2)}, u32[]{:S(2)}) collective-permute-start(bf16[32,8192]{1,0:T(8,128)(2,1)S(1)} %add_convert_fusion.6), channel_id=1, source_target_pairs={{2,0},{4,2},{6,4},{7,6},{5,7},{3,5},{1,3},{0,1},{10,8},{12,10},{14... | collective-permute-start | bytes 1572872 | tf_op jit(solution)/shard_map/ppermute | solution.py:376
  200.3 22.2 %collective-permute-start.48 = (bf16[32,8192]{1,0:T(8,128)(2,1)S(1)}, bf16[32,8192]{1,0:T(8,128)(2,1)S(1)}, u32[]{:S(2)}, u32[]{:S(2)}) collective-permute-start(bf16[32,8192]{1,0:T(8,128)(2,1)S(1)} %add_convert_fusion.5), channel_id=1, source_target_pairs={{2,8},{4,10},{6,12},{7,14},{5,15},{3,13},{1,11},{0,9},{10,16},{12,... | collective-permute-start | bytes 1572872 | tf_op jit(solution)/shard_map/ppermute | solution.py:389
  201.9 20.6 %collective-permute-start.49 = (bf16[32,8192]{1,0:T(8,128)(2,1)S(1)}, bf16[32,8192]{1,0:T(8,128)(2,1)S(1)}, u32[]{:S(2)}, u32[]{:S(2)}) collective-permute-start(bf16[32,8192]{1,0:T(8,128)(2,1)S(1)} %add_convert_fusion.4), channel_id=1, source_target_pairs={{0,10},{2,12},{4,14},{6,15},{7,13},{5,11},{3,9},{1,8},{8,18},{10,2... | collective-permute-start | bytes 1572872 | tf_op jit(solution)/shard_map/ppermute | solution.py:386
  216.1 17.5 %collective-permute-start.51 = (bf16[32,8192]{1,0:T(8,128)(2,1)S(1)}, bf16[32,8192]{1,0:T(8,128)(2,1)S(1)}, u32[]{:S(2)}, u32[]{:S(2)}) collective-permute-start(bf16[32,8192]{1,0:T(8,128)(2,1)S(1)} %add_convert_fusion.1), channel_id=1, source_target_pairs={{2,8},{4,10},{6,12},{7,14},{5,15},{3,13},{1,11},{0,9},{10,16},{12,... | collective-permute-start | bytes 1572872 | tf_op jit(solution)/shard_map/ppermute | solution.py:389
  (50 other events, 791.9 us)

commit v11 on v10

--- a/solution.py
+++ b/solution.py
@@ -20,6 +20,7 @@
 F32 = jnp.float32
 BF16 = jnp.bfloat16
 VMEM_LIMIT = 24 * 1024 * 1024
+VMEM_MOST = 56 * 1024 * 1024
 QUICK = pl.CostEstimate(flops=1, bytes_accessed=1, transcendentals=0)
 VMEM_SMALL = 16 * 1024 * 1024
 
@@ -110,7 +111,7 @@
             out_specs=[pl.BlockSpec((half, wide), lambda i, places: (0, 0))] * (2 * blocks),
         ),
         out_shape=[jax.ShapeDtypeStruct((half, wide), BF16)] * (2 * blocks),
-        compiler_params=params(56 * 1024 * 1024),
+        compiler_params=params(VMEM_MOST),
         cost_estimate=pl.CostEstimate(
             flops=2 * rows * depth * wide * blocks,
             bytes_accessed=2 * (depth + rows) * wide * blocks,
@@ -174,7 +175,7 @@
     )(meta, *pieces, weight)
 
 
-def query(chunks, weight):
+def query(chunks, weight, limit=VMEM_LIMIT):
     rows = sum(chunk.shape[0] for chunk in chunks)
     depth, width = weight.shape
     wide = min(2 * HD, width)
@@ -212,7 +213,7 @@
         out_specs=pl.BlockSpec((rows, wide), lambda i: (0, i)),
         out_shape=jax.ShapeDtypeStruct((rows, width), BF16),
         scratch_shapes=[pltpu.VMEM((rows, depth), BF16), pltpu.VMEM((rows, 1), F32)],
-        compiler_params=params(),
+        compiler_params=params(limit),
         cost_estimate=pl.CostEstimate(
             flops=2 * rows * depth * width,
             bytes_accessed=2 * depth * (width + rows),
@@ -438,7 +439,7 @@
     ]
 
     weight_query, weight_out = w_query[0], w_out[0]
-    queries = [query([text_own, from_below[1], from_above[1]], weight_query)]
+    queries = [query([text_own, from_below[1], from_above[1]], weight_query, VMEM_MOST)]
 
     turns = [0, 3, 1, 2]
     came = ring_sums(

time: 236 us -> 236 us (level)
  local copies, waits for them, and re-layouts: 5.41 us -> 2.04 us
  Pallas kernels: 50.6 us -> 53.7 us
    unnamed x44 -> x52, local copies, waits for them, and re-layouts: 3.47 us -> 0.11 us
    pallas_call x4, Pallas kernels: 11.9 us -> 15.2 us  [query(): pl.pallas_call(kernel, grid=(width // wide,), in_specs=[pl.BlockSpec(chun...]
  transfers between devices with their start and end apart: 52 -> 52, of which waited for: 24 -> 24; matrix products, arithmetic and copies ran while one was open for 2% -> 2% of each run, Pallas kernels for 21% -> 23%
where the time goes in v11:
time: 236 us; the launch traced here: 235 us
  waiting for transfers between devices  119 us (50%)
  starting transfers between devices  54.2 us (23%)
  Pallas kernels  53.7 us (23%)
  other arithmetic  5.36 us (2%)
    ppermute x21, waiting for transfers between devices, up(): return lax.ppermute(value, 'mp', up_pairs)  56.5 us
    ppermute x20, waiting for transfers between devices, down(): return lax.ppermute(value, 'mp', down_pairs)  36.2 us
    ppermute x20, starting transfers between devices, down(): return lax.ppermute(value, 'mp', down_pairs)  28.4 us
    pallas_call x2, Pallas kernels, project(): pl.pallas_call(kernel, grid_spec=pltpu.PrefetchScalarGridSpec(num_scalar_...  17.1 us
    pallas_call x3, Pallas kernels, attend(): pl.pallas_call(kernel, grid_spec=pltpu.PrefetchScalarGridSpec(num_scalar_...  16.8 us
    ppermute x21, starting transfers between devices, up(): return lax.ppermute(value, 'mp', up_pairs)  16.6 us
    pallas_call x4, Pallas kernels, query(): pl.pallas_call(kernel, grid=(width // wide,), in_specs=[pl.BlockSpec(chun...  15.2 us
    ppermute x1, waiting for transfers between devices, local(): lax.ppermute(moving, 'section', [(s, (s + 2) % section_count) for s in ra...  10.8 us
  transfers between devices with their start and end apart: 52, of which 24 were waited for; matrix products, arithmetic and copies ran while one was open for 2% of the time, Pallas kernels for 23%

profile of v11, /device:TPU:0, one launch (start us, length us, event | category | flops | bytes accessed | tf_op | source)
XLA Modules:
  0.0 235.3 jit_solution(5599787332089786474)
XLA Ops:
  0.0 3.0 %collective-permute-start.3 = (bf16[64,8192]{1,0:T(8,128)(2,1)}, bf16[64,8192]{1,0:T(8,128)(2,1)S(1)}, u32[]{:S(2)}, u32[]{:S(2)}) collective-permute-start(bf16[64,8192]{1,0:T(8,128)(2,1)} %bitcast.22), channel_id=1, source_target_pairs={{2,0},{4,2},{6,4},{7,6},{5,7},{3,5},{1,3},{0,1},{10,8},{12,10},{14... | collective-permute-start | bytes 3145736 | tf_op jit(solution)/shard_map/ppermute | solution.py:377
  4.2 4.1 %project.3 = (bf16[160,1024]{1,0:T(8,128)(2,1)}, bf16[160,1024]{1,0:T(8,128)(2,1)}) custom-call(s32[10]{0:T(128)} %get-tuple-element.175.places_ref, bf16[320,960]{1,0:T(8,128)(2,1)} %feats_ref.3, bf16[960,8192]{1,0:T(8,128)(2,1)} %weight_ref.3), custom_call_target="tpu_custom_call" | custom-call | flops 629145600 | bytes 2621440 | tf_op jit(solution)/shard_map/project/pallas_call | solution.py:102
  10.3 13.1 %project.2 = (bf16[160,1024]{1,0:T(8,128)(2,1)}, bf16[160,1024]{1,0:T(8,128)(2,1)}, bf16[160,1024]{1,0:T(8,128)(2,1)}, bf16[160,1024]{1,0:T(8,128)(2,1)}, bf16[1...) custom-call(s32[10]{0:T(128)} %get-tuple-element.175.places_ref, ...), custom_call_target="tpu_custom_call" | custom-call | flops 4404019200 | bytes 18350080 | tf_op jit(solution)/shard_map/project/pallas_call | solution.py:102
  23.4 3.8 %collective-permute-done.3.refs_2_ = bf16[64,8192]{1,0:T(8,128)(2,1)S(1)} collective-permute-done((bf16[64,8192]{1,0:T(8,128)(2,1)}, bf16[64,8192]{1,0:T(8,128)(2,1)S(1)}, u32[]{:S(2)}, u32[]{:S(2)}) %collective-permute-start.3) | collective-permute-done | bytes 1048608 | tf_op jit(solution)/shard_map/ppermute | solution.py:377
  30.9 6.7 %query.4 = bf16[192,512]{1,0:T(8,128)(2,1)} custom-call(bf16[64,8192]{1,0:T(8,128)(2,1)} %bitcast.24, bf16[64,8192]{1,0:T(8,128)(2,1)} %copy-done.6, bf16[64,8192]{1,0:T(8,128)(2,1)} %copy-done.4, bf16[8192,512]{1,0:T(8,128)(2,1)} %bitcast.10), custom_call_target="tpu_custom_call" | custom-call | flops 1610612736 | bytes 11534336 | tf_op jit(solution)/shard_map/query/pallas_call | solution.py:208
  43.7 6.6 %collective-permute-done.5 = bf16[160,1024]{1,0:T(8,128)(2,1)S(1)} collective-permute-done((bf16[160,1024]{1,0:T(8,128)(2,1)S(1)}, bf16[160,1024]{1,0:T(8,128)(2,1)S(1)}, u32[]{:S(2)}, u32[]{:S(2)}) %collective-permute-start.5) | collective-permute-done | bytes 327712 | tf_op jit(solution)/shard_map/ppermute | solution.py:374
  52.7 3.9 %collective-permute-done.11 = bf16[160,1024]{1,0:T(8,128)(2,1)S(1)} collective-permute-done((bf16[160,1024]{1,0:T(8,128)(2,1)S(1)}, bf16[160,1024]{1,0:T(8,128)(2,1)S(1)}, u32[]{:S(2)}, u32[]{:S(2)}) %collective-permute-start.11) | collective-permute-done | bytes 327712 | tf_op jit(solution)/shard_map/ppermute | solution.py:377
  59.0 5.4 %collective-permute-done.9 = bf16[160,1024]{1,0:T(8,128)(2,1)S(1)} collective-permute-done((bf16[160,1024]{1,0:T(8,128)(2,1)S(1)}, bf16[160,1024]{1,0:T(8,128)(2,1)S(1)}, u32[]{:S(2)}, u32[]{:S(2)}) %collective-permute-start.9) | collective-permute-done | bytes 327712 | tf_op jit(solution)/shard_map/ppermute | solution.py:374
  66.7 4.7 %collective-permute-done.15.refs_4_ = bf16[160,1024]{1,0:T(8,128)(2,1)S(1)} collective-permute-done((bf16[160,1024]{1,0:T(8,128)(2,1)S(1)}, bf16[160,1024]{1,0:T(8,128)(2,1)S(1)}, u32[]{:S(2)}, u32[]{:S(2)}) %collective-permute-start.15) | collective-permute-done | bytes 327712 | tf_op jit(solution)/shard_map/ppermute | solution.py:374
  71.4 4.1 %collective-permute-done.17.refs_5_ = bf16[160,1024]{1,0:T(8,128)(2,1)S(1)} collective-permute-done((bf16[160,1024]{1,0:T(8,128)(2,1)S(1)}, bf16[160,1024]{1,0:T(8,128)(2,1)S(1)}, u32[]{:S(2)}, u32[]{:S(2)}) %collective-permute-start.17) | collective-permute-done | bytes 327712 | tf_op jit(solution)/shard_map/ppermute | solution.py:377
  81.8 10.8 %collective-permute-done.20.refs_2_ = bf16[320,1024]{1,0:T(8,128)(2,1)S(1)} collective-permute-done((bf16[320,1024]{1,0:T(8,128)(2,1)S(1)}, bf16[320,1024]{1,0:T(8,128)(2,1)S(1)}, u32[]{:S(2)}, u32[]{:S(2)}) %collective-permute-start.20) | collective-permute-done | bytes 655392 | tf_op jit(solution)/shard_map/ppermute | solution.py:462
  94.7 4.4 %key_values.1 = (bf16[256,256]{1,0:T(8,128)(2,1)S(1)}, bf16[256,256]{1,0:T(8,128)(2,1)S(1)}, bf16[256,256]{1,0:T(8,128)(2,1)S(1)}, bf16[256,256]{1,0:T(8,128)(2,...) custom-call(s32[18]{0:T(128)S(1)} %pad_add_fusion.meta_ref, ...), custom_call_target="tpu_custom_call" | custom-call | flops 1 | bytes 1 | tf_op jit(solution)/shard_map/key_values/pallas_call | solution.py:166
  106.8 10.8 %collective-permute-done.29 = bf16[256,256]{1,0:T(8,128)(2,1)S(1)} collective-permute-done((bf16[256,256]{1,0:T(8,128)(2,1)S(1)}, bf16[256,256]{1,0:T(8,128)(2,1)S(1)}, u32[]{:S(2)}, u32[]{:S(2)}) %collective-permute-start.29) | collective-permute-done | bytes 131104 | tf_op jit(solution)/shard_map/ppermute | solution.py:377
  129.3 9.6 %collective-permute-done.32 = bf16[256,256]{1,0:T(8,128)(2,1)S(1)} collective-permute-done((bf16[256,256]{1,0:T(8,128)(2,1)S(1)}, bf16[256,256]{1,0:T(8,128)(2,1)S(1)}, u32[]{:S(2)}, u32[]{:S(2)}) %collective-permute-start.32) | collective-permute-done | bytes 131104 | tf_op jit(solution)/shard_map/ppermute | solution.py:374
  145.6 5.3 %attend.3 = (bf16[32,8192]{1,0:T(8,128)(2,1)S(1)}, bf16[32,8192]{1,0:T(8,128)(2,1)S(1)}, bf16[32,8192]{1,0:T(8,128)(2,1)S(1)}, bf16[32,8192]{1,0:T(8,128)(2,1)S(1)}) custom-call(s32[18]{0:T(128)S(1)} %pad_add_fusion.meta_ref, bf16[128,512]{1,0:T(8,128)(2,1)S(1)} %query.5.query_ref, bf16[256,256]{1,0:T(8,128)(2,1)S(1)} %add_convert_fusion.22.refs_0_, ...), custom_call_target="tpu_custom_call" | custom-call | flops 4294967296 | bytes 33554432 | tf_op jit(solution)/shard_map/attend/pallas_call | solution.py:299
  153.0 2.8 %query.6 = bf16[128,512]{1,0:T(8,128)(2,1)S(1)} custom-call(bf16[64,8192]{1,0:T(8,128)(2,1)S(1)} %collective-permute-done.18.refs_0_, bf16[64,8192]{1,0:T(8,128)(2,1)S(1)} %collective-permute-done.24.refs_1_, bf16[8192,512]{1,0:T(8,128)(2,1)S(1)} %bitcast.14), custom_call_target="tpu_custom_call" | custom-call | flops 1073741824 | bytes 10485760 | tf_op jit(solution)/shard_map/query/pallas_call | solution.py:208
  156.7 2.8 %query.7.query_ref = bf16[64,512]{1,0:T(8,128)(2,1)S(1)} custom-call(bf16[32,8192]{1,0:T(8,128)(2,1)S(1)} %collective-permute-done.35.refs_0_, bf16[32,8192]{1,0:T(8,128)(2,1)S(1)} %collective-permute-done.36.refs_1_, bf16[8192,512]{1,0:T(8,128)(2,1)S(1)} %bitcast.15), custom_call_target="tpu_custom_call" | custom-call | flops 536870912 | bytes 9437184 | tf_op jit(solution)/shard_map/query/pallas_call | solution.py:208
  161.6 4.5 %attend.4 = (bf16[32,8192]{1,0:T(8,128)(2,1)S(1)}, bf16[32,8192]{1,0:T(8,128)(2,1)S(1)}) custom-call(s32[18]{0:T(128)S(1)} %pad_add_fusion.meta_ref, bf16[64,512]{1,0:T(8,128)(2,1)S(1)} %query.7.query_ref, bf16[256,256]{1,0:T(8,128)(2,1)S(1)} %add_convert_fusion.22.refs_0_, bf16[256,256]{1,0:T(8,128)(2,1)S(1)} %collective-permute-done.34.refs_1_, ...), custom_call_target="tpu_custom_call" | custom-call | flops 2147483648 | bytes 33554432 | tf_op jit(solution)/shard_map/attend/pallas_call | solution.py:299
  166.1 6.9 %attend.5 = (bf16[64,8192]{1,0:T(8,128)(2,1)S(1)}, bf16[32,8192]{1,0:T(8,128)(2,1)S(1)}, bf16[32,8192]{1,0:T(8,128)(2,1)S(1)}, bf16[32,8192]{1,0:T(8,128)(2,1)S(...) custom-call(s32[18]{0:T(128)S(1)} %pad_add_fusion.meta_ref, ...), custom_call_target="tpu_custom_call" | custom-call | flops 10737418240 | bytes 33554432 | tf_op jit(solution)/shard_map/attend/pallas_call | solution.py:299
  177.9 9.8 %collective-permute-done.39 = bf16[32,8192]{1,0:T(8,128)(2,1)S(1)} collective-permute-done((bf16[32,8192]{1,0:T(8,128)(2,1)S(1)}, bf16[32,8192]{1,0:T(8,128)(2,1)S(1)}, u32[]{:S(2)}, u32[]{:S(2)}) %collective-permute-start.39) | collective-permute-done | bytes 524320 | tf_op jit(solution)/shard_map/ppermute | solution.py:374
  190.1 9.9 %collective-permute-done.45 = bf16[32,8192]{1,0:T(8,128)(2,1)S(1)} collective-permute-done((bf16[32,8192]{1,0:T(8,128)(2,1)S(1)}, bf16[32,8192]{1,0:T(8,128)(2,1)S(1)}, u32[]{:S(2)}, u32[]{:S(2)}) %collective-permute-start.45) | collective-permute-done | bytes 524320 | tf_op jit(solution)/shard_map/ppermute | solution.py:377
  203.3 12.5 %collective-permute-done.43 = bf16[32,8192]{1,0:T(8,128)(2,1)S(1)} collective-permute-done((bf16[32,8192]{1,0:T(8,128)(2,1)S(1)}, bf16[32,8192]{1,0:T(8,128)(2,1)S(1)}, u32[]{:S(2)}, u32[]{:S(2)}) %collective-permute-start.43) | collective-permute-done | bytes 524320 | tf_op jit(solution)/shard_map/ppermute | solution.py:374
  216.1 2.9 %collective-permute-start.51 = (bf16[32,8192]{1,0:T(8,128)(2,1)S(1)}, bf16[32,8192]{1,0:T(8,128)(2,1)S(1)}, u32[]{:S(2)}, u32[]{:S(2)}) collective-permute-start(bf16[32,8192]{1,0:T(8,128)(2,1)S(1)} %add_convert_fusion.1), channel_id=1, source_target_pairs={{2,8},{4,10},{6,12},{7,14},{5,15},{3,13},{1,11},{0,9},{10,16},{12,... | collective-permute-start | bytes 1572872 | tf_op jit(solution)/shard_map/ppermute | solution.py:390
  222.5 8.7 %collective-permute-done.47 = bf16[32,8192]{1,0:T(8,128)(2,1)S(1)} collective-permute-done((bf16[32,8192]{1,0:T(8,128)(2,1)S(1)}, bf16[32,8192]{1,0:T(8,128)(2,1)S(1)}, u32[]{:S(2)}, u32[]{:S(2)}) %collective-permute-start.47) | collective-permute-done | bytes 524320 | tf_op jit(solution)/shard_map/ppermute | solution.py:387
  (186 shorter events, 76.8 us)
Async XLA Ops:
  0.0 27.2 %collective-permute-start.3 = (bf16[64,8192]{1,0:T(8,128)(2,1)}, bf16[64,8192]{1,0:T(8,128)(2,1)S(1)}, u32[]{:S(2)}, u32[]{:S(2)}) collective-permute-start(bf16[64,8192]{1,0:T(8,128)(2,1)} %bitcast.22), channel_id=1, source_target_pairs={{2,0},{4,2},{6,4},{7,6},{5,7},{3,5},{1,3},{0,1},{10,8},{12,10},{14... | collective-permute-start | bytes 3145736 | tf_op jit(solution)/shard_map/ppermute | solution.py:377
  3.0 26.3 %collective-permute-start.2 = (bf16[64,8192]{1,0:T(8,128)(2,1)}, bf16[64,8192]{1,0:T(8,128)(2,1)S(1)}, u32[]{:S(2)}, u32[]{:S(2)}) collective-permute-start(bf16[64,8192]{1,0:T(8,128)(2,1)} %bitcast.23), channel_id=1, source_target_pairs={{0,2},{2,4},{4,6},{6,7},{7,5},{5,3},{3,1},{1,0},{8,10},{10,12},{12... | collective-permute-start | bytes 3145736 | tf_op jit(solution)/shard_map/ppermute | solution.py:374
  3.0 34.6 %collective-permute-start.1 = (f32[1]{0:T(128)}, f32[1]{0:T(128)}, u32[]{:S(2)}, u32[]{:S(2)}) collective-permute-start(f32[1]{0:T(128)} %param.16), channel_id=1, source_target_pairs={{0,8},{8,16},{16,24},{24,0},{1,9},{9,17},{17,25},{25,1},{2,10},{10... | collective-permute-start | bytes 20 | tf_op jit(solution)/shard_map/ppermute | solution.py:393
  8.3 29.3 %collective-permute-start.4 = (bf16[160,1024]{1,0:T(8,128)(2,1)}, bf16[160,1024]{1,0:T(8,128)(2,1)S(1)}, u32[]{:S(2)}, u32[]{:S(2)}) collective-permute-start(bf16[160,1024]{1,0:T(8,128)(2,1)} %get-tuple-element.89), channel_id=1, source_target_pairs={{0,2},{2,4},{4,6},{6,7},{7,5},{5,3},{3,1},{1,0},{8,10},{10,12},{12... | collective-permute-start | bytes 983048 | tf_op jit(solution)/shard_map/ppermute | solution.py:374
  10.3 28.4 %collective-permute-start.8 = (bf16[160,1024]{1,0:T(8,128)(2,1)}, bf16[160,1024]{1,0:T(8,128)(2,1)S(1)}, u32[]{:S(2)}, u32[]{:S(2)}) collective-permute-start(bf16[160,1024]{1,0:T(8,128)(2,1)} %get-tuple-element.94), channel_id=1, source_target_pairs={{2,0},{4,2},{6,4},{7,6},{5,7},{3,5},{1,3},{0,1},{10,8},{12,10},{14... | collective-permute-start | bytes 983048 | tf_op jit(solution)/shard_map/ppermute | solution.py:377
  27.2 16.2 %collective-permute-start.6 = (bf16[160,1024]{1,0:T(8,128)(2,1)}, bf16[160,1024]{1,0:T(8,128)(2,1)S(1)}, u32[]{:S(2)}, u32[]{:S(2)}) collective-permute-start(bf16[160,1024]{1,0:T(8,128)(2,1)} %get-tuple-element.92), channel_id=1, source_target_pairs={{0,2},{2,4},{4,6},{6,7},{7,5},{5,3},{3,1},{1,0},{8,10},{10,12},{12... | collective-permute-start | bytes 983048 | tf_op jit(solution)/shard_map/ppermute | solution.py:374
  78.8 23.7 %collective-permute-start.18 = (bf16[64,8192]{1,0:T(8,128)(2,1)S(1)}, bf16[64,8192]{1,0:T(8,128)(2,1)S(1)}, u32[]{:S(2)}, u32[]{:S(2)}) collective-permute-start(bf16[64,8192]{1,0:T(8,128)(2,1)S(1)} %copy-done.7), channel_id=1, source_target_pairs={{0,2},{2,4},{4,6},{6,7},{7,5},{5,3},{3,1},{1,0},{8,10},{10,12},{12... | collective-permute-start | bytes 3145736 | tf_op jit(solution)/shard_map/ppermute | solution.py:374
  79.3 23.6 %collective-permute-start.24 = (bf16[64,8192]{1,0:T(8,128)(2,1)S(1)}, bf16[64,8192]{1,0:T(8,128)(2,1)S(1)}, u32[]{:S(2)}, u32[]{:S(2)}) collective-permute-start(bf16[64,8192]{1,0:T(8,128)(2,1)S(1)} %copy-done.5), channel_id=1, source_target_pairs={{2,0},{4,2},{6,4},{7,6},{5,7},{3,5},{1,3},{0,1},{10,8},{12,10},{14... | collective-permute-start | bytes 3145736 | tf_op jit(solution)/shard_map/ppermute | solution.py:377
  102.5 16.6 %collective-permute-start.22 = (bf16[32,8192]{1,0:T(8,128)(2,1)S(1)}, bf16[32,8192]{1,0:T(8,128)(2,1)S(1)}, u32[]{:S(2)}, u32[]{:S(2)}) collective-permute-start(bf16[32,8192]{1,0:T(8,128)(2,1)S(1)} %slice.30), channel_id=1, source_target_pairs={{0,2},{2,4},{4,6},{6,7},{7,5},{5,3},{3,1},{1,0},{8,10},{10,12},{12... | collective-permute-start | bytes 1572872 | tf_op jit(solution)/shard_map/ppermute | solution.py:374
  102.9 16.1 %collective-permute-start.25 = (bf16[32,8192]{1,0:T(8,128)(2,1)S(1)}, bf16[32,8192]{1,0:T(8,128)(2,1)S(1)}, u32[]{:S(2)}, u32[]{:S(2)}) collective-permute-start(bf16[32,8192]{1,0:T(8,128)(2,1)S(1)} %slice.31), channel_id=1, source_target_pairs={{2,0},{4,2},{6,4},{7,6},{5,7},{3,5},{1,3},{0,1},{10,8},{12,10},{14... | collective-permute-start | bytes 1572872 | tf_op jit(solution)/shard_map/ppermute | solution.py:377
  121.2 17.7 %collective-permute-start.23 = (bf16[32,8192]{1,0:T(8,128)(2,1)S(1)}, bf16[32,8192]{1,0:T(8,128)(2,1)S(1)}, u32[]{:S(2)}, u32[]{:S(2)}) collective-permute-start(bf16[32,8192]{1,0:T(8,128)(2,1)S(1)} %collective-permute-done.22.refs_2_), channel_id=1, source_target_pairs={{0,2},{2,4},{4,6},{6,7},{7,5},{5,3},{3,1},{1,0},{8,10},{10,12},{12... | collective-permute-start | bytes 1572872 | tf_op jit(solution)/shard_map/ppermute | solution.py:374
  121.7 17.2 %collective-permute-start.26 = (bf16[32,8192]{1,0:T(8,128)(2,1)S(1)}, bf16[32,8192]{1,0:T(8,128)(2,1)S(1)}, u32[]{:S(2)}, u32[]{:S(2)}) collective-permute-start(bf16[32,8192]{1,0:T(8,128)(2,1)S(1)} %collective-permute-done.25.refs_3_), channel_id=1, source_target_pairs={{2,0},{4,2},{6,4},{7,6},{5,7},{3,5},{1,3},{0,1},{10,8},{12,10},{14... | collective-permute-start | bytes 1572872 | tf_op jit(solution)/shard_map/ppermute | solution.py:377
  129.3 36.8 %collective-permute-start = (bf16[64,8192]{1,0:T(8,128)(2,1)S(1)}, bf16[64,8192]{1,0:T(8,128)(2,1)S(1)}, u32[]{:S(2)}, u32[]{:S(2)}) collective-permute-start(bf16[64,8192]{1,0:T(8,128)(2,1)S(1)} %bitcast.25), channel_id=1, source_target_pairs={{0,8},{8,16},{16,24},{24,0},{1,9},{9,17},{17,25},{25,1},{2,10},{10... | collective-permute-start | bytes 3145736 | tf_op jit(solution)/shard_map/ppermute | solution.py:393
  150.9 22.2 %collective-permute-start.38 = (bf16[32,8192]{1,0:T(8,128)(2,1)S(1)}, bf16[32,8192]{1,0:T(8,128)(2,1)S(1)}, u32[]{:S(2)}, u32[]{:S(2)}) collective-permute-start(bf16[32,8192]{1,0:T(8,128)(2,1)S(1)} %get-tuple-element.134), channel_id=1, source_target_pairs={{0,2},{2,4},{4,6},{6,7},{7,5},{5,3},{3,1},{1,0},{8,10},{10,12},{12... | collective-permute-start | bytes 1572872 | tf_op jit(solution)/shard_map/ppermute | solution.py:374
  152.5 20.7 %collective-permute-start.42 = (bf16[32,8192]{1,0:T(8,128)(2,1)S(1)}, bf16[32,8192]{1,0:T(8,128)(2,1)S(1)}, u32[]{:S(2)}, u32[]{:S(2)}) collective-permute-start(bf16[32,8192]{1,0:T(8,128)(2,1)S(1)} %get-tuple-element.148), channel_id=1, source_target_pairs={{2,0},{4,2},{6,4},{7,6},{5,7},{3,5},{1,3},{0,1},{10,8},{12,10},{14... | collective-permute-start | bytes 1572872 | tf_op jit(solution)/shard_map/ppermute | solution.py:377
  160.5 17.1 %collective-permute-start.40 = (bf16[32,8192]{1,0:T(8,128)(2,1)S(1)}, bf16[32,8192]{1,0:T(8,128)(2,1)S(1)}, u32[]{:S(2)}, u32[]{:S(2)}) collective-permute-start(bf16[32,8192]{1,0:T(8,128)(2,1)S(1)} %get-tuple-element.145), channel_id=1, source_target_pairs={{0,2},{2,4},{4,6},{6,7},{7,5},{5,3},{3,1},{1,0},{8,10},{10,12},{12... | collective-permute-start | bytes 1572872 | tf_op jit(solution)/shard_map/ppermute | solution.py:374
  173.0 27.2 %collective-permute-start.37 = (bf16[64,8192]{1,0:T(8,128)(2,1)S(1)}, bf16[64,8192]{1,0:T(8,128)(2,1)S(1)}, u32[]{:S(2)}, u32[]{:S(2)}) collective-permute-start(bf16[64,8192]{1,0:T(8,128)(2,1)S(1)} %get-tuple-element.141), channel_id=1, source_target_pairs={{0,8},{8,16},{16,24},{24,0},{1,9},{9,17},{17,25},{25,1},{2,10},{10... | collective-permute-start | bytes 3145736 | tf_op jit(solution)/shard_map/ppermute | solution.py:393
  175.6 24.4 %collective-permute-start.45 = (bf16[32,8192]{1,0:T(8,128)(2,1)S(1)}, bf16[32,8192]{1,0:T(8,128)(2,1)S(1)}, u32[]{:S(2)}, u32[]{:S(2)}) collective-permute-start(bf16[32,8192]{1,0:T(8,128)(2,1)S(1)} %add_convert_fusion.9), channel_id=1, source_target_pairs={{2,0},{4,2},{6,4},{7,6},{5,7},{3,5},{1,3},{0,1},{10,8},{12,10},{14... | collective-permute-start | bytes 1572872 | tf_op jit(solution)/shard_map/ppermute | solution.py:377
  177.7 22.4 %collective-permute-start.44 = (bf16[32,8192]{1,0:T(8,128)(2,1)S(1)}, bf16[32,8192]{1,0:T(8,128)(2,1)S(1)}, u32[]{:S(2)}, u32[]{:S(2)}) collective-permute-start(bf16[32,8192]{1,0:T(8,128)(2,1)S(1)} %add_convert_fusion.8), channel_id=1, source_target_pairs={{0,2},{2,4},{4,6},{6,7},{7,5},{5,3},{3,1},{1,0},{8,10},{10,12},{12... | collective-permute-start | bytes 1572872 | tf_op jit(solution)/shard_map/ppermute | solution.py:374
  187.8 27.9 %collective-permute-start.43 = (bf16[32,8192]{1,0:T(8,128)(2,1)S(1)}, bf16[32,8192]{1,0:T(8,128)(2,1)S(1)}, u32[]{:S(2)}, u32[]{:S(2)}) collective-permute-start(bf16[32,8192]{1,0:T(8,128)(2,1)S(1)} %add_convert_fusion.7), channel_id=1, source_target_pairs={{0,2},{2,4},{4,6},{6,7},{7,5},{5,3},{3,1},{1,0},{8,10},{10,12},{12... | collective-permute-start | bytes 1572872 | tf_op jit(solution)/shard_map/ppermute | solution.py:374
  188.9 27.0 %collective-permute-start.50 = (bf16[32,8192]{1,0:T(8,128)(2,1)S(1)}, bf16[32,8192]{1,0:T(8,128)(2,1)S(1)}, u32[]{:S(2)}, u32[]{:S(2)}) collective-permute-start(bf16[32,8192]{1,0:T(8,128)(2,1)S(1)} %add_convert_fusion.6), channel_id=1, source_target_pairs={{2,0},{4,2},{6,4},{7,6},{5,7},{3,5},{1,3},{0,1},{10,8},{12,10},{14... | collective-permute-start | bytes 1572872 | tf_op jit(solution)/shard_map/ppermute | solution.py:377
  200.3 22.2 %collective-permute-start.48 = (bf16[32,8192]{1,0:T(8,128)(2,1)S(1)}, bf16[32,8192]{1,0:T(8,128)(2,1)S(1)}, u32[]{:S(2)}, u32[]{:S(2)}) collective-permute-start(bf16[32,8192]{1,0:T(8,128)(2,1)S(1)} %add_convert_fusion.5), channel_id=1, source_target_pairs={{2,8},{4,10},{6,12},{7,14},{5,15},{3,13},{1,11},{0,9},{10,16},{12,... | collective-permute-start | bytes 1572872 | tf_op jit(solution)/shard_map/ppermute | solution.py:390
  201.9 20.6 %collective-permute-start.49 = (bf16[32,8192]{1,0:T(8,128)(2,1)S(1)}, bf16[32,8192]{1,0:T(8,128)(2,1)S(1)}, u32[]{:S(2)}, u32[]{:S(2)}) collective-permute-start(bf16[32,8192]{1,0:T(8,128)(2,1)S(1)} %add_convert_fusion.4), channel_id=1, source_target_pairs={{0,10},{2,12},{4,14},{6,15},{7,13},{5,11},{3,9},{1,8},{8,18},{10,2... | collective-permute-start | bytes 1572872 | tf_op jit(solution)/shard_map/ppermute | solution.py:387
  216.1 17.5 %collective-permute-start.51 = (bf16[32,8192]{1,0:T(8,128)(2,1)S(1)}, bf16[32,8192]{1,0:T(8,128)(2,1)S(1)}, u32[]{:S(2)}, u32[]{:S(2)}) collective-permute-start(bf16[32,8192]{1,0:T(8,128)(2,1)S(1)} %add_convert_fusion.1), channel_id=1, source_target_pairs={{2,8},{4,10},{6,12},{7,14},{5,15},{3,13},{1,11},{0,9},{10,16},{12,... | collective-permute-start | bytes 1572872 | tf_op jit(solution)/shard_map/ppermute | solution.py:390
  (54 other events, 849.8 us)

commit v12 on v11

--- a/solution.py
+++ b/solution.py
@@ -175,15 +175,47 @@
     )(meta, *pieces, weight)
 
 
-def query(chunks, weight, limit=VMEM_LIMIT):
+def row_scale(rows):
+    wider = rows.astype(F32)
+    return lax.rsqrt(jnp.mean(wider * wider, axis=-1, keepdims=True) + 1e-05)
+
+
+def row_scales(chunks):
+    rows = sum(chunk.shape[0] for chunk in chunks)
+    depth = chunks[0].shape[1]
+
+    def kernel(*refs):
+        first = 0
+        for chunk_ref in refs[:-1]:
+            size = chunk_ref.shape[0]
+            refs[-1][first : first + size, :] = jnp.broadcast_to(
+                row_scale(chunk_ref[...]), (size, HD)
+            )
+            first += size
+
+    return pl.pallas_call(
+        kernel,
+        in_specs=[pl.BlockSpec(memory_space=pltpu.VMEM)] * len(chunks),
+        out_specs=pl.BlockSpec(memory_space=pltpu.VMEM),
+        out_shape=jax.ShapeDtypeStruct((rows, HD), F32),
+        compiler_params=params(VMEM_SMALL),
+        cost_estimate=pl.CostEstimate(
+            flops=4 * rows * depth, bytes_accessed=8 * rows * depth, transcendentals=0
+        ),
+        name="row_scales",
+    )(*chunks)
+
+
+def query(chunks, weight, scales=None):
     rows = sum(chunk.shape[0] for chunk in chunks)
     depth, width = weight.shape
     wide = min(2 * HD, width)
     count = len(chunks)
+    given = [] if scales is None else [scales]
 
     def kernel(*refs):
-        chunk_refs, weight_ref, out_ref = refs[:count], refs[count], refs[count + 1]
-        rows_ref, scale_ref = refs[count + 2 :]
+        chunk_refs, weight_ref, out_ref = refs[:count], refs[count], refs[-3]
+        rows_ref, scale_ref = refs[-2:]
 
         @pl.when(pl.program_id(0) == 0)
         def _():
@@ -191,12 +223,12 @@
             for chunk_ref in chunk_refs:
                 place = slice(first, first + chunk_ref.shape[0])
                 chunk = chunk_ref[...]
-                wider = chunk.astype(F32)
                 rows_ref[place, :] = chunk
-                scale_ref[place, :] = lax.rsqrt(
-                    jnp.mean(wider * wider, axis=-1, keepdims=True) + 1e-05
-                )
+                if scales is None:
+                    scale_ref[place, :] = row_scale(chunk)
                 first += chunk_ref.shape[0]
+            if scales is not None:
+                scale_ref[...] = refs[count + 1][:, :1]
 
         projected = jnp.dot(rows_ref[...], weight_ref[...], preferred_element_type=F32)
         projected = projected * scale_ref[...]
@@ -209,18 +241,19 @@
         kernel,
         grid=(width // wide,),
         in_specs=[pl.BlockSpec(chunk.shape, lambda i: (0, 0)) for chunk in chunks]
-        + [pl.BlockSpec((depth, wide), lambda i: (0, i))],
+        + [pl.BlockSpec((depth, wide), lambda i: (0, i))]
+        + [pl.BlockSpec((rows, HD), lambda i: (0, 0)) for _ in given],
         out_specs=pl.BlockSpec((rows, wide), lambda i: (0, i)),
         out_shape=jax.ShapeDtypeStruct((rows, width), BF16),
         scratch_shapes=[pltpu.VMEM((rows, depth), BF16), pltpu.VMEM((rows, 1), F32)],
-        compiler_params=params(limit),
+        compiler_params=params(),
         cost_estimate=pl.CostEstimate(
             flops=2 * rows * depth * width,
             bytes_accessed=2 * depth * (width + rows),
             transcendentals=0,
         ),
         name="query",
-    )(*chunks, weight)
+    )(*chunks, weight, *given)
 
 
 def attend(meta, queries, kv_pieces, weight, indices, sizes, shard_rows, order_len):
@@ -438,12 +471,11 @@
         )
     ]
 
-    weight_query, weight_out = w_query[0], w_out[0]
-    queries = [query([text_own, from_below[1], from_above[1]], weight_query, VMEM_MOST)]
+    text_scales = row_scales([text_own, from_below[1], from_above[1]])
 
     turns = [0, 3, 1, 2]
     came = ring_sums(
-        [image_chains[turn] for turn in turns], turn=[gate_next, queries[0]]
+        [image_chains[turn] for turn in turns], turn=[gate_next, text_scales]
     )
     came = [came[turns.index(index)] for index in range(4)]
     image_cols = total_of(
@@ -487,7 +519,9 @@
     kv_own = (
         kv_part[index_of[0]].astype(F32) + came[0].astype(F32) + came[1].astype(F32)
     ).astype(BF16)
-    kv_own = after(kv_own, *far_chunks)
+    weight_query, weight_out = w_query[0], w_out[0]
+    queries = [query([text_own, from_below[1], from_above[1]], weight_query, text_scales)]
+    kv_own = after(kv_own, queries[0], *far_chunks)
     kv_pieces = [kv_own]
     for step in range(1, sharing):
         pairs = [
@@ -546,16 +580,15 @@
     turns = [0, 3, 1, 2] if parts == 2 else [0, 1]
     came = ring_sums([branch_chains[turn] for turn in turns], branch_hold)
     came = [came[turns.index(index)] for index in range(2 * parts)]
-    results = []
+    result = text_next
     for part in range(parts):
         place = slice(part * cut, (part + 1) * cut)
         branch = own_next[place].astype(F32)
         for value in came[2 * part : 2 * part + 2]:
             branch = branch + value.astype(F32)
-        results.append(
-            (text_next[place].astype(F32) + jnp.tanh(gate_next[0]) * branch).astype(BF16)
-        )
-    return jnp.concatenate(results, axis=0)[None]
+        rows = (text_next[place].astype(F32) + jnp.tanh(gate_next[0]) * branch).astype(BF16)
+        result = lax.dynamic_update_slice(result, rows, (part * cut, 0))
+    return result[None]
 
 
 def solution(mesh):

time: 236 us -> 236 us (level)
  other arithmetic: 5.36 us -> 9.93 us
  Pallas kernels: 53.7 us -> 50.6 us
  waiting for transfers between devices: 119 us -> 116 us
    convert_element_type x25, other arithmetic: 2.48 us -> 7.28 us  [add(): return (one.astype(F32) + other.astype(F32)).astype(BF16)]
    pallas_call x4, Pallas kernels: 15.2 us -> 11.4 us  [query(): pl.pallas_call(kernel, grid=(width // wide,), in_specs=[pl.BlockSpec(chun...]
  transfers between devices with their start and end apart: 52 -> 52, of which waited for: 24 -> 25; matrix products, arithmetic and copies ran while one was open for 2% -> 5% of each run, Pallas kernels for 23% -> 21%
where the time goes in v12:
time: 236 us; the launch traced here: 235 us
  waiting for transfers between devices  116 us (49%)
  starting transfers between devices  55 us (23%)
  Pallas kernels  50.6 us (21%)
  other arithmetic  9.93 us (4%)
    ppermute x21, waiting for transfers between devices, up(): return lax.ppermute(value, 'mp', up_pairs)  55.3 us
    ppermute x20, waiting for transfers between devices, down(): return lax.ppermute(value, 'mp', down_pairs)  34.8 us
    ppermute x20, starting transfers between devices, down(): return lax.ppermute(value, 'mp', down_pairs)  28.6 us
    pallas_call x2, Pallas kernels, project(): pl.pallas_call(kernel, grid_spec=pltpu.PrefetchScalarGridSpec(num_scalar_...  17.1 us
    pallas_call x3, Pallas kernels, attend(): pl.pallas_call(kernel, grid_spec=pltpu.PrefetchScalarGridSpec(num_scalar_...  16.8 us
    ppermute x21, starting transfers between devices, up(): return lax.ppermute(value, 'mp', up_pairs)  16.7 us
    pallas_call x4, Pallas kernels, query(): pl.pallas_call(kernel, grid=(width // wide,), in_specs=[pl.BlockSpec(chun...  11.4 us
    ppermute x1, waiting for transfers between devices, local(): lax.ppermute(moving, 'section', [(s, (s + 2) % section_count) for s in ra...  10.8 us
  transfers between devices with their start and end apart: 52, of which 25 were waited for; matrix products, arithmetic and copies ran while one was open for 5% of the time, Pallas kernels for 21%

profile of v12, /device:TPU:0, one launch (start us, length us, event | category | flops | bytes accessed | tf_op | source)
XLA Modules:
  0.0 235.4 jit_solution(9832448296472931042)
XLA Ops:
  0.0 3.0 %collective-permute-start.3 = (bf16[64,8192]{1,0:T(8,128)(2,1)}, bf16[64,8192]{1,0:T(8,128)(2,1)S(1)}, u32[]{:S(2)}, u32[]{:S(2)}) collective-permute-start(bf16[64,8192]{1,0:T(8,128)(2,1)} %bitcast.28), channel_id=1, source_target_pairs={{2,0},{4,2},{6,4},{7,6},{5,7},{3,5},{1,3},{0,1},{10,8},{12,10},{14... | collective-permute-start | bytes 3145736 | tf_op jit(solution)/shard_map/ppermute | solution.py:410
  4.3 4.0 %project.3 = (bf16[160,1024]{1,0:T(8,128)(2,1)}, bf16[160,1024]{1,0:T(8,128)(2,1)}) custom-call(s32[10]{0:T(128)} %get-tuple-element.173.places_ref, bf16[320,960]{1,0:T(8,128)(2,1)} %feats_ref.3, bf16[960,8192]{1,0:T(8,128)(2,1)} %weight_ref.3), custom_call_target="tpu_custom_call" | custom-call | flops 629145600 | bytes 2621440 | tf_op jit(solution)/shard_map/project/pallas_call | solution.py:102
  10.4 13.1 %project.2 = (bf16[160,1024]{1,0:T(8,128)(2,1)}, bf16[160,1024]{1,0:T(8,128)(2,1)}, bf16[160,1024]{1,0:T(8,128)(2,1)}, bf16[160,1024]{1,0:T(8,128)(2,1)}, bf16[1...) custom-call(s32[10]{0:T(128)} %get-tuple-element.173.places_ref, ...), custom_call_target="tpu_custom_call" | custom-call | flops 4404019200 | bytes 18350080 | tf_op jit(solution)/shard_map/project/pallas_call | solution.py:102
  23.5 3.7 %collective-permute-done.3.refs_2_ = bf16[64,8192]{1,0:T(8,128)(2,1)S(1)} collective-permute-done((bf16[64,8192]{1,0:T(8,128)(2,1)}, bf16[64,8192]{1,0:T(8,128)(2,1)S(1)}, u32[]{:S(2)}, u32[]{:S(2)}) %collective-permute-start.3) | collective-permute-done | bytes 1048608 | tf_op jit(solution)/shard_map/ppermute | solution.py:410
  31.5 4.7 %collective-permute-done.4 = bf16[160,1024]{1,0:T(8,128)(2,1)S(1)} collective-permute-done((bf16[160,1024]{1,0:T(8,128)(2,1)}, bf16[160,1024]{1,0:T(8,128)(2,1)S(1)}, u32[]{:S(2)}, u32[]{:S(2)}) %collective-permute-start.4) | collective-permute-done | bytes 327712 | tf_op jit(solution)/shard_map/ppermute | solution.py:407
  45.6 4.7 %collective-permute-done.5 = bf16[160,1024]{1,0:T(8,128)(2,1)S(1)} collective-permute-done((bf16[160,1024]{1,0:T(8,128)(2,1)S(1)}, bf16[160,1024]{1,0:T(8,128)(2,1)S(1)}, u32[]{:S(2)}, u32[]{:S(2)}) %collective-permute-start.5) | collective-permute-done | bytes 327712 | tf_op jit(solution)/shard_map/ppermute | solution.py:407
  58.6 5.7 %collective-permute-done.9 = bf16[160,1024]{1,0:T(8,128)(2,1)S(1)} collective-permute-done((bf16[160,1024]{1,0:T(8,128)(2,1)S(1)}, bf16[160,1024]{1,0:T(8,128)(2,1)S(1)}, u32[]{:S(2)}, u32[]{:S(2)}) %collective-permute-start.9) | collective-permute-done | bytes 327712 | tf_op jit(solution)/shard_map/ppermute | solution.py:407
  66.7 4.7 %collective-permute-done.15.refs_4_ = bf16[160,1024]{1,0:T(8,128)(2,1)S(1)} collective-permute-done((bf16[160,1024]{1,0:T(8,128)(2,1)S(1)}, bf16[160,1024]{1,0:T(8,128)(2,1)S(1)}, u32[]{:S(2)}, u32[]{:S(2)}) %collective-permute-start.15) | collective-permute-done | bytes 327712 | tf_op jit(solution)/shard_map/ppermute | solution.py:407
  71.4 4.1 %collective-permute-done.17.refs_5_ = bf16[160,1024]{1,0:T(8,128)(2,1)S(1)} collective-permute-done((bf16[160,1024]{1,0:T(8,128)(2,1)S(1)}, bf16[160,1024]{1,0:T(8,128)(2,1)S(1)}, u32[]{:S(2)}, u32[]{:S(2)}) %collective-permute-start.17) | collective-permute-done | bytes 327712 | tf_op jit(solution)/shard_map/ppermute | solution.py:410
  81.7 10.8 %collective-permute-done.20.refs_2_ = bf16[320,1024]{1,0:T(8,128)(2,1)S(1)} collective-permute-done((bf16[320,1024]{1,0:T(8,128)(2,1)S(1)}, bf16[320,1024]{1,0:T(8,128)(2,1)S(1)}, u32[]{:S(2)}, u32[]{:S(2)}) %collective-permute-start.20) | collective-permute-done | bytes 655392 | tf_op jit(solution)/shard_map/ppermute | solution.py:494
  94.7 4.4 %key_values.1 = (bf16[256,256]{1,0:T(8,128)(2,1)S(1)}, bf16[256,256]{1,0:T(8,128)(2,1)S(1)}, bf16[256,256]{1,0:T(8,128)(2,1)S(1)}, bf16[256,256]{1,0:T(8,128)(2,...) custom-call(s32[18]{0:T(128)S(1)} %pad_add_fusion.meta_ref, ...), custom_call_target="tpu_custom_call" | custom-call | flops 1 | bytes 1 | tf_op jit(solution)/shard_map/key_values/pallas_call | solution.py:166
  106.8 10.8 %collective-permute-done.29 = bf16[256,256]{1,0:T(8,128)(2,1)S(1)} collective-permute-done((bf16[256,256]{1,0:T(8,128)(2,1)S(1)}, bf16[256,256]{1,0:T(8,128)(2,1)S(1)}, u32[]{:S(2)}, u32[]{:S(2)}) %collective-permute-start.29) | collective-permute-done | bytes 131104 | tf_op jit(solution)/shard_map/ppermute | solution.py:410
  127.9 3.0 %query.4 = bf16[192,512]{1,0:T(8,128)(2,1)S(1)} custom-call(bf16[64,8192]{1,0:T(8,128)(2,1)S(1)} %bitcast.32, bf16[64,8192]{1,0:T(8,128)(2,1)S(1)} %collective-permute-done.2.refs_1_, bf16[64,8192]{1,0:T(8,128)(2,1)S(1)} %collective-permute-done.3.refs_2_, bf16[8192,512]{1,0:T(8,128)(2,1)S(1)} %bitcast.19, f32[192,128]{1,0:T(8,128)S(1)} %row_scales.1.refs_4_), custom_call_target="tpu_custom_call" | custom-call | flops 1610612736 | bytes 11534336 | tf_op jit(solution)/shard_map/query/pallas_call | solution.py:240
  130.9 7.9 %collective-permute-done.32 = bf16[256,256]{1,0:T(8,128)(2,1)S(1)} collective-permute-done((bf16[256,256]{1,0:T(8,128)(2,1)S(1)}, bf16[256,256]{1,0:T(8,128)(2,1)S(1)}, u32[]{:S(2)}, u32[]{:S(2)}) %collective-permute-start.32) | collective-permute-done | bytes 131104 | tf_op jit(solution)/shard_map/ppermute | solution.py:407
  146.2 5.3 %attend.3 = (bf16[32,8192]{1,0:T(8,128)(2,1)S(1)}, bf16[32,8192]{1,0:T(8,128)(2,1)S(1)}, bf16[32,8192]{1,0:T(8,128)(2,1)S(1)}, bf16[32,8192]{1,0:T(8,128)(2,1)S(1)}) custom-call(s32[18]{0:T(128)S(1)} %pad_add_fusion.meta_ref, bf16[128,512]{1,0:T(8,128)(2,1)S(1)} %query.5.query_ref, bf16[256,256]{1,0:T(8,128)(2,1)S(1)} %add_convert_fusion.22.refs_0_, ...), custom_call_target="tpu_custom_call" | custom-call | flops 4294967296 | bytes 33554432 | tf_op jit(solution)/shard_map/attend/pallas_call | solution.py:332
  156.7 2.8 %query.7.query_ref = bf16[64,512]{1,0:T(8,128)(2,1)S(1)} custom-call(bf16[32,8192]{1,0:T(8,128)(2,1)S(1)} %collective-permute-done.35.refs_0_, bf16[32,8192]{1,0:T(8,128)(2,1)S(1)} %collective-permute-done.36.refs_1_, bf16[8192,512]{1,0:T(8,128)(2,1)S(1)} %bitcast.22), custom_call_target="tpu_custom_call" | custom-call | flops 536870912 | bytes 9437184 | tf_op jit(solution)/shard_map/query/pallas_call | solution.py:240
  161.6 4.5 %attend.4 = (bf16[32,8192]{1,0:T(8,128)(2,1)S(1)}, bf16[32,8192]{1,0:T(8,128)(2,1)S(1)}) custom-call(s32[18]{0:T(128)S(1)} %pad_add_fusion.meta_ref, bf16[64,512]{1,0:T(8,128)(2,1)S(1)} %query.7.query_ref, bf16[256,256]{1,0:T(8,128)(2,1)S(1)} %add_convert_fusion.22.refs_0_, bf16[256,256]{1,0:T(8,128)(2,1)S(1)} %collective-permute-done.34.refs_1_, ...), custom_call_target="tpu_custom_call" | custom-call | flops 2147483648 | bytes 33554432 | tf_op jit(solution)/shard_map/attend/pallas_call | solution.py:332
  166.2 6.9 %attend.5 = (bf16[64,8192]{1,0:T(8,128)(2,1)S(1)}, bf16[32,8192]{1,0:T(8,128)(2,1)S(1)}, bf16[32,8192]{1,0:T(8,128)(2,1)S(1)}, bf16[32,8192]{1,0:T(8,128)(2,1)S(...) custom-call(s32[18]{0:T(128)S(1)} %pad_add_fusion.meta_ref, ...), custom_call_target="tpu_custom_call" | custom-call | flops 10737418240 | bytes 33554432 | tf_op jit(solution)/shard_map/attend/pallas_call | solution.py:332
  177.9 9.8 %collective-permute-done.39 = bf16[32,8192]{1,0:T(8,128)(2,1)S(1)} collective-permute-done((bf16[32,8192]{1,0:T(8,128)(2,1)S(1)}, bf16[32,8192]{1,0:T(8,128)(2,1)S(1)}, u32[]{:S(2)}, u32[]{:S(2)}) %collective-permute-start.39) | collective-permute-done | bytes 524320 | tf_op jit(solution)/shard_map/ppermute | solution.py:407
  190.2 10.4 %collective-permute-done.45 = bf16[32,8192]{1,0:T(8,128)(2,1)S(1)} collective-permute-done((bf16[32,8192]{1,0:T(8,128)(2,1)S(1)}, bf16[32,8192]{1,0:T(8,128)(2,1)S(1)}, u32[]{:S(2)}, u32[]{:S(2)}) %collective-permute-start.45) | collective-permute-done | bytes 524320 | tf_op jit(solution)/shard_map/ppermute | solution.py:410
  203.9 11.9 %collective-permute-done.43 = bf16[32,8192]{1,0:T(8,128)(2,1)S(1)} collective-permute-done((bf16[32,8192]{1,0:T(8,128)(2,1)S(1)}, bf16[32,8192]{1,0:T(8,128)(2,1)S(1)}, u32[]{:S(2)}, u32[]{:S(2)}) %collective-permute-start.43) | collective-permute-done | bytes 524320 | tf_op jit(solution)/shard_map/ppermute | solution.py:407
  216.1 3.4 %collective-permute-start.51 = (bf16[32,8192]{1,0:T(8,128)(2,1)S(1)}, bf16[32,8192]{1,0:T(8,128)(2,1)S(1)}, u32[]{:S(2)}, u32[]{:S(2)}) collective-permute-start(bf16[32,8192]{1,0:T(8,128)(2,1)S(1)} %add_convert_fusion.1), channel_id=1, source_target_pairs={{2,8},{4,10},{6,12},{7,14},{5,15},{3,13},{1,11},{0,9},{10,16},{12,... | collective-permute-start | bytes 1572872 | tf_op jit(solution)/shard_map/ppermute | solution.py:423
  219.5 3.6 %collective-permute-done.48 = bf16[32,8192]{1,0:T(8,128)(2,1)S(1)} collective-permute-done((bf16[32,8192]{1,0:T(8,128)(2,1)S(1)}, bf16[32,8192]{1,0:T(8,128)(2,1)S(1)}, u32[]{:S(2)}, u32[]{:S(2)}) %collective-permute-start.48) | collective-permute-done | bytes 524320 | tf_op jit(solution)/shard_map/ppermute | solution.py:423
  223.1 8.5 %collective-permute-done.47 = bf16[32,8192]{1,0:T(8,128)(2,1)S(1)} collective-permute-done((bf16[32,8192]{1,0:T(8,128)(2,1)S(1)}, bf16[32,8192]{1,0:T(8,128)(2,1)S(1)}, u32[]{:S(2)}, u32[]{:S(2)}) %collective-permute-start.47) | collective-permute-done | bytes 524320 | tf_op jit(solution)/shard_map/ppermute | solution.py:420
  (170 shorter events, 82.4 us)
Async XLA Ops:
  0.0 27.2 %collective-permute-start.3 = (bf16[64,8192]{1,0:T(8,128)(2,1)}, bf16[64,8192]{1,0:T(8,128)(2,1)S(1)}, u32[]{:S(2)}, u32[]{:S(2)}) collective-permute-start(bf16[64,8192]{1,0:T(8,128)(2,1)} %bitcast.28), channel_id=1, source_target_pairs={{2,0},{4,2},{6,4},{7,6},{5,7},{3,5},{1,3},{0,1},{10,8},{12,10},{14... | collective-permute-start | bytes 3145736 | tf_op jit(solution)/shard_map/ppermute | solution.py:410
  3.0 26.3 %collective-permute-start.2 = (bf16[64,8192]{1,0:T(8,128)(2,1)}, bf16[64,8192]{1,0:T(8,128)(2,1)S(1)}, u32[]{:S(2)}, u32[]{:S(2)}) collective-permute-start(bf16[64,8192]{1,0:T(8,128)(2,1)} %bitcast.29), channel_id=1, source_target_pairs={{0,2},{2,4},{4,6},{6,7},{7,5},{5,3},{3,1},{1,0},{8,10},{10,12},{12... | collective-permute-start | bytes 3145736 | tf_op jit(solution)/shard_map/ppermute | solution.py:407
  3.0 28.5 %collective-permute-start.1 = (f32[1]{0:T(128)}, f32[1]{0:T(128)}, u32[]{:S(2)}, u32[]{:S(2)}) collective-permute-start(f32[1]{0:T(128)} %param.16), channel_id=1, source_target_pairs={{0,8},{8,16},{16,24},{24,0},{1,9},{9,17},{17,25},{25,1},{2,10},{10... | collective-permute-start | bytes 20 | tf_op jit(solution)/shard_map/ppermute | solution.py:426
  8.4 27.9 %collective-permute-start.4 = (bf16[160,1024]{1,0:T(8,128)(2,1)}, bf16[160,1024]{1,0:T(8,128)(2,1)S(1)}, u32[]{:S(2)}, u32[]{:S(2)}) collective-permute-start(bf16[160,1024]{1,0:T(8,128)(2,1)} %get-tuple-element.89), channel_id=1, source_target_pairs={{0,2},{2,4},{4,6},{6,7},{7,5},{5,3},{3,1},{1,0},{8,10},{10,12},{12... | collective-permute-start | bytes 983048 | tf_op jit(solution)/shard_map/ppermute | solution.py:407
  10.4 27.1 %collective-permute-start.8 = (bf16[160,1024]{1,0:T(8,128)(2,1)}, bf16[160,1024]{1,0:T(8,128)(2,1)S(1)}, u32[]{:S(2)}, u32[]{:S(2)}) collective-permute-start(bf16[160,1024]{1,0:T(8,128)(2,1)} %get-tuple-element.94), channel_id=1, source_target_pairs={{2,0},{4,2},{6,4},{7,6},{5,7},{3,5},{1,3},{0,1},{10,8},{12,10},{14... | collective-permute-start | bytes 983048 | tf_op jit(solution)/shard_map/ppermute | solution.py:410
  27.2 17.2 %collective-permute-start.6 = (bf16[160,1024]{1,0:T(8,128)(2,1)}, bf16[160,1024]{1,0:T(8,128)(2,1)S(1)}, u32[]{:S(2)}, u32[]{:S(2)}) collective-permute-start(bf16[160,1024]{1,0:T(8,128)(2,1)} %get-tuple-element.92), channel_id=1, source_target_pairs={{0,2},{2,4},{4,6},{6,7},{7,5},{5,3},{3,1},{1,0},{8,10},{10,12},{12... | collective-permute-start | bytes 983048 | tf_op jit(solution)/shard_map/ppermute | solution.py:407
  78.8 23.7 %collective-permute-start.18 = (bf16[64,8192]{1,0:T(8,128)(2,1)S(1)}, bf16[64,8192]{1,0:T(8,128)(2,1)S(1)}, u32[]{:S(2)}, u32[]{:S(2)}) collective-permute-start(bf16[64,8192]{1,0:T(8,128)(2,1)S(1)} %collective-permute-done.2.refs_1_), channel_id=1, source_target_pairs={{0,2},{2,4},{4,6},{6,7},{7,5},{5,3},{3,1},{1,0},{8,10},{10,12},{12... | collective-permute-start | bytes 3145736 | tf_op jit(solution)/shard_map/ppermute | solution.py:407
  79.3 23.6 %collective-permute-start.24 = (bf16[64,8192]{1,0:T(8,128)(2,1)S(1)}, bf16[64,8192]{1,0:T(8,128)(2,1)S(1)}, u32[]{:S(2)}, u32[]{:S(2)}) collective-permute-start(bf16[64,8192]{1,0:T(8,128)(2,1)S(1)} %collective-permute-done.3.refs_2_), channel_id=1, source_target_pairs={{2,0},{4,2},{6,4},{7,6},{5,7},{3,5},{1,3},{0,1},{10,8},{12,10},{14... | collective-permute-start | bytes 3145736 | tf_op jit(solution)/shard_map/ppermute | solution.py:410
  102.5 16.5 %collective-permute-start.22 = (bf16[32,8192]{1,0:T(8,128)(2,1)S(1)}, bf16[32,8192]{1,0:T(8,128)(2,1)S(1)}, u32[]{:S(2)}, u32[]{:S(2)}) collective-permute-start(bf16[32,8192]{1,0:T(8,128)(2,1)S(1)} %slice.30), channel_id=1, source_target_pairs={{0,2},{2,4},{4,6},{6,7},{7,5},{5,3},{3,1},{1,0},{8,10},{10,12},{12... | collective-permute-start | bytes 1572872 | tf_op jit(solution)/shard_map/ppermute | solution.py:407
  102.9 16.1 %collective-permute-start.25 = (bf16[32,8192]{1,0:T(8,128)(2,1)S(1)}, bf16[32,8192]{1,0:T(8,128)(2,1)S(1)}, u32[]{:S(2)}, u32[]{:S(2)}) collective-permute-start(bf16[32,8192]{1,0:T(8,128)(2,1)S(1)} %slice.31), channel_id=1, source_target_pairs={{2,0},{4,2},{6,4},{7,6},{5,7},{3,5},{1,3},{0,1},{10,8},{12,10},{14... | collective-permute-start | bytes 1572872 | tf_op jit(solution)/shard_map/ppermute | solution.py:410
  104.7 36.5 %collective-permute-start = (bf16[64,8192]{1,0:T(8,128)(2,1)S(1)}, bf16[64,8192]{1,0:T(8,128)(2,1)S(1)}, u32[]{:S(2)}, u32[]{:S(2)}) collective-permute-start(bf16[64,8192]{1,0:T(8,128)(2,1)S(1)} %bitcast.31), channel_id=1, source_target_pairs={{0,8},{8,16},{16,24},{24,0},{1,9},{9,17},{17,25},{25,1},{2,10},{10... | collective-permute-start | bytes 3145736 | tf_op jit(solution)/shard_map/ppermute | solution.py:426
  121.2 17.7 %collective-permute-start.23 = (bf16[32,8192]{1,0:T(8,128)(2,1)S(1)}, bf16[32,8192]{1,0:T(8,128)(2,1)S(1)}, u32[]{:S(2)}, u32[]{:S(2)}) collective-permute-start(bf16[32,8192]{1,0:T(8,128)(2,1)S(1)} %collective-permute-done.22.refs_2_), channel_id=1, source_target_pairs={{0,2},{2,4},{4,6},{6,7},{7,5},{5,3},{3,1},{1,0},{8,10},{10,12},{12... | collective-permute-start | bytes 1572872 | tf_op jit(solution)/shard_map/ppermute | solution.py:407
  121.7 17.2 %collective-permute-start.26 = (bf16[32,8192]{1,0:T(8,128)(2,1)S(1)}, bf16[32,8192]{1,0:T(8,128)(2,1)S(1)}, u32[]{:S(2)}, u32[]{:S(2)}) collective-permute-start(bf16[32,8192]{1,0:T(8,128)(2,1)S(1)} %collective-permute-done.25.refs_3_), channel_id=1, source_target_pairs={{2,0},{4,2},{6,4},{7,6},{5,7},{3,5},{1,3},{0,1},{10,8},{12,10},{14... | collective-permute-start | bytes 1572872 | tf_op jit(solution)/shard_map/ppermute | solution.py:410
  151.6 21.6 %collective-permute-start.38 = (bf16[32,8192]{1,0:T(8,128)(2,1)S(1)}, bf16[32,8192]{1,0:T(8,128)(2,1)S(1)}, u32[]{:S(2)}, u32[]{:S(2)}) collective-permute-start(bf16[32,8192]{1,0:T(8,128)(2,1)S(1)} %get-tuple-element.134), channel_id=1, source_target_pairs={{0,2},{2,4},{4,6},{6,7},{7,5},{5,3},{3,1},{1,0},{8,10},{10,12},{12... | collective-permute-start | bytes 1572872 | tf_op jit(solution)/shard_map/ppermute | solution.py:407
  153.2 20.1 %collective-permute-start.42 = (bf16[32,8192]{1,0:T(8,128)(2,1)S(1)}, bf16[32,8192]{1,0:T(8,128)(2,1)S(1)}, u32[]{:S(2)}, u32[]{:S(2)}) collective-permute-start(bf16[32,8192]{1,0:T(8,128)(2,1)S(1)} %get-tuple-element.148), channel_id=1, source_target_pairs={{2,0},{4,2},{6,4},{7,6},{5,7},{3,5},{1,3},{0,1},{10,8},{12,10},{14... | collective-permute-start | bytes 1572872 | tf_op jit(solution)/shard_map/ppermute | solution.py:410
  160.1 17.4 %collective-permute-start.40 = (bf16[32,8192]{1,0:T(8,128)(2,1)S(1)}, bf16[32,8192]{1,0:T(8,128)(2,1)S(1)}, u32[]{:S(2)}, u32[]{:S(2)}) collective-permute-start(bf16[32,8192]{1,0:T(8,128)(2,1)S(1)} %get-tuple-element.145), channel_id=1, source_target_pairs={{0,2},{2,4},{4,6},{6,7},{7,5},{5,3},{3,1},{1,0},{8,10},{10,12},{12... | collective-permute-start | bytes 1572872 | tf_op jit(solution)/shard_map/ppermute | solution.py:407
  173.1 27.8 %collective-permute-start.37 = (bf16[64,8192]{1,0:T(8,128)(2,1)S(1)}, bf16[64,8192]{1,0:T(8,128)(2,1)S(1)}, u32[]{:S(2)}, u32[]{:S(2)}) collective-permute-start(bf16[64,8192]{1,0:T(8,128)(2,1)S(1)} %get-tuple-element.141), channel_id=1, source_target_pairs={{0,8},{8,16},{16,24},{24,0},{1,9},{9,17},{17,25},{25,1},{2,10},{10... | collective-permute-start | bytes 3145736 | tf_op jit(solution)/shard_map/ppermute | solution.py:426
  175.6 25.0 %collective-permute-start.45 = (bf16[32,8192]{1,0:T(8,128)(2,1)S(1)}, bf16[32,8192]{1,0:T(8,128)(2,1)S(1)}, u32[]{:S(2)}, u32[]{:S(2)}) collective-permute-start(bf16[32,8192]{1,0:T(8,128)(2,1)S(1)} %add_convert_fusion.9), channel_id=1, source_target_pairs={{2,0},{4,2},{6,4},{7,6},{5,7},{3,5},{1,3},{0,1},{10,8},{12,10},{14... | collective-permute-start | bytes 1572872 | tf_op jit(solution)/shard_map/ppermute | solution.py:410
  177.7 23.1 %collective-permute-start.44 = (bf16[32,8192]{1,0:T(8,128)(2,1)S(1)}, bf16[32,8192]{1,0:T(8,128)(2,1)S(1)}, u32[]{:S(2)}, u32[]{:S(2)}) collective-permute-start(bf16[32,8192]{1,0:T(8,128)(2,1)S(1)} %add_convert_fusion.8), channel_id=1, source_target_pairs={{0,2},{2,4},{4,6},{6,7},{7,5},{5,3},{3,1},{1,0},{8,10},{10,12},{12... | collective-permute-start | bytes 1572872 | tf_op jit(solution)/shard_map/ppermute | solution.py:407
  187.8 28.0 %collective-permute-start.43 = (bf16[32,8192]{1,0:T(8,128)(2,1)S(1)}, bf16[32,8192]{1,0:T(8,128)(2,1)S(1)}, u32[]{:S(2)}, u32[]{:S(2)}) collective-permute-start(bf16[32,8192]{1,0:T(8,128)(2,1)S(1)} %add_convert_fusion.7), channel_id=1, source_target_pairs={{0,2},{2,4},{4,6},{6,7},{7,5},{5,3},{3,1},{1,0},{8,10},{10,12},{12... | collective-permute-start | bytes 1572872 | tf_op jit(solution)/shard_map/ppermute | solution.py:407
  189.6 26.4 %collective-permute-start.50 = (bf16[32,8192]{1,0:T(8,128)(2,1)S(1)}, bf16[32,8192]{1,0:T(8,128)(2,1)S(1)}, u32[]{:S(2)}, u32[]{:S(2)}) collective-permute-start(bf16[32,8192]{1,0:T(8,128)(2,1)S(1)} %add_convert_fusion.6), channel_id=1, source_target_pairs={{2,0},{4,2},{6,4},{7,6},{5,7},{3,5},{1,3},{0,1},{10,8},{12,10},{14... | collective-permute-start | bytes 1572872 | tf_op jit(solution)/shard_map/ppermute | solution.py:410
  200.9 22.2 %collective-permute-start.48 = (bf16[32,8192]{1,0:T(8,128)(2,1)S(1)}, bf16[32,8192]{1,0:T(8,128)(2,1)S(1)}, u32[]{:S(2)}, u32[]{:S(2)}) collective-permute-start(bf16[32,8192]{1,0:T(8,128)(2,1)S(1)} %add_convert_fusion.5), channel_id=1, source_target_pairs={{2,8},{4,10},{6,12},{7,14},{5,15},{3,13},{1,11},{0,9},{10,16},{12,... | collective-permute-start | bytes 1572872 | tf_op jit(solution)/shard_map/ppermute | solution.py:423
  201.9 30.0 %collective-permute-start.49 = (bf16[32,8192]{1,0:T(8,128)(2,1)S(1)}, bf16[32,8192]{1,0:T(8,128)(2,1)S(1)}, u32[]{:S(2)}, u32[]{:S(2)}) collective-permute-start(bf16[32,8192]{1,0:T(8,128)(2,1)S(1)} %add_convert_fusion.4), channel_id=1, source_target_pairs={{0,10},{2,12},{4,14},{6,15},{7,13},{5,11},{3,9},{1,8},{8,18},{10,2... | collective-permute-start | bytes 1572872 | tf_op jit(solution)/shard_map/ppermute | solution.py:420
  216.1 18.2 %collective-permute-start.51 = (bf16[32,8192]{1,0:T(8,128)(2,1)S(1)}, bf16[32,8192]{1,0:T(8,128)(2,1)S(1)}, u32[]{:S(2)}, u32[]{:S(2)}) collective-permute-start(bf16[32,8192]{1,0:T(8,128)(2,1)S(1)} %add_convert_fusion.1), channel_id=1, source_target_pairs={{2,8},{4,10},{6,12},{7,14},{5,15},{3,13},{1,11},{0,9},{10,16},{12,... | collective-permute-start | bytes 1572872 | tf_op jit(solution)/shard_map/ppermute | solution.py:423
  (45 other events, 1034.2 us)

commit v13 on v12

--- a/solution.py
+++ b/solution.py
@@ -20,7 +20,7 @@
 F32 = jnp.float32
 BF16 = jnp.bfloat16
 VMEM_LIMIT = 24 * 1024 * 1024
-VMEM_MOST = 56 * 1024 * 1024
+VMEM_MOST = 50 * 1024 * 1024
 QUICK = pl.CostEstimate(flops=1, bytes_accessed=1, transcendentals=0)
 VMEM_SMALL = 16 * 1024 * 1024
 
@@ -580,15 +580,16 @@
     turns = [0, 3, 1, 2] if parts == 2 else [0, 1]
     came = ring_sums([branch_chains[turn] for turn in turns], branch_hold)
     came = [came[turns.index(index)] for index in range(2 * parts)]
-    result = text_next
+    results = []
     for part in range(parts):
         place = slice(part * cut, (part + 1) * cut)
         branch = own_next[place].astype(F32)
         for value in came[2 * part : 2 * part + 2]:
             branch = branch + value.astype(F32)
-        rows = (text_next[place].astype(F32) + jnp.tanh(gate_next[0]) * branch).astype(BF16)
-        result = lax.dynamic_update_slice(result, rows, (part * cut, 0))
-    return result[None]
+        results.append(
+            (text_next[place].astype(F32) + jnp.tanh(gate_next[0]) * branch).astype(BF16)
+        )
+    return jnp.concatenate(results, axis=0)[None]
 
 
 def solution(mesh):

time: 236 us -> 236 us (level)
  waiting for transfers between devices: 116 us -> 124 us
  other arithmetic: 9.93 us -> 5.3 us
  Pallas kernels: 50.6 us -> 48 us
    convert_element_type x25, other arithmetic: 7.28 us -> 2.43 us  [add(): return (one.astype(F32) + other.astype(F32)).astype(BF16)]
    ppermute x21, waiting for transfers between devices: 55.3 us -> 59.3 us  [up(): return lax.ppermute(value, 'mp', up_pairs)]
    ppermute x20, waiting for transfers between devices: 34.8 us -> 38.4 us  [down(): return lax.ppermute(value, 'mp', down_pairs)]
    pallas_call x2, Pallas kernels: 17.1 us -> 14.5 us  [project(): pl.pallas_call(kernel, grid_spec=pltpu.PrefetchScalarGridSpec(num_scalar_...]
  transfers between devices with their start and end apart: 52 -> 52, of which waited for: 25 -> 25; matrix products, arithmetic and copies ran while one was open for 5% -> 2% of each run, Pallas kernels for 21% -> 20%
where the time goes in v13:
time: 236 us; the launch traced here: 235 us
  waiting for transfers between devices  124 us (53%)
  starting transfers between devices  54.6 us (23%)
  Pallas kernels  48 us (20%)
  other arithmetic  5.3 us (2%)
  local copies, waits for them, and re-layouts  2.54 us (1%)
    ppermute x21, waiting for transfers between devices, up(): return lax.ppermute(value, 'mp', up_pairs)  59.3 us
    ppermute x20, waiting for transfers between devices, down(): return lax.ppermute(value, 'mp', down_pairs)  38.4 us
    ppermute x20, starting transfers between devices, down(): return lax.ppermute(value, 'mp', down_pairs)  30 us
    pallas_call x3, Pallas kernels, attend(): pl.pallas_call(kernel, grid_spec=pltpu.PrefetchScalarGridSpec(num_scalar_...  16.7 us
    ppermute x21, starting transfers between devices, up(): return lax.ppermute(value, 'mp', up_pairs)  15.3 us
    pallas_call x2, Pallas kernels, project(): pl.pallas_call(kernel, grid_spec=pltpu.PrefetchScalarGridSpec(num_scalar_...  14.5 us
    pallas_call x4, Pallas kernels, query(): pl.pallas_call(kernel, grid=(width // wide,), in_specs=[pl.BlockSpec(chun...  11.4 us
    ppermute x1, waiting for transfers between devices, local(): lax.ppermute(moving, 'section', [(s, (s + 2) % section_count) for s in ra...  10.8 us
  transfers between devices with their start and end apart: 52, of which 25 were waited for; matrix products, arithmetic and copies ran while one was open for 2% of the time, Pallas kernels for 20%

profile of v13, /device:TPU:0, one launch (start us, length us, event | category | flops | bytes accessed | tf_op | source)
XLA Modules:
  0.0 235.2 jit_solution(9735880171614137916)
XLA Ops:
  0.0 3.0 %collective-permute-start.3 = (bf16[64,8192]{1,0:T(8,128)(2,1)}, bf16[64,8192]{1,0:T(8,128)(2,1)S(1)}, u32[]{:S(2)}, u32[]{:S(2)}) collective-permute-start(bf16[64,8192]{1,0:T(8,128)(2,1)} %bitcast.21), channel_id=1, source_target_pairs={{2,0},{4,2},{6,4},{7,6},{5,7},{3,5},{1,3},{0,1},{10,8},{12,10},{14... | collective-permute-start | bytes 3145736 | tf_op jit(solution)/shard_map/ppermute | solution.py:410
  4.8 2.9 %project.3 = (bf16[160,1024]{1,0:T(8,128)(2,1)S(1)}, bf16[160,1024]{1,0:T(8,128)(2,1)S(1)}) custom-call(s32[10]{0:T(128)S(1)} %get-tuple-element.175.places_ref, bf16[320,960]{1,0:T(8,128)(2,1)S(1)} %copy-done.1, bf16[960,8192]{1,0:T(8,128)(2,1)} %weight_ref.3), custom_call_target="tpu_custom_call" | custom-call | flops 629145600 | bytes 2621440 | tf_op jit(solution)/shard_map/project/pallas_call | solution.py:102
  9.8 11.6 %project.2 = (bf16[160,1024]{1,0:T(8,128)(2,1)S(1)}, bf16[160,1024]{1,0:T(8,128)(2,1)S(1)}, bf16[160,1024]{1,0:T(8,128)(2,1)S(1)}, bf16[160,1024]{1,0:T(8,128)(2...) custom-call(s32[10]{0:T(128)S(1)} %get-tuple-element.175.places_ref,, ...), custom_call_target="tpu_custom_call" | custom-call | flops 4404019200 | bytes 18350080 | tf_op jit(solution)/shard_map/project/pallas_call | solution.py:102
  21.4 5.8 %collective-permute-done.3.refs_2_ = bf16[64,8192]{1,0:T(8,128)(2,1)S(1)} collective-permute-done((bf16[64,8192]{1,0:T(8,128)(2,1)}, bf16[64,8192]{1,0:T(8,128)(2,1)S(1)}, u32[]{:S(2)}, u32[]{:S(2)}) %collective-permute-start.3) | collective-permute-done | bytes 1048608 | tf_op jit(solution)/shard_map/ppermute | solution.py:410
  31.5 4.7 %collective-permute-done.4 = bf16[160,1024]{1,0:T(8,128)(2,1)S(1)} collective-permute-done((bf16[160,1024]{1,0:T(8,128)(2,1)S(1)}, bf16[160,1024]{1,0:T(8,128)(2,1)S(1)}, u32[]{:S(2)}, u32[]{:S(2)}) %collective-permute-start.4) | collective-permute-done | bytes 327712 | tf_op jit(solution)/shard_map/ppermute | solution.py:407
  43.7 6.7 %collective-permute-done.5 = bf16[160,1024]{1,0:T(8,128)(2,1)S(1)} collective-permute-done((bf16[160,1024]{1,0:T(8,128)(2,1)S(1)}, bf16[160,1024]{1,0:T(8,128)(2,1)S(1)}, u32[]{:S(2)}, u32[]{:S(2)}) %collective-permute-start.5) | collective-permute-done | bytes 327712 | tf_op jit(solution)/shard_map/ppermute | solution.py:407
  57.7 6.7 %collective-permute-done.9 = bf16[160,1024]{1,0:T(8,128)(2,1)S(1)} collective-permute-done((bf16[160,1024]{1,0:T(8,128)(2,1)S(1)}, bf16[160,1024]{1,0:T(8,128)(2,1)S(1)}, u32[]{:S(2)}, u32[]{:S(2)}) %collective-permute-start.9) | collective-permute-done | bytes 327712 | tf_op jit(solution)/shard_map/ppermute | solution.py:407
  66.7 4.7 %collective-permute-done.15.refs_4_ = bf16[160,1024]{1,0:T(8,128)(2,1)S(1)} collective-permute-done((bf16[160,1024]{1,0:T(8,128)(2,1)S(1)}, bf16[160,1024]{1,0:T(8,128)(2,1)S(1)}, u32[]{:S(2)}, u32[]{:S(2)}) %collective-permute-start.15) | collective-permute-done | bytes 327712 | tf_op jit(solution)/shard_map/ppermute | solution.py:407
  71.4 4.1 %collective-permute-done.17.refs_5_ = bf16[160,1024]{1,0:T(8,128)(2,1)S(1)} collective-permute-done((bf16[160,1024]{1,0:T(8,128)(2,1)S(1)}, bf16[160,1024]{1,0:T(8,128)(2,1)S(1)}, u32[]{:S(2)}, u32[]{:S(2)}) %collective-permute-start.17) | collective-permute-done | bytes 327712 | tf_op jit(solution)/shard_map/ppermute | solution.py:410
  81.7 10.8 %collective-permute-done.20.refs_2_ = bf16[320,1024]{1,0:T(8,128)(2,1)S(1)} collective-permute-done((bf16[320,1024]{1,0:T(8,128)(2,1)S(1)}, bf16[320,1024]{1,0:T(8,128)(2,1)S(1)}, u32[]{:S(2)}, u32[]{:S(2)}) %collective-permute-start.20) | collective-permute-done | bytes 655392 | tf_op jit(solution)/shard_map/ppermute | solution.py:494
  94.7 4.4 %key_values.1 = (bf16[256,256]{1,0:T(8,128)(2,1)S(1)}, bf16[256,256]{1,0:T(8,128)(2,1)S(1)}, bf16[256,256]{1,0:T(8,128)(2,1)S(1)}, bf16[256,256]{1,0:T(8,128)(2,...) custom-call(s32[18]{0:T(128)S(1)} %pad_add_fusion.meta_ref, ...), custom_call_target="tpu_custom_call" | custom-call | flops 1 | bytes 1 | tf_op jit(solution)/shard_map/key_values/pallas_call | solution.py:166
  106.8 11.0 %collective-permute-done.29 = bf16[256,256]{1,0:T(8,128)(2,1)S(1)} collective-permute-done((bf16[256,256]{1,0:T(8,128)(2,1)S(1)}, bf16[256,256]{1,0:T(8,128)(2,1)S(1)}, u32[]{:S(2)}, u32[]{:S(2)}) %collective-permute-start.29) | collective-permute-done | bytes 131104 | tf_op jit(solution)/shard_map/ppermute | solution.py:410
  127.9 3.0 %query.4 = bf16[192,512]{1,0:T(8,128)(2,1)S(1)} custom-call(bf16[64,8192]{1,0:T(8,128)(2,1)S(1)} %bitcast.25, bf16[64,8192]{1,0:T(8,128)(2,1)S(1)} %collective-permute-done.2.refs_1_, bf16[64,8192]{1,0:T(8,128)(2,1)S(1)} %collective-permute-done.3.refs_2_, bf16[8192,512]{1,0:T(8,128)(2,1)S(1)} %bitcast.12, f32[192,128]{1,0:T(8,128)S(1)} %row_scales.1.refs_4_), custom_call_target="tpu_custom_call" | custom-call | flops 1610612736 | bytes 11534336 | tf_op jit(solution)/shard_map/query/pallas_call | solution.py:240
  130.9 7.9 %collective-permute-done.32 = bf16[256,256]{1,0:T(8,128)(2,1)S(1)} collective-permute-done((bf16[256,256]{1,0:T(8,128)(2,1)S(1)}, bf16[256,256]{1,0:T(8,128)(2,1)S(1)}, u32[]{:S(2)}, u32[]{:S(2)}) %collective-permute-start.32) | collective-permute-done | bytes 131104 | tf_op jit(solution)/shard_map/ppermute | solution.py:407
  142.7 2.8 %query.5.query_ref = bf16[128,512]{1,0:T(8,128)(2,1)S(1)} custom-call(bf16[32,8192]{1,0:T(8,128)(2,1)S(1)} %collective-permute-done.23.refs_0_, bf16[32,8192]{1,0:T(8,128)(2,1)S(1)} %collective-permute-done.26.refs_1_, bf16[32,8192]{1,0:T(8,128)(2,1)S(1)} %collective-permute-done.22.refs_2_, bf16[32,8192]{1,0:T(8,128)(2,1)S(1)} %collective-permute-done.25.refs_3_, ...), custom_call_target="tpu_custom_call" | custom-call | flops 1073741824 | bytes 10485760 | tf_op jit(solution)/shard_map/query/pallas_call | solution.py:240
  145.6 5.3 %attend.3 = (bf16[32,8192]{1,0:T(8,128)(2,1)S(1)}, bf16[32,8192]{1,0:T(8,128)(2,1)S(1)}, bf16[32,8192]{1,0:T(8,128)(2,1)S(1)}, bf16[32,8192]{1,0:T(8,128)(2,1)S(1)}) custom-call(s32[18]{0:T(128)S(1)} %pad_add_fusion.meta_ref, bf16[128,512]{1,0:T(8,128)(2,1)S(1)} %query.5.query_ref, bf16[256,256]{1,0:T(8,128)(2,1)S(1)} %add_convert_fusion.22.refs_0_, ...), custom_call_target="tpu_custom_call" | custom-call | flops 4294967296 | bytes 33554432 | tf_op jit(solution)/shard_map/attend/pallas_call | solution.py:332
  156.6 2.8 %query.7.query_ref = bf16[64,512]{1,0:T(8,128)(2,1)S(1)} custom-call(bf16[32,8192]{1,0:T(8,128)(2,1)S(1)} %collective-permute-done.35.refs_0_, bf16[32,8192]{1,0:T(8,128)(2,1)S(1)} %collective-permute-done.36.refs_1_, bf16[8192,512]{1,0:T(8,128)(2,1)S(1)} %bitcast.15), custom_call_target="tpu_custom_call" | custom-call | flops 536870912 | bytes 9437184 | tf_op jit(solution)/shard_map/query/pallas_call | solution.py:240
  161.6 4.5 %attend.4 = (bf16[32,8192]{1,0:T(8,128)(2,1)S(1)}, bf16[32,8192]{1,0:T(8,128)(2,1)S(1)}) custom-call(s32[18]{0:T(128)S(1)} %pad_add_fusion.meta_ref, bf16[64,512]{1,0:T(8,128)(2,1)S(1)} %query.7.query_ref, bf16[256,256]{1,0:T(8,128)(2,1)S(1)} %add_convert_fusion.22.refs_0_, bf16[256,256]{1,0:T(8,128)(2,1)S(1)} %collective-permute-done.34.refs_1_, ...), custom_call_target="tpu_custom_call" | custom-call | flops 2147483648 | bytes 33554432 | tf_op jit(solution)/shard_map/attend/pallas_call | solution.py:332
  166.1 6.9 %attend.5 = (bf16[64,8192]{1,0:T(8,128)(2,1)S(1)}, bf16[32,8192]{1,0:T(8,128)(2,1)S(1)}, bf16[32,8192]{1,0:T(8,128)(2,1)S(1)}, bf16[32,8192]{1,0:T(8,128)(2,1)S(...) custom-call(s32[18]{0:T(128)S(1)} %pad_add_fusion.meta_ref, ...), custom_call_target="tpu_custom_call" | custom-call | flops 10737418240 | bytes 33554432 | tf_op jit(solution)/shard_map/attend/pallas_call | solution.py:332
  177.9 9.8 %collective-permute-done.39 = bf16[32,8192]{1,0:T(8,128)(2,1)S(1)} collective-permute-done((bf16[32,8192]{1,0:T(8,128)(2,1)S(1)}, bf16[32,8192]{1,0:T(8,128)(2,1)S(1)}, u32[]{:S(2)}, u32[]{:S(2)}) %collective-permute-start.39) | collective-permute-done | bytes 524320 | tf_op jit(solution)/shard_map/ppermute | solution.py:407
  190.1 9.8 %collective-permute-done.45 = bf16[32,8192]{1,0:T(8,128)(2,1)S(1)} collective-permute-done((bf16[32,8192]{1,0:T(8,128)(2,1)S(1)}, bf16[32,8192]{1,0:T(8,128)(2,1)S(1)}, u32[]{:S(2)}, u32[]{:S(2)}) %collective-permute-start.45) | collective-permute-done | bytes 524320 | tf_op jit(solution)/shard_map/ppermute | solution.py:410
  203.2 12.5 %collective-permute-done.43 = bf16[32,8192]{1,0:T(8,128)(2,1)S(1)} collective-permute-done((bf16[32,8192]{1,0:T(8,128)(2,1)S(1)}, bf16[32,8192]{1,0:T(8,128)(2,1)S(1)}, u32[]{:S(2)}, u32[]{:S(2)}) %collective-permute-start.43) | collective-permute-done | bytes 524320 | tf_op jit(solution)/shard_map/ppermute | solution.py:407
  216.1 2.9 %collective-permute-start.51 = (bf16[32,8192]{1,0:T(8,128)(2,1)S(1)}, bf16[32,8192]{1,0:T(8,128)(2,1)S(1)}, u32[]{:S(2)}, u32[]{:S(2)}) collective-permute-start(bf16[32,8192]{1,0:T(8,128)(2,1)S(1)} %add_convert_fusion.1), channel_id=1, source_target_pairs={{2,8},{4,10},{6,12},{7,14},{5,15},{3,13},{1,11},{0,9},{10,16},{12,... | collective-permute-start | bytes 1572872 | tf_op jit(solution)/shard_map/ppermute | solution.py:423
  222.5 8.7 %collective-permute-done.47 = bf16[32,8192]{1,0:T(8,128)(2,1)S(1)} collective-permute-done((bf16[32,8192]{1,0:T(8,128)(2,1)S(1)}, bf16[32,8192]{1,0:T(8,128)(2,1)S(1)}, u32[]{:S(2)}, u32[]{:S(2)}) %collective-permute-start.47) | collective-permute-done | bytes 524320 | tf_op jit(solution)/shard_map/ppermute | solution.py:420
  (157 shorter events, 80.6 us)
Async XLA Ops:
  0.0 27.2 %collective-permute-start.3 = (bf16[64,8192]{1,0:T(8,128)(2,1)}, bf16[64,8192]{1,0:T(8,128)(2,1)S(1)}, u32[]{:S(2)}, u32[]{:S(2)}) collective-permute-start(bf16[64,8192]{1,0:T(8,128)(2,1)} %bitcast.21), channel_id=1, source_target_pairs={{2,0},{4,2},{6,4},{7,6},{5,7},{3,5},{1,3},{0,1},{10,8},{12,10},{14... | collective-permute-start | bytes 3145736 | tf_op jit(solution)/shard_map/ppermute | solution.py:410
  3.0 26.3 %collective-permute-start.2 = (bf16[64,8192]{1,0:T(8,128)(2,1)}, bf16[64,8192]{1,0:T(8,128)(2,1)S(1)}, u32[]{:S(2)}, u32[]{:S(2)}) collective-permute-start(bf16[64,8192]{1,0:T(8,128)(2,1)} %bitcast.22), channel_id=1, source_target_pairs={{0,2},{2,4},{4,6},{6,7},{7,5},{5,3},{3,1},{1,0},{8,10},{10,12},{12... | collective-permute-start | bytes 3145736 | tf_op jit(solution)/shard_map/ppermute | solution.py:407
  3.0 28.5 %collective-permute-start.1 = (f32[1]{0:T(128)}, f32[1]{0:T(128)}, u32[]{:S(2)}, u32[]{:S(2)}) collective-permute-start(f32[1]{0:T(128)} %param.16), channel_id=1, source_target_pairs={{0,8},{8,16},{16,24},{24,0},{1,9},{9,17},{17,25},{25,1},{2,10},{10... | collective-permute-start | bytes 20 | tf_op jit(solution)/shard_map/ppermute | solution.py:426
  7.7 28.5 %collective-permute-start.4 = (bf16[160,1024]{1,0:T(8,128)(2,1)S(1)}, bf16[160,1024]{1,0:T(8,128)(2,1)S(1)}, u32[]{:S(2)}, u32[]{:S(2)}) collective-permute-start(bf16[160,1024]{1,0:T(8,128)(2,1)S(1)} %get-tuple-element.89), channel_id=1, source_target_pairs={{0,2},{2,4},{4,6},{6,7},{7,5},{5,3},{3,1},{1,0},{8,10},{10,12},{12... | collective-permute-start | bytes 983048 | tf_op jit(solution)/shard_map/ppermute | solution.py:407
  9.8 26.7 %collective-permute-start.8 = (bf16[160,1024]{1,0:T(8,128)(2,1)S(1)}, bf16[160,1024]{1,0:T(8,128)(2,1)S(1)}, u32[]{:S(2)}, u32[]{:S(2)}) collective-permute-start(bf16[160,1024]{1,0:T(8,128)(2,1)S(1)} %get-tuple-element.94), channel_id=1, source_target_pairs={{2,0},{4,2},{6,4},{7,6},{5,7},{3,5},{1,3},{0,1},{10,8},{12,10},{14... | collective-permute-start | bytes 983048 | tf_op jit(solution)/shard_map/ppermute | solution.py:410
  27.2 16.2 %collective-permute-start.6 = (bf16[160,1024]{1,0:T(8,128)(2,1)S(1)}, bf16[160,1024]{1,0:T(8,128)(2,1)S(1)}, u32[]{:S(2)}, u32[]{:S(2)}) collective-permute-start(bf16[160,1024]{1,0:T(8,128)(2,1)S(1)} %get-tuple-element.92), channel_id=1, source_target_pairs={{0,2},{2,4},{4,6},{6,7},{7,5},{5,3},{3,1},{1,0},{8,10},{10,12},{12... | collective-permute-start | bytes 983048 | tf_op jit(solution)/shard_map/ppermute | solution.py:407
  78.8 23.7 %collective-permute-start.18 = (bf16[64,8192]{1,0:T(8,128)(2,1)S(1)}, bf16[64,8192]{1,0:T(8,128)(2,1)S(1)}, u32[]{:S(2)}, u32[]{:S(2)}) collective-permute-start(bf16[64,8192]{1,0:T(8,128)(2,1)S(1)} %collective-permute-done.2.refs_1_), channel_id=1, source_target_pairs={{0,2},{2,4},{4,6},{6,7},{7,5},{5,3},{3,1},{1,0},{8,10},{10,12},{12... | collective-permute-start | bytes 3145736 | tf_op jit(solution)/shard_map/ppermute | solution.py:407
  79.3 23.9 %collective-permute-start.24 = (bf16[64,8192]{1,0:T(8,128)(2,1)S(1)}, bf16[64,8192]{1,0:T(8,128)(2,1)S(1)}, u32[]{:S(2)}, u32[]{:S(2)}) collective-permute-start(bf16[64,8192]{1,0:T(8,128)(2,1)S(1)} %collective-permute-done.3.refs_2_), channel_id=1, source_target_pairs={{2,0},{4,2},{6,4},{7,6},{5,7},{3,5},{1,3},{0,1},{10,8},{12,10},{14... | collective-permute-start | bytes 3145736 | tf_op jit(solution)/shard_map/ppermute | solution.py:410
  102.5 16.5 %collective-permute-start.22 = (bf16[32,8192]{1,0:T(8,128)(2,1)S(1)}, bf16[32,8192]{1,0:T(8,128)(2,1)S(1)}, u32[]{:S(2)}, u32[]{:S(2)}) collective-permute-start(bf16[32,8192]{1,0:T(8,128)(2,1)S(1)} %slice.30), channel_id=1, source_target_pairs={{0,2},{2,4},{4,6},{6,7},{7,5},{5,3},{3,1},{1,0},{8,10},{10,12},{12... | collective-permute-start | bytes 1572872 | tf_op jit(solution)/shard_map/ppermute | solution.py:407
  104.7 61.4 %collective-permute-start = (bf16[64,8192]{1,0:T(8,128)(2,1)S(1)}, bf16[64,8192]{1,0:T(8,128)(2,1)S(1)}, u32[]{:S(2)}, u32[]{:S(2)}) collective-permute-start(bf16[64,8192]{1,0:T(8,128)(2,1)S(1)} %bitcast.24), channel_id=1, source_target_pairs={{0,8},{8,16},{16,24},{24,0},{1,9},{9,17},{17,25},{25,1},{2,10},{10... | collective-permute-start | bytes 3145736 | tf_op jit(solution)/shard_map/ppermute | solution.py:426
  121.2 17.7 %collective-permute-start.23 = (bf16[32,8192]{1,0:T(8,128)(2,1)S(1)}, bf16[32,8192]{1,0:T(8,128)(2,1)S(1)}, u32[]{:S(2)}, u32[]{:S(2)}) collective-permute-start(bf16[32,8192]{1,0:T(8,128)(2,1)S(1)} %collective-permute-done.22.refs_2_), channel_id=1, source_target_pairs={{0,2},{2,4},{4,6},{6,7},{7,5},{5,3},{3,1},{1,0},{8,10},{10,12},{12... | collective-permute-start | bytes 1572872 | tf_op jit(solution)/shard_map/ppermute | solution.py:407
  121.8 17.1 %collective-permute-start.26 = (bf16[32,8192]{1,0:T(8,128)(2,1)S(1)}, bf16[32,8192]{1,0:T(8,128)(2,1)S(1)}, u32[]{:S(2)}, u32[]{:S(2)}) collective-permute-start(bf16[32,8192]{1,0:T(8,128)(2,1)S(1)} %collective-permute-done.25.refs_3_), channel_id=1, source_target_pairs={{2,0},{4,2},{6,4},{7,6},{5,7},{3,5},{1,3},{0,1},{10,8},{12,10},{14... | collective-permute-start | bytes 1572872 | tf_op jit(solution)/shard_map/ppermute | solution.py:410
  150.9 22.2 %collective-permute-start.38 = (bf16[32,8192]{1,0:T(8,128)(2,1)S(1)}, bf16[32,8192]{1,0:T(8,128)(2,1)S(1)}, u32[]{:S(2)}, u32[]{:S(2)}) collective-permute-start(bf16[32,8192]{1,0:T(8,128)(2,1)S(1)} %get-tuple-element.134), channel_id=1, source_target_pairs={{0,2},{2,4},{4,6},{6,7},{7,5},{5,3},{3,1},{1,0},{8,10},{10,12},{12... | collective-permute-start | bytes 1572872 | tf_op jit(solution)/shard_map/ppermute | solution.py:407
  152.5 20.7 %collective-permute-start.42 = (bf16[32,8192]{1,0:T(8,128)(2,1)S(1)}, bf16[32,8192]{1,0:T(8,128)(2,1)S(1)}, u32[]{:S(2)}, u32[]{:S(2)}) collective-permute-start(bf16[32,8192]{1,0:T(8,128)(2,1)S(1)} %get-tuple-element.148), channel_id=1, source_target_pairs={{2,0},{4,2},{6,4},{7,6},{5,7},{3,5},{1,3},{0,1},{10,8},{12,10},{14... | collective-permute-start | bytes 1572872 | tf_op jit(solution)/shard_map/ppermute | solution.py:410
  159.5 16.0 %collective-permute-start.41 = (bf16[32,8192]{1,0:T(8,128)(2,1)S(1)}, bf16[32,8192]{1,0:T(8,128)(2,1)S(1)}, u32[]{:S(2)}, u32[]{:S(2)}) collective-permute-start(bf16[32,8192]{1,0:T(8,128)(2,1)S(1)} %get-tuple-element.147), channel_id=1, source_target_pairs={{2,0},{4,2},{6,4},{7,6},{5,7},{3,5},{1,3},{0,1},{10,8},{12,10},{14... | collective-permute-start | bytes 1572872 | tf_op jit(solution)/shard_map/ppermute | solution.py:410
  160.5 17.1 %collective-permute-start.40 = (bf16[32,8192]{1,0:T(8,128)(2,1)S(1)}, bf16[32,8192]{1,0:T(8,128)(2,1)S(1)}, u32[]{:S(2)}, u32[]{:S(2)}) collective-permute-start(bf16[32,8192]{1,0:T(8,128)(2,1)S(1)} %get-tuple-element.145), channel_id=1, source_target_pairs={{0,2},{2,4},{4,6},{6,7},{7,5},{5,3},{3,1},{1,0},{8,10},{10,12},{12... | collective-permute-start | bytes 1572872 | tf_op jit(solution)/shard_map/ppermute | solution.py:407
  173.0 27.2 %collective-permute-start.37 = (bf16[64,8192]{1,0:T(8,128)(2,1)S(1)}, bf16[64,8192]{1,0:T(8,128)(2,1)S(1)}, u32[]{:S(2)}, u32[]{:S(2)}) collective-permute-start(bf16[64,8192]{1,0:T(8,128)(2,1)S(1)} %get-tuple-element.141), channel_id=1, source_target_pairs={{0,8},{8,16},{16,24},{24,0},{1,9},{9,17},{17,25},{25,1},{2,10},{10... | collective-permute-start | bytes 3145736 | tf_op jit(solution)/shard_map/ppermute | solution.py:426
  175.6 24.3 %collective-permute-start.45 = (bf16[32,8192]{1,0:T(8,128)(2,1)S(1)}, bf16[32,8192]{1,0:T(8,128)(2,1)S(1)}, u32[]{:S(2)}, u32[]{:S(2)}) collective-permute-start(bf16[32,8192]{1,0:T(8,128)(2,1)S(1)} %add_convert_fusion.9), channel_id=1, source_target_pairs={{2,0},{4,2},{6,4},{7,6},{5,7},{3,5},{1,3},{0,1},{10,8},{12,10},{14... | collective-permute-start | bytes 1572872 | tf_op jit(solution)/shard_map/ppermute | solution.py:410
  177.7 22.3 %collective-permute-start.44 = (bf16[32,8192]{1,0:T(8,128)(2,1)S(1)}, bf16[32,8192]{1,0:T(8,128)(2,1)S(1)}, u32[]{:S(2)}, u32[]{:S(2)}) collective-permute-start(bf16[32,8192]{1,0:T(8,128)(2,1)S(1)} %add_convert_fusion.8), channel_id=1, source_target_pairs={{0,2},{2,4},{4,6},{6,7},{7,5},{5,3},{3,1},{1,0},{8,10},{10,12},{12... | collective-permute-start | bytes 1572872 | tf_op jit(solution)/shard_map/ppermute | solution.py:407
  187.8 28.0 %collective-permute-start.43 = (bf16[32,8192]{1,0:T(8,128)(2,1)S(1)}, bf16[32,8192]{1,0:T(8,128)(2,1)S(1)}, u32[]{:S(2)}, u32[]{:S(2)}) collective-permute-start(bf16[32,8192]{1,0:T(8,128)(2,1)S(1)} %add_convert_fusion.7), channel_id=1, source_target_pairs={{0,2},{2,4},{4,6},{6,7},{7,5},{5,3},{3,1},{1,0},{8,10},{10,12},{12... | collective-permute-start | bytes 1572872 | tf_op jit(solution)/shard_map/ppermute | solution.py:407
  188.8 27.1 %collective-permute-start.50 = (bf16[32,8192]{1,0:T(8,128)(2,1)S(1)}, bf16[32,8192]{1,0:T(8,128)(2,1)S(1)}, u32[]{:S(2)}, u32[]{:S(2)}) collective-permute-start(bf16[32,8192]{1,0:T(8,128)(2,1)S(1)} %add_convert_fusion.6), channel_id=1, source_target_pairs={{2,0},{4,2},{6,4},{7,6},{5,7},{3,5},{1,3},{0,1},{10,8},{12,10},{14... | collective-permute-start | bytes 1572872 | tf_op jit(solution)/shard_map/ppermute | solution.py:410
  200.2 22.3 %collective-permute-start.48 = (bf16[32,8192]{1,0:T(8,128)(2,1)S(1)}, bf16[32,8192]{1,0:T(8,128)(2,1)S(1)}, u32[]{:S(2)}, u32[]{:S(2)}) collective-permute-start(bf16[32,8192]{1,0:T(8,128)(2,1)S(1)} %add_convert_fusion.5), channel_id=1, source_target_pairs={{2,8},{4,10},{6,12},{7,14},{5,15},{3,13},{1,11},{0,9},{10,16},{12,... | collective-permute-start | bytes 1572872 | tf_op jit(solution)/shard_map/ppermute | solution.py:423
  201.9 20.6 %collective-permute-start.49 = (bf16[32,8192]{1,0:T(8,128)(2,1)S(1)}, bf16[32,8192]{1,0:T(8,128)(2,1)S(1)}, u32[]{:S(2)}, u32[]{:S(2)}) collective-permute-start(bf16[32,8192]{1,0:T(8,128)(2,1)S(1)} %add_convert_fusion.4), channel_id=1, source_target_pairs={{0,10},{2,12},{4,14},{6,15},{7,13},{5,11},{3,9},{1,8},{8,18},{10,2... | collective-permute-start | bytes 1572872 | tf_op jit(solution)/shard_map/ppermute | solution.py:420
  216.1 17.5 %collective-permute-start.51 = (bf16[32,8192]{1,0:T(8,128)(2,1)S(1)}, bf16[32,8192]{1,0:T(8,128)(2,1)S(1)}, u32[]{:S(2)}, u32[]{:S(2)}) collective-permute-start(bf16[32,8192]{1,0:T(8,128)(2,1)S(1)} %add_convert_fusion.1), channel_id=1, source_target_pairs={{2,8},{4,10},{6,12},{7,14},{5,15},{3,13},{1,11},{0,9},{10,16},{12,... | collective-permute-start | bytes 1572872 | tf_op jit(solution)/shard_map/ppermute | solution.py:423
  (39 other events, 613.5 us)

commit v14 on v13

--- a/solution.py
+++ b/solution.py
@@ -503,13 +503,29 @@
         text_round(*([kv_part[0]] if distance == 3 else []))
     below, above = (after(value[-1], kv_part[0]) for value in (from_below, from_above))
     low = slice(text_rows - cut, text_rows)
-    onward = [up(below[:cut]), down(above[low])]
-    far_chunks = [up(onward[0])]
-    if parts == 2:
-        far_chunks.append(down(onward[1]))
+    fine = 2 if parts == 2 and cut % 32 == 0 and far > 3 else 1
+    size = cut // fine
+
+    def both(values, *first):
+        return [up(after(values[0], *first)), down(after(values[1], *first))]
+
+    def piece(index):
+        start = index * size
+        return [below[start : start + size], above[low][start : start + size]]
+
+    onward, distant, sent = [both(piece(0))], [], []
 
     def kv_hold(left, value):
-        return after(value, *onward) if left == min(2, far - 1) else value
+        sent.append(value)
+        if fine == 2 and len(sent) == 4:
+            onward.append(both(piece(1), *sent[2:]))
+        if fine == 2 and len(sent) == 6:
+            distant.append(both(onward[0], *sent[4:]))
+        if fine == 2 and len(sent) == 7:
+            distant.append(both(onward[1], sent[6]))
+        if left == min(2, far - 1):
+            return after(value, *onward[0])
+        return after(value, *onward[-1]) if left == 1 else value
 
     came = ring_sums(
         both_ways(lambda offset: kv_part[index_of[offset]], far, far - 1),
@@ -521,7 +537,9 @@
     ).astype(BF16)
     weight_query, weight_out = w_query[0], w_out[0]
     queries = [query([text_own, from_below[1], from_above[1]], weight_query, text_scales)]
-    kv_own = after(kv_own, queries[0], *far_chunks)
+    if fine == 1:
+        distant = [both(onward[0])[:parts]]
+    kv_own = after(kv_own, queries[0], *distant[0])
     kv_pieces = [kv_own]
     for step in range(1, sharing):
         pairs = [
@@ -541,7 +559,13 @@
     near = [sign * distance for distance in range(1, last) for sign in (-1, 1)]
     out_parts = {offset: [None] * parts for offset in [last, -last]}
     first = [far] * parts + [-last, last]
-    first_queries = query(far_chunks + onward, weight_query)
+    first_chunks = [
+        pair[side]
+        for pieces in (distant, onward)
+        for side in range(len(pieces[0]))
+        for pair in pieces
+    ]
+    first_queries = query(first_chunks, weight_query)
     first_part = attend_to(first, first_queries, [cut] * len(first))
     out_parts[far] = out_parts[-far] = first_part[:parts]
     out_parts[-last][0], out_parts[last][parts - 1] = first_part[parts:]

time: 236 us -> 252 us (1.068)
  waiting for transfers between devices: 124 us -> 137 us
  starting transfers between devices: 54.6 us -> 57.2 us
    ppermute x20 -> x22, waiting for transfers between devices: 38.4 us -> 47.5 us  [down(): return lax.ppermute(value, 'mp', down_pairs)]
    ppermute x20 -> x22, starting transfers between devices: 30 us -> 35.7 us  [down(): return lax.ppermute(value, 'mp', down_pairs)]
    ppermute x1, waiting for transfers between devices: 10.8 us -> 14.2 us  [local(): lax.ppermute(moving, 'section', [(s, (s + 2) % section_count) for s in ra...]
    ppermute x21 -> x23, starting transfers between devices: 15.3 us -> 12.5 us  [up(): return lax.ppermute(value, 'mp', up_pairs)]
    ppermute x21 -> x23, waiting for transfers between devices: 59.3 us -> 61.5 us  [up(): return lax.ppermute(value, 'mp', up_pairs)]
  transfers between devices with their start and end apart: 52 -> 56, of which waited for: 25 -> 24; matrix products, arithmetic and copies ran while one was open for 2% -> 2% of each run, Pallas kernels for 20% -> 19%
where the time goes in v14:
time: 252 us; the launch traced here: 251 us
  waiting for transfers between devices  137 us (54%)
  starting transfers between devices  57.2 us (23%)
  Pallas kernels  48 us (19%)
  other arithmetic  5.26 us (2%)
  local copies, waits for them, and re-layouts  2.54 us (1%)
    ppermute x23, waiting for transfers between devices, up(): return lax.ppermute(value, 'mp', up_pairs)  61.5 us
    ppermute x22, waiting for transfers between devices, down(): return lax.ppermute(value, 'mp', down_pairs)  47.5 us
    ppermute x22, starting transfers between devices, down(): return lax.ppermute(value, 'mp', down_pairs)  35.7 us
    pallas_call x3, Pallas kernels, attend(): pl.pallas_call(kernel, grid_spec=pltpu.PrefetchScalarGridSpec(num_scalar_...  16.7 us
    pallas_call x2, Pallas kernels, project(): pl.pallas_call(kernel, grid_spec=pltpu.PrefetchScalarGridSpec(num_scalar_...  14.5 us
    ppermute x1, waiting for transfers between devices, local(): lax.ppermute(moving, 'section', [(s, (s + 2) % section_count) for s in ra...  14.2 us
    ppermute x23, starting transfers between devices, up(): return lax.ppermute(value, 'mp', up_pairs)  12.5 us
    pallas_call x4, Pallas kernels, query(): pl.pallas_call(kernel, grid=(width // wide,), in_specs=[pl.BlockSpec(chun...  11.3 us
  transfers between devices with their start and end apart: 56, of which 24 were waited for; matrix products, arithmetic and copies ran while one was open for 2% of the time, Pallas kernels for 19%

profile of v14, /device:TPU:0, one launch (start us, length us, event | category | flops | bytes accessed | tf_op | source)
XLA Modules:
  0.0 251.2 jit_solution(6229215269581508665)
XLA Ops:
  0.0 3.0 %collective-permute-start.3 = (bf16[64,8192]{1,0:T(8,128)(2,1)}, bf16[64,8192]{1,0:T(8,128)(2,1)S(1)}, u32[]{:S(2)}, u32[]{:S(2)}) collective-permute-start(bf16[64,8192]{1,0:T(8,128)(2,1)} %bitcast.21), channel_id=1, source_target_pairs={{2,0},{4,2},{6,4},{7,6},{5,7},{3,5},{1,3},{0,1},{10,8},{12,10},{14... | collective-permute-start | bytes 3145736 | tf_op jit(solution)/shard_map/ppermute | solution.py:410
  4.8 2.9 %project.3 = (bf16[160,1024]{1,0:T(8,128)(2,1)S(1)}, bf16[160,1024]{1,0:T(8,128)(2,1)S(1)}) custom-call(s32[10]{0:T(128)S(1)} %get-tuple-element.195.places_ref, bf16[320,960]{1,0:T(8,128)(2,1)S(1)} %copy-done.1, bf16[960,8192]{1,0:T(8,128)(2,1)} %weight_ref.3), custom_call_target="tpu_custom_call" | custom-call | flops 629145600 | bytes 2621440 | tf_op jit(solution)/shard_map/project/pallas_call | solution.py:102
  9.8 11.6 %project.2 = (bf16[160,1024]{1,0:T(8,128)(2,1)S(1)}, bf16[160,1024]{1,0:T(8,128)(2,1)S(1)}, bf16[160,1024]{1,0:T(8,128)(2,1)S(1)}, bf16[160,1024]{1,0:T(8,128)(2...) custom-call(s32[10]{0:T(128)S(1)} %get-tuple-element.195.places_ref,, ...), custom_call_target="tpu_custom_call" | custom-call | flops 4404019200 | bytes 18350080 | tf_op jit(solution)/shard_map/project/pallas_call | solution.py:102
  21.4 5.8 %collective-permute-done.3.refs_2_ = bf16[64,8192]{1,0:T(8,128)(2,1)S(1)} collective-permute-done((bf16[64,8192]{1,0:T(8,128)(2,1)}, bf16[64,8192]{1,0:T(8,128)(2,1)S(1)}, u32[]{:S(2)}, u32[]{:S(2)}) %collective-permute-start.3) | collective-permute-done | bytes 1048608 | tf_op jit(solution)/shard_map/ppermute | solution.py:410
  31.5 4.7 %collective-permute-done.4 = bf16[160,1024]{1,0:T(8,128)(2,1)S(1)} collective-permute-done((bf16[160,1024]{1,0:T(8,128)(2,1)S(1)}, bf16[160,1024]{1,0:T(8,128)(2,1)S(1)}, u32[]{:S(2)}, u32[]{:S(2)}) %collective-permute-start.4) | collective-permute-done | bytes 327712 | tf_op jit(solution)/shard_map/ppermute | solution.py:407
  43.7 6.7 %collective-permute-done.5 = bf16[160,1024]{1,0:T(8,128)(2,1)S(1)} collective-permute-done((bf16[160,1024]{1,0:T(8,128)(2,1)S(1)}, bf16[160,1024]{1,0:T(8,128)(2,1)S(1)}, u32[]{:S(2)}, u32[]{:S(2)}) %collective-permute-start.5) | collective-permute-done | bytes 327712 | tf_op jit(solution)/shard_map/ppermute | solution.py:407
  57.7 6.7 %collective-permute-done.9 = bf16[160,1024]{1,0:T(8,128)(2,1)S(1)} collective-permute-done((bf16[160,1024]{1,0:T(8,128)(2,1)S(1)}, bf16[160,1024]{1,0:T(8,128)(2,1)S(1)}, u32[]{:S(2)}, u32[]{:S(2)}) %collective-permute-start.9) | collective-permute-done | bytes 327712 | tf_op jit(solution)/shard_map/ppermute | solution.py:407
  66.7 4.7 %collective-permute-done.15.refs_4_ = bf16[160,1024]{1,0:T(8,128)(2,1)S(1)} collective-permute-done((bf16[160,1024]{1,0:T(8,128)(2,1)S(1)}, bf16[160,1024]{1,0:T(8,128)(2,1)S(1)}, u32[]{:S(2)}, u32[]{:S(2)}) %collective-permute-start.15) | collective-permute-done | bytes 327712 | tf_op jit(solution)/shard_map/ppermute | solution.py:407
  71.4 4.1 %collective-permute-done.17.refs_5_ = bf16[160,1024]{1,0:T(8,128)(2,1)S(1)} collective-permute-done((bf16[160,1024]{1,0:T(8,128)(2,1)S(1)}, bf16[160,1024]{1,0:T(8,128)(2,1)S(1)}, u32[]{:S(2)}, u32[]{:S(2)}) %collective-permute-start.17) | collective-permute-done | bytes 327712 | tf_op jit(solution)/shard_map/ppermute | solution.py:410
  80.7 14.2 %collective-permute-done.20.refs_2_ = bf16[320,1024]{1,0:T(8,128)(2,1)S(1)} collective-permute-done((bf16[320,1024]{1,0:T(8,128)(2,1)S(1)}, bf16[320,1024]{1,0:T(8,128)(2,1)S(1)}, u32[]{:S(2)}, u32[]{:S(2)}) %collective-permute-start.20) | collective-permute-done | bytes 655392 | tf_op jit(solution)/shard_map/ppermute | solution.py:494
  97.4 4.4 %key_values.1 = (bf16[256,256]{1,0:T(8,128)(2,1)S(1)}, bf16[256,256]{1,0:T(8,128)(2,1)S(1)}, bf16[256,256]{1,0:T(8,128)(2,1)S(1)}, bf16[256,256]{1,0:T(8,128)(2,...) custom-call(s32[18]{0:T(128)S(1)} %pad_add_fusion.meta_ref, ...), custom_call_target="tpu_custom_call" | custom-call | flops 1 | bytes 1 | tf_op jit(solution)/shard_map/key_values/pallas_call | solution.py:166
  104.5 17.3 %collective-permute-done.24.refs_1_ = bf16[64,8192]{1,0:T(8,128)(2,1)S(1)} collective-permute-done((bf16[64,8192]{1,0:T(8,128)(2,1)S(1)}, bf16[64,8192]{1,0:T(8,128)(2,1)S(1)}, u32[]{:S(2)}, u32[]{:S(2)}) %collective-permute-start.24) | collective-permute-done | bytes 1048608 | tf_op jit(solution)/shard_map/ppermute | solution.py:410
  125.0 4.8 %collective-permute-done.25 = bf16[256,256]{1,0:T(8,128)(2,1)S(1)} collective-permute-done((bf16[256,256]{1,0:T(8,128)(2,1)S(1)}, bf16[256,256]{1,0:T(8,128)(2,1)S(1)}, u32[]{:S(2)}, u32[]{:S(2)}) %collective-permute-start.25) | collective-permute-done | bytes 131104 | tf_op jit(solution)/shard_map/ppermute | solution.py:407
  133.5 5.5 %collective-permute-done.28 = bf16[256,256]{1,0:T(8,128)(2,1)S(1)} collective-permute-done((bf16[256,256]{1,0:T(8,128)(2,1)S(1)}, bf16[256,256]{1,0:T(8,128)(2,1)S(1)}, u32[]{:S(2)}, u32[]{:S(2)}) %collective-permute-start.28) | collective-permute-done | bytes 131104 | tf_op jit(solution)/shard_map/ppermute | solution.py:410
  143.3 3.0 %query.4 = bf16[192,512]{1,0:T(8,128)(2,1)S(1)} custom-call(bf16[64,8192]{1,0:T(8,128)(2,1)S(1)} %bitcast.25, bf16[64,8192]{1,0:T(8,128)(2,1)S(1)} %collective-permute-done.2.refs_1_, bf16[64,8192]{1,0:T(8,128)(2,1)S(1)} %collective-permute-done.3.refs_2_, bf16[8192,512]{1,0:T(8,128)(2,1)S(1)} %bitcast.12, f32[192,128]{1,0:T(8,128)S(1)} %row_scales.1.refs_4_), custom_call_target="tpu_custom_call" | custom-call | flops 1610612736 | bytes 11534336 | tf_op jit(solution)/shard_map/query/pallas_call | solution.py:240
  148.4 3.9 %collective-permute-done.29.refs_0_ = bf16[16,8192]{1,0:T(8,128)(2,1)S(1)} collective-permute-done((bf16[16,8192]{1,0:T(8,128)(2,1)S(1)}, bf16[16,8192]{1,0:T(8,128)(2,1)S(1)}, u32[]{:S(2)}, u32[]{:S(2)}) %collective-permute-start.29) | collective-permute-done | bytes 262176 | tf_op jit(solution)/shard_map/ppermute | solution.py:407
  154.5 3.4 %collective-permute-done.32.refs_1_ = bf16[16,8192]{1,0:T(8,128)(2,1)S(1)} collective-permute-done((bf16[16,8192]{1,0:T(8,128)(2,1)S(1)}, bf16[16,8192]{1,0:T(8,128)(2,1)S(1)}, u32[]{:S(2)}, u32[]{:S(2)}) %collective-permute-start.32) | collective-permute-done | bytes 262176 | tf_op jit(solution)/shard_map/ppermute | solution.py:407
  160.8 5.3 %attend.3 = (bf16[32,8192]{1,0:T(8,128)(2,1)S(1)}, bf16[32,8192]{1,0:T(8,128)(2,1)S(1)}, bf16[32,8192]{1,0:T(8,128)(2,1)S(1)}, bf16[32,8192]{1,0:T(8,128)(2,1)S(1)}) custom-call(s32[18]{0:T(128)S(1)} %pad_add_fusion.meta_ref, bf16[128,512]{1,0:T(8,128)(2,1)S(1)} %query.5.query_ref, bf16[256,256]{1,0:T(8,128)(2,1)S(1)} %add_convert_fusion.22.refs_0_, ...), custom_call_target="tpu_custom_call" | custom-call | flops 4294967296 | bytes 33554432 | tf_op jit(solution)/shard_map/attend/pallas_call | solution.py:332
  177.7 4.5 %attend.4 = (bf16[32,8192]{1,0:T(8,128)(2,1)S(1)}, bf16[32,8192]{1,0:T(8,128)(2,1)S(1)}) custom-call(s32[18]{0:T(128)S(1)} %pad_add_fusion.meta_ref, bf16[64,512]{1,0:T(8,128)(2,1)S(1)} %query.7.query_ref, bf16[256,256]{1,0:T(8,128)(2,1)S(1)} %add_convert_fusion.22.refs_0_, bf16[256,256]{1,0:T(8,128)(2,1)S(1)} %collective-permute-done.38.refs_1_, ...), custom_call_target="tpu_custom_call" | custom-call | flops 2147483648 | bytes 33554432 | tf_op jit(solution)/shard_map/attend/pallas_call | solution.py:332
  182.2 6.9 %attend.5 = (bf16[64,8192]{1,0:T(8,128)(2,1)S(1)}, bf16[32,8192]{1,0:T(8,128)(2,1)S(1)}, bf16[32,8192]{1,0:T(8,128)(2,1)S(1)}, bf16[32,8192]{1,0:T(8,128)(2,1)S(...) custom-call(s32[18]{0:T(128)S(1)} %pad_add_fusion.meta_ref, ...), custom_call_target="tpu_custom_call" | custom-call | flops 10737418240 | bytes 33554432 | tf_op jit(solution)/shard_map/attend/pallas_call | solution.py:332
  194.0 9.8 %collective-permute-done.43 = bf16[32,8192]{1,0:T(8,128)(2,1)S(1)} collective-permute-done((bf16[32,8192]{1,0:T(8,128)(2,1)S(1)}, bf16[32,8192]{1,0:T(8,128)(2,1)S(1)}, u32[]{:S(2)}, u32[]{:S(2)}) %collective-permute-start.43) | collective-permute-done | bytes 524320 | tf_op jit(solution)/shard_map/ppermute | solution.py:407
  206.2 8.9 %collective-permute-done.49 = bf16[32,8192]{1,0:T(8,128)(2,1)S(1)} collective-permute-done((bf16[32,8192]{1,0:T(8,128)(2,1)S(1)}, bf16[32,8192]{1,0:T(8,128)(2,1)S(1)}, u32[]{:S(2)}, u32[]{:S(2)}) %collective-permute-start.49) | collective-permute-done | bytes 524320 | tf_op jit(solution)/shard_map/ppermute | solution.py:410
  218.7 13.2 %collective-permute-done.47 = bf16[32,8192]{1,0:T(8,128)(2,1)S(1)} collective-permute-done((bf16[32,8192]{1,0:T(8,128)(2,1)S(1)}, bf16[32,8192]{1,0:T(8,128)(2,1)S(1)}, u32[]{:S(2)}, u32[]{:S(2)}) %collective-permute-start.47) | collective-permute-done | bytes 524320 | tf_op jit(solution)/shard_map/ppermute | solution.py:407
  238.6 8.7 %collective-permute-done.51 = bf16[32,8192]{1,0:T(8,128)(2,1)S(1)} collective-permute-done((bf16[32,8192]{1,0:T(8,128)(2,1)S(1)}, bf16[32,8192]{1,0:T(8,128)(2,1)S(1)}, u32[]{:S(2)}, u32[]{:S(2)}) %collective-permute-start.51) | collective-permute-done | bytes 524320 | tf_op jit(solution)/shard_map/ppermute | solution.py:420
  (165 shorter events, 86.0 us)
Async XLA Ops:
  0.0 27.2 %collective-permute-start.3 = (bf16[64,8192]{1,0:T(8,128)(2,1)}, bf16[64,8192]{1,0:T(8,128)(2,1)S(1)}, u32[]{:S(2)}, u32[]{:S(2)}) collective-permute-start(bf16[64,8192]{1,0:T(8,128)(2,1)} %bitcast.21), channel_id=1, source_target_pairs={{2,0},{4,2},{6,4},{7,6},{5,7},{3,5},{1,3},{0,1},{10,8},{12,10},{14... | collective-permute-start | bytes 3145736 | tf_op jit(solution)/shard_map/ppermute | solution.py:410
  3.0 26.3 %collective-permute-start.2 = (bf16[64,8192]{1,0:T(8,128)(2,1)}, bf16[64,8192]{1,0:T(8,128)(2,1)S(1)}, u32[]{:S(2)}, u32[]{:S(2)}) collective-permute-start(bf16[64,8192]{1,0:T(8,128)(2,1)} %bitcast.22), channel_id=1, source_target_pairs={{0,2},{2,4},{4,6},{6,7},{7,5},{5,3},{3,1},{1,0},{8,10},{10,12},{12... | collective-permute-start | bytes 3145736 | tf_op jit(solution)/shard_map/ppermute | solution.py:407
  3.0 28.5 %collective-permute-start.1 = (f32[1]{0:T(128)}, f32[1]{0:T(128)}, u32[]{:S(2)}, u32[]{:S(2)}) collective-permute-start(f32[1]{0:T(128)} %param.16), channel_id=1, source_target_pairs={{0,8},{8,16},{16,24},{24,0},{1,9},{9,17},{17,25},{25,1},{2,10},{10... | collective-permute-start | bytes 20 | tf_op jit(solution)/shard_map/ppermute | solution.py:426
  7.7 28.5 %collective-permute-start.4 = (bf16[160,1024]{1,0:T(8,128)(2,1)S(1)}, bf16[160,1024]{1,0:T(8,128)(2,1)S(1)}, u32[]{:S(2)}, u32[]{:S(2)}) collective-permute-start(bf16[160,1024]{1,0:T(8,128)(2,1)S(1)} %get-tuple-element.97), channel_id=1, source_target_pairs={{0,2},{2,4},{4,6},{6,7},{7,5},{5,3},{3,1},{1,0},{8,10},{10,12},{12... | collective-permute-start | bytes 983048 | tf_op jit(solution)/shard_map/ppermute | solution.py:407
  9.8 26.7 %collective-permute-start.8 = (bf16[160,1024]{1,0:T(8,128)(2,1)S(1)}, bf16[160,1024]{1,0:T(8,128)(2,1)S(1)}, u32[]{:S(2)}, u32[]{:S(2)}) collective-permute-start(bf16[160,1024]{1,0:T(8,128)(2,1)S(1)} %get-tuple-element.102), channel_id=1, source_target_pairs={{2,0},{4,2},{6,4},{7,6},{5,7},{3,5},{1,3},{0,1},{10,8},{12,10},{14... | collective-permute-start | bytes 983048 | tf_op jit(solution)/shard_map/ppermute | solution.py:410
  77.2 17.7 %collective-permute-start.20 = (bf16[320,1024]{1,0:T(8,128)(2,1)S(1)}, bf16[320,1024]{1,0:T(8,128)(2,1)S(1)}, u32[]{:S(2)}, u32[]{:S(2)}) collective-permute-start(bf16[320,1024]{1,0:T(8,128)(2,1)S(1)} %total_of.1.refs_0_), channel_id=1, source_target_pairs={{0,16},{8,24},{16,0},{24,8},{1,17},{9,25},{17,1},{25,9},{2,18},{10... | collective-permute-start | bytes 1966088 | tf_op jit(solution)/shard_map/ppermute | solution.py:494
  78.8 25.2 %collective-permute-start.18 = (bf16[64,8192]{1,0:T(8,128)(2,1)S(1)}, bf16[64,8192]{1,0:T(8,128)(2,1)S(1)}, u32[]{:S(2)}, u32[]{:S(2)}) collective-permute-start(bf16[64,8192]{1,0:T(8,128)(2,1)S(1)} %collective-permute-done.2.refs_1_), channel_id=1, source_target_pairs={{0,2},{2,4},{4,6},{6,7},{7,5},{5,3},{3,1},{1,0},{8,10},{10,12},{12... | collective-permute-start | bytes 3145736 | tf_op jit(solution)/shard_map/ppermute | solution.py:407
  79.3 103.0 %collective-permute-start = (bf16[64,8192]{1,0:T(8,128)(2,1)S(1)}, bf16[64,8192]{1,0:T(8,128)(2,1)S(1)}, u32[]{:S(2)}, u32[]{:S(2)}) collective-permute-start(bf16[64,8192]{1,0:T(8,128)(2,1)S(1)} %bitcast.24), channel_id=1, source_target_pairs={{0,8},{8,16},{16,24},{24,0},{1,9},{9,17},{17,25},{25,1},{2,10},{10... | collective-permute-start | bytes 3145736 | tf_op jit(solution)/shard_map/ppermute | solution.py:426
  80.1 17.3 %collective-permute-start.19 = (bf16[320,1024]{1,0:T(8,128)(2,1)S(1)}, bf16[320,1024]{1,0:T(8,128)(2,1)S(1)}, u32[]{:S(2)}, u32[]{:S(2)}) collective-permute-start(bf16[320,1024]{1,0:T(8,128)(2,1)S(1)} %total_of.1.refs_0_), channel_id=1, source_target_pairs={{0,8},{8,0},{16,24},{24,16},{1,9},{9,1},{17,25},{25,17},{2,10},{10... | collective-permute-start | bytes 1966088 | tf_op jit(solution)/shard_map/ppermute | solution.py:491
  95.8 26.0 %collective-permute-start.24 = (bf16[64,8192]{1,0:T(8,128)(2,1)S(1)}, bf16[64,8192]{1,0:T(8,128)(2,1)S(1)}, u32[]{:S(2)}, u32[]{:S(2)}) collective-permute-start(bf16[64,8192]{1,0:T(8,128)(2,1)S(1)} %collective-permute-done.3.refs_2_), channel_id=1, source_target_pairs={{2,0},{4,2},{6,4},{7,6},{5,7},{3,5},{1,3},{0,1},{10,8},{12,10},{14... | collective-permute-start | bytes 3145736 | tf_op jit(solution)/shard_map/ppermute | solution.py:410
  101.9 22.7 %collective-permute-start.26 = (bf16[256,256]{1,0:T(8,128)(2,1)S(1)}, bf16[256,256]{1,0:T(8,128)(2,1)S(1)}, u32[]{:S(2)}, u32[]{:S(2)}) collective-permute-start(bf16[256,256]{1,0:T(8,128)(2,1)S(1)} %get-tuple-element.128), channel_id=1, source_target_pairs={{2,0},{4,2},{6,4},{7,6},{5,7},{3,5},{1,3},{0,1},{10,8},{12,10},{14... | collective-permute-start | bytes 393224 | tf_op jit(solution)/shard_map/ppermute | solution.py:410
  103.5 20.0 %collective-permute-start.23 = (bf16[256,256]{1,0:T(8,128)(2,1)S(1)}, bf16[256,256]{1,0:T(8,128)(2,1)S(1)}, u32[]{:S(2)}, u32[]{:S(2)}) collective-permute-start(bf16[256,256]{1,0:T(8,128)(2,1)S(1)} %get-tuple-element.123), channel_id=1, source_target_pairs={{0,2},{2,4},{4,6},{6,7},{7,5},{5,3},{3,1},{1,0},{8,10},{10,12},{12... | collective-permute-start | bytes 393224 | tf_op jit(solution)/shard_map/ppermute | solution.py:407
  104.0 27.5 %collective-permute-start.22 = (bf16[16,8192]{1,0:T(8,128)(2,1)S(1)}, bf16[16,8192]{1,0:T(8,128)(2,1)S(1)}, u32[]{:S(2)}, u32[]{:S(2)}) collective-permute-start(bf16[16,8192]{1,0:T(8,128)(2,1)S(1)} %get-tuple-element.194), channel_id=1, source_target_pairs={{0,2},{2,4},{4,6},{6,7},{7,5},{5,3},{3,1},{1,0},{8,10},{10,12},{12... | collective-permute-start | bytes 786440 | tf_op jit(solution)/shard_map/ppermute | solution.py:407
  153.1 17.9 %collective-permute-start.40 = (bf16[32,8192]{1,0:T(8,128)(2,1)S(1)}, bf16[32,8192]{1,0:T(8,128)(2,1)S(1)}, u32[]{:S(2)}, u32[]{:S(2)}) collective-permute-start(bf16[32,8192]{1,0:T(8,128)(2,1)S(1)} %slice.45), channel_id=1, source_target_pairs={{2,0},{4,2},{6,4},{7,6},{5,7},{3,5},{1,3},{0,1},{10,8},{12,10},{14... | collective-permute-start | bytes 1572872 | tf_op jit(solution)/shard_map/ppermute | solution.py:410
  166.1 23.1 %collective-permute-start.42 = (bf16[32,8192]{1,0:T(8,128)(2,1)S(1)}, bf16[32,8192]{1,0:T(8,128)(2,1)S(1)}, u32[]{:S(2)}, u32[]{:S(2)}) collective-permute-start(bf16[32,8192]{1,0:T(8,128)(2,1)S(1)} %get-tuple-element.150), channel_id=1, source_target_pairs={{0,2},{2,4},{4,6},{6,7},{7,5},{5,3},{3,1},{1,0},{8,10},{10,12},{12... | collective-permute-start | bytes 1572872 | tf_op jit(solution)/shard_map/ppermute | solution.py:407
  166.1 23.2 %collective-permute-start.46 = (bf16[32,8192]{1,0:T(8,128)(2,1)S(1)}, bf16[32,8192]{1,0:T(8,128)(2,1)S(1)}, u32[]{:S(2)}, u32[]{:S(2)}) collective-permute-start(bf16[32,8192]{1,0:T(8,128)(2,1)S(1)} %get-tuple-element.164), channel_id=1, source_target_pairs={{2,0},{4,2},{6,4},{7,6},{5,7},{3,5},{1,3},{0,1},{10,8},{12,10},{14... | collective-permute-start | bytes 1572872 | tf_op jit(solution)/shard_map/ppermute | solution.py:410
  189.1 26.2 %collective-permute-start.41 = (bf16[64,8192]{1,0:T(8,128)(2,1)S(1)}, bf16[64,8192]{1,0:T(8,128)(2,1)S(1)}, u32[]{:S(2)}, u32[]{:S(2)}) collective-permute-start(bf16[64,8192]{1,0:T(8,128)(2,1)S(1)} %get-tuple-element.157), channel_id=1, source_target_pairs={{0,8},{8,16},{16,24},{24,0},{1,9},{9,17},{17,25},{25,1},{2,10},{10... | collective-permute-start | bytes 3145736 | tf_op jit(solution)/shard_map/ppermute | solution.py:426
  191.7 23.4 %collective-permute-start.49 = (bf16[32,8192]{1,0:T(8,128)(2,1)S(1)}, bf16[32,8192]{1,0:T(8,128)(2,1)S(1)}, u32[]{:S(2)}, u32[]{:S(2)}) collective-permute-start(bf16[32,8192]{1,0:T(8,128)(2,1)S(1)} %add_convert_fusion.9), channel_id=1, source_target_pairs={{2,0},{4,2},{6,4},{7,6},{5,7},{3,5},{1,3},{0,1},{10,8},{12,10},{14... | collective-permute-start | bytes 1572872 | tf_op jit(solution)/shard_map/ppermute | solution.py:410
  192.1 23.1 %collective-permute-start.48 = (bf16[32,8192]{1,0:T(8,128)(2,1)S(1)}, bf16[32,8192]{1,0:T(8,128)(2,1)S(1)}, u32[]{:S(2)}, u32[]{:S(2)}) collective-permute-start(bf16[32,8192]{1,0:T(8,128)(2,1)S(1)} %add_convert_fusion.8), channel_id=1, source_target_pairs={{0,2},{2,4},{4,6},{6,7},{7,5},{5,3},{3,1},{1,0},{8,10},{10,12},{12... | collective-permute-start | bytes 1572872 | tf_op jit(solution)/shard_map/ppermute | solution.py:407
  203.9 28.0 %collective-permute-start.47 = (bf16[32,8192]{1,0:T(8,128)(2,1)S(1)}, bf16[32,8192]{1,0:T(8,128)(2,1)S(1)}, u32[]{:S(2)}, u32[]{:S(2)}) collective-permute-start(bf16[32,8192]{1,0:T(8,128)(2,1)S(1)} %add_convert_fusion.7), channel_id=1, source_target_pairs={{0,2},{2,4},{4,6},{6,7},{7,5},{5,3},{3,1},{1,0},{8,10},{10,12},{12... | collective-permute-start | bytes 1572872 | tf_op jit(solution)/shard_map/ppermute | solution.py:407
  204.1 27.9 %collective-permute-start.54 = (bf16[32,8192]{1,0:T(8,128)(2,1)S(1)}, bf16[32,8192]{1,0:T(8,128)(2,1)S(1)}, u32[]{:S(2)}, u32[]{:S(2)}) collective-permute-start(bf16[32,8192]{1,0:T(8,128)(2,1)S(1)} %add_convert_fusion.6), channel_id=1, source_target_pairs={{2,0},{4,2},{6,4},{7,6},{5,7},{3,5},{1,3},{0,1},{10,8},{12,10},{14... | collective-permute-start | bytes 1572872 | tf_op jit(solution)/shard_map/ppermute | solution.py:410
  215.4 23.2 %collective-permute-start.52 = (bf16[32,8192]{1,0:T(8,128)(2,1)S(1)}, bf16[32,8192]{1,0:T(8,128)(2,1)S(1)}, u32[]{:S(2)}, u32[]{:S(2)}) collective-permute-start(bf16[32,8192]{1,0:T(8,128)(2,1)S(1)} %add_convert_fusion.5), channel_id=1, source_target_pairs={{2,8},{4,10},{6,12},{7,14},{5,15},{3,13},{1,11},{0,9},{10,16},{12,... | collective-permute-start | bytes 1572872 | tf_op jit(solution)/shard_map/ppermute | solution.py:423
  218.0 20.6 %collective-permute-start.53 = (bf16[32,8192]{1,0:T(8,128)(2,1)S(1)}, bf16[32,8192]{1,0:T(8,128)(2,1)S(1)}, u32[]{:S(2)}, u32[]{:S(2)}) collective-permute-start(bf16[32,8192]{1,0:T(8,128)(2,1)S(1)} %add_convert_fusion.4), channel_id=1, source_target_pairs={{0,10},{2,12},{4,14},{6,15},{7,13},{5,11},{3,9},{1,8},{8,18},{10,2... | collective-permute-start | bytes 1572872 | tf_op jit(solution)/shard_map/ppermute | solution.py:420
  232.2 17.4 %collective-permute-start.55 = (bf16[32,8192]{1,0:T(8,128)(2,1)S(1)}, bf16[32,8192]{1,0:T(8,128)(2,1)S(1)}, u32[]{:S(2)}, u32[]{:S(2)}) collective-permute-start(bf16[32,8192]{1,0:T(8,128)(2,1)S(1)} %add_convert_fusion.1), channel_id=1, source_target_pairs={{2,8},{4,10},{6,12},{7,14},{5,15},{3,13},{1,11},{0,9},{10,16},{12,... | collective-permute-start | bytes 1572872 | tf_op jit(solution)/shard_map/ppermute | solution.py:423
  (43 other events, 680.6 us)

commit v15 on v13

--- a/solution.py
+++ b/solution.py
@@ -131,28 +131,32 @@
 
     def kernel(meta_ref, *refs):
         piece_refs, weight_ref = refs[:count], refs[count]
-        out_refs, kv_ref = refs[count + 1 : -1], refs[-1]
+        out_refs, (image_ref, kv_ref) = refs[count + 1 : -2], refs[-2:]
         section = meta_ref[order_len + 1]
-        slot = lax.broadcasted_iota(jnp.int32, (BLOCK, feat_rows), 0)
-        packed = lax.broadcasted_iota(jnp.int32, (BLOCK, feat_rows), 1)
-        for sample in range(SAMP_SECTION):
-            start = meta_ref[order_len + 2 + sample]
-            live = TT * meta_ref[order_len + 2 + SAMP_SECTION + sample]
-            image = jnp.zeros((BLOCK, depth), F32)
+        origins = []
+        for index in range(count):
+            origin = lax.rem(section + (section_count - 2 * (index // 2)), section_count)
+            origins.append(origin + 1 - 2 * lax.rem(origin, 2) if index % 2 else origin)
+        for slot in range(SAMP_SECTION * MAXT):
+            sample, tile = slot // MAXT, slot % MAXT
+            live = tile < meta_ref[order_len + 2 + SAMP_SECTION + sample]
+            row = meta_ref[order_len + 2 + sample] + TT * tile
+            origin_of = lax.div(row, feat_rows)
+            place = pl.ds(pl.multiple_of(row - origin_of * feat_rows, TT), TT)
+            own = slice(slot * TT, (slot + 1) * TT)
             for index in range(count):
-                step, swapped = index // 2, index % 2
-                origin = lax.rem(section + (section_count - 2 * step), section_count)
-                if swapped:
-                    origin = origin + 1 - 2 * lax.rem(origin, 2)
-                chosen = (slot < live) & (packed == slot + (start - origin * feat_rows))
-                image += jnp.dot(
-                    chosen.astype(F32).astype(BF16),
-                    piece_refs[index][...],
-                    preferred_element_type=F32,
-                )
-            kv_ref[sample * BLOCK : (sample + 1) * BLOCK, :] = jnp.dot(
-                image.astype(BF16), weight_ref[...], preferred_element_type=F32
-            ).astype(BF16)
+
+                @pl.when(live & (origin_of == origins[index]))
+                def _(index=index, own=own, place=place):
+                    image_ref[own, :] = piece_refs[index][place, :]
+
+            @pl.when(jnp.logical_not(live))
+            def _(own=own):
+                image_ref[own, :] = jnp.zeros((TT, depth), BF16)
+
+        kv_ref[...] = jnp.dot(
+            image_ref[...], weight_ref[...], preferred_element_type=F32
+        ).astype(BF16)
         for index in range(order_len):
             target = meta_ref[index]
             row = pl.multiple_of(lax.rem(target, sharing) * kv_rows, kv_rows)
@@ -168,7 +172,7 @@
         in_specs=[pl.BlockSpec(memory_space=pltpu.SMEM)] + [whole] * (count + 1),
         out_specs=[whole] * order_len,
         out_shape=[jax.ShapeDtypeStruct((kv_rows, 2 * HD), BF16)] * order_len,
-        scratch_shapes=[pltpu.VMEM((SLOTS, width), BF16)],
+        scratch_shapes=[pltpu.VMEM((SLOTS, depth), BF16), pltpu.VMEM((SLOTS, width), BF16)],
         compiler_params=params(),
         cost_estimate=QUICK,
         name="key_values",

time: 236 us -> 234 us (level)
  starting transfers between devices: 54.6 us -> 51.9 us
    ppermute x21, waiting for transfers between devices: 59.3 us -> 63.3 us  [up(): return lax.ppermute(value, 'mp', up_pairs)]
    ppermute x20, waiting for transfers between devices: 38.4 us -> 35.1 us  [down(): return lax.ppermute(value, 'mp', down_pairs)]
    ppermute x2, starting transfers between devices: 4.59 us -> 1.95 us  [down_across(): return lax.ppermute(value, ('section', 'mp'), across(down_pairs))]
  transfers between devices with their start and end apart: 52 -> 52, of which waited for: 25 -> 24; matrix products, arithmetic and copies ran while one was open for 2% -> 2% of each run, Pallas kernels for 20% -> 20%
where the time goes in v15:
time: 234 us
  waiting for transfers between devices  126 us (54%)
  starting transfers between devices  51.9 us (22%)
  Pallas kernels  46.2 us (20%)
  other arithmetic  5.3 us (2%)
  local copies, waits for them, and re-layouts  2.54 us (1%)
    ppermute x21, waiting for transfers between devices, up(): return lax.ppermute(value, 'mp', up_pairs)  63.3 us
    ppermute x20, waiting for transfers between devices, down(): return lax.ppermute(value, 'mp', down_pairs)  35.1 us
    ppermute x20, starting transfers between devices, down(): return lax.ppermute(value, 'mp', down_pairs)  31.4 us
    pallas_call x3, Pallas kernels, attend(): pl.pallas_call(kernel, grid_spec=pltpu.PrefetchScalarGridSpec(num_scalar_...  16.7 us
    pallas_call x2, Pallas kernels, project(): pl.pallas_call(kernel, grid_spec=pltpu.PrefetchScalarGridSpec(num_scalar_...  14.5 us
    ppermute x21, starting transfers between devices, up(): return lax.ppermute(value, 'mp', up_pairs)  13.8 us
    pallas_call x4, Pallas kernels, query(): pl.pallas_call(kernel, grid=(width // wide,), in_specs=[pl.BlockSpec(chun...  11.4 us
    ppermute x1, waiting for transfers between devices, local(): lax.ppermute(moving, 'section', [(s, (s + 2) % section_count) for s in ra...  10.8 us
  transfers between devices with their start and end apart: 52, of which 24 were waited for; matrix products, arithmetic and copies ran while one was open for 2% of the time, Pallas kernels for 20%

profile of v15, /device:TPU:0, one launch (start us, length us, event | category | flops | bytes accessed | tf_op | source)
XLA Modules:
  0.0 233.5 jit_solution(5562874037423447261)
XLA Ops:
  0.0 3.0 %collective-permute-start.3 = (bf16[64,8192]{1,0:T(8,128)(2,1)}, bf16[64,8192]{1,0:T(8,128)(2,1)S(1)}, u32[]{:S(2)}, u32[]{:S(2)}) collective-permute-start(bf16[64,8192]{1,0:T(8,128)(2,1)} %bitcast.21), channel_id=1, source_target_pairs={{2,0},{4,2},{6,4},{7,6},{5,7},{3,5},{1,3},{0,1},{10,8},{12,10},{14... | collective-permute-start | bytes 3145736 | tf_op jit(solution)/shard_map/ppermute | solution.py:414
  4.8 2.9 %project.3 = (bf16[160,1024]{1,0:T(8,128)(2,1)S(1)}, bf16[160,1024]{1,0:T(8,128)(2,1)S(1)}) custom-call(s32[10]{0:T(128)S(1)} %get-tuple-element.175.places_ref, bf16[320,960]{1,0:T(8,128)(2,1)S(1)} %copy-done.1, bf16[960,8192]{1,0:T(8,128)(2,1)} %weight_ref.3), custom_call_target="tpu_custom_call" | custom-call | flops 629145600 | bytes 2621440 | tf_op jit(solution)/shard_map/project/pallas_call | solution.py:102
  9.8 11.6 %project.2 = (bf16[160,1024]{1,0:T(8,128)(2,1)S(1)}, bf16[160,1024]{1,0:T(8,128)(2,1)S(1)}, bf16[160,1024]{1,0:T(8,128)(2,1)S(1)}, bf16[160,1024]{1,0:T(8,128)(2...) custom-call(s32[10]{0:T(128)S(1)} %get-tuple-element.175.places_ref,, ...), custom_call_target="tpu_custom_call" | custom-call | flops 4404019200 | bytes 18350080 | tf_op jit(solution)/shard_map/project/pallas_call | solution.py:102
  21.4 5.8 %collective-permute-done.3.refs_2_ = bf16[64,8192]{1,0:T(8,128)(2,1)S(1)} collective-permute-done((bf16[64,8192]{1,0:T(8,128)(2,1)}, bf16[64,8192]{1,0:T(8,128)(2,1)S(1)}, u32[]{:S(2)}, u32[]{:S(2)}) %collective-permute-start.3) | collective-permute-done | bytes 1048608 | tf_op jit(solution)/shard_map/ppermute | solution.py:414
  31.5 4.7 %collective-permute-done.4 = bf16[160,1024]{1,0:T(8,128)(2,1)S(1)} collective-permute-done((bf16[160,1024]{1,0:T(8,128)(2,1)S(1)}, bf16[160,1024]{1,0:T(8,128)(2,1)S(1)}, u32[]{:S(2)}, u32[]{:S(2)}) %collective-permute-start.4) | collective-permute-done | bytes 327712 | tf_op jit(solution)/shard_map/ppermute | solution.py:411
  43.7 6.7 %collective-permute-done.5 = bf16[160,1024]{1,0:T(8,128)(2,1)S(1)} collective-permute-done((bf16[160,1024]{1,0:T(8,128)(2,1)S(1)}, bf16[160,1024]{1,0:T(8,128)(2,1)S(1)}, u32[]{:S(2)}, u32[]{:S(2)}) %collective-permute-start.5) | collective-permute-done | bytes 327712 | tf_op jit(solution)/shard_map/ppermute | solution.py:411
  57.7 6.7 %collective-permute-done.9 = bf16[160,1024]{1,0:T(8,128)(2,1)S(1)} collective-permute-done((bf16[160,1024]{1,0:T(8,128)(2,1)S(1)}, bf16[160,1024]{1,0:T(8,128)(2,1)S(1)}, u32[]{:S(2)}, u32[]{:S(2)}) %collective-permute-start.9) | collective-permute-done | bytes 327712 | tf_op jit(solution)/shard_map/ppermute | solution.py:411
  66.7 4.7 %collective-permute-done.15.refs_4_ = bf16[160,1024]{1,0:T(8,128)(2,1)S(1)} collective-permute-done((bf16[160,1024]{1,0:T(8,128)(2,1)S(1)}, bf16[160,1024]{1,0:T(8,128)(2,1)S(1)}, u32[]{:S(2)}, u32[]{:S(2)}) %collective-permute-start.15) | collective-permute-done | bytes 327712 | tf_op jit(solution)/shard_map/ppermute | solution.py:411
  71.4 4.1 %collective-permute-done.17.refs_5_ = bf16[160,1024]{1,0:T(8,128)(2,1)S(1)} collective-permute-done((bf16[160,1024]{1,0:T(8,128)(2,1)S(1)}, bf16[160,1024]{1,0:T(8,128)(2,1)S(1)}, u32[]{:S(2)}, u32[]{:S(2)}) %collective-permute-start.17) | collective-permute-done | bytes 327712 | tf_op jit(solution)/shard_map/ppermute | solution.py:414
  81.7 10.8 %collective-permute-done.20.refs_2_ = bf16[320,1024]{1,0:T(8,128)(2,1)S(1)} collective-permute-done((bf16[320,1024]{1,0:T(8,128)(2,1)S(1)}, bf16[320,1024]{1,0:T(8,128)(2,1)S(1)}, u32[]{:S(2)}, u32[]{:S(2)}) %collective-permute-start.20) | collective-permute-done | bytes 655392 | tf_op jit(solution)/shard_map/ppermute | solution.py:498
  98.0 6.2 %collective-permute-done.18.refs_0_ = bf16[64,8192]{1,0:T(8,128)(2,1)S(1)} collective-permute-done((bf16[64,8192]{1,0:T(8,128)(2,1)S(1)}, bf16[64,8192]{1,0:T(8,128)(2,1)S(1)}, u32[]{:S(2)}, u32[]{:S(2)}) %collective-permute-start.18) | collective-permute-done | bytes 1048608 | tf_op jit(solution)/shard_map/ppermute | solution.py:411
  108.5 8.5 %collective-permute-done.29 = bf16[256,256]{1,0:T(8,128)(2,1)S(1)} collective-permute-done((bf16[256,256]{1,0:T(8,128)(2,1)S(1)}, bf16[256,256]{1,0:T(8,128)(2,1)S(1)}, u32[]{:S(2)}, u32[]{:S(2)}) %collective-permute-start.29) | collective-permute-done | bytes 131104 | tf_op jit(solution)/shard_map/ppermute | solution.py:414
  127.7 3.0 %query.4 = bf16[192,512]{1,0:T(8,128)(2,1)S(1)} custom-call(bf16[64,8192]{1,0:T(8,128)(2,1)S(1)} %bitcast.25, bf16[64,8192]{1,0:T(8,128)(2,1)S(1)} %collective-permute-done.2.refs_1_, bf16[64,8192]{1,0:T(8,128)(2,1)S(1)} %collective-permute-done.3.refs_2_, bf16[8192,512]{1,0:T(8,128)(2,1)S(1)} %bitcast.12, f32[192,128]{1,0:T(8,128)S(1)} %row_scales.1.refs_4_), custom_call_target="tpu_custom_call" | custom-call | flops 1610612736 | bytes 11534336 | tf_op jit(solution)/shard_map/query/pallas_call | solution.py:244
  130.7 7.6 %collective-permute-done.32 = bf16[256,256]{1,0:T(8,128)(2,1)S(1)} collective-permute-done((bf16[256,256]{1,0:T(8,128)(2,1)S(1)}, bf16[256,256]{1,0:T(8,128)(2,1)S(1)}, u32[]{:S(2)}, u32[]{:S(2)}) %collective-permute-start.32) | collective-permute-done | bytes 131104 | tf_op jit(solution)/shard_map/ppermute | solution.py:411
  141.0 2.8 %query.5.query_ref = bf16[128,512]{1,0:T(8,128)(2,1)S(1)} custom-call(bf16[32,8192]{1,0:T(8,128)(2,1)S(1)} %collective-permute-done.23.refs_0_, bf16[32,8192]{1,0:T(8,128)(2,1)S(1)} %collective-permute-done.26.refs_1_, bf16[32,8192]{1,0:T(8,128)(2,1)S(1)} %collective-permute-done.22.refs_2_, bf16[32,8192]{1,0:T(8,128)(2,1)S(1)} %collective-permute-done.25.refs_3_, ...), custom_call_target="tpu_custom_call" | custom-call | flops 1073741824 | bytes 10485760 | tf_op jit(solution)/shard_map/query/pallas_call | solution.py:244
  144.9 5.3 %attend.3 = (bf16[32,8192]{1,0:T(8,128)(2,1)S(1)}, bf16[32,8192]{1,0:T(8,128)(2,1)S(1)}, bf16[32,8192]{1,0:T(8,128)(2,1)S(1)}, bf16[32,8192]{1,0:T(8,128)(2,1)S(1)}) custom-call(s32[18]{0:T(128)S(1)} %pad_add_fusion.meta_ref, bf16[128,512]{1,0:T(8,128)(2,1)S(1)} %query.5.query_ref, bf16[256,256]{1,0:T(8,128)(2,1)S(1)} %add_convert_fusion.22.refs_0_, ...), custom_call_target="tpu_custom_call" | custom-call | flops 4294967296 | bytes 33554432 | tf_op jit(solution)/shard_map/attend/pallas_call | solution.py:336
  155.2 2.8 %query.7.query_ref = bf16[64,512]{1,0:T(8,128)(2,1)S(1)} custom-call(bf16[32,8192]{1,0:T(8,128)(2,1)S(1)} %collective-permute-done.35.refs_0_, bf16[32,8192]{1,0:T(8,128)(2,1)S(1)} %collective-permute-done.36.refs_1_, bf16[8192,512]{1,0:T(8,128)(2,1)S(1)} %bitcast.15), custom_call_target="tpu_custom_call" | custom-call | flops 536870912 | bytes 9437184 | tf_op jit(solution)/shard_map/query/pallas_call | solution.py:244
  160.1 4.5 %attend.4 = (bf16[32,8192]{1,0:T(8,128)(2,1)S(1)}, bf16[32,8192]{1,0:T(8,128)(2,1)S(1)}) custom-call(s32[18]{0:T(128)S(1)} %pad_add_fusion.meta_ref, bf16[64,512]{1,0:T(8,128)(2,1)S(1)} %query.7.query_ref, bf16[256,256]{1,0:T(8,128)(2,1)S(1)} %add_convert_fusion.22.refs_0_, bf16[256,256]{1,0:T(8,128)(2,1)S(1)} %collective-permute-done.34.refs_1_, ...), custom_call_target="tpu_custom_call" | custom-call | flops 2147483648 | bytes 33554432 | tf_op jit(solution)/shard_map/attend/pallas_call | solution.py:336
  164.6 6.9 %attend.5 = (bf16[64,8192]{1,0:T(8,128)(2,1)S(1)}, bf16[32,8192]{1,0:T(8,128)(2,1)S(1)}, bf16[32,8192]{1,0:T(8,128)(2,1)S(1)}, bf16[32,8192]{1,0:T(8,128)(2,1)S(...) custom-call(s32[18]{0:T(128)S(1)} %pad_add_fusion.meta_ref, ...), custom_call_target="tpu_custom_call" | custom-call | flops 10737418240 | bytes 33554432 | tf_op jit(solution)/shard_map/attend/pallas_call | solution.py:336
  176.4 10.3 %collective-permute-done.39 = bf16[32,8192]{1,0:T(8,128)(2,1)S(1)} collective-permute-done((bf16[32,8192]{1,0:T(8,128)(2,1)S(1)}, bf16[32,8192]{1,0:T(8,128)(2,1)S(1)}, u32[]{:S(2)}, u32[]{:S(2)}) %collective-permute-start.39) | collective-permute-done | bytes 524320 | tf_op jit(solution)/shard_map/ppermute | solution.py:411
  189.1 9.1 %collective-permute-done.45 = bf16[32,8192]{1,0:T(8,128)(2,1)S(1)} collective-permute-done((bf16[32,8192]{1,0:T(8,128)(2,1)S(1)}, bf16[32,8192]{1,0:T(8,128)(2,1)S(1)}, u32[]{:S(2)}, u32[]{:S(2)}) %collective-permute-start.45) | collective-permute-done | bytes 524320 | tf_op jit(solution)/shard_map/ppermute | solution.py:414
  201.4 13.1 %collective-permute-done.43 = bf16[32,8192]{1,0:T(8,128)(2,1)S(1)} collective-permute-done((bf16[32,8192]{1,0:T(8,128)(2,1)S(1)}, bf16[32,8192]{1,0:T(8,128)(2,1)S(1)}, u32[]{:S(2)}, u32[]{:S(2)}) %collective-permute-start.43) | collective-permute-done | bytes 524320 | tf_op jit(solution)/shard_map/ppermute | solution.py:411
  217.0 3.7 %collective-permute-done.48 = bf16[32,8192]{1,0:T(8,128)(2,1)S(1)} collective-permute-done((bf16[32,8192]{1,0:T(8,128)(2,1)S(1)}, bf16[32,8192]{1,0:T(8,128)(2,1)S(1)}, u32[]{:S(2)}, u32[]{:S(2)}) %collective-permute-start.48) | collective-permute-done | bytes 524320 | tf_op jit(solution)/shard_map/ppermute | solution.py:427
  220.7 9.2 %collective-permute-done.47 = bf16[32,8192]{1,0:T(8,128)(2,1)S(1)} collective-permute-done((bf16[32,8192]{1,0:T(8,128)(2,1)S(1)}, bf16[32,8192]{1,0:T(8,128)(2,1)S(1)}, u32[]{:S(2)}, u32[]{:S(2)}) %collective-permute-start.47) | collective-permute-done | bytes 524320 | tf_op jit(solution)/shard_map/ppermute | solution.py:424
  (157 shorter events, 78.5 us)
Async XLA Ops:
  0.0 27.2 %collective-permute-start.3 = (bf16[64,8192]{1,0:T(8,128)(2,1)}, bf16[64,8192]{1,0:T(8,128)(2,1)S(1)}, u32[]{:S(2)}, u32[]{:S(2)}) collective-permute-start(bf16[64,8192]{1,0:T(8,128)(2,1)} %bitcast.21), channel_id=1, source_target_pairs={{2,0},{4,2},{6,4},{7,6},{5,7},{3,5},{1,3},{0,1},{10,8},{12,10},{14... | collective-permute-start | bytes 3145736 | tf_op jit(solution)/shard_map/ppermute | solution.py:414
  3.0 26.3 %collective-permute-start.2 = (bf16[64,8192]{1,0:T(8,128)(2,1)}, bf16[64,8192]{1,0:T(8,128)(2,1)S(1)}, u32[]{:S(2)}, u32[]{:S(2)}) collective-permute-start(bf16[64,8192]{1,0:T(8,128)(2,1)} %bitcast.22), channel_id=1, source_target_pairs={{0,2},{2,4},{4,6},{6,7},{7,5},{5,3},{3,1},{1,0},{8,10},{10,12},{12... | collective-permute-start | bytes 3145736 | tf_op jit(solution)/shard_map/ppermute | solution.py:411
  3.0 28.5 %collective-permute-start.1 = (f32[1]{0:T(128)}, f32[1]{0:T(128)}, u32[]{:S(2)}, u32[]{:S(2)}) collective-permute-start(f32[1]{0:T(128)} %param.16), channel_id=1, source_target_pairs={{0,8},{8,16},{16,24},{24,0},{1,9},{9,17},{17,25},{25,1},{2,10},{10... | collective-permute-start | bytes 20 | tf_op jit(solution)/shard_map/ppermute | solution.py:430
  7.7 28.5 %collective-permute-start.4 = (bf16[160,1024]{1,0:T(8,128)(2,1)S(1)}, bf16[160,1024]{1,0:T(8,128)(2,1)S(1)}, u32[]{:S(2)}, u32[]{:S(2)}) collective-permute-start(bf16[160,1024]{1,0:T(8,128)(2,1)S(1)} %get-tuple-element.89), channel_id=1, source_target_pairs={{0,2},{2,4},{4,6},{6,7},{7,5},{5,3},{3,1},{1,0},{8,10},{10,12},{12... | collective-permute-start | bytes 983048 | tf_op jit(solution)/shard_map/ppermute | solution.py:411
  9.8 26.7 %collective-permute-start.8 = (bf16[160,1024]{1,0:T(8,128)(2,1)S(1)}, bf16[160,1024]{1,0:T(8,128)(2,1)S(1)}, u32[]{:S(2)}, u32[]{:S(2)}) collective-permute-start(bf16[160,1024]{1,0:T(8,128)(2,1)S(1)} %get-tuple-element.94), channel_id=1, source_target_pairs={{2,0},{4,2},{6,4},{7,6},{5,7},{3,5},{1,3},{0,1},{10,8},{12,10},{14... | collective-permute-start | bytes 983048 | tf_op jit(solution)/shard_map/ppermute | solution.py:414
  27.2 16.2 %collective-permute-start.6 = (bf16[160,1024]{1,0:T(8,128)(2,1)S(1)}, bf16[160,1024]{1,0:T(8,128)(2,1)S(1)}, u32[]{:S(2)}, u32[]{:S(2)}) collective-permute-start(bf16[160,1024]{1,0:T(8,128)(2,1)S(1)} %get-tuple-element.92), channel_id=1, source_target_pairs={{0,2},{2,4},{4,6},{6,7},{7,5},{5,3},{3,1},{1,0},{8,10},{10,12},{12... | collective-permute-start | bytes 983048 | tf_op jit(solution)/shard_map/ppermute | solution.py:411
  78.8 25.4 %collective-permute-start.18 = (bf16[64,8192]{1,0:T(8,128)(2,1)S(1)}, bf16[64,8192]{1,0:T(8,128)(2,1)S(1)}, u32[]{:S(2)}, u32[]{:S(2)}) collective-permute-start(bf16[64,8192]{1,0:T(8,128)(2,1)S(1)} %collective-permute-done.2.refs_1_), channel_id=1, source_target_pairs={{0,2},{2,4},{4,6},{6,7},{7,5},{5,3},{3,1},{1,0},{8,10},{10,12},{12... | collective-permute-start | bytes 3145736 | tf_op jit(solution)/shard_map/ppermute | solution.py:411
  79.3 25.7 %collective-permute-start.24 = (bf16[64,8192]{1,0:T(8,128)(2,1)S(1)}, bf16[64,8192]{1,0:T(8,128)(2,1)S(1)}, u32[]{:S(2)}, u32[]{:S(2)}) collective-permute-start(bf16[64,8192]{1,0:T(8,128)(2,1)S(1)} %collective-permute-done.3.refs_2_), channel_id=1, source_target_pairs={{2,0},{4,2},{6,4},{7,6},{5,7},{3,5},{1,3},{0,1},{10,8},{12,10},{14... | collective-permute-start | bytes 3145736 | tf_op jit(solution)/shard_map/ppermute | solution.py:414
  106.4 58.2 %collective-permute-start = (bf16[64,8192]{1,0:T(8,128)(2,1)S(1)}, bf16[64,8192]{1,0:T(8,128)(2,1)S(1)}, u32[]{:S(2)}, u32[]{:S(2)}) collective-permute-start(bf16[64,8192]{1,0:T(8,128)(2,1)S(1)} %bitcast.24), channel_id=1, source_target_pairs={{0,8},{8,16},{16,24},{24,0},{1,9},{9,17},{17,25},{25,1},{2,10},{10... | collective-permute-start | bytes 3145736 | tf_op jit(solution)/shard_map/ppermute | solution.py:430
  121.2 17.2 %collective-permute-start.23 = (bf16[32,8192]{1,0:T(8,128)(2,1)S(1)}, bf16[32,8192]{1,0:T(8,128)(2,1)S(1)}, u32[]{:S(2)}, u32[]{:S(2)}) collective-permute-start(bf16[32,8192]{1,0:T(8,128)(2,1)S(1)} %collective-permute-done.22.refs_2_), channel_id=1, source_target_pairs={{0,2},{2,4},{4,6},{6,7},{7,5},{5,3},{3,1},{1,0},{8,10},{10,12},{12... | collective-permute-start | bytes 1572872 | tf_op jit(solution)/shard_map/ppermute | solution.py:411
  121.8 16.5 %collective-permute-start.26 = (bf16[32,8192]{1,0:T(8,128)(2,1)S(1)}, bf16[32,8192]{1,0:T(8,128)(2,1)S(1)}, u32[]{:S(2)}, u32[]{:S(2)}) collective-permute-start(bf16[32,8192]{1,0:T(8,128)(2,1)S(1)} %collective-permute-done.25.refs_3_), channel_id=1, source_target_pairs={{2,0},{4,2},{6,4},{7,6},{5,7},{3,5},{1,3},{0,1},{10,8},{12,10},{14... | collective-permute-start | bytes 1572872 | tf_op jit(solution)/shard_map/ppermute | solution.py:414
  138.9 16.2 %collective-permute-start.36 = (bf16[32,8192]{1,0:T(8,128)(2,1)S(1)}, bf16[32,8192]{1,0:T(8,128)(2,1)S(1)}, u32[]{:S(2)}, u32[]{:S(2)}) collective-permute-start(bf16[32,8192]{1,0:T(8,128)(2,1)S(1)} %slice.33), channel_id=1, source_target_pairs={{2,0},{4,2},{6,4},{7,6},{5,7},{3,5},{1,3},{0,1},{10,8},{12,10},{14... | collective-permute-start | bytes 1572872 | tf_op jit(solution)/shard_map/ppermute | solution.py:414
  150.2 21.4 %collective-permute-start.38 = (bf16[32,8192]{1,0:T(8,128)(2,1)S(1)}, bf16[32,8192]{1,0:T(8,128)(2,1)S(1)}, u32[]{:S(2)}, u32[]{:S(2)}) collective-permute-start(bf16[32,8192]{1,0:T(8,128)(2,1)S(1)} %get-tuple-element.134), channel_id=1, source_target_pairs={{0,2},{2,4},{4,6},{6,7},{7,5},{5,3},{3,1},{1,0},{8,10},{10,12},{12... | collective-permute-start | bytes 1572872 | tf_op jit(solution)/shard_map/ppermute | solution.py:411
  150.8 21.0 %collective-permute-start.42 = (bf16[32,8192]{1,0:T(8,128)(2,1)S(1)}, bf16[32,8192]{1,0:T(8,128)(2,1)S(1)}, u32[]{:S(2)}, u32[]{:S(2)}) collective-permute-start(bf16[32,8192]{1,0:T(8,128)(2,1)S(1)} %get-tuple-element.148), channel_id=1, source_target_pairs={{2,0},{4,2},{6,4},{7,6},{5,7},{3,5},{1,3},{0,1},{10,8},{12,10},{14... | collective-permute-start | bytes 1572872 | tf_op jit(solution)/shard_map/ppermute | solution.py:414
  158.0 16.0 %collective-permute-start.41 = (bf16[32,8192]{1,0:T(8,128)(2,1)S(1)}, bf16[32,8192]{1,0:T(8,128)(2,1)S(1)}, u32[]{:S(2)}, u32[]{:S(2)}) collective-permute-start(bf16[32,8192]{1,0:T(8,128)(2,1)S(1)} %get-tuple-element.147), channel_id=1, source_target_pairs={{2,0},{4,2},{6,4},{7,6},{5,7},{3,5},{1,3},{0,1},{10,8},{12,10},{14... | collective-permute-start | bytes 1572872 | tf_op jit(solution)/shard_map/ppermute | solution.py:414
  158.6 16.1 %collective-permute-start.40 = (bf16[32,8192]{1,0:T(8,128)(2,1)S(1)}, bf16[32,8192]{1,0:T(8,128)(2,1)S(1)}, u32[]{:S(2)}, u32[]{:S(2)}) collective-permute-start(bf16[32,8192]{1,0:T(8,128)(2,1)S(1)} %get-tuple-element.145), channel_id=1, source_target_pairs={{0,2},{2,4},{4,6},{6,7},{7,5},{5,3},{3,1},{1,0},{8,10},{10,12},{12... | collective-permute-start | bytes 1572872 | tf_op jit(solution)/shard_map/ppermute | solution.py:411
  171.5 26.9 %collective-permute-start.37 = (bf16[64,8192]{1,0:T(8,128)(2,1)S(1)}, bf16[64,8192]{1,0:T(8,128)(2,1)S(1)}, u32[]{:S(2)}, u32[]{:S(2)}) collective-permute-start(bf16[64,8192]{1,0:T(8,128)(2,1)S(1)} %get-tuple-element.141), channel_id=1, source_target_pairs={{0,8},{8,16},{16,24},{24,0},{1,9},{9,17},{17,25},{25,1},{2,10},{10... | collective-permute-start | bytes 3145736 | tf_op jit(solution)/shard_map/ppermute | solution.py:430
  174.1 24.0 %collective-permute-start.45 = (bf16[32,8192]{1,0:T(8,128)(2,1)S(1)}, bf16[32,8192]{1,0:T(8,128)(2,1)S(1)}, u32[]{:S(2)}, u32[]{:S(2)}) collective-permute-start(bf16[32,8192]{1,0:T(8,128)(2,1)S(1)} %add_convert_fusion.9), channel_id=1, source_target_pairs={{2,0},{4,2},{6,4},{7,6},{5,7},{3,5},{1,3},{0,1},{10,8},{12,10},{14... | collective-permute-start | bytes 1572872 | tf_op jit(solution)/shard_map/ppermute | solution.py:414
  174.8 23.4 %collective-permute-start.44 = (bf16[32,8192]{1,0:T(8,128)(2,1)S(1)}, bf16[32,8192]{1,0:T(8,128)(2,1)S(1)}, u32[]{:S(2)}, u32[]{:S(2)}) collective-permute-start(bf16[32,8192]{1,0:T(8,128)(2,1)S(1)} %add_convert_fusion.8), channel_id=1, source_target_pairs={{0,2},{2,4},{4,6},{6,7},{7,5},{5,3},{3,1},{1,0},{8,10},{10,12},{12... | collective-permute-start | bytes 1572872 | tf_op jit(solution)/shard_map/ppermute | solution.py:411
  186.8 27.7 %collective-permute-start.43 = (bf16[32,8192]{1,0:T(8,128)(2,1)S(1)}, bf16[32,8192]{1,0:T(8,128)(2,1)S(1)}, u32[]{:S(2)}, u32[]{:S(2)}) collective-permute-start(bf16[32,8192]{1,0:T(8,128)(2,1)S(1)} %add_convert_fusion.7), channel_id=1, source_target_pairs={{0,2},{2,4},{4,6},{6,7},{7,5},{5,3},{3,1},{1,0},{8,10},{10,12},{12... | collective-permute-start | bytes 1572872 | tf_op jit(solution)/shard_map/ppermute | solution.py:411
  187.0 27.6 %collective-permute-start.50 = (bf16[32,8192]{1,0:T(8,128)(2,1)S(1)}, bf16[32,8192]{1,0:T(8,128)(2,1)S(1)}, u32[]{:S(2)}, u32[]{:S(2)}) collective-permute-start(bf16[32,8192]{1,0:T(8,128)(2,1)S(1)} %add_convert_fusion.6), channel_id=1, source_target_pairs={{2,0},{4,2},{6,4},{7,6},{5,7},{3,5},{1,3},{0,1},{10,8},{12,10},{14... | collective-permute-start | bytes 1572872 | tf_op jit(solution)/shard_map/ppermute | solution.py:414
  198.4 22.3 %collective-permute-start.48 = (bf16[32,8192]{1,0:T(8,128)(2,1)S(1)}, bf16[32,8192]{1,0:T(8,128)(2,1)S(1)}, u32[]{:S(2)}, u32[]{:S(2)}) collective-permute-start(bf16[32,8192]{1,0:T(8,128)(2,1)S(1)} %add_convert_fusion.5), channel_id=1, source_target_pairs={{2,8},{4,10},{6,12},{7,14},{5,15},{3,13},{1,11},{0,9},{10,16},{12,... | collective-permute-start | bytes 1572872 | tf_op jit(solution)/shard_map/ppermute | solution.py:427
  198.9 21.8 %collective-permute-start.49 = (bf16[32,8192]{1,0:T(8,128)(2,1)S(1)}, bf16[32,8192]{1,0:T(8,128)(2,1)S(1)}, u32[]{:S(2)}, u32[]{:S(2)}) collective-permute-start(bf16[32,8192]{1,0:T(8,128)(2,1)S(1)} %add_convert_fusion.4), channel_id=1, source_target_pairs={{0,10},{2,12},{4,14},{6,15},{7,13},{5,11},{3,9},{1,8},{8,18},{10,2... | collective-permute-start | bytes 1572872 | tf_op jit(solution)/shard_map/ppermute | solution.py:424
  214.8 17.1 %collective-permute-start.51 = (bf16[32,8192]{1,0:T(8,128)(2,1)S(1)}, bf16[32,8192]{1,0:T(8,128)(2,1)S(1)}, u32[]{:S(2)}, u32[]{:S(2)}) collective-permute-start(bf16[32,8192]{1,0:T(8,128)(2,1)S(1)} %add_convert_fusion.1), channel_id=1, source_target_pairs={{2,8},{4,10},{6,12},{7,14},{5,15},{3,13},{1,11},{0,9},{10,16},{12,... | collective-permute-start | bytes 1572872 | tf_op jit(solution)/shard_map/ppermute | solution.py:427
  (39 other events, 608.0 us)

commit v16 on v15

--- a/solution.py
+++ b/solution.py
@@ -268,7 +268,6 @@
     kv_rows = SLOTS // sharing
     columns = weight.shape[1]
     wide = min(1024, columns)
-    tall = min(64, width)
 
     def kernel(meta_ref, query_ref, *refs):
         kv_refs, weight_ref = refs[:sharing], refs[sharing]
@@ -277,14 +276,14 @@
         step = pl.program_id(0)
 
         def fetch(index):
-            place = pl.ds(index * tall, tall)
+            place = pl.ds(pl.multiple_of(index * wide, wide), wide)
             return pltpu.make_async_copy(
-                weight_ref.at[place, :], held_ref.at[place, :], sems.at[index]
+                weight_ref.at[:, place], held_ref.at[index], sems.at[index]
             )
 
         @pl.when(step == 0)
         def _():
-            for index in range(width // tall):
+            for index in range(columns // wide):
                 fetch(index).start()
             mine = lax.rem(meta_ref[order_len], sharing)
             for piece in range(sharing):
@@ -320,13 +319,10 @@
                     attended_ref[first : first + text_rows, h * HD : (h + 1) * HD] = result[
                         h * text_rows : (h + 1) * text_rows
                     ]
-            for index in range(width // tall):
-                fetch(index).wait()
-
+
+        fetch(step).wait()
         product = jnp.dot(
-            attended_ref[...],
-            held_ref[:, pl.ds(pl.multiple_of(step * wide, wide), wide)],
-            preferred_element_type=F32,
+            attended_ref[...], held_ref[step], preferred_element_type=F32
         ).astype(BF16)
         first = 0
         for out_ref, size in zip(out_refs, sizes):
@@ -346,8 +342,8 @@
                 pltpu.VMEM((SLOTS, HD), BF16),
                 pltpu.VMEM((SLOTS, HD), BF16),
                 pltpu.VMEM((rows, width), BF16),
-                pltpu.VMEM((width, columns), BF16),
-                pltpu.SemaphoreType.DMA((width // tall,)),
+                pltpu.VMEM((columns // wide, width, wide), BF16),
+                pltpu.SemaphoreType.DMA((columns // wide,)),
             ],
         ),
         out_shape=[jax.ShapeDtypeStruct((size, columns), BF16) for size in sizes],

time: 234 us -> 237 us (1.013)
  Pallas kernels: 46.2 us -> 49.2 us
    pallas_call x3, Pallas kernels: 16.7 us -> 19.7 us  [attend(): pl.pallas_call(kernel, grid_spec=pltpu.PrefetchScalarGridSpec(num_scalar_...]
  transfers between devices with their start and end apart: 52 -> 52, of which waited for: 24 -> 23; matrix products, arithmetic and copies ran while one was open for 2% -> 2% of each run, Pallas kernels for 20% -> 21%
where the time goes in v16:
time: 237 us; the launch traced here: 236 us
  waiting for transfers between devices  127 us (54%)
  starting transfers between devices  51.8 us (22%)
  Pallas kernels  49.2 us (21%)
  other arithmetic  5.3 us (2%)
  local copies, waits for them, and re-layouts  2.54 us (1%)
    ppermute x21, waiting for transfers between devices, up(): return lax.ppermute(value, 'mp', up_pairs)  63.2 us
    ppermute x20, waiting for transfers between devices, down(): return lax.ppermute(value, 'mp', down_pairs)  35.2 us
    ppermute x20, starting transfers between devices, down(): return lax.ppermute(value, 'mp', down_pairs)  31.4 us
    pallas_call x3, Pallas kernels, attend(): pl.pallas_call(kernel, grid_spec=pltpu.PrefetchScalarGridSpec(num_scalar_...  19.7 us
    pallas_call x2, Pallas kernels, project(): pl.pallas_call(kernel, grid_spec=pltpu.PrefetchScalarGridSpec(num_scalar_...  14.5 us
    ppermute x21, starting transfers between devices, up(): return lax.ppermute(value, 'mp', up_pairs)  13.8 us
    pallas_call x4, Pallas kernels, query(): pl.pallas_call(kernel, grid=(width // wide,), in_specs=[pl.BlockSpec(chun...  11.4 us
    ppermute x1, waiting for transfers between devices, local(): lax.ppermute(moving, 'section', [(s, (s + 2) % section_count) for s in ra...  10.8 us
  transfers between devices with their start and end apart: 52, of which 23 were waited for; matrix products, arithmetic and copies ran while one was open for 2% of the time, Pallas kernels for 21%

profile of v16, /device:TPU:0, one launch (start us, length us, event | category | flops | bytes accessed | tf_op | source)
XLA Modules:
  0.0 236.5 jit_solution(15927460193889009652)
XLA Ops:
  0.0 3.0 %collective-permute-start.3 = (bf16[64,8192]{1,0:T(8,128)(2,1)}, bf16[64,8192]{1,0:T(8,128)(2,1)S(1)}, u32[]{:S(2)}, u32[]{:S(2)}) collective-permute-start(bf16[64,8192]{1,0:T(8,128)(2,1)} %bitcast.21), channel_id=1, source_target_pairs={{2,0},{4,2},{6,4},{7,6},{5,7},{3,5},{1,3},{0,1},{10,8},{12,10},{14... | collective-permute-start | bytes 3145736 | tf_op jit(solution)/shard_map/ppermute | solution.py:410
  4.8 2.9 %project.3 = (bf16[160,1024]{1,0:T(8,128)(2,1)S(1)}, bf16[160,1024]{1,0:T(8,128)(2,1)S(1)}) custom-call(s32[10]{0:T(128)S(1)} %get-tuple-element.175.places_ref, bf16[320,960]{1,0:T(8,128)(2,1)S(1)} %copy-done.1, bf16[960,8192]{1,0:T(8,128)(2,1)} %weight_ref.3), custom_call_target="tpu_custom_call" | custom-call | flops 629145600 | bytes 2621440 | tf_op jit(solution)/shard_map/project/pallas_call | solution.py:102
  9.8 11.6 %project.2 = (bf16[160,1024]{1,0:T(8,128)(2,1)S(1)}, bf16[160,1024]{1,0:T(8,128)(2,1)S(1)}, bf16[160,1024]{1,0:T(8,128)(2,1)S(1)}, bf16[160,1024]{1,0:T(8,128)(2...) custom-call(s32[10]{0:T(128)S(1)} %get-tuple-element.175.places_ref,, ...), custom_call_target="tpu_custom_call" | custom-call | flops 4404019200 | bytes 18350080 | tf_op jit(solution)/shard_map/project/pallas_call | solution.py:102
  21.4 5.8 %collective-permute-done.3.refs_2_ = bf16[64,8192]{1,0:T(8,128)(2,1)S(1)} collective-permute-done((bf16[64,8192]{1,0:T(8,128)(2,1)}, bf16[64,8192]{1,0:T(8,128)(2,1)S(1)}, u32[]{:S(2)}, u32[]{:S(2)}) %collective-permute-start.3) | collective-permute-done | bytes 1048608 | tf_op jit(solution)/shard_map/ppermute | solution.py:410
  31.5 4.7 %collective-permute-done.4 = bf16[160,1024]{1,0:T(8,128)(2,1)S(1)} collective-permute-done((bf16[160,1024]{1,0:T(8,128)(2,1)S(1)}, bf16[160,1024]{1,0:T(8,128)(2,1)S(1)}, u32[]{:S(2)}, u32[]{:S(2)}) %collective-permute-start.4) | collective-permute-done | bytes 327712 | tf_op jit(solution)/shard_map/ppermute | solution.py:407
  43.7 6.7 %collective-permute-done.5 = bf16[160,1024]{1,0:T(8,128)(2,1)S(1)} collective-permute-done((bf16[160,1024]{1,0:T(8,128)(2,1)S(1)}, bf16[160,1024]{1,0:T(8,128)(2,1)S(1)}, u32[]{:S(2)}, u32[]{:S(2)}) %collective-permute-start.5) | collective-permute-done | bytes 327712 | tf_op jit(solution)/shard_map/ppermute | solution.py:407
  57.7 6.7 %collective-permute-done.9 = bf16[160,1024]{1,0:T(8,128)(2,1)S(1)} collective-permute-done((bf16[160,1024]{1,0:T(8,128)(2,1)S(1)}, bf16[160,1024]{1,0:T(8,128)(2,1)S(1)}, u32[]{:S(2)}, u32[]{:S(2)}) %collective-permute-start.9) | collective-permute-done | bytes 327712 | tf_op jit(solution)/shard_map/ppermute | solution.py:407
  66.7 4.7 %collective-permute-done.15.refs_4_ = bf16[160,1024]{1,0:T(8,128)(2,1)S(1)} collective-permute-done((bf16[160,1024]{1,0:T(8,128)(2,1)S(1)}, bf16[160,1024]{1,0:T(8,128)(2,1)S(1)}, u32[]{:S(2)}, u32[]{:S(2)}) %collective-permute-start.15) | collective-permute-done | bytes 327712 | tf_op jit(solution)/shard_map/ppermute | solution.py:407
  71.4 4.1 %collective-permute-done.17.refs_5_ = bf16[160,1024]{1,0:T(8,128)(2,1)S(1)} collective-permute-done((bf16[160,1024]{1,0:T(8,128)(2,1)S(1)}, bf16[160,1024]{1,0:T(8,128)(2,1)S(1)}, u32[]{:S(2)}, u32[]{:S(2)}) %collective-permute-start.17) | collective-permute-done | bytes 327712 | tf_op jit(solution)/shard_map/ppermute | solution.py:410
  81.7 10.8 %collective-permute-done.20.refs_2_ = bf16[320,1024]{1,0:T(8,128)(2,1)S(1)} collective-permute-done((bf16[320,1024]{1,0:T(8,128)(2,1)S(1)}, bf16[320,1024]{1,0:T(8,128)(2,1)S(1)}, u32[]{:S(2)}, u32[]{:S(2)}) %collective-permute-start.20) | collective-permute-done | bytes 655392 | tf_op jit(solution)/shard_map/ppermute | solution.py:494
  98.0 6.2 %collective-permute-done.18.refs_0_ = bf16[64,8192]{1,0:T(8,128)(2,1)S(1)} collective-permute-done((bf16[64,8192]{1,0:T(8,128)(2,1)S(1)}, bf16[64,8192]{1,0:T(8,128)(2,1)S(1)}, u32[]{:S(2)}, u32[]{:S(2)}) %collective-permute-start.18) | collective-permute-done | bytes 1048608 | tf_op jit(solution)/shard_map/ppermute | solution.py:407
  108.5 8.5 %collective-permute-done.29 = bf16[256,256]{1,0:T(8,128)(2,1)S(1)} collective-permute-done((bf16[256,256]{1,0:T(8,128)(2,1)S(1)}, bf16[256,256]{1,0:T(8,128)(2,1)S(1)}, u32[]{:S(2)}, u32[]{:S(2)}) %collective-permute-start.29) | collective-permute-done | bytes 131104 | tf_op jit(solution)/shard_map/ppermute | solution.py:410
  127.7 3.0 %query.4 = bf16[192,512]{1,0:T(8,128)(2,1)S(1)} custom-call(bf16[64,8192]{1,0:T(8,128)(2,1)S(1)} %bitcast.25, bf16[64,8192]{1,0:T(8,128)(2,1)S(1)} %collective-permute-done.2.refs_1_, bf16[64,8192]{1,0:T(8,128)(2,1)S(1)} %collective-permute-done.3.refs_2_, bf16[8192,512]{1,0:T(8,128)(2,1)S(1)} %bitcast.12, f32[192,128]{1,0:T(8,128)S(1)} %row_scales.1.refs_4_), custom_call_target="tpu_custom_call" | custom-call | flops 1610612736 | bytes 11534336 | tf_op jit(solution)/shard_map/query/pallas_call | solution.py:244
  130.7 7.6 %collective-permute-done.32 = bf16[256,256]{1,0:T(8,128)(2,1)S(1)} collective-permute-done((bf16[256,256]{1,0:T(8,128)(2,1)S(1)}, bf16[256,256]{1,0:T(8,128)(2,1)S(1)}, u32[]{:S(2)}, u32[]{:S(2)}) %collective-permute-start.32) | collective-permute-done | bytes 131104 | tf_op jit(solution)/shard_map/ppermute | solution.py:407
  141.0 2.8 %query.5.query_ref = bf16[128,512]{1,0:T(8,128)(2,1)S(1)} custom-call(bf16[32,8192]{1,0:T(8,128)(2,1)S(1)} %collective-permute-done.23.refs_0_, bf16[32,8192]{1,0:T(8,128)(2,1)S(1)} %collective-permute-done.26.refs_1_, bf16[32,8192]{1,0:T(8,128)(2,1)S(1)} %collective-permute-done.22.refs_2_, bf16[32,8192]{1,0:T(8,128)(2,1)S(1)} %collective-permute-done.25.refs_3_, ...), custom_call_target="tpu_custom_call" | custom-call | flops 1073741824 | bytes 10485760 | tf_op jit(solution)/shard_map/query/pallas_call | solution.py:244
  144.9 6.3 %attend.3 = (bf16[32,8192]{1,0:T(8,128)(2,1)S(1)}, bf16[32,8192]{1,0:T(8,128)(2,1)S(1)}, bf16[32,8192]{1,0:T(8,128)(2,1)S(1)}, bf16[32,8192]{1,0:T(8,128)(2,1)S(1)}) custom-call(s32[18]{0:T(128)S(1)} %pad_add_fusion.meta_ref, bf16[128,512]{1,0:T(8,128)(2,1)S(1)} %query.5.query_ref, bf16[256,256]{1,0:T(8,128)(2,1)S(1)} %add_convert_fusion.22.refs_0_, ...), custom_call_target="tpu_custom_call" | custom-call | flops 4294967296 | bytes 33554432 | tf_op jit(solution)/shard_map/attend/pallas_call | solution.py:332
  156.1 2.8 %query.7.query_ref = bf16[64,512]{1,0:T(8,128)(2,1)S(1)} custom-call(bf16[32,8192]{1,0:T(8,128)(2,1)S(1)} %collective-permute-done.35.refs_0_, bf16[32,8192]{1,0:T(8,128)(2,1)S(1)} %collective-permute-done.36.refs_1_, bf16[8192,512]{1,0:T(8,128)(2,1)S(1)} %bitcast.15), custom_call_target="tpu_custom_call" | custom-call | flops 536870912 | bytes 9437184 | tf_op jit(solution)/shard_map/query/pallas_call | solution.py:244
  161.0 5.5 %attend.4 = (bf16[32,8192]{1,0:T(8,128)(2,1)S(1)}, bf16[32,8192]{1,0:T(8,128)(2,1)S(1)}) custom-call(s32[18]{0:T(128)S(1)} %pad_add_fusion.meta_ref, bf16[64,512]{1,0:T(8,128)(2,1)S(1)} %query.7.query_ref, bf16[256,256]{1,0:T(8,128)(2,1)S(1)} %add_convert_fusion.22.refs_0_, bf16[256,256]{1,0:T(8,128)(2,1)S(1)} %collective-permute-done.34.refs_1_, ...), custom_call_target="tpu_custom_call" | custom-call | flops 2147483648 | bytes 33554432 | tf_op jit(solution)/shard_map/attend/pallas_call | solution.py:332
  166.5 7.9 %attend.5 = (bf16[64,8192]{1,0:T(8,128)(2,1)S(1)}, bf16[32,8192]{1,0:T(8,128)(2,1)S(1)}, bf16[32,8192]{1,0:T(8,128)(2,1)S(1)}, bf16[32,8192]{1,0:T(8,128)(2,1)S(...) custom-call(s32[18]{0:T(128)S(1)} %pad_add_fusion.meta_ref, ...), custom_call_target="tpu_custom_call" | custom-call | flops 10737418240 | bytes 33554432 | tf_op jit(solution)/shard_map/attend/pallas_call | solution.py:332
  179.2 10.3 %collective-permute-done.39 = bf16[32,8192]{1,0:T(8,128)(2,1)S(1)} collective-permute-done((bf16[32,8192]{1,0:T(8,128)(2,1)S(1)}, bf16[32,8192]{1,0:T(8,128)(2,1)S(1)}, u32[]{:S(2)}, u32[]{:S(2)}) %collective-permute-start.39) | collective-permute-done | bytes 524320 | tf_op jit(solution)/shard_map/ppermute | solution.py:407
  191.9 9.1 %collective-permute-done.45 = bf16[32,8192]{1,0:T(8,128)(2,1)S(1)} collective-permute-done((bf16[32,8192]{1,0:T(8,128)(2,1)S(1)}, bf16[32,8192]{1,0:T(8,128)(2,1)S(1)}, u32[]{:S(2)}, u32[]{:S(2)}) %collective-permute-start.45) | collective-permute-done | bytes 524320 | tf_op jit(solution)/shard_map/ppermute | solution.py:410
  204.3 13.0 %collective-permute-done.43 = bf16[32,8192]{1,0:T(8,128)(2,1)S(1)} collective-permute-done((bf16[32,8192]{1,0:T(8,128)(2,1)S(1)}, bf16[32,8192]{1,0:T(8,128)(2,1)S(1)}, u32[]{:S(2)}, u32[]{:S(2)}) %collective-permute-start.43) | collective-permute-done | bytes 524320 | tf_op jit(solution)/shard_map/ppermute | solution.py:407
  219.8 3.8 %collective-permute-done.48 = bf16[32,8192]{1,0:T(8,128)(2,1)S(1)} collective-permute-done((bf16[32,8192]{1,0:T(8,128)(2,1)S(1)}, bf16[32,8192]{1,0:T(8,128)(2,1)S(1)}, u32[]{:S(2)}, u32[]{:S(2)}) %collective-permute-start.48) | collective-permute-done | bytes 524320 | tf_op jit(solution)/shard_map/ppermute | solution.py:423
  223.6 9.2 %collective-permute-done.47 = bf16[32,8192]{1,0:T(8,128)(2,1)S(1)} collective-permute-done((bf16[32,8192]{1,0:T(8,128)(2,1)S(1)}, bf16[32,8192]{1,0:T(8,128)(2,1)S(1)}, u32[]{:S(2)}, u32[]{:S(2)}) %collective-permute-start.47) | collective-permute-done | bytes 524320 | tf_op jit(solution)/shard_map/ppermute | solution.py:420
  (157 shorter events, 78.4 us)
Async XLA Ops:
  0.0 27.2 %collective-permute-start.3 = (bf16[64,8192]{1,0:T(8,128)(2,1)}, bf16[64,8192]{1,0:T(8,128)(2,1)S(1)}, u32[]{:S(2)}, u32[]{:S(2)}) collective-permute-start(bf16[64,8192]{1,0:T(8,128)(2,1)} %bitcast.21), channel_id=1, source_target_pairs={{2,0},{4,2},{6,4},{7,6},{5,7},{3,5},{1,3},{0,1},{10,8},{12,10},{14... | collective-permute-start | bytes 3145736 | tf_op jit(solution)/shard_map/ppermute | solution.py:410
  3.0 26.3 %collective-permute-start.2 = (bf16[64,8192]{1,0:T(8,128)(2,1)}, bf16[64,8192]{1,0:T(8,128)(2,1)S(1)}, u32[]{:S(2)}, u32[]{:S(2)}) collective-permute-start(bf16[64,8192]{1,0:T(8,128)(2,1)} %bitcast.22), channel_id=1, source_target_pairs={{0,2},{2,4},{4,6},{6,7},{7,5},{5,3},{3,1},{1,0},{8,10},{10,12},{12... | collective-permute-start | bytes 3145736 | tf_op jit(solution)/shard_map/ppermute | solution.py:407
  3.0 28.5 %collective-permute-start.1 = (f32[1]{0:T(128)}, f32[1]{0:T(128)}, u32[]{:S(2)}, u32[]{:S(2)}) collective-permute-start(f32[1]{0:T(128)} %param.16), channel_id=1, source_target_pairs={{0,8},{8,16},{16,24},{24,0},{1,9},{9,17},{17,25},{25,1},{2,10},{10... | collective-permute-start | bytes 20 | tf_op jit(solution)/shard_map/ppermute | solution.py:426
  7.7 28.5 %collective-permute-start.4 = (bf16[160,1024]{1,0:T(8,128)(2,1)S(1)}, bf16[160,1024]{1,0:T(8,128)(2,1)S(1)}, u32[]{:S(2)}, u32[]{:S(2)}) collective-permute-start(bf16[160,1024]{1,0:T(8,128)(2,1)S(1)} %get-tuple-element.89), channel_id=1, source_target_pairs={{0,2},{2,4},{4,6},{6,7},{7,5},{5,3},{3,1},{1,0},{8,10},{10,12},{12... | collective-permute-start | bytes 983048 | tf_op jit(solution)/shard_map/ppermute | solution.py:407
  9.8 26.7 %collective-permute-start.8 = (bf16[160,1024]{1,0:T(8,128)(2,1)S(1)}, bf16[160,1024]{1,0:T(8,128)(2,1)S(1)}, u32[]{:S(2)}, u32[]{:S(2)}) collective-permute-start(bf16[160,1024]{1,0:T(8,128)(2,1)S(1)} %get-tuple-element.94), channel_id=1, source_target_pairs={{2,0},{4,2},{6,4},{7,6},{5,7},{3,5},{1,3},{0,1},{10,8},{12,10},{14... | collective-permute-start | bytes 983048 | tf_op jit(solution)/shard_map/ppermute | solution.py:410
  27.2 16.2 %collective-permute-start.6 = (bf16[160,1024]{1,0:T(8,128)(2,1)S(1)}, bf16[160,1024]{1,0:T(8,128)(2,1)S(1)}, u32[]{:S(2)}, u32[]{:S(2)}) collective-permute-start(bf16[160,1024]{1,0:T(8,128)(2,1)S(1)} %get-tuple-element.92), channel_id=1, source_target_pairs={{0,2},{2,4},{4,6},{6,7},{7,5},{5,3},{3,1},{1,0},{8,10},{10,12},{12... | collective-permute-start | bytes 983048 | tf_op jit(solution)/shard_map/ppermute | solution.py:407
  78.8 25.4 %collective-permute-start.18 = (bf16[64,8192]{1,0:T(8,128)(2,1)S(1)}, bf16[64,8192]{1,0:T(8,128)(2,1)S(1)}, u32[]{:S(2)}, u32[]{:S(2)}) collective-permute-start(bf16[64,8192]{1,0:T(8,128)(2,1)S(1)} %collective-permute-done.2.refs_1_), channel_id=1, source_target_pairs={{0,2},{2,4},{4,6},{6,7},{7,5},{5,3},{3,1},{1,0},{8,10},{10,12},{12... | collective-permute-start | bytes 3145736 | tf_op jit(solution)/shard_map/ppermute | solution.py:407
  79.3 25.7 %collective-permute-start.24 = (bf16[64,8192]{1,0:T(8,128)(2,1)S(1)}, bf16[64,8192]{1,0:T(8,128)(2,1)S(1)}, u32[]{:S(2)}, u32[]{:S(2)}) collective-permute-start(bf16[64,8192]{1,0:T(8,128)(2,1)S(1)} %collective-permute-done.3.refs_2_), channel_id=1, source_target_pairs={{2,0},{4,2},{6,4},{7,6},{5,7},{3,5},{1,3},{0,1},{10,8},{12,10},{14... | collective-permute-start | bytes 3145736 | tf_op jit(solution)/shard_map/ppermute | solution.py:410
  106.4 60.1 %collective-permute-start = (bf16[64,8192]{1,0:T(8,128)(2,1)S(1)}, bf16[64,8192]{1,0:T(8,128)(2,1)S(1)}, u32[]{:S(2)}, u32[]{:S(2)}) collective-permute-start(bf16[64,8192]{1,0:T(8,128)(2,1)S(1)} %bitcast.24), channel_id=1, source_target_pairs={{0,8},{8,16},{16,24},{24,0},{1,9},{9,17},{17,25},{25,1},{2,10},{10... | collective-permute-start | bytes 3145736 | tf_op jit(solution)/shard_map/ppermute | solution.py:426
  121.2 17.2 %collective-permute-start.23 = (bf16[32,8192]{1,0:T(8,128)(2,1)S(1)}, bf16[32,8192]{1,0:T(8,128)(2,1)S(1)}, u32[]{:S(2)}, u32[]{:S(2)}) collective-permute-start(bf16[32,8192]{1,0:T(8,128)(2,1)S(1)} %collective-permute-done.22.refs_2_), channel_id=1, source_target_pairs={{0,2},{2,4},{4,6},{6,7},{7,5},{5,3},{3,1},{1,0},{8,10},{10,12},{12... | collective-permute-start | bytes 1572872 | tf_op jit(solution)/shard_map/ppermute | solution.py:407
  121.8 16.5 %collective-permute-start.26 = (bf16[32,8192]{1,0:T(8,128)(2,1)S(1)}, bf16[32,8192]{1,0:T(8,128)(2,1)S(1)}, u32[]{:S(2)}, u32[]{:S(2)}) collective-permute-start(bf16[32,8192]{1,0:T(8,128)(2,1)S(1)} %collective-permute-done.25.refs_3_), channel_id=1, source_target_pairs={{2,0},{4,2},{6,4},{7,6},{5,7},{3,5},{1,3},{0,1},{10,8},{12,10},{14... | collective-permute-start | bytes 1572872 | tf_op jit(solution)/shard_map/ppermute | solution.py:410
  138.9 17.2 %collective-permute-start.36 = (bf16[32,8192]{1,0:T(8,128)(2,1)S(1)}, bf16[32,8192]{1,0:T(8,128)(2,1)S(1)}, u32[]{:S(2)}, u32[]{:S(2)}) collective-permute-start(bf16[32,8192]{1,0:T(8,128)(2,1)S(1)} %slice.33), channel_id=1, source_target_pairs={{2,0},{4,2},{6,4},{7,6},{5,7},{3,5},{1,3},{0,1},{10,8},{12,10},{14... | collective-permute-start | bytes 1572872 | tf_op jit(solution)/shard_map/ppermute | solution.py:410
  151.2 23.3 %collective-permute-start.38 = (bf16[32,8192]{1,0:T(8,128)(2,1)S(1)}, bf16[32,8192]{1,0:T(8,128)(2,1)S(1)}, u32[]{:S(2)}, u32[]{:S(2)}) collective-permute-start(bf16[32,8192]{1,0:T(8,128)(2,1)S(1)} %get-tuple-element.134), channel_id=1, source_target_pairs={{0,2},{2,4},{4,6},{6,7},{7,5},{5,3},{3,1},{1,0},{8,10},{10,12},{12... | collective-permute-start | bytes 1572872 | tf_op jit(solution)/shard_map/ppermute | solution.py:407
  151.7 22.9 %collective-permute-start.42 = (bf16[32,8192]{1,0:T(8,128)(2,1)S(1)}, bf16[32,8192]{1,0:T(8,128)(2,1)S(1)}, u32[]{:S(2)}, u32[]{:S(2)}) collective-permute-start(bf16[32,8192]{1,0:T(8,128)(2,1)S(1)} %get-tuple-element.148), channel_id=1, source_target_pairs={{2,0},{4,2},{6,4},{7,6},{5,7},{3,5},{1,3},{0,1},{10,8},{12,10},{14... | collective-permute-start | bytes 1572872 | tf_op jit(solution)/shard_map/ppermute | solution.py:410
  158.9 17.9 %collective-permute-start.41 = (bf16[32,8192]{1,0:T(8,128)(2,1)S(1)}, bf16[32,8192]{1,0:T(8,128)(2,1)S(1)}, u32[]{:S(2)}, u32[]{:S(2)}) collective-permute-start(bf16[32,8192]{1,0:T(8,128)(2,1)S(1)} %get-tuple-element.147), channel_id=1, source_target_pairs={{2,0},{4,2},{6,4},{7,6},{5,7},{3,5},{1,3},{0,1},{10,8},{12,10},{14... | collective-permute-start | bytes 1572872 | tf_op jit(solution)/shard_map/ppermute | solution.py:410
  159.6 18.1 %collective-permute-start.40 = (bf16[32,8192]{1,0:T(8,128)(2,1)S(1)}, bf16[32,8192]{1,0:T(8,128)(2,1)S(1)}, u32[]{:S(2)}, u32[]{:S(2)}) collective-permute-start(bf16[32,8192]{1,0:T(8,128)(2,1)S(1)} %get-tuple-element.145), channel_id=1, source_target_pairs={{0,2},{2,4},{4,6},{6,7},{7,5},{5,3},{3,1},{1,0},{8,10},{10,12},{12... | collective-permute-start | bytes 1572872 | tf_op jit(solution)/shard_map/ppermute | solution.py:407
  174.4 26.9 %collective-permute-start.37 = (bf16[64,8192]{1,0:T(8,128)(2,1)S(1)}, bf16[64,8192]{1,0:T(8,128)(2,1)S(1)}, u32[]{:S(2)}, u32[]{:S(2)}) collective-permute-start(bf16[64,8192]{1,0:T(8,128)(2,1)S(1)} %get-tuple-element.141), channel_id=1, source_target_pairs={{0,8},{8,16},{16,24},{24,0},{1,9},{9,17},{17,25},{25,1},{2,10},{10... | collective-permute-start | bytes 3145736 | tf_op jit(solution)/shard_map/ppermute | solution.py:426
  177.0 24.1 %collective-permute-start.45 = (bf16[32,8192]{1,0:T(8,128)(2,1)S(1)}, bf16[32,8192]{1,0:T(8,128)(2,1)S(1)}, u32[]{:S(2)}, u32[]{:S(2)}) collective-permute-start(bf16[32,8192]{1,0:T(8,128)(2,1)S(1)} %add_convert_fusion.9), channel_id=1, source_target_pairs={{2,0},{4,2},{6,4},{7,6},{5,7},{3,5},{1,3},{0,1},{10,8},{12,10},{14... | collective-permute-start | bytes 1572872 | tf_op jit(solution)/shard_map/ppermute | solution.py:410
  177.8 23.4 %collective-permute-start.44 = (bf16[32,8192]{1,0:T(8,128)(2,1)S(1)}, bf16[32,8192]{1,0:T(8,128)(2,1)S(1)}, u32[]{:S(2)}, u32[]{:S(2)}) collective-permute-start(bf16[32,8192]{1,0:T(8,128)(2,1)S(1)} %add_convert_fusion.8), channel_id=1, source_target_pairs={{0,2},{2,4},{4,6},{6,7},{7,5},{5,3},{3,1},{1,0},{8,10},{10,12},{12... | collective-permute-start | bytes 1572872 | tf_op jit(solution)/shard_map/ppermute | solution.py:407
  189.7 27.7 %collective-permute-start.43 = (bf16[32,8192]{1,0:T(8,128)(2,1)S(1)}, bf16[32,8192]{1,0:T(8,128)(2,1)S(1)}, u32[]{:S(2)}, u32[]{:S(2)}) collective-permute-start(bf16[32,8192]{1,0:T(8,128)(2,1)S(1)} %add_convert_fusion.7), channel_id=1, source_target_pairs={{0,2},{2,4},{4,6},{6,7},{7,5},{5,3},{3,1},{1,0},{8,10},{10,12},{12... | collective-permute-start | bytes 1572872 | tf_op jit(solution)/shard_map/ppermute | solution.py:407
  189.9 27.5 %collective-permute-start.50 = (bf16[32,8192]{1,0:T(8,128)(2,1)S(1)}, bf16[32,8192]{1,0:T(8,128)(2,1)S(1)}, u32[]{:S(2)}, u32[]{:S(2)}) collective-permute-start(bf16[32,8192]{1,0:T(8,128)(2,1)S(1)} %add_convert_fusion.6), channel_id=1, source_target_pairs={{2,0},{4,2},{6,4},{7,6},{5,7},{3,5},{1,3},{0,1},{10,8},{12,10},{14... | collective-permute-start | bytes 1572872 | tf_op jit(solution)/shard_map/ppermute | solution.py:410
  201.3 22.3 %collective-permute-start.48 = (bf16[32,8192]{1,0:T(8,128)(2,1)S(1)}, bf16[32,8192]{1,0:T(8,128)(2,1)S(1)}, u32[]{:S(2)}, u32[]{:S(2)}) collective-permute-start(bf16[32,8192]{1,0:T(8,128)(2,1)S(1)} %add_convert_fusion.5), channel_id=1, source_target_pairs={{2,8},{4,10},{6,12},{7,14},{5,15},{3,13},{1,11},{0,9},{10,16},{12,... | collective-permute-start | bytes 1572872 | tf_op jit(solution)/shard_map/ppermute | solution.py:423
  201.7 21.9 %collective-permute-start.49 = (bf16[32,8192]{1,0:T(8,128)(2,1)S(1)}, bf16[32,8192]{1,0:T(8,128)(2,1)S(1)}, u32[]{:S(2)}, u32[]{:S(2)}) collective-permute-start(bf16[32,8192]{1,0:T(8,128)(2,1)S(1)} %add_convert_fusion.4), channel_id=1, source_target_pairs={{0,10},{2,12},{4,14},{6,15},{7,13},{5,11},{3,9},{1,8},{8,18},{10,2... | collective-permute-start | bytes 1572872 | tf_op jit(solution)/shard_map/ppermute | solution.py:420
  217.7 17.2 %collective-permute-start.51 = (bf16[32,8192]{1,0:T(8,128)(2,1)S(1)}, bf16[32,8192]{1,0:T(8,128)(2,1)S(1)}, u32[]{:S(2)}, u32[]{:S(2)}) collective-permute-start(bf16[32,8192]{1,0:T(8,128)(2,1)S(1)} %add_convert_fusion.1), channel_id=1, source_target_pairs={{2,8},{4,10},{6,12},{7,14},{5,15},{3,13},{1,11},{0,9},{10,16},{12,... | collective-permute-start | bytes 1572872 | tf_op jit(solution)/shard_map/ppermute | solution.py:423
  (39 other events, 609.0 us)

commit v17 on v15

--- a/solution.py
+++ b/solution.py
@@ -267,7 +267,7 @@
     sharing = len(kv_pieces)
     kv_rows = SLOTS // sharing
     columns = weight.shape[1]
-    wide = min(1024, columns)
+    wide = min(2048, columns)
     tall = min(64, width)
 
     def kernel(meta_ref, query_ref, *refs):

time: 234 us -> 233 us (level)
  waiting for transfers between devices: 126 us -> 130 us
    ppermute x21, waiting for transfers between devices: 63.3 us -> 66.8 us  [up(): return lax.ppermute(value, 'mp', up_pairs)]
  transfers between devices with their start and end apart: 52 -> 52, of which waited for: 24 -> 24; matrix products, arithmetic and copies ran while one was open for 2% -> 2% of each run, Pallas kernels for 20% -> 19%
where the time goes in v17:
time: 233 us
  waiting for transfers between devices  130 us (56%)
  starting transfers between devices  50.2 us (22%)
  Pallas kernels  44 us (19%)
  other arithmetic  5.3 us (2%)
  local copies, waits for them, and re-layouts  2.54 us (1%)
    ppermute x21, waiting for transfers between devices, up(): return lax.ppermute(value, 'mp', up_pairs)  66.8 us
    ppermute x20, waiting for transfers between devices, down(): return lax.ppermute(value, 'mp', down_pairs)  35 us
    ppermute x20, starting transfers between devices, down(): return lax.ppermute(value, 'mp', down_pairs)  31.5 us
    pallas_call x3, Pallas kernels, attend(): pl.pallas_call(kernel, grid_spec=pltpu.PrefetchScalarGridSpec(num_scalar_...  14.5 us
    pallas_call x2, Pallas kernels, project(): pl.pallas_call(kernel, grid_spec=pltpu.PrefetchScalarGridSpec(num_scalar_...  14.5 us
    ppermute x21, starting transfers between devices, up(): return lax.ppermute(value, 'mp', up_pairs)  13.7 us
    pallas_call x4, Pallas kernels, query(): pl.pallas_call(kernel, grid=(width // wide,), in_specs=[pl.BlockSpec(chun...  11.4 us
    ppermute x1, waiting for transfers between devices, local(): lax.ppermute(moving, 'section', [(s, (s + 2) % section_count) for s in ra...  10.8 us
  transfers between devices with their start and end apart: 52, of which 24 were waited for; matrix products, arithmetic and copies ran while one was open for 2% of the time, Pallas kernels for 19%

profile of v17, /device:TPU:0, one launch (start us, length us, event | category | flops | bytes accessed | tf_op | source)
XLA Modules:
  0.0 232.7 jit_solution(10795906039875861083)
XLA Ops:
  0.0 3.0 %collective-permute-start.3 = (bf16[64,8192]{1,0:T(8,128)(2,1)}, bf16[64,8192]{1,0:T(8,128)(2,1)S(1)}, u32[]{:S(2)}, u32[]{:S(2)}) collective-permute-start(bf16[64,8192]{1,0:T(8,128)(2,1)} %bitcast.21), channel_id=1, source_target_pairs={{2,0},{4,2},{6,4},{7,6},{5,7},{3,5},{1,3},{0,1},{10,8},{12,10},{14... | collective-permute-start | bytes 3145736 | tf_op jit(solution)/shard_map/ppermute | solution.py:414
  4.8 2.9 %project.3 = (bf16[160,1024]{1,0:T(8,128)(2,1)S(1)}, bf16[160,1024]{1,0:T(8,128)(2,1)S(1)}) custom-call(s32[10]{0:T(128)S(1)} %get-tuple-element.175.places_ref, bf16[320,960]{1,0:T(8,128)(2,1)S(1)} %copy-done.1, bf16[960,8192]{1,0:T(8,128)(2,1)} %weight_ref.3), custom_call_target="tpu_custom_call" | custom-call | flops 629145600 | bytes 2621440 | tf_op jit(solution)/shard_map/project/pallas_call | solution.py:102
  9.8 11.6 %project.2 = (bf16[160,1024]{1,0:T(8,128)(2,1)S(1)}, bf16[160,1024]{1,0:T(8,128)(2,1)S(1)}, bf16[160,1024]{1,0:T(8,128)(2,1)S(1)}, bf16[160,1024]{1,0:T(8,128)(2...) custom-call(s32[10]{0:T(128)S(1)} %get-tuple-element.175.places_ref,, ...), custom_call_target="tpu_custom_call" | custom-call | flops 4404019200 | bytes 18350080 | tf_op jit(solution)/shard_map/project/pallas_call | solution.py:102
  21.4 5.8 %collective-permute-done.3.refs_2_ = bf16[64,8192]{1,0:T(8,128)(2,1)S(1)} collective-permute-done((bf16[64,8192]{1,0:T(8,128)(2,1)}, bf16[64,8192]{1,0:T(8,128)(2,1)S(1)}, u32[]{:S(2)}, u32[]{:S(2)}) %collective-permute-start.3) | collective-permute-done | bytes 1048608 | tf_op jit(solution)/shard_map/ppermute | solution.py:414
  31.5 4.7 %collective-permute-done.4 = bf16[160,1024]{1,0:T(8,128)(2,1)S(1)} collective-permute-done((bf16[160,1024]{1,0:T(8,128)(2,1)S(1)}, bf16[160,1024]{1,0:T(8,128)(2,1)S(1)}, u32[]{:S(2)}, u32[]{:S(2)}) %collective-permute-start.4) | collective-permute-done | bytes 327712 | tf_op jit(solution)/shard_map/ppermute | solution.py:411
  43.7 6.7 %collective-permute-done.5 = bf16[160,1024]{1,0:T(8,128)(2,1)S(1)} collective-permute-done((bf16[160,1024]{1,0:T(8,128)(2,1)S(1)}, bf16[160,1024]{1,0:T(8,128)(2,1)S(1)}, u32[]{:S(2)}, u32[]{:S(2)}) %collective-permute-start.5) | collective-permute-done | bytes 327712 | tf_op jit(solution)/shard_map/ppermute | solution.py:411
  57.7 6.7 %collective-permute-done.9 = bf16[160,1024]{1,0:T(8,128)(2,1)S(1)} collective-permute-done((bf16[160,1024]{1,0:T(8,128)(2,1)S(1)}, bf16[160,1024]{1,0:T(8,128)(2,1)S(1)}, u32[]{:S(2)}, u32[]{:S(2)}) %collective-permute-start.9) | collective-permute-done | bytes 327712 | tf_op jit(solution)/shard_map/ppermute | solution.py:411
  66.7 4.7 %collective-permute-done.15.refs_4_ = bf16[160,1024]{1,0:T(8,128)(2,1)S(1)} collective-permute-done((bf16[160,1024]{1,0:T(8,128)(2,1)S(1)}, bf16[160,1024]{1,0:T(8,128)(2,1)S(1)}, u32[]{:S(2)}, u32[]{:S(2)}) %collective-permute-start.15) | collective-permute-done | bytes 327712 | tf_op jit(solution)/shard_map/ppermute | solution.py:411
  71.4 4.1 %collective-permute-done.17.refs_5_ = bf16[160,1024]{1,0:T(8,128)(2,1)S(1)} collective-permute-done((bf16[160,1024]{1,0:T(8,128)(2,1)S(1)}, bf16[160,1024]{1,0:T(8,128)(2,1)S(1)}, u32[]{:S(2)}, u32[]{:S(2)}) %collective-permute-start.17) | collective-permute-done | bytes 327712 | tf_op jit(solution)/shard_map/ppermute | solution.py:414
  81.7 10.8 %collective-permute-done.20.refs_2_ = bf16[320,1024]{1,0:T(8,128)(2,1)S(1)} collective-permute-done((bf16[320,1024]{1,0:T(8,128)(2,1)S(1)}, bf16[320,1024]{1,0:T(8,128)(2,1)S(1)}, u32[]{:S(2)}, u32[]{:S(2)}) %collective-permute-start.20) | collective-permute-done | bytes 655392 | tf_op jit(solution)/shard_map/ppermute | solution.py:498
  98.0 6.2 %collective-permute-done.18.refs_0_ = bf16[64,8192]{1,0:T(8,128)(2,1)S(1)} collective-permute-done((bf16[64,8192]{1,0:T(8,128)(2,1)S(1)}, bf16[64,8192]{1,0:T(8,128)(2,1)S(1)}, u32[]{:S(2)}, u32[]{:S(2)}) %collective-permute-start.18) | collective-permute-done | bytes 1048608 | tf_op jit(solution)/shard_map/ppermute | solution.py:411
  108.5 8.5 %collective-permute-done.29 = bf16[256,256]{1,0:T(8,128)(2,1)S(1)} collective-permute-done((bf16[256,256]{1,0:T(8,128)(2,1)S(1)}, bf16[256,256]{1,0:T(8,128)(2,1)S(1)}, u32[]{:S(2)}, u32[]{:S(2)}) %collective-permute-start.29) | collective-permute-done | bytes 131104 | tf_op jit(solution)/shard_map/ppermute | solution.py:414
  127.7 3.0 %query.4 = bf16[192,512]{1,0:T(8,128)(2,1)S(1)} custom-call(bf16[64,8192]{1,0:T(8,128)(2,1)S(1)} %bitcast.25, bf16[64,8192]{1,0:T(8,128)(2,1)S(1)} %collective-permute-done.2.refs_1_, bf16[64,8192]{1,0:T(8,128)(2,1)S(1)} %collective-permute-done.3.refs_2_, bf16[8192,512]{1,0:T(8,128)(2,1)S(1)} %bitcast.12, f32[192,128]{1,0:T(8,128)S(1)} %row_scales.1.refs_4_), custom_call_target="tpu_custom_call" | custom-call | flops 1610612736 | bytes 11534336 | tf_op jit(solution)/shard_map/query/pallas_call | solution.py:244
  130.7 7.6 %collective-permute-done.32 = bf16[256,256]{1,0:T(8,128)(2,1)S(1)} collective-permute-done((bf16[256,256]{1,0:T(8,128)(2,1)S(1)}, bf16[256,256]{1,0:T(8,128)(2,1)S(1)}, u32[]{:S(2)}, u32[]{:S(2)}) %collective-permute-start.32) | collective-permute-done | bytes 131104 | tf_op jit(solution)/shard_map/ppermute | solution.py:411
  141.0 2.8 %query.5.query_ref = bf16[128,512]{1,0:T(8,128)(2,1)S(1)} custom-call(bf16[32,8192]{1,0:T(8,128)(2,1)S(1)} %collective-permute-done.23.refs_0_, bf16[32,8192]{1,0:T(8,128)(2,1)S(1)} %collective-permute-done.26.refs_1_, bf16[32,8192]{1,0:T(8,128)(2,1)S(1)} %collective-permute-done.22.refs_2_, bf16[32,8192]{1,0:T(8,128)(2,1)S(1)} %collective-permute-done.25.refs_3_, ...), custom_call_target="tpu_custom_call" | custom-call | flops 1073741824 | bytes 10485760 | tf_op jit(solution)/shard_map/query/pallas_call | solution.py:244
  144.9 4.5 %attend.3 = (bf16[32,8192]{1,0:T(8,128)(2,1)S(1)}, bf16[32,8192]{1,0:T(8,128)(2,1)S(1)}, bf16[32,8192]{1,0:T(8,128)(2,1)S(1)}, bf16[32,8192]{1,0:T(8,128)(2,1)S(1)}) custom-call(s32[18]{0:T(128)S(1)} %pad_add_fusion.meta_ref, bf16[128,512]{1,0:T(8,128)(2,1)S(1)} %query.5.query_ref, bf16[256,256]{1,0:T(8,128)(2,1)S(1)} %add_convert_fusion.22.refs_0_, ...), custom_call_target="tpu_custom_call" | custom-call | flops 4294967296 | bytes 33554432 | tf_op jit(solution)/shard_map/attend/pallas_call | solution.py:336
  156.0 2.8 %query.7.query_ref = bf16[64,512]{1,0:T(8,128)(2,1)S(1)} custom-call(bf16[32,8192]{1,0:T(8,128)(2,1)S(1)} %collective-permute-done.35.refs_0_, bf16[32,8192]{1,0:T(8,128)(2,1)S(1)} %collective-permute-done.36.refs_1_, bf16[8192,512]{1,0:T(8,128)(2,1)S(1)} %bitcast.15), custom_call_target="tpu_custom_call" | custom-call | flops 536870912 | bytes 9437184 | tf_op jit(solution)/shard_map/query/pallas_call | solution.py:244
  160.9 4.0 %attend.4 = (bf16[32,8192]{1,0:T(8,128)(2,1)S(1)}, bf16[32,8192]{1,0:T(8,128)(2,1)S(1)}) custom-call(s32[18]{0:T(128)S(1)} %pad_add_fusion.meta_ref, bf16[64,512]{1,0:T(8,128)(2,1)S(1)} %query.7.query_ref, bf16[256,256]{1,0:T(8,128)(2,1)S(1)} %add_convert_fusion.22.refs_0_, bf16[256,256]{1,0:T(8,128)(2,1)S(1)} %collective-permute-done.34.refs_1_, ...), custom_call_target="tpu_custom_call" | custom-call | flops 2147483648 | bytes 33554432 | tf_op jit(solution)/shard_map/attend/pallas_call | solution.py:336
  164.9 6.0 %attend.5 = (bf16[64,8192]{1,0:T(8,128)(2,1)S(1)}, bf16[32,8192]{1,0:T(8,128)(2,1)S(1)}, bf16[32,8192]{1,0:T(8,128)(2,1)S(1)}, bf16[32,8192]{1,0:T(8,128)(2,1)S(...) custom-call(s32[18]{0:T(128)S(1)} %pad_add_fusion.meta_ref, ...), custom_call_target="tpu_custom_call" | custom-call | flops 10737418240 | bytes 33554432 | tf_op jit(solution)/shard_map/attend/pallas_call | solution.py:336
  175.8 10.3 %collective-permute-done.39 = bf16[32,8192]{1,0:T(8,128)(2,1)S(1)} collective-permute-done((bf16[32,8192]{1,0:T(8,128)(2,1)S(1)}, bf16[32,8192]{1,0:T(8,128)(2,1)S(1)}, u32[]{:S(2)}, u32[]{:S(2)}) %collective-permute-start.39) | collective-permute-done | bytes 524320 | tf_op jit(solution)/shard_map/ppermute | solution.py:411
  188.4 8.9 %collective-permute-done.45 = bf16[32,8192]{1,0:T(8,128)(2,1)S(1)} collective-permute-done((bf16[32,8192]{1,0:T(8,128)(2,1)S(1)}, bf16[32,8192]{1,0:T(8,128)(2,1)S(1)}, u32[]{:S(2)}, u32[]{:S(2)}) %collective-permute-start.45) | collective-permute-done | bytes 524320 | tf_op jit(solution)/shard_map/ppermute | solution.py:414
  198.9 15.0 %collective-permute-done.43 = bf16[32,8192]{1,0:T(8,128)(2,1)S(1)} collective-permute-done((bf16[32,8192]{1,0:T(8,128)(2,1)S(1)}, bf16[32,8192]{1,0:T(8,128)(2,1)S(1)}, u32[]{:S(2)}, u32[]{:S(2)}) %collective-permute-start.43) | collective-permute-done | bytes 524320 | tf_op jit(solution)/shard_map/ppermute | solution.py:411
  216.4 4.1 %collective-permute-done.48 = bf16[32,8192]{1,0:T(8,128)(2,1)S(1)} collective-permute-done((bf16[32,8192]{1,0:T(8,128)(2,1)S(1)}, bf16[32,8192]{1,0:T(8,128)(2,1)S(1)}, u32[]{:S(2)}, u32[]{:S(2)}) %collective-permute-start.48) | collective-permute-done | bytes 524320 | tf_op jit(solution)/shard_map/ppermute | solution.py:427
  220.4 8.9 %collective-permute-done.47 = bf16[32,8192]{1,0:T(8,128)(2,1)S(1)} collective-permute-done((bf16[32,8192]{1,0:T(8,128)(2,1)S(1)}, bf16[32,8192]{1,0:T(8,128)(2,1)S(1)}, u32[]{:S(2)}, u32[]{:S(2)}) %collective-permute-start.47) | collective-permute-done | bytes 524320 | tf_op jit(solution)/shard_map/ppermute | solution.py:424
  (157 shorter events, 78.1 us)
Async XLA Ops:
  0.0 27.2 %collective-permute-start.3 = (bf16[64,8192]{1,0:T(8,128)(2,1)}, bf16[64,8192]{1,0:T(8,128)(2,1)S(1)}, u32[]{:S(2)}, u32[]{:S(2)}) collective-permute-start(bf16[64,8192]{1,0:T(8,128)(2,1)} %bitcast.21), channel_id=1, source_target_pairs={{2,0},{4,2},{6,4},{7,6},{5,7},{3,5},{1,3},{0,1},{10,8},{12,10},{14... | collective-permute-start | bytes 3145736 | tf_op jit(solution)/shard_map/ppermute | solution.py:414
  3.0 26.3 %collective-permute-start.2 = (bf16[64,8192]{1,0:T(8,128)(2,1)}, bf16[64,8192]{1,0:T(8,128)(2,1)S(1)}, u32[]{:S(2)}, u32[]{:S(2)}) collective-permute-start(bf16[64,8192]{1,0:T(8,128)(2,1)} %bitcast.22), channel_id=1, source_target_pairs={{0,2},{2,4},{4,6},{6,7},{7,5},{5,3},{3,1},{1,0},{8,10},{10,12},{12... | collective-permute-start | bytes 3145736 | tf_op jit(solution)/shard_map/ppermute | solution.py:411
  3.0 28.5 %collective-permute-start.1 = (f32[1]{0:T(128)}, f32[1]{0:T(128)}, u32[]{:S(2)}, u32[]{:S(2)}) collective-permute-start(f32[1]{0:T(128)} %param.16), channel_id=1, source_target_pairs={{0,8},{8,16},{16,24},{24,0},{1,9},{9,17},{17,25},{25,1},{2,10},{10... | collective-permute-start | bytes 20 | tf_op jit(solution)/shard_map/ppermute | solution.py:430
  7.7 28.5 %collective-permute-start.4 = (bf16[160,1024]{1,0:T(8,128)(2,1)S(1)}, bf16[160,1024]{1,0:T(8,128)(2,1)S(1)}, u32[]{:S(2)}, u32[]{:S(2)}) collective-permute-start(bf16[160,1024]{1,0:T(8,128)(2,1)S(1)} %get-tuple-element.89), channel_id=1, source_target_pairs={{0,2},{2,4},{4,6},{6,7},{7,5},{5,3},{3,1},{1,0},{8,10},{10,12},{12... | collective-permute-start | bytes 983048 | tf_op jit(solution)/shard_map/ppermute | solution.py:411
  9.8 26.7 %collective-permute-start.8 = (bf16[160,1024]{1,0:T(8,128)(2,1)S(1)}, bf16[160,1024]{1,0:T(8,128)(2,1)S(1)}, u32[]{:S(2)}, u32[]{:S(2)}) collective-permute-start(bf16[160,1024]{1,0:T(8,128)(2,1)S(1)} %get-tuple-element.94), channel_id=1, source_target_pairs={{2,0},{4,2},{6,4},{7,6},{5,7},{3,5},{1,3},{0,1},{10,8},{12,10},{14... | collective-permute-start | bytes 983048 | tf_op jit(solution)/shard_map/ppermute | solution.py:414
  27.2 16.2 %collective-permute-start.6 = (bf16[160,1024]{1,0:T(8,128)(2,1)S(1)}, bf16[160,1024]{1,0:T(8,128)(2,1)S(1)}, u32[]{:S(2)}, u32[]{:S(2)}) collective-permute-start(bf16[160,1024]{1,0:T(8,128)(2,1)S(1)} %get-tuple-element.92), channel_id=1, source_target_pairs={{0,2},{2,4},{4,6},{6,7},{7,5},{5,3},{3,1},{1,0},{8,10},{10,12},{12... | collective-permute-start | bytes 983048 | tf_op jit(solution)/shard_map/ppermute | solution.py:411
  55.4 16.0 %collective-permute-start.14 = (bf16[160,1024]{1,0:T(8,128)(2,1)S(1)}, bf16[160,1024]{1,0:T(8,128)(2,1)S(1)}, u32[]{:S(2)}, u32[]{:S(2)}) collective-permute-start(bf16[160,1024]{1,0:T(8,128)(2,1)S(1)} %add_convert_fusion.15), channel_id=1, source_target_pairs={{2,0},{4,2},{6,4},{7,6},{5,7},{3,5},{1,3},{0,1},{10,8},{12,10},{14... | collective-permute-start | bytes 983048 | tf_op jit(solution)/shard_map/ppermute | solution.py:414
  78.8 25.4 %collective-permute-start.18 = (bf16[64,8192]{1,0:T(8,128)(2,1)S(1)}, bf16[64,8192]{1,0:T(8,128)(2,1)S(1)}, u32[]{:S(2)}, u32[]{:S(2)}) collective-permute-start(bf16[64,8192]{1,0:T(8,128)(2,1)S(1)} %collective-permute-done.2.refs_1_), channel_id=1, source_target_pairs={{0,2},{2,4},{4,6},{6,7},{7,5},{5,3},{3,1},{1,0},{8,10},{10,12},{12... | collective-permute-start | bytes 3145736 | tf_op jit(solution)/shard_map/ppermute | solution.py:411
  79.3 25.7 %collective-permute-start.24 = (bf16[64,8192]{1,0:T(8,128)(2,1)S(1)}, bf16[64,8192]{1,0:T(8,128)(2,1)S(1)}, u32[]{:S(2)}, u32[]{:S(2)}) collective-permute-start(bf16[64,8192]{1,0:T(8,128)(2,1)S(1)} %collective-permute-done.3.refs_2_), channel_id=1, source_target_pairs={{2,0},{4,2},{6,4},{7,6},{5,7},{3,5},{1,3},{0,1},{10,8},{12,10},{14... | collective-permute-start | bytes 3145736 | tf_op jit(solution)/shard_map/ppermute | solution.py:414
  106.4 58.5 %collective-permute-start = (bf16[64,8192]{1,0:T(8,128)(2,1)S(1)}, bf16[64,8192]{1,0:T(8,128)(2,1)S(1)}, u32[]{:S(2)}, u32[]{:S(2)}) collective-permute-start(bf16[64,8192]{1,0:T(8,128)(2,1)S(1)} %bitcast.24), channel_id=1, source_target_pairs={{0,8},{8,16},{16,24},{24,0},{1,9},{9,17},{17,25},{25,1},{2,10},{10... | collective-permute-start | bytes 3145736 | tf_op jit(solution)/shard_map/ppermute | solution.py:430
  121.2 17.2 %collective-permute-start.23 = (bf16[32,8192]{1,0:T(8,128)(2,1)S(1)}, bf16[32,8192]{1,0:T(8,128)(2,1)S(1)}, u32[]{:S(2)}, u32[]{:S(2)}) collective-permute-start(bf16[32,8192]{1,0:T(8,128)(2,1)S(1)} %collective-permute-done.22.refs_2_), channel_id=1, source_target_pairs={{0,2},{2,4},{4,6},{6,7},{7,5},{5,3},{3,1},{1,0},{8,10},{10,12},{12... | collective-permute-start | bytes 1572872 | tf_op jit(solution)/shard_map/ppermute | solution.py:411
  121.8 16.5 %collective-permute-start.26 = (bf16[32,8192]{1,0:T(8,128)(2,1)S(1)}, bf16[32,8192]{1,0:T(8,128)(2,1)S(1)}, u32[]{:S(2)}, u32[]{:S(2)}) collective-permute-start(bf16[32,8192]{1,0:T(8,128)(2,1)S(1)} %collective-permute-done.25.refs_3_), channel_id=1, source_target_pairs={{2,0},{4,2},{6,4},{7,6},{5,7},{3,5},{1,3},{0,1},{10,8},{12,10},{14... | collective-permute-start | bytes 1572872 | tf_op jit(solution)/shard_map/ppermute | solution.py:414
  138.9 15.4 %collective-permute-start.36 = (bf16[32,8192]{1,0:T(8,128)(2,1)S(1)}, bf16[32,8192]{1,0:T(8,128)(2,1)S(1)}, u32[]{:S(2)}, u32[]{:S(2)}) collective-permute-start(bf16[32,8192]{1,0:T(8,128)(2,1)S(1)} %slice.33), channel_id=1, source_target_pairs={{2,0},{4,2},{6,4},{7,6},{5,7},{3,5},{1,3},{0,1},{10,8},{12,10},{14... | collective-permute-start | bytes 1572872 | tf_op jit(solution)/shard_map/ppermute | solution.py:414
  149.4 21.6 %collective-permute-start.38 = (bf16[32,8192]{1,0:T(8,128)(2,1)S(1)}, bf16[32,8192]{1,0:T(8,128)(2,1)S(1)}, u32[]{:S(2)}, u32[]{:S(2)}) collective-permute-start(bf16[32,8192]{1,0:T(8,128)(2,1)S(1)} %get-tuple-element.134), channel_id=1, source_target_pairs={{0,2},{2,4},{4,6},{6,7},{7,5},{5,3},{3,1},{1,0},{8,10},{10,12},{12... | collective-permute-start | bytes 1572872 | tf_op jit(solution)/shard_map/ppermute | solution.py:411
  150.0 21.2 %collective-permute-start.42 = (bf16[32,8192]{1,0:T(8,128)(2,1)S(1)}, bf16[32,8192]{1,0:T(8,128)(2,1)S(1)}, u32[]{:S(2)}, u32[]{:S(2)}) collective-permute-start(bf16[32,8192]{1,0:T(8,128)(2,1)S(1)} %get-tuple-element.148), channel_id=1, source_target_pairs={{2,0},{4,2},{6,4},{7,6},{5,7},{3,5},{1,3},{0,1},{10,8},{12,10},{14... | collective-permute-start | bytes 1572872 | tf_op jit(solution)/shard_map/ppermute | solution.py:414
  158.8 15.4 %collective-permute-start.40 = (bf16[32,8192]{1,0:T(8,128)(2,1)S(1)}, bf16[32,8192]{1,0:T(8,128)(2,1)S(1)}, u32[]{:S(2)}, u32[]{:S(2)}) collective-permute-start(bf16[32,8192]{1,0:T(8,128)(2,1)S(1)} %get-tuple-element.145), channel_id=1, source_target_pairs={{0,2},{2,4},{4,6},{6,7},{7,5},{5,3},{3,1},{1,0},{8,10},{10,12},{12... | collective-permute-start | bytes 1572872 | tf_op jit(solution)/shard_map/ppermute | solution.py:411
  170.9 26.7 %collective-permute-start.37 = (bf16[64,8192]{1,0:T(8,128)(2,1)S(1)}, bf16[64,8192]{1,0:T(8,128)(2,1)S(1)}, u32[]{:S(2)}, u32[]{:S(2)}) collective-permute-start(bf16[64,8192]{1,0:T(8,128)(2,1)S(1)} %get-tuple-element.141), channel_id=1, source_target_pairs={{0,8},{8,16},{16,24},{24,0},{1,9},{9,17},{17,25},{25,1},{2,10},{10... | collective-permute-start | bytes 3145736 | tf_op jit(solution)/shard_map/ppermute | solution.py:430
  173.5 23.8 %collective-permute-start.45 = (bf16[32,8192]{1,0:T(8,128)(2,1)S(1)}, bf16[32,8192]{1,0:T(8,128)(2,1)S(1)}, u32[]{:S(2)}, u32[]{:S(2)}) collective-permute-start(bf16[32,8192]{1,0:T(8,128)(2,1)S(1)} %add_convert_fusion.9), channel_id=1, source_target_pairs={{2,0},{4,2},{6,4},{7,6},{5,7},{3,5},{1,3},{0,1},{10,8},{12,10},{14... | collective-permute-start | bytes 1572872 | tf_op jit(solution)/shard_map/ppermute | solution.py:414
  174.4 23.1 %collective-permute-start.44 = (bf16[32,8192]{1,0:T(8,128)(2,1)S(1)}, bf16[32,8192]{1,0:T(8,128)(2,1)S(1)}, u32[]{:S(2)}, u32[]{:S(2)}) collective-permute-start(bf16[32,8192]{1,0:T(8,128)(2,1)S(1)} %add_convert_fusion.8), channel_id=1, source_target_pairs={{0,2},{2,4},{4,6},{6,7},{7,5},{5,3},{3,1},{1,0},{8,10},{10,12},{12... | collective-permute-start | bytes 1572872 | tf_op jit(solution)/shard_map/ppermute | solution.py:411
  186.2 27.7 %collective-permute-start.43 = (bf16[32,8192]{1,0:T(8,128)(2,1)S(1)}, bf16[32,8192]{1,0:T(8,128)(2,1)S(1)}, u32[]{:S(2)}, u32[]{:S(2)}) collective-permute-start(bf16[32,8192]{1,0:T(8,128)(2,1)S(1)} %add_convert_fusion.7), channel_id=1, source_target_pairs={{0,2},{2,4},{4,6},{6,7},{7,5},{5,3},{3,1},{1,0},{8,10},{10,12},{12... | collective-permute-start | bytes 1572872 | tf_op jit(solution)/shard_map/ppermute | solution.py:411
  186.4 27.6 %collective-permute-start.50 = (bf16[32,8192]{1,0:T(8,128)(2,1)S(1)}, bf16[32,8192]{1,0:T(8,128)(2,1)S(1)}, u32[]{:S(2)}, u32[]{:S(2)}) collective-permute-start(bf16[32,8192]{1,0:T(8,128)(2,1)S(1)} %add_convert_fusion.6), channel_id=1, source_target_pairs={{2,0},{4,2},{6,4},{7,6},{5,7},{3,5},{1,3},{0,1},{10,8},{12,10},{14... | collective-permute-start | bytes 1572872 | tf_op jit(solution)/shard_map/ppermute | solution.py:414
  197.6 22.8 %collective-permute-start.48 = (bf16[32,8192]{1,0:T(8,128)(2,1)S(1)}, bf16[32,8192]{1,0:T(8,128)(2,1)S(1)}, u32[]{:S(2)}, u32[]{:S(2)}) collective-permute-start(bf16[32,8192]{1,0:T(8,128)(2,1)S(1)} %add_convert_fusion.5), channel_id=1, source_target_pairs={{2,8},{4,10},{6,12},{7,14},{5,15},{3,13},{1,11},{0,9},{10,16},{12,... | collective-permute-start | bytes 1572872 | tf_op jit(solution)/shard_map/ppermute | solution.py:427
  198.3 22.2 %collective-permute-start.49 = (bf16[32,8192]{1,0:T(8,128)(2,1)S(1)}, bf16[32,8192]{1,0:T(8,128)(2,1)S(1)}, u32[]{:S(2)}, u32[]{:S(2)}) collective-permute-start(bf16[32,8192]{1,0:T(8,128)(2,1)S(1)} %add_convert_fusion.4), channel_id=1, source_target_pairs={{0,10},{2,12},{4,14},{6,15},{7,13},{5,11},{3,9},{1,8},{8,18},{10,2... | collective-permute-start | bytes 1572872 | tf_op jit(solution)/shard_map/ppermute | solution.py:424
  214.2 16.9 %collective-permute-start.51 = (bf16[32,8192]{1,0:T(8,128)(2,1)S(1)}, bf16[32,8192]{1,0:T(8,128)(2,1)S(1)}, u32[]{:S(2)}, u32[]{:S(2)}) collective-permute-start(bf16[32,8192]{1,0:T(8,128)(2,1)S(1)} %add_convert_fusion.1), channel_id=1, source_target_pairs={{2,8},{4,10},{6,12},{7,14},{5,15},{3,13},{1,11},{0,9},{10,16},{12,... | collective-permute-start | bytes 1572872 | tf_op jit(solution)/shard_map/ppermute | solution.py:427
  (39 other events, 608.0 us)
